TPU v7x, 128 devices: a whole 4x4x4 slice. The times are simulated.
128 devices in a mesh: grp: 4 (over z), dev: 32 (over x, y, core).
Axes of the slice: x: 4, y: 4, z: 4, core: 2. Of those that a mesh axis runs over, the one named last changes fastest.
Arguments:
- tokens: bfloat16 [512, 7168], P(('grp', 'dev')), may hold values from -6 to 6
- expert_ids: int32 [512, 8], P(('grp', 'dev')), may hold values from 0 to 31, all different within a row; in each aligned block of 4 rows (0 to 3, 4 to 7, ...) at most 2 rows name the same one
- route_weights: float32 [512, 8], P(('grp', 'dev')), may hold values from 0.1 to 0.6
- gate_weight: bfloat16 [32, 7168, 2048], P('dev', None, 'grp'), may hold values from -0.0625 to 0.0625
- up_weight: bfloat16 [32, 7168, 2048], P('dev', None, 'grp'), may hold values from -0.0625 to 0.0625
- down_weight: bfloat16 [32, 2048, 7168], P('dev', 'grp'), may hold values from -0.125 to 0.125
Outputs:
- mixed: bfloat16 [512, 7168], P(('grp', 'dev'))
Inputs may be any that keep to these rules, and one draw needn't show every extreme that they name: `expert_ids`: each row names 8 different experts. Among the 4 tokens of one device no expert is named more than 2 times, a bound that some block reaches.
All inputs are finite; a program needn't handle non-finite values.
Results may differ from a plain program's by a relative error of at most 0.012.
Values may be sent and summed in bfloat16 or wider, within the bound.
No kernel may reach another device: no remote copies, remote signals or barrier semaphores. Data moves between devices by JAX's collectives and lax.ppermute only.
A program may use at most 128 MiB of HBM per device.

v0:
```python
import jax
import jax.numpy as jnp
from jax import lax
from jax.sharding import PartitionSpec as P


def expert_block(block, gate_weight, up_weight, down_weight):
    row_shape = block.shape
    flat_rows = block.reshape(-1, row_shape[-1])
    gate_out = jnp.dot(flat_rows, gate_weight[0], preferred_element_type=jnp.float32)
    up_out = jnp.dot(flat_rows, up_weight[0], preferred_element_type=jnp.float32)
    hidden = (jax.nn.silu(gate_out) * up_out).astype(jnp.bfloat16)
    partial_value = jnp.dot(hidden, down_weight[0], preferred_element_type=jnp.float32).astype(
        jnp.bfloat16
    )
    return partial_value.reshape(row_shape)


def body(tokens, expert_ids, route_weights, gate_weight, up_weight, down_weight):
    experts = lax.axis_size("dev")
    groups = lax.axis_size("grp")
    tok_count = tokens.shape[0]
    choose = expert_ids.shape[1]
    width = tokens.shape[1]
    capacity = max(2, 3 * tok_count * choose // (2 * experts))
    flat_ids = expert_ids.reshape(-1)
    onehot = (flat_ids[:, None] == jnp.arange(experts, dtype=jnp.int32)[None, :]).astype(jnp.int32)
    before = jnp.cumsum(onehot, axis=0) - onehot
    slot_index = jnp.sum(before * onehot, axis=1)
    target = (flat_ids * capacity + slot_index).reshape(tok_count, choose)
    columns = jnp.arange(experts * capacity, dtype=jnp.int32)
    matches = target[None, :, :] == columns[:, None, None]
    select = jnp.any(matches, axis=2).astype(jnp.bfloat16)
    buffer = jnp.dot(select, tokens, preferred_element_type=jnp.float32).astype(jnp.bfloat16)
    buffer = buffer.reshape(experts, capacity, width)
    outgoing = jnp.tile(buffer, (groups, 1, 1))
    partials = expert_block(
        lax.all_to_all(outgoing, ("grp", "dev"), split_axis=0, concat_axis=0, tiled=True),
        gate_weight,
        up_weight,
        down_weight,
    )
    returned = lax.all_to_all(partials, ("grp", "dev"), split_axis=0, concat_axis=0, tiled=True)
    expert_out = jnp.sum(
        returned.reshape(groups, experts * capacity, width).astype(jnp.float32), axis=0
    )
    weighted = jnp.sum(matches.astype(jnp.float32) * route_weights[None, :, :], axis=2)
    mixed = jnp.dot(
        jnp.transpose(weighted),
        expert_out,
        precision=lax.Precision.HIGHEST,
        preferred_element_type=jnp.float32,
    )
    return mixed.astype(jnp.bfloat16)


def solution(mesh):
    in_specs = (
        P(("grp", "dev"), None),
        P(("grp", "dev"), None),
        P(("grp", "dev"), None),
        P("dev", None, "grp"),
        P("dev", None, "grp"),
        P("dev", "grp", None),
    )
    out_specs = P(("grp", "dev"), None)
    return jax.shard_map(body, mesh=mesh, in_specs=in_specs, out_specs=out_specs, check_vma=False)
```

profile of v0, /device:TPU:1, one launch (start us, length us, event | category | flops | bytes accessed | tf_op | source)
XLA Modules:
  0.0 165.4 jit_solution(10895635566578306034)
XLA Ops:
  0.0 0.0 copy-start
  0.0 0.8 eq.28
  0.8 0.1 fusion.20
  0.8 0.1 reduce_window_sum.11
  0.9 0.2 select_reduce_fusion.1
  1.1 0.1 reduce_sum.30
  1.2 0.7 multiply_add_fusion
  1.9 0.1 fusion.19
  2.0 0.0 copy-done
  2.0 0.5 convolution_convert_fusion.1
  2.4 0.3 tile.10
  2.8 1.9 %tile.11 = bf16[4,32,2,7168]{3,2,1,0:T(2,128)(2,1)S(1)} broadcast(bf16[32,2,7168]{2,1,0:T(2,128)(2,1)S(1)} %tile.10), dimensions={1,2,3} | broadcast | bytes 4587520 | tf_op jit(solution)/shard_map/tile | solution.py:36
  4.7 59.0 %all_to_all.10 = bf16[128,2,7168]{2,1,0:T(2,128)(2,1)} all-to-all(bf16[128,2,7168]{2,1,0:T(2,128)(2,1)S(1)} %bitcast.22), channel_id=1, replica_groups=mesh['grp'=4,'dev'=32] {'grp','dev'}, dimensions={0} | all-to-all | bytes 7340032 | tf_op jit(solution)/shard_map/all_to_all | solution.py:38
  63.6 8.4 %reshape.22 = bf16[256,7168]{1,0:T(8,128)(2,1)} reshape(bf16[128,2,7168]{2,1,0:T(2,128)(2,1)} %all_to_all.10) | data formatting | bytes 7340032 | tf_op jit(solution)/shard_map/reshape | solution.py:9
  72.0 6.2 %fusion.3 = f32[256,512]{1,0:T(8,128)S(1)} fusion(bf16[256,7168]{1,0:T(8,128)(2,1)} %reshape.22, bf16[1,7168,512]{2,1,0:T(8,128)(2,1)} %param.9), kind=kOutput, calls=%fused_computation.6 | convolution fusion | flops 1879048192 | bytes 11534336 | tf_op jit(solution)/shard_map/dot_general | solution.py:10
  78.3 12.1 %convolution_convert_fusion = bf16[256,7168]{1,0:T(8,128)(2,1)} fusion(bf16[1,512,7168]{2,1,0:T(8,128)(2,1)} %param.11, bf16[256,7168]{1,0:T(8,128)(2,1)} %reshape.22, bf16[1,7168,512]{2,1,0:T(8,128)(2,1)} %param.10, f32[256,512]{1,0:T(8,128)S(1)} %fusion.3), kind=kOutput, calls=%fused_computation | convolution fusion | flops 3760717824 | bytes 22544384 | tf_op jit(solution)/shard_map/dot_general | solution.py:13
  90.4 8.1 %reshape.23 = bf16[128,2,7168]{2,1,0:T(2,128)(2,1)} reshape(bf16[256,7168]{1,0:T(8,128)(2,1)} %convolution_convert_fusion) | data formatting | bytes 7340032 | tf_op jit(solution)/shard_map/reshape | solution.py:16
  98.5 0.0 copy-start.1
  98.5 5.5 %all-to-all-start.1 = ((bf16[128,2,7168]{2,1,0:T(2,128)(2,1)}), bf16[128,2,7168]{2,1,0:T(2,128)(2,1)}, u32[]{:S(2)}, u32[]{:S(2)}) async-start(bf16[128,2,7168]{2,1,0:T(2,128)(2,1)} %reshape.23), calls=%async_computation.1 | async-start | bytes 7340032 | tf_op jit(solution)/shard_map/all_to_all | solution.py:43
  104.0 0.0 copy-done.1
  104.0 0.1 select_reduce_fusion
  104.1 47.3 %all-to-all-done.1 = bf16[128,2,7168]{2,1,0:T(2,128)(2,1)} async-done(((bf16[128,2,7168]{2,1,0:T(2,128)(2,1)}), bf16[128,2,7168]{2,1,0:T(2,128)(2,1)}, u32[]{:S(2)}, u32[]{:S(2)}) %all-to-all-start.1) | async-done | bytes 3670048 | tf_op jit(solution)/shard_map/all_to_all | solution.py:43
  151.4 8.7 %reshape.24 = f32[4,64,7168]{2,1,0:T(8,128)} reshape(bf16[128,2,7168]{2,1,0:T(2,128)(2,1)} %all-to-all-done.1) | data formatting | bytes 11010048 | tf_op jit(solution)/shard_map/convert_element_type | solution.py:45
  160.1 3.8 %reduce_sum.32 = f32[64,7168]{1,0:T(8,128)S(1)} reduce(f32[4,64,7168]{2,1,0:T(8,128)} %reshape.24, f32[]{:T(128)} %constant.13.clone.1), dimensions={0}, to_apply=%region_4.5 | reduce | flops 1376256 | bytes 9175044 | tf_op jit(solution)/shard_map/reduce_sum | solution.py:44
  163.8 1.6 convolution_convert_fusion.2
Async XLA Ops:
  0.0 2.0 %copy-start = (bf16[4,7168]{1,0:T(4,128)(2,1)S(1)}, bf16[4,7168]{1,0:T(4,128)(2,1)}, u32[]{:S(2)}) copy-start(bf16[4,7168]{1,0:T(4,128)(2,1)} %param.6) | copy-start | bytes 172036
  98.5 5.5 %copy-start.1 = (f32[4,8]{1,0:T(4,128)S(1)}, f32[4,8]{1,0:T(4,128)}, u32[]{:S(2)}) copy-start(f32[4,8]{1,0:T(4,128)} %param.8) | copy-start | bytes 388
  98.5 52.8 %all-to-all-start.1 = ((bf16[128,2,7168]{2,1,0:T(2,128)(2,1)}), bf16[128,2,7168]{2,1,0:T(2,128)(2,1)}, u32[]{:S(2)}, u32[]{:S(2)}) async-start(bf16[128,2,7168]{2,1,0:T(2,128)(2,1)} %reshape.23), calls=%async_computation.1 | async-start | bytes 7340032 | tf_op jit(solution)/shard_map/all_to_all | solution.py:43
where the time goes:
time: 166 us; the launch traced here: 165 us
  blocking collectives  59 us (36%)
  waiting for transfers between devices  47.3 us (28%)
  local copies, waits for them, and re-layouts  28.3 us (17%)
  matrix products  20.4 us (12%)
  starting transfers between devices  5.46 us (3%)
  other arithmetic  4.96 us (3%)
    all_to_all x1, blocking collectives, body(): lax.all_to_all(outgoing, ('grp', 'dev'), split_axis=0, concat_axis=0, til...  59 us
    all_to_all x1, waiting for transfers between devices, body(): lax.all_to_all(partials, ('grp', 'dev'), split_axis=0, concat_axis=0, til...  47.3 us
    dot_general x1, matrix products, expert_block(): jnp.dot(hidden, down_weight[0], preferred_element_type=jnp.float32)  12.1 us
    convert_element_type x1, local copies, waits for them, and re-layouts, body(): returned.reshape(groups, experts * capacity, width).astype(jnp.float32)  8.68 us
    reshape x1, local copies, waits for them, and re-layouts, expert_block(): flat_rows = block.reshape(-1, row_shape[-1])  8.4 us
    reshape x1, local copies, waits for them, and re-layouts, expert_block(): return partial_value.reshape(row_shape)  8.12 us
    dot_general x1, matrix products, expert_block(): jnp.dot(flat_rows, gate_weight[0], preferred_element_type=jnp.float32)  6.25 us
    all_to_all x1, starting transfers between devices, body(): lax.all_to_all(partials, ('grp', 'dev'), split_axis=0, concat_axis=0, til...  5.46 us
  transfers between devices with their start and end apart: 1, of which 1 were waited for; matrix products, arithmetic and copies ran while one was open for 0% of the time, Pallas kernels for 0%

commit v1 on v0

v1 whole, which is shorter than its diff:
```python
import functools

import jax
import jax.numpy as jnp
from jax import lax
from jax.experimental import pallas as pl
from jax.experimental.pallas import tpu as pltpu
from jax.sharding import PartitionSpec as P

AXES = ("grp", "dev")
D = 7168
HALF = D // 2
EXT = 128
WIDE = HALF + EXT
ROWS = 512
SEL = 128
F32 = jnp.float32
BF16 = jnp.bfloat16
MIB = 1 << 20


def flat(z, x, y, c):
    return ((z * 4 + x) * 4 + y) * 2 + c


def cube_groups(stage):
    seen, groups = set(), []
    for z in range(4):
        for x in range(4):
            for y in range(4):
                for c in range(2):
                    if flat(z, x, y, c) in seen:
                        continue
                    m = 1 if c == stage else 3
                    members = [
                        flat(z ^ (m * i), x ^ (m * j), y ^ (m * k), c)
                        for i in (0, 1) for j in (0, 1) for k in (0, 1)
                    ]
                    seen.update(members)
                    groups.append(members)
    return groups


NEAR, FAR = cube_groups(0), cube_groups(1)


def swap_groups(values, groups):
    return lax.all_to_all(values, AXES, 0, 0, axis_index_groups=groups, tiled=True)


def to_sibling(values):
    return lax.ppermute(values, "dev", [(i, i ^ 1) for i in range(32)])


def pack_kernel(tokens_ref, ids_ref, weights_ref, out_ref):
    lane = lax.broadcasted_iota(jnp.int32, (4, EXT), 1)
    dense = jnp.zeros((4, EXT), F32)
    for k in range(8):
        dense += jnp.where(ids_ref[:, k : k + 1] == lane % 32, weights_ref[:, k : k + 1], 0.0)
    high = dense.astype(BF16).astype(F32)
    route = jnp.where(lane < 32, high, jnp.where(lane < 64, dense - high, 0.0))
    rows = tokens_ref[...].astype(F32)
    left = jnp.concatenate([rows[:, :HALF], route], axis=1)
    right = jnp.concatenate([rows[:, HALF:], route], axis=1)
    block = jnp.concatenate([left, right], axis=0).astype(BF16)
    for i in range(8):
        out_ref[i] = block


def pack(tokens, ids, weights):
    return pl.pallas_call(
        pack_kernel,
        out_shape=jax.ShapeDtypeStruct((8, 8, WIDE), BF16),
        name="pack",
    )(tokens, ids, weights)


def expert_lanes(expert, shape, dim):
    lane = lax.broadcasted_iota(jnp.int32, shape, dim)
    return (lane < 64) & (lane % 32 == expert)


def select_kernel(expert_ref, x_ref, out_ref, pick):
    own = expert_ref[0]
    turn = lax.broadcasted_iota(jnp.int32, (8, EXT), 0)
    experts = jnp.where(turn == 0, own, own ^ 1)
    wanted = jnp.where(expert_lanes(experts, (8, EXT), 1) & (turn < 2), 1.0, 0.0).astype(BF16)
    route = lax.dot_general(
        wanted, x_ref[:, HALF:], (((1,), (1,)), ((), ())), preferred_element_type=F32
    )
    chosen = route > 0
    first = lax.broadcasted_iota(jnp.int32, (ROWS, ROWS), 0)
    second = lax.broadcasted_iota(jnp.int32, (ROWS, ROWS), 1)
    earlier = jnp.where((first // 4 == second // 4) & (first < second), 1.0, 0.0).astype(BF16)
    rank = jnp.dot(jnp.where(chosen, 1.0, 0.0).astype(BF16), earlier, preferred_element_type=F32)
    column = lax.broadcasted_iota(jnp.int32, (8, ROWS), 1)
    place = jnp.where(chosen, column // 8 * 2 + rank.astype(jnp.int32), -1)
    row = lax.broadcasted_iota(jnp.int32, (SEL, ROWS), 0)
    is_left = lax.broadcasted_iota(jnp.int32, (SEL, ROWS), 1) % 8 < 4
    for e in range(2):
        hit = place[e : e + 1, :] == row
        pick[0, e * SEL : (e + 1) * SEL, :] = jnp.where(hit & is_left, 1.0, 0.0).astype(BF16)
        pick[1, e * SEL : (e + 1) * SEL, :] = jnp.where(hit & ~is_left, 1.0, 0.0).astype(BF16)

    def put(start, size, side, to):
        value = jnp.dot(pick[side], x_ref[:, start : start + size], preferred_element_type=F32).astype(BF16)
        out_ref[0, :, to : to + size] = value[:SEL]
        out_ref[1, :, to : to + size] = value[SEL:]

    for n in range(0, HALF, 512):
        put(n, 512, 0, n)
        put(n, 512, 1, HALF + n)
    put(HALF, EXT, 0, D)


def select(expert, x):
    return pl.pallas_call(
        select_kernel,
        out_shape=jax.ShapeDtypeStruct((2, SEL, D + EXT), BF16),
        in_specs=[pl.BlockSpec(memory_space=pltpu.SMEM), pl.BlockSpec(memory_space=pltpu.VMEM)],
        scratch_shapes=[pltpu.VMEM((2, 2 * SEL, ROWS), BF16)],
        compiler_params=pltpu.CompilerParams(vmem_limit_bytes=40 * MIB),
        name="select",
    )(expert, x)


STEPS = 7
BLOCK = D // STEPS


def ffn_kernel(expert_ref, mine_ref, theirs_ref, gate_ref, up_ref, down_ref, out_ref, gate_sum, up_sum, hidden):
    i = pl.program_id(0)

    @pl.when(i == 0)
    def _():
        gate_sum[...] = jnp.zeros_like(gate_sum)
        up_sum[...] = jnp.zeros_like(up_sum)

    @pl.when(i < STEPS)
    def _():
        columns = pl.ds(pl.multiple_of(i * BLOCK, BLOCK), BLOCK)
        for part, ref in enumerate((mine_ref, theirs_ref)):
            rows = slice(part * SEL, (part + 1) * SEL)
            x = ref[:, columns]
            gate_sum[rows, :] += jnp.dot(x, gate_ref[0], preferred_element_type=F32)
            up_sum[rows, :] += jnp.dot(x, up_ref[0], preferred_element_type=F32)

    @pl.when(i == STEPS - 1)
    def _():
        lanes = expert_lanes(expert_ref[0], (SEL, EXT), 1)
        for part, ref in enumerate((mine_ref, theirs_ref)):
            rows = slice(part * SEL, (part + 1) * SEL)
            route = ref[:, D:].astype(F32)
            scale = jnp.sum(jnp.where(lanes, route, 0.0), axis=1, keepdims=True)
            v = gate_sum[rows, :]
            hidden[rows, :] = (v / (1.0 + jnp.exp(-v)) * up_sum[rows, :] * scale).astype(BF16)

    @pl.when(i >= STEPS)
    def _():
        y = jnp.dot(hidden[...], down_ref[0], preferred_element_type=F32).astype(BF16)
        out_ref[0] = y[:SEL]
        out_ref[1] = y[SEL:]


def ffn(expert, mine, theirs, gate, up, down):
    first = lambda i: jnp.minimum(i, STEPS - 1)
    second = lambda i: jnp.maximum(i - STEPS, 0)
    whole = pl.BlockSpec((SEL, D + EXT), lambda i: (0, 0))
    return pl.pallas_call(
        ffn_kernel,
        grid=(2 * STEPS,),
        out_shape=jax.ShapeDtypeStruct((2, SEL, D), BF16),
        in_specs=[
            pl.BlockSpec(memory_space=pltpu.SMEM),
            whole,
            whole,
            pl.BlockSpec((1, BLOCK, 512), lambda i: (0, first(i), 0)),
            pl.BlockSpec((1, BLOCK, 512), lambda i: (0, first(i), 0)),
            pl.BlockSpec((1, 512, BLOCK), lambda i: (0, 0, second(i))),
        ],
        out_specs=pl.BlockSpec((2, SEL, BLOCK), lambda i: (0, 0, second(i))),
        scratch_shapes=[
            pltpu.VMEM((2 * SEL, 512), F32),
            pltpu.VMEM((2 * SEL, 512), F32),
            pltpu.VMEM((2 * SEL, 512), BF16),
        ],
        compiler_params=pltpu.CompilerParams(vmem_limit_bytes=40 * MIB),
        name="ffn",
    )(expert, mine, theirs, gate, up, down)


def spread_kernel(expert_ref, route_ref, mine_ref, theirs_ref, out_ref, place_scr, y):
    own = expert_ref[0]
    turn = lax.broadcasted_iota(jnp.int32, (EXT, EXT), 1)
    experts = jnp.where(turn == 0, own, own ^ 1)
    wanted = jnp.where(expert_lanes(experts, (EXT, EXT), 0) & (turn < 2), 1.0, 0.0).astype(BF16)
    chosen = jnp.dot(route_ref[...], wanted, preferred_element_type=F32) > 0
    first = lax.broadcasted_iota(jnp.int32, (ROWS, ROWS), 0)
    second = lax.broadcasted_iota(jnp.int32, (ROWS, ROWS), 1)
    earlier = jnp.where((first // 4 == second // 4) & (second < first), 1.0, 0.0).astype(BF16)
    rank = jnp.dot(earlier, jnp.where(chosen, 1.0, 0.0).astype(BF16), preferred_element_type=F32)
    token = lax.broadcasted_iota(jnp.int32, (ROWS, EXT), 0)
    place = jnp.where(chosen, token // 8 * 2 + rank.astype(jnp.int32), -1)
    column = lax.broadcasted_iota(jnp.int32, (ROWS, SEL), 1)
    is_left = lax.broadcasted_iota(jnp.int32, (ROWS, SEL), 0) % 8 < 4
    for e in range(2):
        hit = place[:, e : e + 1] == column
        place_scr[:, e * SEL : (e + 1) * SEL] = jnp.where(hit & is_left, 1.0, 0.0).astype(BF16)
        place_scr[:, (2 + e) * SEL : (3 + e) * SEL] = jnp.where(hit & ~is_left, 1.0, 0.0).astype(BF16)
    for n in range(0, HALF, 512):
        y[0 * SEL : 1 * SEL, :] = mine_ref[:, n : n + 512]
        y[1 * SEL : 2 * SEL, :] = theirs_ref[:, n : n + 512]
        y[2 * SEL : 3 * SEL, :] = mine_ref[:, HALF + n : HALF + n + 512]
        y[3 * SEL : 4 * SEL, :] = theirs_ref[:, HALF + n : HALF + n + 512]
        out_ref[:, n : n + 512] = jnp.dot(place_scr[...], y[...], preferred_element_type=F32).astype(BF16)


def spread(expert, route, mine, theirs):
    vmem = pl.BlockSpec(memory_space=pltpu.VMEM)
    return pl.pallas_call(
        spread_kernel,
        out_shape=jax.ShapeDtypeStruct((ROWS, HALF), BF16),
        in_specs=[pl.BlockSpec(memory_space=pltpu.SMEM), vmem, vmem, vmem],
        scratch_shapes=[pltpu.VMEM((ROWS, 4 * SEL), BF16), pltpu.VMEM((4 * SEL, 512), BF16)],
        compiler_params=pltpu.CompilerParams(vmem_limit_bytes=40 * MIB),
        name="spread",
    )(expert, route, mine, theirs)


def body(tokens, ids, weights, gate, up, down):
    expert = lax.axis_index("dev").astype(jnp.int32).reshape(1)
    near = swap_groups(pack(tokens, ids, weights), NEAR)
    copies = jnp.broadcast_to(near.reshape(1, 64, WIDE), (8, 64, WIDE))
    x = swap_groups(copies, FAR).reshape(ROWS, WIDE)
    picked = select(expert, x)
    mine, sent = picked[0], picked[1]
    results = ffn(expert, mine, to_sibling(sent), gate, up, down)
    returned = to_sibling(results[1])
    y = spread(expert, x[:, HALF:], results[0], returned)
    far = swap_groups(y.reshape(8, 64, HALF), FAR)
    far = jnp.sum(far.astype(F32), axis=0).astype(BF16)
    near = swap_groups(far.reshape(8, 8, HALF), NEAR)
    near = jnp.sum(near.astype(F32), axis=0)
    return jnp.concatenate([near[:4], near[4:]], axis=1).astype(BF16)


def solution(mesh):
    in_specs = (
        P(AXES, None),
        P(AXES, None),
        P(AXES, None),
        P("dev", None, "grp"),
        P("dev", None, "grp"),
        P("dev", "grp", None),
    )
    return jax.shard_map(body, mesh=mesh, in_specs=in_specs, out_specs=P(AXES, None), check_vma=False)
```

time: 166 us -> 138 us (0.83)
  Pallas kernels: 0 us -> 24.7 us
  local copies, waits for them, and re-layouts: 28.3 us -> 3.6 us
  matrix products: 20.4 us -> 0 us
  waiting for transfers between devices: 47.3 us -> 38.3 us
  blocking collectives: 59 us -> 61.6 us
    pallas_call x0 -> x4, Pallas kernels: none -> 24.7 us  [the longest x1 15.8 us: ffn(): pl.pallas_call(ffn_kernel, grid=(2 * STEPS,), out_shape=jax.ShapeDtypeStr...]
    dot_general x4 -> x0, matrix products: 20.4 us -> none  [the longest x1 12.1 us: expert_block(): jnp.dot(hidden, down_weight[0], preferred_element_type=jnp.float32)]
    reshape x2 -> x0, local copies, waits for them, and re-layouts: 16.5 us -> none  [the longest x1 8.4 us: expert_block(): flat_rows = block.reshape(-1, row_shape[-1])]
    all_to_all x1, waiting for transfers between devices: 47.3 us -> 31.7 us  [swap_groups(): lax.all_to_all(values, AXES, 0, 0, axis_index_groups=groups, tiled=True)]
    convert_element_type x1 -> x0, local copies, waits for them, and re-layouts: 8.68 us -> none  [body(): returned.reshape(groups, experts * capacity, width).astype(jnp.float32)]
    ppermute x0 -> x2, waiting for transfers between devices: none -> 6.56 us  [to_sibling(): return lax.ppermute(values, 'dev', [(i, i ^ 1) for i in range(32)])]
    all_to_all x1 -> x3, blocking collectives: 59 us -> 61.6 us  [swap_groups(): lax.all_to_all(values, AXES, 0, 0, axis_index_groups=groups, tiled=True)]
    another operation x2 -> x0, local copies, waits for them, and re-layouts: 2.24 us -> none  [body(): outgoing = jnp.tile(buffer, (groups, 1, 1))]
  transfers between devices with their start and end apart: 1 -> 3, of which waited for: 1 -> 3; matrix products, arithmetic and copies ran while one was open for 0% -> 1% of each run, Pallas kernels for 0% -> 0%
where the time goes in v1:
time: 138 us; the launch traced here: 136 us
  blocking collectives  61.6 us (45%)
  waiting for transfers between devices  38.3 us (28%)
  Pallas kernels  24.7 us (18%)
  starting transfers between devices  4.8 us (3%)
  local copies, waits for them, and re-layouts  3.6 us (3%)
  other arithmetic  3.31 us (2%)
    all_to_all x3, blocking collectives, swap_groups(): lax.all_to_all(values, AXES, 0, 0, axis_index_groups=groups, tiled=True)  61.6 us
    all_to_all x1, waiting for transfers between devices, swap_groups(): lax.all_to_all(values, AXES, 0, 0, axis_index_groups=groups, tiled=True)  31.7 us
    pallas_call x1, Pallas kernels, ffn(): pl.pallas_call(ffn_kernel, grid=(2 * STEPS,), out_shape=jax.ShapeDtypeStr...  15.8 us
    ppermute x2, waiting for transfers between devices, to_sibling(): return lax.ppermute(values, 'dev', [(i, i ^ 1) for i in range(32)])  6.56 us
    all_to_all x1, starting transfers between devices, swap_groups(): lax.all_to_all(values, AXES, 0, 0, axis_index_groups=groups, tiled=True)  4.51 us
    pallas_call x1, Pallas kernels, select(): pl.pallas_call(select_kernel, out_shape=jax.ShapeDtypeStruct((2, SEL, D +...  4.46 us
    pallas_call x1, Pallas kernels, spread(): pl.pallas_call(spread_kernel, out_shape=jax.ShapeDtypeStruct((ROWS, HALF)...  2.77 us
  transfers between devices with their start and end apart: 3, of which 3 were waited for; matrix products, arithmetic and copies ran while one was open for 1% of the time, Pallas kernels for 0%

profile of v1, /device:TPU:1, one launch (start us, length us, event | category | flops | bytes accessed | tf_op | source)
XLA Modules:
  0.0 136.4 jit_solution(1966790505925324995)
XLA Ops:
  0.0 1.7 %pack.1 = bf16[8,8,3712]{2,1,0:T(8,128)(2,1)} custom-call(bf16[4,7168]{1,0:T(4,128)(2,1)} %tokens_ref.1, s32[4,8]{1,0:T(4,128)} %ids_ref.1, f32[4,8]{1,0:T(4,128)} %weights_ref.1), custom_call_target="tpu_custom_call" | custom-call | tf_op jit(solution)/shard_map/pack/pallas_call | solution.py:71
  1.7 21.1 %all_to_all.20 = bf16[8,8,3712]{2,1,0:T(8,128)(2,1)S(1)} all-to-all(bf16[8,8,3712]{2,1,0:T(8,128)(2,1)} %pack.1), channel_id=1, replica_groups={{0,2,8,10,32,34,40,42},{1,7,25,31,97,103,121,127},{3,5,27,29,99,101,123..., dimensions={0} | all-to-all | bytes 950272 | tf_op jit(solution)/shard_map/all_to_all | solution.py:48
  22.8 2.2 %broadcast_in_dim.8 = bf16[8,64,3712]{2,1,0:T(8,128)(2,1)} broadcast(bf16[64,3712]{1,0:T(8,128)(2,1)S(1)} %bitcast.14), dimensions={1,2} | broadcast | bytes 4276224 | tf_op jit(solution)/shard_map/broadcast_in_dim | solution.py:233
  25.0 4.5 %all-to-all-start.1 = ((bf16[8,64,3712]{2,1,0:T(8,128)(2,1)}), bf16[8,64,3712]{2,1,0:T(8,128)(2,1)}, u32[]{:S(2)}, u32[]{:S(2)}) async-start(bf16[8,64,3712]{2,1,0:T(8,128)(2,1)} %broadcast_in_dim.8), calls=%async_computation.1 | async-start | bytes 7602176 | tf_op jit(solution)/shard_map/all_to_all | solution.py:48
  29.5 31.7 %all-to-all-done.1 = bf16[8,64,3712]{2,1,0:T(8,128)(2,1)} async-done(((bf16[8,64,3712]{2,1,0:T(8,128)(2,1)}), bf16[8,64,3712]{2,1,0:T(8,128)(2,1)}, u32[]{:S(2)}, u32[]{:S(2)}) %all-to-all-start.1) | async-done | bytes 3801120 | tf_op jit(solution)/shard_map/all_to_all | solution.py:48
  61.2 4.5 %select.1 = bf16[2,128,7296]{2,1,0:T(8,128)(2,1)S(1)} custom-call(s32[1]{0:T(128)} %bitcast.expert_ref, bf16[512,3712]{1,0:T(8,128)(2,1)} %bitcast.2.x_ref), custom_call_target="tpu_custom_call" | custom-call | tf_op jit(solution)/shard_map/select/pallas_call | solution.py:117
  65.7 0.2 slice_bitcast_fusion
  66.0 0.1 collective-permute-start
  66.1 3.8 %collective-permute-done.theirs_ref = bf16[128,7296]{1,0:T(8,128)(2,1)S(1)} collective-permute-done((bf16[128,7296]{1,0:T(8,128)(2,1)S(1)}, bf16[128,7296]{1,0:T(8,128)(2,1)S(1)}, u32[]{:S(2)}, u32[]{:S(2)}) %collective-permute-start) | collective-permute-done | bytes 1867808 | tf_op jit(solution)/shard_map/ppermute | solution.py:52
  69.9 15.8 %ffn.1 = bf16[2,128,7168]{2,1,0:T(8,128)(2,1)S(1)} custom-call(s32[1]{0:T(128)} %bitcast.expert_ref, bf16[128,7296]{1,0:T(8,128)(2,1)S(1)} %get-tuple-element.6.mine_ref, bf16[128,7296]{1,0:T(8,128)(2,1)S(1)} %collective-permute-done.theirs_ref, bf16[1,7168,512]{2,1,0:T(8,128)(2,1)} %gate_ref.1, bf16[1,7168,512]{2,1,0:T(8,128)(2,1)} %up_ref.1, ...), custom_call_target="tpu_custom_call" | custom-call | tf_op jit(solution)/shard_map/ffn/pallas_call | solution.py:169
  85.6 0.2 slice_bitcast_fusion.2
  85.9 0.2 collective-permute-start.1
  86.1 0.9 slice.30.route_ref
  87.0 2.7 %collective-permute-done.1.theirs_ref = bf16[128,7168]{1,0:T(8,128)(2,1)S(1)} collective-permute-done((bf16[128,7168]{1,0:T(8,128)(2,1)S(1)}, bf16[128,7168]{1,0:T(8,128)(2,1)S(1)}, u32[]{:S(2)}, u32[]{:S(2)}) %collective-permute-start.1) | collective-permute-done | bytes 1835040 | tf_op jit(solution)/shard_map/ppermute | solution.py:52
  89.8 2.8 %spread.1 = bf16[512,3584]{1,0:T(8,128)(2,1)S(1)} custom-call(s32[1]{0:T(128)} %bitcast.expert_ref, bf16[512,128]{1,0:T(8,128)(2,1)S(1)} %slice.30.route_ref, bf16[128,7168]{1,0:T(8,128)(2,1)S(1)} %get-tuple-element.8.mine_ref, bf16[128,7168]{1,0:T(8,128)(2,1)S(1)} %collective-permute-done.1.theirs_ref), custom_call_target="tpu_custom_call" | custom-call | tf_op jit(solution)/shard_map/spread/pallas_call | solution.py:220
  92.5 27.6 %all_to_all.21 = bf16[8,64,3584]{2,1,0:T(8,128)(2,1)} all-to-all(bf16[8,64,3584]{2,1,0:T(8,128)(2,1)S(1)} %bitcast.13), channel_id=1, replica_groups={{0,6,24,30,96,102,120,126},{1,3,9,11,33,35,41,43},{2,4,26,28,98,100,122..., dimensions={0} | all-to-all | bytes 7340032 | tf_op jit(solution)/shard_map/all_to_all | solution.py:48
  120.1 2.6 %reduce_sum.21 = bf16[64,3584]{1,0:T(8,128)(2,1)S(1)} reduce(bf16[8,64,3584]{2,1,0:T(8,128)(2,1)} %all_to_all.21, bf16[]{:T(256)} %constant.6.clone.1), dimensions={0}, to_apply=%region_0.0 | reduce | flops 1605632 | bytes 4128770 | tf_op jit(solution)/shard_map/reduce_sum | solution.py:241
  122.7 12.9 %all_to_all.22 = bf16[8,8,3584]{2,1,0:T(8,128)(2,1)S(1)} all-to-all(bf16[8,8,3584]{2,1,0:T(8,128)(2,1)S(1)} %bitcast.15), channel_id=1, replica_groups={{0,2,8,10,32,34,40,42},{1,7,25,31,97,103,121,127},{3,5,27,29,99,101,123..., dimensions={0} | all-to-all | bytes 917504 | tf_op jit(solution)/shard_map/all_to_all | solution.py:48
  135.6 0.1 reduce.1
  135.7 0.7 pad_maximum_fusion
  (1 shorter events, 0.0 us)
Async XLA Ops:
  25.0 36.2 %all-to-all-start.1 = ((bf16[8,64,3712]{2,1,0:T(8,128)(2,1)}), bf16[8,64,3712]{2,1,0:T(8,128)(2,1)}, u32[]{:S(2)}, u32[]{:S(2)}) async-start(bf16[8,64,3712]{2,1,0:T(8,128)(2,1)} %broadcast_in_dim.8), calls=%async_computation.1 | async-start | bytes 7602176 | tf_op jit(solution)/shard_map/all_to_all | solution.py:48
  66.0 3.9 %collective-permute-start = (bf16[128,7296]{1,0:T(8,128)(2,1)S(1)}, bf16[128,7296]{1,0:T(8,128)(2,1)S(1)}, u32[]{:S(2)}, u32[]{:S(2)}) collective-permute-start(bf16[128,7296]{1,0:T(8,128)(2,1)S(1)} %get-tuple-element.5), channel_id=1, source_target_pairs={{0,1},{1,0},{2,3},{3,2},{4,5},{5,4},{6,7},{7,6},{8,9},{9,8},{10,11... | collective-permute-start | bytes 5603336 | tf_op jit(solution)/shard_map/ppermute | solution.py:52
  85.9 3.9 %collective-permute-start.1 = (bf16[128,7168]{1,0:T(8,128)(2,1)S(1)}, bf16[128,7168]{1,0:T(8,128)(2,1)S(1)}, u32[]{:S(2)}, u32[]{:S(2)}) collective-permute-start(bf16[128,7168]{1,0:T(8,128)(2,1)S(1)} %get-tuple-element.7), channel_id=1, source_target_pairs={{0,1},{1,0},{2,3},{3,2},{4,5},{5,4},{6,7},{7,6},{8,9},{9,8},{10,11... | collective-permute-start | bytes 5505032 | tf_op jit(solution)/shard_map/ppermute | solution.py:52

commit v2 on v1

--- a/solution.py
+++ b/solution.py
@@ -17,6 +17,8 @@
 F32 = jnp.float32
 BF16 = jnp.bfloat16
 MIB = 1 << 20
+VMEM = pl.BlockSpec(memory_space=pltpu.VMEM)
+SMEM = pl.BlockSpec(memory_space=pltpu.SMEM)
 
 
 def flat(z, x, y, c):
@@ -52,7 +54,8 @@
     return lax.ppermute(values, "dev", [(i, i ^ 1) for i in range(32)])
 
 
-def pack_kernel(tokens_ref, ids_ref, weights_ref, out_ref):
+def pack_kernel(expert_ref, tokens_ref, ids_ref, weights_ref, out_ref):
+    del expert_ref
     lane = lax.broadcasted_iota(jnp.int32, (4, EXT), 1)
     dense = jnp.zeros((4, EXT), F32)
     for k in range(8):
@@ -67,12 +70,15 @@
         out_ref[i] = block
 
 
-def pack(tokens, ids, weights):
+def pack(expert, tokens, ids, weights):
     return pl.pallas_call(
         pack_kernel,
         out_shape=jax.ShapeDtypeStruct((8, 8, WIDE), BF16),
+        compiler_params=pltpu.CompilerParams(vmem_limit_bytes=4 * MIB),
+        in_specs=[SMEM, VMEM, VMEM, VMEM],
+        out_specs=VMEM,
         name="pack",
-    )(tokens, ids, weights)
+    )(expert, tokens, ids, weights)
 
 
 def expert_lanes(expert, shape, dim):
@@ -80,7 +86,7 @@
     return (lane < 64) & (lane % 32 == expert)
 
 
-def select_kernel(expert_ref, x_ref, out_ref, pick):
+def select_kernel(expert_ref, x_ref, mine_ref, sent_ref, pick):
     own = expert_ref[0]
     turn = lax.broadcasted_iota(jnp.int32, (8, EXT), 0)
     experts = jnp.where(turn == 0, own, own ^ 1)
@@ -104,8 +110,8 @@
 
     def put(start, size, side, to):
         value = jnp.dot(pick[side], x_ref[:, start : start + size], preferred_element_type=F32).astype(BF16)
-        out_ref[0, :, to : to + size] = value[:SEL]
-        out_ref[1, :, to : to + size] = value[SEL:]
+        mine_ref[:, to : to + size] = value[:SEL]
+        sent_ref[:, to : to + size] = value[SEL:]
 
     for n in range(0, HALF, 512):
         put(n, 512, 0, n)
@@ -116,77 +122,73 @@
 def select(expert, x):
     return pl.pallas_call(
         select_kernel,
-        out_shape=jax.ShapeDtypeStruct((2, SEL, D + EXT), BF16),
+        out_shape=[jax.ShapeDtypeStruct((SEL, D + EXT), BF16)] * 2,
         in_specs=[pl.BlockSpec(memory_space=pltpu.SMEM), pl.BlockSpec(memory_space=pltpu.VMEM)],
         scratch_shapes=[pltpu.VMEM((2, 2 * SEL, ROWS), BF16)],
-        compiler_params=pltpu.CompilerParams(vmem_limit_bytes=40 * MIB),
+        compiler_params=pltpu.CompilerParams(vmem_limit_bytes=12 * MIB),
         name="select",
     )(expert, x)
 
 
-STEPS = 7
-BLOCK = D // STEPS
-
-
-def ffn_kernel(expert_ref, mine_ref, theirs_ref, gate_ref, up_ref, down_ref, out_ref, gate_sum, up_sum, hidden):
-    i = pl.program_id(0)
-
-    @pl.when(i == 0)
-    def _():
-        gate_sum[...] = jnp.zeros_like(gate_sum)
-        up_sum[...] = jnp.zeros_like(up_sum)
-
-    @pl.when(i < STEPS)
-    def _():
-        columns = pl.ds(pl.multiple_of(i * BLOCK, BLOCK), BLOCK)
-        for part, ref in enumerate((mine_ref, theirs_ref)):
-            rows = slice(part * SEL, (part + 1) * SEL)
-            x = ref[:, columns]
-            gate_sum[rows, :] += jnp.dot(x, gate_ref[0], preferred_element_type=F32)
-            up_sum[rows, :] += jnp.dot(x, up_ref[0], preferred_element_type=F32)
-
-    @pl.when(i == STEPS - 1)
-    def _():
-        lanes = expert_lanes(expert_ref[0], (SEL, EXT), 1)
-        for part, ref in enumerate((mine_ref, theirs_ref)):
-            rows = slice(part * SEL, (part + 1) * SEL)
-            route = ref[:, D:].astype(F32)
-            scale = jnp.sum(jnp.where(lanes, route, 0.0), axis=1, keepdims=True)
-            v = gate_sum[rows, :]
-            hidden[rows, :] = (v / (1.0 + jnp.exp(-v)) * up_sum[rows, :] * scale).astype(BF16)
-
-    @pl.when(i >= STEPS)
-    def _():
-        y = jnp.dot(hidden[...], down_ref[0], preferred_element_type=F32).astype(BF16)
-        out_ref[0] = y[:SEL]
-        out_ref[1] = y[SEL:]
-
-
-def ffn(expert, mine, theirs, gate, up, down):
-    first = lambda i: jnp.minimum(i, STEPS - 1)
-    second = lambda i: jnp.maximum(i - STEPS, 0)
-    whole = pl.BlockSpec((SEL, D + EXT), lambda i: (0, 0))
-    return pl.pallas_call(
-        ffn_kernel,
-        grid=(2 * STEPS,),
-        out_shape=jax.ShapeDtypeStruct((2, SEL, D), BF16),
-        in_specs=[
-            pl.BlockSpec(memory_space=pltpu.SMEM),
-            whole,
-            whole,
-            pl.BlockSpec((1, BLOCK, 512), lambda i: (0, first(i), 0)),
-            pl.BlockSpec((1, BLOCK, 512), lambda i: (0, first(i), 0)),
-            pl.BlockSpec((1, 512, BLOCK), lambda i: (0, 0, second(i))),
-        ],
-        out_specs=pl.BlockSpec((2, SEL, BLOCK), lambda i: (0, 0, second(i))),
-        scratch_shapes=[
-            pltpu.VMEM((2 * SEL, 512), F32),
-            pltpu.VMEM((2 * SEL, 512), F32),
-            pltpu.VMEM((2 * SEL, 512), BF16),
-        ],
-        compiler_params=pltpu.CompilerParams(vmem_limit_bytes=40 * MIB),
-        name="ffn",
-    )(expert, mine, theirs, gate, up, down)
+DEPTH = 1792
+
+
+def hidden_units(expert_ref, x_ref, gate_ref, up_ref, hidden, gate_sum, up_sum):
+    gate_sum[...] = jnp.zeros_like(gate_sum)
+    up_sum[...] = jnp.zeros_like(up_sum)
+
+    @pl.loop(0, D // DEPTH)
+    def _(i):
+        block = pl.ds(pl.multiple_of(i * DEPTH, DEPTH), DEPTH)
+        x = x_ref[:, block]
+        gate_sum[...] += jnp.dot(x, gate_ref[0, block, :], preferred_element_type=F32)
+        up_sum[...] += jnp.dot(x, up_ref[0, block, :], preferred_element_type=F32)
+
+    lanes = expert_lanes(expert_ref[0], (SEL, EXT), 1)
+    scale = jnp.sum(jnp.where(lanes, x_ref[:, D:].astype(F32), 0.0), axis=1, keepdims=True)
+    v = gate_sum[...]
+    hidden[...] = (v / (1.0 + jnp.exp(-v)) * up_sum[...] * scale).astype(BF16)
+
+
+def down_rows(hidden, down_ref, out_ref):
+    @pl.loop(0, D // 1024)
+    def _(i):
+        block = pl.ds(pl.multiple_of(i * 1024, 1024), 1024)
+        out_ref[:, block] = jnp.dot(hidden[...], down_ref[0, :, block], preferred_element_type=F32).astype(BF16)
+
+
+def hidden_units_after(expert_ref, x_ref, gate_ref, up_ref, earlier_ref, *rest):
+    del earlier_ref
+    hidden_units(expert_ref, x_ref, gate_ref, up_ref, *rest)
+
+
+SUMS = [pltpu.VMEM((SEL, 512), F32), pltpu.VMEM((SEL, 512), F32)]
+SMALL = pltpu.CompilerParams(vmem_limit_bytes=8 * MIB)
+
+
+def first_half(expert, x, gate, up, earlier=()):
+    return pl.pallas_call(
+        hidden_units_after if earlier else hidden_units,
+        out_shape=jax.ShapeDtypeStruct((SEL, 512), BF16),
+        in_specs=[SMEM, VMEM, VMEM, VMEM] + [VMEM] * len(earlier),
+        out_specs=VMEM,
+        scratch_shapes=SUMS,
+        compiler_params=SMALL,
+        cost_estimate=pl.CostEstimate(flops=4 * SEL * D * 512, bytes_accessed=17 << 20, transcendentals=0),
+        name="hidden",
+    )(expert, x, gate, up, *earlier)
+
+
+def second_half(hidden, down):
+    return pl.pallas_call(
+        down_rows,
+        out_shape=jax.ShapeDtypeStruct((SEL, D), BF16),
+        in_specs=[VMEM, VMEM],
+        out_specs=VMEM,
+        compiler_params=SMALL,
+        cost_estimate=pl.CostEstimate(flops=2 * SEL * D * 512, bytes_accessed=9 << 20, transcendentals=0),
+        name="down",
+    )(hidden, down)
 
 
 def spread_kernel(expert_ref, route_ref, mine_ref, theirs_ref, out_ref, place_scr, y):
@@ -222,26 +224,62 @@
         out_shape=jax.ShapeDtypeStruct((ROWS, HALF), BF16),
         in_specs=[pl.BlockSpec(memory_space=pltpu.SMEM), vmem, vmem, vmem],
         scratch_shapes=[pltpu.VMEM((ROWS, 4 * SEL), BF16), pltpu.VMEM((4 * SEL, 512), BF16)],
-        compiler_params=pltpu.CompilerParams(vmem_limit_bytes=40 * MIB),
+        compiler_params=pltpu.CompilerParams(vmem_limit_bytes=12 * MIB),
         name="spread",
     )(expert, route, mine, theirs)
 
 
+def total_kernel(parts_ref, out_ref):
+    for n in range(0, HALF, 512):
+        total = parts_ref[0, :, n : n + 512].astype(F32)
+        for i in range(1, 8):
+            total += parts_ref[i, :, n : n + 512].astype(F32)
+        out_ref[:, n : n + 512] = total.astype(BF16)
+
+
+def total(parts):
+    return pl.pallas_call(
+        total_kernel,
+        out_shape=jax.ShapeDtypeStruct((64, HALF), BF16),
+        in_specs=[VMEM],
+        out_specs=VMEM,
+        compiler_params=SMALL,
+        name="total",
+    )(parts)
+
+
+def finish_kernel(parts_ref, out_ref):
+    total = parts_ref[0].astype(F32)
+    for i in range(1, 8):
+        total += parts_ref[i].astype(F32)
+    out_ref[:, :HALF] = total[:4].astype(BF16)
+    out_ref[:, HALF:] = total[4:].astype(BF16)
+
+
+def finish(parts):
+    return pl.pallas_call(
+        finish_kernel,
+        out_shape=jax.ShapeDtypeStruct((4, D), BF16),
+        in_specs=[VMEM],
+        out_specs=VMEM,
+        compiler_params=SMALL,
+        name="finish",
+    )(parts)
+
+
 def body(tokens, ids, weights, gate, up, down):
     expert = lax.axis_index("dev").astype(jnp.int32).reshape(1)
-    near = swap_groups(pack(tokens, ids, weights), NEAR)
+    near = swap_groups(pack(expert, tokens, ids, weights), NEAR)
     copies = jnp.broadcast_to(near.reshape(1, 64, WIDE), (8, 64, WIDE))
     x = swap_groups(copies, FAR).reshape(ROWS, WIDE)
-    picked = select(expert, x)
-    mine, sent = picked[0], picked[1]
-    results = ffn(expert, mine, to_sibling(sent), gate, up, down)
-    returned = to_sibling(results[1])
-    y = spread(expert, x[:, HALF:], results[0], returned)
-    far = swap_groups(y.reshape(8, 64, HALF), FAR)
-    far = jnp.sum(far.astype(F32), axis=0).astype(BF16)
-    near = swap_groups(far.reshape(8, 8, HALF), NEAR)
-    near = jnp.sum(near.astype(F32), axis=0)
-    return jnp.concatenate([near[:4], near[4:]], axis=1).astype(BF16)
+    mine, sent = select(expert, x)
+    arrived = to_sibling(sent)
+    hidden = first_half(expert, mine, gate, up)
+    hidden_sent = first_half(expert, arrived, gate, up, (hidden,))
+    returned = to_sibling(second_half(hidden_sent, down))
+    y = spread(expert, x[:, HALF:], second_half(hidden, down), returned)
+    far = total(swap_groups(y.reshape(8, 64, HALF), FAR))
+    return finish(swap_groups(far.reshape(8, 8, HALF), NEAR))
 
 
 def solution(mesh):

time: 138 us -> 113 us (0.82)
  waiting for transfers between devices: 38.3 us -> 1.74 us
  blocking collectives: 61.6 us -> 88.7 us
  Pallas kernels: 24.7 us -> 16.6 us
  other arithmetic: 3.31 us -> 0.01 us
  starting transfers between devices: 4.8 us -> 2.41 us
    all_to_all x1 -> x0, waiting for transfers between devices: 31.7 us -> none  [swap_groups(): lax.all_to_all(values, AXES, 0, 0, axis_index_groups=groups, tiled=True)]
    all_to_all x3 -> x4, blocking collectives: 61.6 us -> 88.7 us  [swap_groups(): lax.all_to_all(values, AXES, 0, 0, axis_index_groups=groups, tiled=True)]
    pallas_call x2 -> x7, Pallas kernels: 20.2 us -> 13.7 us  [the longest x2 5.64 us: first_half(): pl.pallas_call(hidden_units_after if earlier else hidden_units, out_shape...]
    ppermute x2, waiting for transfers between devices: 6.56 us -> 1.74 us  [to_sibling(): return lax.ppermute(values, 'dev', [(i, i ^ 1) for i in range(32)])]
    all_to_all x1 -> x0, starting transfers between devices: 4.51 us -> none  [swap_groups(): lax.all_to_all(values, AXES, 0, 0, axis_index_groups=groups, tiled=True)]
    reduce_sum x2 -> x0, other arithmetic: 2.66 us -> none  [the longest x1 2.6 us: body(): far = jnp.sum(far.astype(F32), axis=0).astype(BF16)]
    unnamed x0 -> x16, local copies, waits for them, and re-layouts: none -> 2.21 us
    ppermute x2, starting transfers between devices: 0.29 us -> 2.41 us  [to_sibling(): return lax.ppermute(values, 'dev', [(i, i ^ 1) for i in range(32)])]
  transfers between devices with their start and end apart: 3 -> 2, of which waited for: 3 -> 2; matrix products, arithmetic and copies ran while one was open for 1% -> 0% of each run, Pallas kernels for 0% -> 5%
where the time goes in v2:
time: 113 us; the launch traced here: 112 us
  blocking collectives  88.7 us (78%)
  Pallas kernels  16.6 us (15%)
  local copies, waits for them, and re-layouts  2.5 us (2%)
  starting transfers between devices  2.41 us (2%)
  waiting for transfers between devices  1.74 us (2%)
    all_to_all x4, blocking collectives, swap_groups(): lax.all_to_all(values, AXES, 0, 0, axis_index_groups=groups, tiled=True)  88.7 us
    pallas_call x2, Pallas kernels, first_half(): pl.pallas_call(hidden_units_after if earlier else hidden_units, out_shape...  5.64 us
    pallas_call x2, Pallas kernels, second_half(): pl.pallas_call(down_rows, out_shape=jax.ShapeDtypeStruct((SEL, D), BF16),...  4.47 us
    pallas_call x1, Pallas kernels, spread(): pl.pallas_call(spread_kernel, out_shape=jax.ShapeDtypeStruct((ROWS, HALF)...  2.84 us
    ppermute x2, starting transfers between devices, to_sibling(): return lax.ppermute(values, 'dev', [(i, i ^ 1) for i in range(32)])  2.41 us
    pallas_call x1, Pallas kernels, select(): pl.pallas_call(select_kernel, out_shape=[jax.ShapeDtypeStruct((SEL, D + E...  2.4 us
  transfers between devices with their start and end apart: 2, of which 2 were waited for; matrix products, arithmetic and copies ran while one was open for 0% of the time, Pallas kernels for 5%

profile of v2, /device:TPU:1, one launch (start us, length us, event | category | flops | bytes accessed | tf_op | source)
XLA Modules:
  0.0 112.1 jit_solution(2353139066022572529)
XLA Ops:
  0.0 0.0 copy-start.1
  0.0 0.8 copy-done.1
  0.8 0.0 copy-start.2
  0.8 0.7 copy-done.2
  1.5 0.0 copy-start.3
  1.5 0.7 copy-done.3
  2.2 0.1 pack.1
  2.3 20.9 %all_to_all.20 = bf16[8,8,3712]{2,1,0:T(8,128)(2,1)S(1)} all-to-all(bf16[8,8,3712]{2,1,0:T(8,128)(2,1)S(1)} %pack.1), channel_id=1, replica_groups={{0,2,8,10,32,34,40,42},{1,7,25,31,97,103,121,127},{3,5,27,29,99,101,123..., dimensions={0} | all-to-all | bytes 950272 | tf_op jit(solution)/shard_map/all_to_all | solution.py:50
  23.2 0.3 broadcast_in_dim.8
  23.5 0.0 slice-start.1
  23.5 28.1 %all_to_all.21 = bf16[8,64,3712]{2,1,0:T(8,128)(2,1)S(1)} all-to-all(bf16[8,64,3712]{2,1,0:T(8,128)(2,1)S(1)} %broadcast_in_dim.8), channel_id=1, replica_groups={{0,6,24,30,96,102,120,126},{1,3,9,11,33,35,41,43},{2,4,26,28,98,100,122..., dimensions={0} | all-to-all | bytes 7602176 | tf_op jit(solution)/shard_map/all_to_all | solution.py:50
  51.6 2.4 %select.1 = (bf16[128,7296]{1,0:T(8,128)(2,1)S(1)}, bf16[128,7296]{1,0:T(8,128)(2,1)S(1)}) custom-call(s32[1]{0:T(128)} %bitcast.expert_ref, bf16[512,3712]{1,0:T(8,128)(2,1)S(1)} %bitcast.9), custom_call_target="tpu_custom_call" | custom-call | tf_op jit(solution)/shard_map/select/pallas_call | solution.py:123
  54.0 2.0 %collective-permute-start = (bf16[128,7296]{1,0:T(8,128)(2,1)S(1)}, bf16[128,7296]{1,0:T(8,128)(2,1)S(1)}, u32[]{:S(2)}, u32[]{:S(2)}) collective-permute-start(bf16[128,7296]{1,0:T(8,128)(2,1)S(1)} %get-tuple-element.8), channel_id=1, source_target_pairs={{0,1},{1,0},{2,3},{3,2},{4,5},{5,4},{6,7},{7,6},{8,9},{9,8},{10,11... | collective-permute-start | bytes 5603336 | tf_op jit(solution)/shard_map/ppermute | solution.py:54
  55.9 0.0 slice-done
  55.9 0.0 copy-done
  55.9 0.0 slice-done.1
  55.9 0.0 slice-start.2
  55.9 2.8 %hidden.2.earlier_ref = bf16[128,512]{1,0:T(8,128)(2,1)S(1)} custom-call(s32[1]{0:T(128)} %bitcast.expert_ref, bf16[128,7296]{1,0:T(8,128)(2,1)S(1)} %get-tuple-element.7.x_ref, bf16[1,7168,512]{2,1,0:T(8,128)(2,1)S(1)} %bitcast.6, bf16[1,7168,512]{2,1,0:T(8,128)(2,1)S(1)} %copy-done), custom_call_target="tpu_custom_call" | custom-call | flops 1879048192 | bytes 17825792 | tf_op jit(solution)/shard_map/hidden/pallas_call | solution.py:170
  58.8 0.0 slice-start.3
  58.8 0.6 collective-permute-done.x_ref
  59.4 2.8 %hidden.3 = bf16[128,512]{1,0:T(8,128)(2,1)S(1)} custom-call(s32[1]{0:T(128)} %bitcast.expert_ref, bf16[128,7296]{1,0:T(8,128)(2,1)S(1)} %collective-permute-done.x_ref, bf16[1,7168,512]{2,1,0:T(8,128)(2,1)S(1)} %bitcast.6, bf16[1,7168,512]{2,1,0:T(8,128)(2,1)S(1)} %copy-done, bf16[128,512]{1,0:T(8,128)(2,1)S(1)} %hidden.2.earlier_ref), custom_call_target="tpu_custom_call" | custom-call | flops 1879048192 | bytes 17825792 | tf_op jit(solution)/shard_map/hidden/pallas_call | solution.py:170
  62.2 0.0 slice-done.2
  62.2 0.0 slice-done.3
  62.2 2.2 %down.3 = bf16[128,7168]{1,0:T(8,128)(2,1)S(1)} custom-call(bf16[128,512]{1,0:T(8,128)(2,1)S(1)} %hidden.3, bf16[1,512,7168]{2,1,0:T(8,128)(2,1)S(1)} %bitcast.8), custom_call_target="tpu_custom_call" | custom-call | flops 939524096 | bytes 9437184 | tf_op jit(solution)/shard_map/down/pallas_call | solution.py:183
  64.5 0.5 collective-permute-start.1
  64.9 2.2 %down.2.mine_ref = bf16[128,7168]{1,0:T(8,128)(2,1)S(1)} custom-call(bf16[128,512]{1,0:T(8,128)(2,1)S(1)} %hidden.2.earlier_ref, bf16[1,512,7168]{2,1,0:T(8,128)(2,1)S(1)} %bitcast.8), custom_call_target="tpu_custom_call" | custom-call | flops 939524096 | bytes 9437184 | tf_op jit(solution)/shard_map/down/pallas_call | solution.py:183
  67.2 1.2 %collective-permute-done.1.theirs_ref = bf16[128,7168]{1,0:T(8,128)(2,1)S(1)} collective-permute-done((bf16[128,7168]{1,0:T(8,128)(2,1)S(1)}, bf16[128,7168]{1,0:T(8,128)(2,1)S(1)}, u32[]{:S(2)}, u32[]{:S(2)}) %collective-permute-start.1) | collective-permute-done | bytes 1835040 | tf_op jit(solution)/shard_map/ppermute | solution.py:54
  68.3 2.8 %spread.1 = bf16[512,3584]{1,0:T(8,128)(2,1)S(1)} custom-call(s32[1]{0:T(128)} %bitcast.expert_ref, bf16[512,128]{1,0:T(8,128)(2,1)S(1)} %slice.4.route_ref, bf16[128,7168]{1,0:T(8,128)(2,1)S(1)} %down.2.mine_ref, bf16[128,7168]{1,0:T(8,128)(2,1)S(1)} %collective-permute-done.1.theirs_ref), custom_call_target="tpu_custom_call" | custom-call | tf_op jit(solution)/shard_map/spread/pallas_call | solution.py:222
  71.2 26.9 %all_to_all.22.parts_ref = bf16[8,64,3584]{2,1,0:T(8,128)(2,1)S(1)} all-to-all(bf16[8,64,3584]{2,1,0:T(8,128)(2,1)S(1)} %bitcast.11), channel_id=1, replica_groups={{0,6,24,30,96,102,120,126},{1,3,9,11,33,35,41,43},{2,4,26,28,98,100,122..., dimensions={0} | all-to-all | bytes 7340032 | tf_op jit(solution)/shard_map/all_to_all | solution.py:50
  98.0 0.5 total.1
  98.5 12.9 %all_to_all.23.parts_ref = bf16[8,8,3584]{2,1,0:T(8,128)(2,1)S(1)} all-to-all(bf16[8,8,3584]{2,1,0:T(8,128)(2,1)S(1)} %bitcast.12), channel_id=1, replica_groups={{0,2,8,10,32,34,40,42},{1,7,25,31,97,103,121,127},{3,5,27,29,99,101,123..., dimensions={0} | all-to-all | bytes 917504 | tf_op jit(solution)/shard_map/all_to_all | solution.py:50
  111.4 0.7 finish.1
  (5 shorter events, 0.0 us)
Async XLA Ops:
  0.0 0.8 copy-start.1
  0.8 0.7 copy-start.2
  1.5 0.7 copy-start.3
  23.2 32.7 %slice-start = ((s8[7340032]{0:T(1024)(128)(4,1)}), s8[3145728]{0:T(1024)(128)(4,1)S(1)}, s32[]{:S(2)}) async-start(s8[7340032]{0:T(1024)(128)(4,1)} %bitcast.5), calls=%async_computation.4 | async-start | bytes 6291456
  23.2 32.7 %copy-start = (bf16[1,7168,512]{2,1,0:T(8,128)(2,1)S(1)}, bf16[1,7168,512]{2,1,0:T(8,128)(2,1)}, u32[]{:S(2)}) copy-start(bf16[1,7168,512]{2,1,0:T(8,128)(2,1)} %up_ref.3) | copy-start | bytes 22020100
  23.5 32.5 %slice-start.1 = ((s8[7340032]{0:T(1024)(128)(4,1)}), s8[4194304]{0:T(1024)(128)(4,1)S(1)}, s32[]{:S(2)}) async-start(s8[7340032]{0:T(1024)(128)(4,1)} %bitcast.5), calls=%async_computation.5 | async-start | bytes 8388608
  54.0 5.4 %collective-permute-start = (bf16[128,7296]{1,0:T(8,128)(2,1)S(1)}, bf16[128,7296]{1,0:T(8,128)(2,1)S(1)}, u32[]{:S(2)}, u32[]{:S(2)}) collective-permute-start(bf16[128,7296]{1,0:T(8,128)(2,1)S(1)} %get-tuple-element.8), channel_id=1, source_target_pairs={{0,1},{1,0},{2,3},{3,2},{4,5},{5,4},{6,7},{7,6},{8,9},{9,8},{10,11... | collective-permute-start | bytes 5603336 | tf_op jit(solution)/shard_map/ppermute | solution.py:54
  55.9 6.3 %slice-start.2 = ((s8[7340032]{0:T(1024)(128)(4,1)}), s8[4194304]{0:T(1024)(128)(4,1)S(1)}, s32[]{:S(2)}) async-start(s8[7340032]{0:T(1024)(128)(4,1)} %bitcast.7), calls=%async_computation.6 | async-start | bytes 8388608
  58.8 3.4 %slice-start.3 = ((s8[7340032]{0:T(1024)(128)(4,1)}), s8[3145728]{0:T(1024)(128)(4,1)S(1)}, s32[]{:S(2)}) async-start(s8[7340032]{0:T(1024)(128)(4,1)} %bitcast.7), calls=%async_computation.7 | async-start | bytes 6291456
  64.5 3.9 %collective-permute-start.1 = (bf16[128,7168]{1,0:T(8,128)(2,1)S(1)}, bf16[128,7168]{1,0:T(8,128)(2,1)S(1)}, u32[]{:S(2)}, u32[]{:S(2)}) collective-permute-start(bf16[128,7168]{1,0:T(8,128)(2,1)S(1)} %down.3), channel_id=1, source_target_pairs={{0,1},{1,0},{2,3},{3,2},{4,5},{5,4},{6,7},{7,6},{8,9},{9,8},{10,11... | collective-permute-start | bytes 5505032 | tf_op jit(solution)/shard_map/ppermute | solution.py:54

commit v3 on v2

v3 whole, which is shorter than its diff:
```python
import functools

import jax
import jax.numpy as jnp
from jax import lax
from jax.experimental import pallas as pl
from jax.experimental.pallas import tpu as pltpu
from jax.sharding import PartitionSpec as P

AXES = ("grp", "dev")
D = 7168
HALF = D // 2
EXT = 128
WIDE = HALF + EXT
BLOCK = 64
PART = 4 * BLOCK
SEL = 64
F32 = jnp.float32
BF16 = jnp.bfloat16
MIB = 1 << 20
VMEM = pl.BlockSpec(memory_space=pltpu.VMEM)
SMEM = pl.BlockSpec(memory_space=pltpu.SMEM)


BRIEF = pl.CostEstimate(flops=1000, bytes_accessed=1000, transcendentals=0)


def flat(z, x, y, c):
    return ((z * 4 + x) * 4 + y) * 2 + c


def near_groups():
    seen, groups = set(), []
    for z in range(4):
        for x in range(4):
            for y in range(4):
                for c in range(2):
                    if flat(z, x, y, c) in seen:
                        continue
                    m = 3 if c else 1
                    members = [
                        flat(z ^ (m * i), x ^ (m * j), y ^ (m * k), c)
                        for i in (0, 1) for j in (0, 1) for k in (0, 1)
                    ]
                    seen.update(members)
                    groups.append(members)
    return groups


def far_pairs(axis):
    pairs = []
    for z in range(4):
        for x in range(4):
            for y in range(4):
                for c in range(2):
                    at = [z, x, y]
                    at[axis] ^= 1 if c else 3
                    pairs.append((flat(z, x, y, c), flat(*at, c)))
    return pairs


NEAR = near_groups()
FAR = [far_pairs(axis) for axis in range(3)]


def swap_near(values):
    return lax.all_to_all(values, AXES, 0, 0, axis_index_groups=NEAR, tiled=True)


def swap_far(values, axis):
    return lax.ppermute(values, AXES, FAR[axis])


def to_sibling(values):
    return lax.ppermute(values, "dev", [(i, i ^ 1) for i in range(32)])


def pack_kernel(expert_ref, tokens_ref, ids_ref, weights_ref, out_ref):
    del expert_ref
    lane = lax.broadcasted_iota(jnp.int32, (4, EXT), 1)
    dense = jnp.zeros((4, EXT), F32)
    for k in range(8):
        dense += jnp.where(ids_ref[:, k : k + 1] == lane % 32, weights_ref[:, k : k + 1], 0.0)
    high = dense.astype(BF16).astype(F32)
    route = jnp.where(lane < 32, high, jnp.where(lane < 64, dense - high, 0.0))
    rows = tokens_ref[...].astype(F32)
    left = jnp.concatenate([rows[:, :HALF], route], axis=1)
    right = jnp.concatenate([rows[:, HALF:], route], axis=1)
    block = jnp.concatenate([left, right], axis=0).astype(BF16)
    for i in range(8):
        out_ref[i] = block


def pack(expert, tokens, ids, weights):
    return pl.pallas_call(
        pack_kernel,
        out_shape=jax.ShapeDtypeStruct((8, 8, WIDE), BF16),
        compiler_params=pltpu.CompilerParams(vmem_limit_bytes=4 * MIB),
        in_specs=[SMEM, VMEM, VMEM, VMEM],
        out_specs=VMEM,
        name="pack",
    )(expert, tokens, ids, weights)


def expert_lanes(expert, shape, dim):
    lane = lax.broadcasted_iota(jnp.int32, shape, dim)
    return (lane < 64) & (lane % 32 == expert)


def select_kernel(expert_ref, a_ref, b_ref, c_ref, d_ref, after_ref, mine_ref, sent_ref, pick):
    del after_ref
    blocks = (a_ref, b_ref, c_ref, d_ref)
    own = expert_ref[0]
    turn = lax.broadcasted_iota(jnp.int32, (8, EXT), 0)
    experts = jnp.where(turn == 0, own, own ^ 1)
    wanted = jnp.where(expert_lanes(experts, (8, EXT), 1) & (turn < 2), 1.0, 0.0).astype(BF16)
    ext = jnp.concatenate([ref[:, HALF:] for ref in blocks], axis=0)
    route = lax.dot_general(wanted, ext, (((1,), (1,)), ((), ())), preferred_element_type=F32)
    chosen = route > 0
    first = lax.broadcasted_iota(jnp.int32, (PART, PART), 0)
    second = lax.broadcasted_iota(jnp.int32, (PART, PART), 1)
    earlier = jnp.where((first // 4 == second // 4) & (first < second), 1.0, 0.0).astype(BF16)
    rank = jnp.dot(jnp.where(chosen, 1.0, 0.0).astype(BF16), earlier, preferred_element_type=F32)
    column = lax.broadcasted_iota(jnp.int32, (8, PART), 1)
    place = jnp.where(chosen, column // 8 * 2 + rank.astype(jnp.int32), -1)
    row = lax.broadcasted_iota(jnp.int32, (SEL, PART), 0)
    is_left = lax.broadcasted_iota(jnp.int32, (SEL, PART), 1) % 8 < 4
    for e in range(2):
        hit = place[e : e + 1, :] == row
        pick[e * SEL : (e + 1) * SEL, :] = jnp.where(hit & is_left, 1.0, 0.0).astype(BF16)
        pick[(2 + e) * SEL : (3 + e) * SEL, :] = jnp.where(hit & ~is_left, 1.0, 0.0).astype(BF16)
    for n in range(0, HALF, 512):
        x = jnp.concatenate([ref[:, n : n + 512] for ref in blocks], axis=0)
        value = jnp.dot(pick[...], x, preferred_element_type=F32).astype(BF16)
        mine_ref[:, n : n + 512] = value[:SEL]
        sent_ref[:, n : n + 512] = value[SEL : 2 * SEL]
        mine_ref[:, HALF + n : HALF + n + 512] = value[2 * SEL : 3 * SEL]
        sent_ref[:, HALF + n : HALF + n + 512] = value[3 * SEL :]
    value = jnp.dot(pick[: 2 * SEL, :], ext, preferred_element_type=F32).astype(BF16)
    mine_ref[:, D:] = value[:SEL]
    sent_ref[:, D:] = value[SEL:]


def select(expert, blocks, after):
    return pl.pallas_call(
        select_kernel,
        out_shape=[jax.ShapeDtypeStruct((SEL, D + EXT), BF16)] * 2,
        in_specs=[SMEM] + [VMEM] * 4 + [pl.BlockSpec(memory_space=pl.ANY)],
        out_specs=[VMEM, VMEM],
        scratch_shapes=[pltpu.VMEM((PART, PART), BF16)],
        compiler_params=SMALL,
        cost_estimate=BRIEF,
        name="select",
    )(expert, *blocks, after)


DEPTH = 1792


def hidden_units(expert_ref, x_ref, gate_ref, up_ref, hidden, gate_sum, up_sum):
    for i in range(0, D, DEPTH):
        block = slice(i, i + DEPTH)
        x = x_ref[:, block]
        gate = jnp.dot(x, gate_ref[0, block, :], preferred_element_type=F32)
        up = jnp.dot(x, up_ref[0, block, :], preferred_element_type=F32)
        gate_sum[...] = gate if i == 0 else gate_sum[...] + gate
        up_sum[...] = up if i == 0 else up_sum[...] + up
    lanes = expert_lanes(expert_ref[0], (SEL, EXT), 1)
    scale = jnp.sum(jnp.where(lanes, x_ref[:, D:].astype(F32), 0.0), axis=1, keepdims=True)
    v = gate_sum[...]
    hidden[...] = (v / (1.0 + jnp.exp(-v)) * up_sum[...] * scale).astype(BF16)


def down_rows(hidden, down_ref, out_ref):
    for n in range(0, D, 1024):
        block = slice(n, n + 1024)
        out_ref[:, block] = jnp.dot(hidden[...], down_ref[0, :, block], preferred_element_type=F32).astype(BF16)


def hidden_units_after(expert_ref, x_ref, gate_ref, up_ref, earlier_ref, *rest):
    del earlier_ref
    hidden_units(expert_ref, x_ref, gate_ref, up_ref, *rest)


SUMS = [pltpu.VMEM((SEL, 512), F32), pltpu.VMEM((SEL, 512), F32)]
SMALL = pltpu.CompilerParams(vmem_limit_bytes=8 * MIB)


def load_kernel(source_ref, after_ref, out_ref, sem):
    del after_ref
    copy = pltpu.make_async_copy(source_ref, out_ref, sem)
    copy.start()
    copy.wait()


def load(source, after):
    return pl.pallas_call(
        load_kernel,
        out_shape=jax.ShapeDtypeStruct(source.shape, source.dtype),
        in_specs=[pl.BlockSpec(memory_space=pltpu.HBM), pl.BlockSpec(memory_space=pl.ANY)],
        out_specs=VMEM,
        scratch_shapes=[pltpu.SemaphoreType.DMA],
        compiler_params=SMALL,
        cost_estimate=BRIEF,
        name="load",
    )(pltpu.with_memory_space_constraint(source, pltpu.HBM), after)


def first_half(expert, x, gate, up, earlier=()):
    return pl.pallas_call(
        hidden_units_after if earlier else hidden_units,
        out_shape=jax.ShapeDtypeStruct((SEL, 512), BF16),
        in_specs=[SMEM, VMEM, VMEM, VMEM] + [VMEM] * len(earlier),
        out_specs=VMEM,
        scratch_shapes=SUMS,
        compiler_params=SMALL,
        cost_estimate=BRIEF,
        name="hidden",
    )(expert, x, gate, up, *earlier)


def second_half(hidden, down):
    return pl.pallas_call(
        down_rows,
        out_shape=jax.ShapeDtypeStruct((SEL, D), BF16),
        in_specs=[VMEM, VMEM],
        out_specs=VMEM,
        compiler_params=SMALL,
        cost_estimate=BRIEF,
        name="down",
    )(hidden, down)


def spread_kernel(count, expert_ref, a_ref, b_ref, c_ref, d_ref, mine_ref, theirs_ref, *refs):
    arrived, outs, place_scr = refs[:count], refs[count : count + 4], refs[count + 4]
    own = expert_ref[0]
    turn = lax.broadcasted_iota(jnp.int32, (EXT, EXT), 1)
    experts = jnp.where(turn == 0, own, own ^ 1)
    wanted = jnp.where(expert_lanes(experts, (EXT, EXT), 0) & (turn < 2), 1.0, 0.0).astype(BF16)
    ext = jnp.concatenate([ref[:, HALF:] for ref in (a_ref, b_ref, c_ref, d_ref)], axis=0)
    chosen = jnp.dot(ext, wanted, preferred_element_type=F32) > 0
    first = lax.broadcasted_iota(jnp.int32, (PART, PART), 0)
    second = lax.broadcasted_iota(jnp.int32, (PART, PART), 1)
    earlier = jnp.where((first // 4 == second // 4) & (second < first), 1.0, 0.0).astype(BF16)
    rank = jnp.dot(earlier, jnp.where(chosen, 1.0, 0.0).astype(BF16), preferred_element_type=F32)
    token = lax.broadcasted_iota(jnp.int32, (PART, EXT), 0)
    place = jnp.where(chosen, token // 8 * 2 + rank.astype(jnp.int32), -1)
    column = lax.broadcasted_iota(jnp.int32, (PART, 2 * SEL), 1)
    hit = jnp.where(column < SEL, place[:, 0:1], place[:, 1:2]) == column % SEL
    is_left = lax.broadcasted_iota(jnp.int32, (PART, 2 * SEL), 0) % 8 < 4
    place_scr[:, : 2 * SEL] = jnp.where(hit & is_left, 1.0, 0.0).astype(BF16)
    place_scr[:, 2 * SEL :] = jnp.where(hit & ~is_left, 1.0, 0.0).astype(BF16)
    for n in range(0, HALF, 512):
        left, right = slice(n, n + 512), slice(HALF + n, HALF + n + 512)
        y = jnp.concatenate([mine_ref[:, left], theirs_ref[:, left], mine_ref[:, right], theirs_ref[:, right]], axis=0)
        value = jnp.dot(place_scr[...], y, preferred_element_type=F32)
        for i in range(4):
            block = value[i * BLOCK : (i + 1) * BLOCK]
            if i < count:
                block += arrived[i][:, left].astype(F32)
            outs[i][:, left] = block.astype(BF16)


def spread(expert, blocks, mine, theirs, arrived=()):
    return pl.pallas_call(
        functools.partial(spread_kernel, len(arrived)),
        out_shape=[jax.ShapeDtypeStruct((BLOCK, HALF), BF16)] * 4,
        in_specs=[SMEM] + [VMEM] * (6 + len(arrived)),
        out_specs=[VMEM] * 4,
        scratch_shapes=[pltpu.VMEM((PART, 4 * SEL), BF16)],
        compiler_params=SMALL,
        cost_estimate=BRIEF,
        name="spread",
    )(expert, *blocks, mine, theirs, *arrived)


def add(*terms):
    total = terms[0].astype(F32)
    for term in terms[1:]:
        total += term.astype(F32)
    return total.astype(BF16)


def finish_kernel(parts_ref, out_ref):
    total = parts_ref[0].astype(F32)
    for i in range(1, 8):
        total += parts_ref[i].astype(F32)
    out_ref[:, :HALF] = total[:4].astype(BF16)
    out_ref[:, HALF:] = total[4:].astype(BF16)


def finish(parts):
    return pl.pallas_call(
        finish_kernel,
        out_shape=jax.ShapeDtypeStruct((4, D), BF16),
        in_specs=[VMEM],
        out_specs=VMEM,
        compiler_params=SMALL,
        name="finish",
    )(parts)


def body(tokens, ids, weights, gate, up, down):
    expert = lax.axis_index("dev").astype(jnp.int32).reshape(1)
    own = swap_near(pack(expert, tokens, ids, weights)).reshape(BLOCK, WIDE)
    x, y, z = swap_far(own, 0), swap_far(own, 1), swap_far(own, 2)
    up = load(up, own)
    xy, yz, zx = swap_far(y, 0), swap_far(z, 1), swap_far(x, 2)
    mine_near, sent_near = select(expert, (x, y, z, own), up)
    got_near = to_sibling(sent_near)
    hidden_mine_near = first_half(expert, mine_near, gate, up)
    xy, yz, zx, hidden_mine_near = lax.optimization_barrier((xy, yz, zx, hidden_mine_near))
    xyz = swap_far(yz, 0)
    hidden_got_near = first_half(expert, got_near, gate, up, (hidden_mine_near,))
    mine_far, sent_far = select(expert, (xy, zx, yz, xyz), hidden_got_near)
    got_far = to_sibling(sent_far)
    hidden_mine_far = first_half(expert, mine_far, gate, up, (hidden_got_near,))
    hidden_got_far = first_half(expert, got_far, gate, up, (hidden_mine_far,))
    returned = to_sibling(second_half(hidden_got_far, down))
    y_xy, y_zx, y_yz, y_xyz = spread(expert, (xy, zx, yz, xyz), second_half(hidden_mine_far, down), returned)
    at_yz = swap_far(y_xyz, 0)
    at_y, at_x = swap_far(y_xy, 0), swap_far(y_zx, 2)
    returned = to_sibling(second_half(hidden_got_near, down))
    at_z = swap_far(add(y_yz, at_yz), 1)
    y_x, y_y, y_z, y_own = spread(
        expert, (x, y, z, own), second_half(hidden_mine_near, down), returned, (at_x, at_y)
    )
    total = add(y_own, swap_far(y_x, 0), swap_far(y_y, 1), swap_far(add(y_z, at_z), 2))
    return finish(swap_near(total.reshape(8, 8, HALF)))


def solution(mesh):
    in_specs = (
        P(AXES, None),
        P(AXES, None),
        P(AXES, None),
        P("dev", None, "grp"),
        P("dev", None, "grp"),
        P("dev", "grp", None),
    )
    return jax.shard_map(body, mesh=mesh, in_specs=in_specs, out_specs=P(AXES, None), check_vma=False)
```

time: 113 us -> 103 us (0.912)
  blocking collectives: 88.7 us -> 36.6 us
  waiting for transfers between devices: 1.74 us -> 29.6 us
  Pallas kernels: 16.6 us -> 23.9 us
  starting transfers between devices: 2.41 us -> 9.49 us
    all_to_all x4 -> x2, blocking collectives: 88.7 us -> 36.6 us  [swap_near(): lax.all_to_all(values, AXES, 0, 0, axis_index_groups=NEAR, tiled=True)]
    ppermute x0 -> x14, waiting for transfers between devices: none -> 28.5 us  [swap_far(): return lax.ppermute(values, AXES, FAR[axis])]
    pallas_call x2 -> x4, Pallas kernels: 5.64 us -> 10.5 us  [first_half(): pl.pallas_call(hidden_units_after if earlier else hidden_units, out_shape...]
    ppermute x2 -> x4, starting transfers between devices: 2.41 us -> 6.29 us  [to_sibling(): return lax.ppermute(values, 'dev', [(i, i ^ 1) for i in range(32)])]
    ppermute x0 -> x14, starting transfers between devices: none -> 3.2 us  [swap_far(): return lax.ppermute(values, AXES, FAR[axis])]
    pallas_call x2 -> x3, Pallas kernels: 3.3 us -> 5.22 us  [the longest x1 3.09 us: load(): pl.pallas_call(load_kernel, out_shape=jax.ShapeDtypeStruct(source.shape,...]
    pallas_call x2 -> x4, Pallas kernels: 4.47 us -> 5.53 us  [second_half(): pl.pallas_call(down_rows, out_shape=jax.ShapeDtypeStruct((SEL, D), BF16),...]
    pallas_call x1 -> x2, Pallas kernels: 2.4 us -> 1.79 us  [select(): pl.pallas_call(select_kernel, out_shape=[jax.ShapeDtypeStruct((SEL, D + E...]
  transfers between devices with their start and end apart: 2 -> 18, of which waited for: 2 -> 11; matrix products, arithmetic and copies ran while one was open for 0% -> 0% of each run, Pallas kernels for 5% -> 17%
where the time goes in v3:
time: 103 us; the launch traced here: 102 us
  blocking collectives  36.6 us (36%)
  waiting for transfers between devices  29.6 us (29%)
  Pallas kernels  23.9 us (23%)
  starting transfers between devices  9.49 us (9%)
  local copies, waits for them, and re-layouts  2.2 us (2%)
    all_to_all x2, blocking collectives, swap_near(): lax.all_to_all(values, AXES, 0, 0, axis_index_groups=NEAR, tiled=True)  36.6 us
    ppermute x14, waiting for transfers between devices, swap_far(): return lax.ppermute(values, AXES, FAR[axis])  28.5 us
    pallas_call x4, Pallas kernels, first_half(): pl.pallas_call(hidden_units_after if earlier else hidden_units, out_shape...  10.5 us
    ppermute x4, starting transfers between devices, to_sibling(): return lax.ppermute(values, 'dev', [(i, i ^ 1) for i in range(32)])  6.29 us
    pallas_call x4, Pallas kernels, second_half(): pl.pallas_call(down_rows, out_shape=jax.ShapeDtypeStruct((SEL, D), BF16),...  5.53 us
    ppermute x14, starting transfers between devices, swap_far(): return lax.ppermute(values, AXES, FAR[axis])  3.2 us
    pallas_call x1, Pallas kernels, load(): pl.pallas_call(load_kernel, out_shape=jax.ShapeDtypeStruct(source.shape,...  3.09 us
    unnamed x14, local copies, waits for them, and re-layouts  2.2 us
  transfers between devices with their start and end apart: 18, of which 11 were waited for; matrix products, arithmetic and copies ran while one was open for 0% of the time, Pallas kernels for 17%

profile of v3, /device:TPU:1, one launch (start us, length us, event | category | flops | bytes accessed | tf_op | source)
XLA Modules:
  0.0 102.4 jit_solution(4408871600186144928)
XLA Ops:
  0.0 0.8 copy-done
  0.8 0.7 copy-done.1
  1.5 0.7 copy-done.2
  2.3 21.2 %all_to_all.10 = bf16[8,8,3712]{2,1,0:T(8,128)(2,1)S(1)} all-to-all(bf16[8,8,3712]{2,1,0:T(8,128)(2,1)S(1)} %pack.1), channel_id=1, replica_groups={{0,2,8,10,32,34,40,42},{1,7,25,31,97,103,121,127},{3,5,27,29,99,101,123..., dimensions={0} | all-to-all | bytes 950272 | tf_op jit(solution)/shard_map/all_to_all | solution.py:67
  23.6 7.4 %collective-permute-done.1.b_ref = bf16[64,3712]{1,0:T(8,128)(2,1)S(1)} collective-permute-done((bf16[64,3712]{1,0:T(8,128)(2,1)S(1)}, bf16[64,3712]{1,0:T(8,128)(2,1)S(1)}, u32[]{:S(2)}, u32[]{:S(2)}) %collective-permute-start.1) | collective-permute-done | bytes 475168 | tf_op jit(solution)/shard_map/ppermute | solution.py:71
  31.0 1.8 %collective-permute-start.4 = (bf16[64,3712]{1,0:T(8,128)(2,1)S(1)}, bf16[64,3712]{1,0:T(8,128)(2,1)S(1)}, u32[]{:S(2)}, u32[]{:S(2)}) collective-permute-start(bf16[64,3712]{1,0:T(8,128)(2,1)S(1)} %collective-permute-done.2.c_ref), channel_id=1, source_target_pairs={{0,24},{1,9},{2,26},{3,11},{4,28},{5,13},{6,30},{7,15},{8,16},{9,1... | collective-permute-start | bytes 1425416 | tf_op jit(solution)/shard_map/ppermute | solution.py:71
  32.7 3.1 %load.1.after_ref.up_ref = bf16[1,7168,512]{2,1,0:T(8,128)(2,1)S(1)} custom-call(bf16[1,7168,512]{2,1,0:T(8,128)(2,1)} %source_ref.1, bf16[64,3712]{1,0:T(8,128)(2,1)S(1)} %bitcast.11), custom_call_target="tpu_custom_call" | custom-call | flops 1000 | bytes 1000 | tf_op jit(solution)/shard_map/load/pallas_call | solution.py:197
  35.8 0.9 select.2
  36.7 0.8 collective-permute-start.6
  37.6 2.6 %hidden.4.earlier_ref = bf16[64,512]{1,0:T(8,128)(2,1)S(1)} custom-call(s32[1]{0:T(128)} %bitcast.expert_ref, bf16[64,7296]{1,0:T(8,128)(2,1)S(1)} %get-tuple-element.21.x_ref, bf16[1,7168,512]{2,1,0:T(8,128)(2,1)S(1)} %bitcast.5, bf16[1,7168,512]{2,1,0:T(8,128)(2,1)S(1)} %load.1.after_ref.up_ref), custom_call_target="tpu_custom_call" | custom-call | flops 1000 | bytes 1000 | tf_op jit(solution)/shard_map/hidden/pallas_call | solution.py:210
  40.9 2.6 %hidden.5.after_ref.earlier_ref = bf16[64,512]{1,0:T(8,128)(2,1)S(1)} custom-call(s32[1]{0:T(128)} %bitcast.expert_ref, bf16[64,7296]{1,0:T(8,128)(2,1)S(1)} %collective-permute-done.6.x_ref, bf16[1,7168,512]{2,1,0:T(8,128)(2,1)S(1)} %bitcast.5, bf16[1,7168,512]{2,1,0:T(8,128)(2,1)S(1)} %load.1.after_ref.up_ref, bf16[64,512]{1,0:T(8,128)(2,1)S(1)} %hidden.4.earlier_ref), custom_call_target="tpu_custom_call" | custom-call | flops 1000 | bytes 1000 | tf_op jit(solution)/shard_map/hidden/pallas_call | solution.py:210
  43.6 4.8 %collective-permute-done.8.d_ref = bf16[64,3712]{1,0:T(8,128)(2,1)S(1)} collective-permute-done((bf16[64,3712]{1,0:T(8,128)(2,1)S(1)}, bf16[64,3712]{1,0:T(8,128)(2,1)S(1)}, u32[]{:S(2)}, u32[]{:S(2)}) %collective-permute-start.8) | collective-permute-done | bytes 475168 | tf_op jit(solution)/shard_map/ppermute | solution.py:71
  48.3 0.9 select.3
  49.2 3.0 %collective-permute-start.9 = (bf16[64,7296]{1,0:T(8,128)(2,1)S(1)}, bf16[64,7296]{1,0:T(8,128)(2,1)S(1)}, u32[]{:S(2)}, u32[]{:S(2)}) collective-permute-start(bf16[64,7296]{1,0:T(8,128)(2,1)S(1)} %get-tuple-element.28), channel_id=1, source_target_pairs={{0,1},{1,0},{2,3},{3,2},{4,5},{5,4},{6,7},{7,6},{8,9},{9,8},{10,11... | collective-permute-start | bytes 2801672 | tf_op jit(solution)/shard_map/ppermute | solution.py:75
  52.2 2.6 %hidden.6.earlier_ref = bf16[64,512]{1,0:T(8,128)(2,1)S(1)} custom-call(s32[1]{0:T(128)} %bitcast.expert_ref, bf16[64,7296]{1,0:T(8,128)(2,1)S(1)} %get-tuple-element.27.x_ref, bf16[1,7168,512]{2,1,0:T(8,128)(2,1)S(1)} %bitcast.5, bf16[1,7168,512]{2,1,0:T(8,128)(2,1)S(1)} %load.1.after_ref.up_ref, bf16[64,512]{1,0:T(8,128)(2,1)S(1)} %hidden.5.after_ref.earlier_ref), custom_call_target="tpu_custom_call" | custom-call | flops 1000 | bytes 1000 | tf_op jit(solution)/shard_map/hidden/pallas_call | solution.py:210
  54.9 2.6 %hidden.7 = bf16[64,512]{1,0:T(8,128)(2,1)S(1)} custom-call(s32[1]{0:T(128)} %bitcast.expert_ref, bf16[64,7296]{1,0:T(8,128)(2,1)S(1)} %collective-permute-done.9.x_ref, bf16[1,7168,512]{2,1,0:T(8,128)(2,1)S(1)} %bitcast.5, bf16[1,7168,512]{2,1,0:T(8,128)(2,1)S(1)} %load.1.after_ref.up_ref, bf16[64,512]{1,0:T(8,128)(2,1)S(1)} %hidden.6.earlier_ref), custom_call_target="tpu_custom_call" | custom-call | flops 1000 | bytes 1000 | tf_op jit(solution)/shard_map/hidden/pallas_call | solution.py:210
  57.5 1.4 %down.7 = bf16[64,7168]{1,0:T(8,128)(2,1)S(1)} custom-call(bf16[64,512]{1,0:T(8,128)(2,1)S(1)} %hidden.7, bf16[1,512,7168]{2,1,0:T(8,128)(2,1)S(1)} %bitcast.7), custom_call_target="tpu_custom_call" | custom-call | flops 1000 | bytes 1000 | tf_op jit(solution)/shard_map/down/pallas_call | solution.py:223
  59.2 1.4 %down.6.mine_ref = bf16[64,7168]{1,0:T(8,128)(2,1)S(1)} custom-call(bf16[64,512]{1,0:T(8,128)(2,1)S(1)} %hidden.6.earlier_ref, bf16[1,512,7168]{2,1,0:T(8,128)(2,1)S(1)} %bitcast.7), custom_call_target="tpu_custom_call" | custom-call | flops 1000 | bytes 1000 | tf_op jit(solution)/shard_map/down/pallas_call | solution.py:223
  60.6 1.1 %collective-permute-done.10.theirs_ref = bf16[64,7168]{1,0:T(8,128)(2,1)S(1)} collective-permute-done((bf16[64,7168]{1,0:T(8,128)(2,1)S(1)}, bf16[64,7168]{1,0:T(8,128)(2,1)S(1)}, u32[]{:S(2)}, u32[]{:S(2)}) %collective-permute-start.10) | collective-permute-done | bytes 917536 | tf_op jit(solution)/shard_map/ppermute | solution.py:75
  61.7 1.1 %spread.2 = (bf16[64,3584]{1,0:T(8,128)(2,1)S(1)}, bf16[64,3584]{1,0:T(8,128)(2,1)S(1)}, bf16[64,3584]{1,0:T(8,128)(2,1)S(1)}, bf16[64,3584]{1,0:T(8,128)(2,1)S(1)}) custom-call(s32[1]{0:T(128)} %bitcast.expert_ref, bf16[64,3712]{1,0:T(8,128)(2,1)S(1)} %collective-permute-done.3.a_ref, bf16[64,3712]{1,0:T(8,128)(2,1)S(1)} %collective-permute-done.5.b_ref, ...), custom_call_target="tpu_custom_call" | custom-call | flops 1000 | bytes 1000 | tf_op jit(solution)/shard_map/spread/pallas_call | solution.py:265
  62.8 1.4 %down.5 = bf16[64,7168]{1,0:T(8,128)(2,1)S(1)} custom-call(bf16[64,512]{1,0:T(8,128)(2,1)S(1)} %hidden.5.after_ref.earlier_ref, bf16[1,512,7168]{2,1,0:T(8,128)(2,1)S(1)} %bitcast.7), custom_call_target="tpu_custom_call" | custom-call | flops 1000 | bytes 1000 | tf_op jit(solution)/shard_map/down/pallas_call | solution.py:223
  64.2 2.2 %collective-permute-start.7 = (bf16[64,7168]{1,0:T(8,128)(2,1)S(1)}, bf16[64,7168]{1,0:T(8,128)(2,1)S(1)}, u32[]{:S(2)}, u32[]{:S(2)}) collective-permute-start(bf16[64,7168]{1,0:T(8,128)(2,1)S(1)} %down.5), channel_id=1, source_target_pairs={{0,1},{1,0},{2,3},{3,2},{4,5},{5,4},{6,7},{7,6},{8,9},{9,8},{10,11... | collective-permute-start | bytes 2752520 | tf_op jit(solution)/shard_map/ppermute | solution.py:75
  66.4 4.0 %collective-permute-done.15 = bf16[64,3584]{1,0:T(8,128)(2,1)S(1)} collective-permute-done((bf16[64,3584]{1,0:T(8,128)(2,1)S(1)}, bf16[64,3584]{1,0:T(8,128)(2,1)S(1)}, u32[]{:S(2)}, u32[]{:S(2)}) %collective-permute-start.15) | collective-permute-done | bytes 458784 | tf_op jit(solution)/shard_map/ppermute | solution.py:71
  70.8 1.4 %down.4.mine_ref = bf16[64,7168]{1,0:T(8,128)(2,1)S(1)} custom-call(bf16[64,512]{1,0:T(8,128)(2,1)S(1)} %hidden.4.earlier_ref, bf16[1,512,7168]{2,1,0:T(8,128)(2,1)S(1)} %bitcast.7), custom_call_target="tpu_custom_call" | custom-call | flops 1000 | bytes 1000 | tf_op jit(solution)/shard_map/down/pallas_call | solution.py:223
  72.2 1.8 %collective-permute-done.11.refs_0_ = bf16[64,3584]{1,0:T(8,128)(2,1)S(1)} collective-permute-done((bf16[64,3584]{1,0:T(8,128)(2,1)S(1)}, bf16[64,3584]{1,0:T(8,128)(2,1)S(1)}, u32[]{:S(2)}, u32[]{:S(2)}) %collective-permute-start.11) | collective-permute-done | bytes 458784 | tf_op jit(solution)/shard_map/ppermute | solution.py:71
  74.0 1.3 %collective-permute-done.12.refs_1_ = bf16[64,3584]{1,0:T(8,128)(2,1)S(1)} collective-permute-done((bf16[64,3584]{1,0:T(8,128)(2,1)S(1)}, bf16[64,3584]{1,0:T(8,128)(2,1)S(1)}, u32[]{:S(2)}, u32[]{:S(2)}) %collective-permute-start.12) | collective-permute-done | bytes 458784 | tf_op jit(solution)/shard_map/ppermute | solution.py:71
  75.4 1.1 %spread.3 = (bf16[64,3584]{1,0:T(8,128)(2,1)S(1)}, bf16[64,3584]{1,0:T(8,128)(2,1)S(1)}, bf16[64,3584]{1,0:T(8,128)(2,1)S(1)}, bf16[64,3584]{1,0:T(8,128)(2,1)S(1)}) custom-call(s32[1]{0:T(128)} %bitcast.expert_ref, bf16[64,3712]{1,0:T(8,128)(2,1)S(1)} %collective-permute-done.a_ref, bf16[64,3712]{1,0:T(8,128)(2,1)S(1)} %collective-permute-done.1.b_ref, ...), custom_call_target="tpu_custom_call" | custom-call | flops 1000 | bytes 1000 | tf_op jit(solution)/shard_map/spread/pallas_call | solution.py:265
  76.8 1.5 %collective-permute-done.16 = bf16[64,3584]{1,0:T(8,128)(2,1)S(1)} collective-permute-done((bf16[64,3584]{1,0:T(8,128)(2,1)S(1)}, bf16[64,3584]{1,0:T(8,128)(2,1)S(1)}, u32[]{:S(2)}, u32[]{:S(2)}) %collective-permute-start.16) | collective-permute-done | bytes 458784 | tf_op jit(solution)/shard_map/ppermute | solution.py:71
  78.6 5.5 %collective-permute-done.13 = bf16[64,3584]{1,0:T(8,128)(2,1)S(1)} collective-permute-done((bf16[64,3584]{1,0:T(8,128)(2,1)S(1)}, bf16[64,3584]{1,0:T(8,128)(2,1)S(1)}, u32[]{:S(2)}, u32[]{:S(2)}) %collective-permute-start.13) | collective-permute-done | bytes 458784 | tf_op jit(solution)/shard_map/ppermute | solution.py:71
  84.2 1.8 %collective-permute-done.17 = bf16[64,3584]{1,0:T(8,128)(2,1)S(1)} collective-permute-done((bf16[64,3584]{1,0:T(8,128)(2,1)S(1)}, bf16[64,3584]{1,0:T(8,128)(2,1)S(1)}, u32[]{:S(2)}, u32[]{:S(2)}) %collective-permute-start.17) | collective-permute-done | bytes 458784 | tf_op jit(solution)/shard_map/ppermute | solution.py:71
  86.3 15.4 %all_to_all.11.parts_ref = bf16[8,8,3584]{2,1,0:T(8,128)(2,1)S(1)} all-to-all(bf16[8,8,3584]{2,1,0:T(8,128)(2,1)S(1)} %fusion), channel_id=1, replica_groups={{0,2,8,10,32,34,40,42},{1,7,25,31,97,103,121,127},{3,5,27,29,99,101,123..., dimensions={0} | all-to-all | bytes 917504 | tf_op jit(solution)/shard_map/all_to_all | solution.py:67
  101.7 0.7 finish.1
  (40 shorter events, 2.7 us)
Async XLA Ops:
  0.0 0.8 copy-start
  0.8 0.7 copy-start.1
  1.5 0.7 copy-start.2
  2.3 35.3 %slice-start = ((s8[7340032]{0:T(1024)(128)(4,1)}), s8[4194304]{0:T(1024)(128)(4,1)S(1)}, s32[]{:S(2)}) async-start(s8[7340032]{0:T(1024)(128)(4,1)} %bitcast.4), calls=%async_computation.2 | async-start | bytes 8388608
  23.5 14.1 %slice-start.1 = ((s8[7340032]{0:T(1024)(128)(4,1)}), s8[3145728]{0:T(1024)(128)(4,1)S(1)}, s32[]{:S(2)}) async-start(s8[7340032]{0:T(1024)(128)(4,1)} %bitcast.4), calls=%async_computation.3 | async-start | bytes 6291456
  23.5 7.5 %collective-permute-start.1 = (bf16[64,3712]{1,0:T(8,128)(2,1)S(1)}, bf16[64,3712]{1,0:T(8,128)(2,1)S(1)}, u32[]{:S(2)}, u32[]{:S(2)}) collective-permute-start(bf16[64,3712]{1,0:T(8,128)(2,1)S(1)} %bitcast.8), channel_id=1, source_target_pairs={{0,24},{1,9},{2,26},{3,11},{4,28},{5,13},{6,30},{7,15},{8,16},{9,1... | collective-permute-start | bytes 1425416 | tf_op jit(solution)/shard_map/ppermute | solution.py:71
  23.5 7.5 %collective-permute-start.2 = (bf16[64,3712]{1,0:T(8,128)(2,1)S(1)}, bf16[64,3712]{1,0:T(8,128)(2,1)S(1)}, u32[]{:S(2)}, u32[]{:S(2)}) collective-permute-start(bf16[64,3712]{1,0:T(8,128)(2,1)S(1)} %bitcast.9), channel_id=1, source_target_pairs={{0,6},{1,3},{2,4},{3,1},{4,2},{5,7},{6,0},{7,5},{8,14},{9,11},{10,... | collective-permute-start | bytes 1425416 | tf_op jit(solution)/shard_map/ppermute | solution.py:71
  23.5 9.3 %collective-permute-start = (bf16[64,3712]{1,0:T(8,128)(2,1)S(1)}, bf16[64,3712]{1,0:T(8,128)(2,1)S(1)}, u32[]{:S(2)}, u32[]{:S(2)}) collective-permute-start(bf16[64,3712]{1,0:T(8,128)(2,1)S(1)} %bitcast.10), channel_id=1, source_target_pairs={{0,96},{1,33},{2,98},{3,35},{4,100},{5,37},{6,102},{7,39},{8,104},... | collective-permute-start | bytes 1425416 | tf_op jit(solution)/shard_map/ppermute | solution.py:71
  31.0 9.3 %collective-permute-start.3 = (bf16[64,3712]{1,0:T(8,128)(2,1)S(1)}, bf16[64,3712]{1,0:T(8,128)(2,1)S(1)}, u32[]{:S(2)}, u32[]{:S(2)}) collective-permute-start(bf16[64,3712]{1,0:T(8,128)(2,1)S(1)} %collective-permute-done.1.b_ref), channel_id=1, source_target_pairs={{0,96},{1,33},{2,98},{3,35},{4,100},{5,37},{6,102},{7,39},{8,104},... | collective-permute-start | bytes 1425416 | tf_op jit(solution)/shard_map/ppermute | solution.py:71
  31.0 9.3 %collective-permute-start.4 = (bf16[64,3712]{1,0:T(8,128)(2,1)S(1)}, bf16[64,3712]{1,0:T(8,128)(2,1)S(1)}, u32[]{:S(2)}, u32[]{:S(2)}) collective-permute-start(bf16[64,3712]{1,0:T(8,128)(2,1)S(1)} %collective-permute-done.2.c_ref), channel_id=1, source_target_pairs={{0,24},{1,9},{2,26},{3,11},{4,28},{5,13},{6,30},{7,15},{8,16},{9,1... | collective-permute-start | bytes 1425416 | tf_op jit(solution)/shard_map/ppermute | solution.py:71
  32.7 7.8 %collective-permute-start.5 = (bf16[64,3712]{1,0:T(8,128)(2,1)S(1)}, bf16[64,3712]{1,0:T(8,128)(2,1)S(1)}, u32[]{:S(2)}, u32[]{:S(2)}) collective-permute-start(bf16[64,3712]{1,0:T(8,128)(2,1)S(1)} %collective-permute-done.a_ref), channel_id=1, source_target_pairs={{0,6},{1,3},{2,4},{3,1},{4,2},{5,7},{6,0},{7,5},{8,14},{9,11},{10,... | collective-permute-start | bytes 1425416 | tf_op jit(solution)/shard_map/ppermute | solution.py:71
  36.7 4.2 %collective-permute-start.6 = (bf16[64,7296]{1,0:T(8,128)(2,1)S(1)}, bf16[64,7296]{1,0:T(8,128)(2,1)S(1)}, u32[]{:S(2)}, u32[]{:S(2)}) collective-permute-start(bf16[64,7296]{1,0:T(8,128)(2,1)S(1)} %get-tuple-element.23), channel_id=1, source_target_pairs={{0,1},{1,0},{2,3},{3,2},{4,5},{5,4},{6,7},{7,6},{8,9},{9,8},{10,11... | collective-permute-start | bytes 2801672 | tf_op jit(solution)/shard_map/ppermute | solution.py:75
  40.5 7.8 %collective-permute-start.8 = (bf16[64,3712]{1,0:T(8,128)(2,1)S(1)}, bf16[64,3712]{1,0:T(8,128)(2,1)S(1)}, u32[]{:S(2)}, u32[]{:S(2)}) collective-permute-start(bf16[64,3712]{1,0:T(8,128)(2,1)S(1)} %collective-permute-done.4.c_ref), channel_id=1, source_target_pairs={{0,96},{1,33},{2,98},{3,35},{4,100},{5,37},{6,102},{7,39},{8,104},... | collective-permute-start | bytes 1425416 | tf_op jit(solution)/shard_map/ppermute | solution.py:71
  49.2 5.6 %collective-permute-start.9 = (bf16[64,7296]{1,0:T(8,128)(2,1)S(1)}, bf16[64,7296]{1,0:T(8,128)(2,1)S(1)}, u32[]{:S(2)}, u32[]{:S(2)}) collective-permute-start(bf16[64,7296]{1,0:T(8,128)(2,1)S(1)} %get-tuple-element.28), channel_id=1, source_target_pairs={{0,1},{1,0},{2,3},{3,2},{4,5},{5,4},{6,7},{7,6},{8,9},{9,8},{10,11... | collective-permute-start | bytes 2801672 | tf_op jit(solution)/shard_map/ppermute | solution.py:75
  52.2 5.3 %slice-start.2 = ((s8[7340032]{0:T(1024)(128)(4,1)}), s8[4194304]{0:T(1024)(128)(4,1)S(1)}, s32[]{:S(2)}) async-start(s8[7340032]{0:T(1024)(128)(4,1)} %bitcast.6), calls=%async_computation.4 | async-start | bytes 8388608
  54.9 2.7 %slice-start.3 = ((s8[7340032]{0:T(1024)(128)(4,1)}), s8[3145728]{0:T(1024)(128)(4,1)S(1)}, s32[]{:S(2)}) async-start(s8[7340032]{0:T(1024)(128)(4,1)} %bitcast.6), calls=%async_computation.5 | async-start | bytes 6291456
  58.9 2.7 %collective-permute-start.10 = (bf16[64,7168]{1,0:T(8,128)(2,1)S(1)}, bf16[64,7168]{1,0:T(8,128)(2,1)S(1)}, u32[]{:S(2)}, u32[]{:S(2)}) collective-permute-start(bf16[64,7168]{1,0:T(8,128)(2,1)S(1)} %down.7), channel_id=1, source_target_pairs={{0,1},{1,0},{2,3},{3,2},{4,5},{5,4},{6,7},{7,6},{8,9},{9,8},{10,11... | collective-permute-start | bytes 2752520 | tf_op jit(solution)/shard_map/ppermute | solution.py:75
  62.7 7.7 %collective-permute-start.15 = (bf16[64,3584]{1,0:T(8,128)(2,1)S(1)}, bf16[64,3584]{1,0:T(8,128)(2,1)S(1)}, u32[]{:S(2)}, u32[]{:S(2)}) collective-permute-start(bf16[64,3584]{1,0:T(8,128)(2,1)S(1)} %get-tuple-element.36), channel_id=1, source_target_pairs={{0,96},{1,33},{2,98},{3,35},{4,100},{5,37},{6,102},{7,39},{8,104},... | collective-permute-start | bytes 1376264 | tf_op jit(solution)/shard_map/ppermute | solution.py:71
  64.2 8.0 %collective-permute-start.7 = (bf16[64,7168]{1,0:T(8,128)(2,1)S(1)}, bf16[64,7168]{1,0:T(8,128)(2,1)S(1)}, u32[]{:S(2)}, u32[]{:S(2)}) collective-permute-start(bf16[64,7168]{1,0:T(8,128)(2,1)S(1)} %down.5), channel_id=1, source_target_pairs={{0,1},{1,0},{2,3},{3,2},{4,5},{5,4},{6,7},{7,6},{8,9},{9,8},{10,11... | collective-permute-start | bytes 2752520 | tf_op jit(solution)/shard_map/ppermute | solution.py:75
  66.4 7.6 %collective-permute-start.11 = (bf16[64,3584]{1,0:T(8,128)(2,1)S(1)}, bf16[64,3584]{1,0:T(8,128)(2,1)S(1)}, u32[]{:S(2)}, u32[]{:S(2)}) collective-permute-start(bf16[64,3584]{1,0:T(8,128)(2,1)S(1)} %get-tuple-element.29), channel_id=1, source_target_pairs={{0,6},{1,3},{2,4},{3,1},{4,2},{5,7},{6,0},{7,5},{8,14},{9,11},{10,... | collective-permute-start | bytes 1376264 | tf_op jit(solution)/shard_map/ppermute | solution.py:71
  66.4 8.9 %collective-permute-start.12 = (bf16[64,3584]{1,0:T(8,128)(2,1)S(1)}, bf16[64,3584]{1,0:T(8,128)(2,1)S(1)}, u32[]{:S(2)}, u32[]{:S(2)}) collective-permute-start(bf16[64,3584]{1,0:T(8,128)(2,1)S(1)} %get-tuple-element.30), channel_id=1, source_target_pairs={{0,96},{1,33},{2,98},{3,35},{4,100},{5,37},{6,102},{7,39},{8,104},... | collective-permute-start | bytes 1376264 | tf_op jit(solution)/shard_map/ppermute | solution.py:71
  70.6 7.7 %collective-permute-start.16 = (bf16[64,3584]{1,0:T(8,128)(2,1)S(1)}, bf16[64,3584]{1,0:T(8,128)(2,1)S(1)}, u32[]{:S(2)}, u32[]{:S(2)}) collective-permute-start(bf16[64,3584]{1,0:T(8,128)(2,1)S(1)} %add_convert_fusion.2), channel_id=1, source_target_pairs={{0,24},{1,9},{2,26},{3,11},{4,28},{5,13},{6,30},{7,15},{8,16},{9,1... | collective-permute-start | bytes 1376264 | tf_op jit(solution)/shard_map/ppermute | solution.py:71
  76.4 7.7 %collective-permute-start.13 = (bf16[64,3584]{1,0:T(8,128)(2,1)S(1)}, bf16[64,3584]{1,0:T(8,128)(2,1)S(1)}, u32[]{:S(2)}, u32[]{:S(2)}) collective-permute-start(bf16[64,3584]{1,0:T(8,128)(2,1)S(1)} %get-tuple-element.32), channel_id=1, source_target_pairs={{0,96},{1,33},{2,98},{3,35},{4,100},{5,37},{6,102},{7,39},{8,104},... | collective-permute-start | bytes 1376264 | tf_op jit(solution)/shard_map/ppermute | solution.py:71
  76.5 7.7 %collective-permute-start.14 = (bf16[64,3584]{1,0:T(8,128)(2,1)S(1)}, bf16[64,3584]{1,0:T(8,128)(2,1)S(1)}, u32[]{:S(2)}, u32[]{:S(2)}) collective-permute-start(bf16[64,3584]{1,0:T(8,128)(2,1)S(1)} %get-tuple-element.33), channel_id=1, source_target_pairs={{0,24},{1,9},{2,26},{3,11},{4,28},{5,13},{6,30},{7,15},{8,16},{9,1... | collective-permute-start | bytes 1376264 | tf_op jit(solution)/shard_map/ppermute | solution.py:71
  78.4 7.7 %collective-permute-start.17 = (bf16[64,3584]{1,0:T(8,128)(2,1)S(1)}, bf16[64,3584]{1,0:T(8,128)(2,1)S(1)}, u32[]{:S(2)}, u32[]{:S(2)}) collective-permute-start(bf16[64,3584]{1,0:T(8,128)(2,1)S(1)} %add_convert_fusion.1), channel_id=1, source_target_pairs={{0,6},{1,3},{2,4},{3,1},{4,2},{5,7},{6,0},{7,5},{8,14},{9,11},{10,... | collective-permute-start | bytes 1376264 | tf_op jit(solution)/shard_map/ppermute | solution.py:71

commit v4 on v3

v4 whole, which is shorter than its diff:
```python
import functools

import jax
import jax.numpy as jnp
from jax import lax
from jax.experimental import pallas as pl
from jax.experimental.pallas import tpu as pltpu
from jax.sharding import PartitionSpec as P

AXES = ("grp", "dev")
D = 7168
HALF = D // 2
EXT = 128
WIDE = HALF + EXT
BLOCK = 64
PART = 4 * BLOCK
SEL = 64
F32 = jnp.float32
BF16 = jnp.bfloat16
MIB = 1 << 20
VMEM = pl.BlockSpec(memory_space=pltpu.VMEM)
SMEM = pl.BlockSpec(memory_space=pltpu.SMEM)
HBM = pl.BlockSpec(memory_space=pltpu.HBM)
ANY = pl.BlockSpec(memory_space=pl.ANY)
SMALL = pltpu.CompilerParams(vmem_limit_bytes=8 * MIB)
CUT = 2048


BRIEF = pl.CostEstimate(flops=1000, bytes_accessed=1000, transcendentals=0)


def flat(z, x, y, c):
    return ((z * 4 + x) * 4 + y) * 2 + c


def near_groups():
    seen, groups = set(), []
    for z in range(4):
        for x in range(4):
            for y in range(4):
                for c in range(2):
                    if flat(z, x, y, c) in seen:
                        continue
                    m = 3 if c else 1
                    members = [
                        flat(z ^ (m * i), x ^ (m * j), y ^ (m * k), c)
                        for i in (0, 1) for j in (0, 1) for k in (0, 1)
                    ]
                    seen.update(members)
                    groups.append(members)
    return groups


def far_pairs(axis):
    pairs = []
    for z in range(4):
        for x in range(4):
            for y in range(4):
                for c in range(2):
                    at = [z, x, y]
                    at[axis] ^= 1 if c else 3
                    pairs.append((flat(z, x, y, c), flat(*at, c)))
    return pairs


NEAR = near_groups()
FAR = [far_pairs(axis) for axis in range(3)]


def swap_near(values):
    return lax.all_to_all(values, AXES, 0, 0, axis_index_groups=NEAR, tiled=True)


def swap_far(values, axis):
    return lax.ppermute(values, AXES, FAR[axis])


def to_sibling(values):
    return lax.ppermute(values, "dev", [(i, i ^ 1) for i in range(32)])


def pack_kernel(expert_ref, tokens_hbm, ids_hbm, weights_hbm, out_ref, tokens_ref, ids_ref, weights_ref, sems):
    del expert_ref
    pairs = ((tokens_hbm, tokens_ref), (ids_hbm, ids_ref), (weights_hbm, weights_ref))
    copies = [pltpu.make_async_copy(source, target, sems.at[i]) for i, (source, target) in enumerate(pairs)]
    for copy in copies:
        copy.start()
    for copy in copies:
        copy.wait()
    lane = lax.broadcasted_iota(jnp.int32, (4, EXT), 1)
    dense = jnp.zeros((4, EXT), F32)
    for k in range(8):
        dense += jnp.where(ids_ref[:, k : k + 1] == lane % 32, weights_ref[:, k : k + 1], 0.0)
    high = dense.astype(BF16).astype(F32)
    route = jnp.where(lane < 32, high, jnp.where(lane < 64, dense - high, 0.0))
    rows = tokens_ref[...].astype(F32)
    left = jnp.concatenate([rows[:, :HALF], route], axis=1)
    right = jnp.concatenate([rows[:, HALF:], route], axis=1)
    block = jnp.concatenate([left, right], axis=0).astype(BF16)
    for i in range(8):
        out_ref[i] = block


def in_hbm(values):
    return pltpu.with_memory_space_constraint(values, pltpu.HBM)


def pack(expert, tokens, ids, weights):
    return pl.pallas_call(
        pack_kernel,
        out_shape=jax.ShapeDtypeStruct((8, 8, WIDE), BF16),
        in_specs=[SMEM, HBM, HBM, HBM],
        out_specs=VMEM,
        scratch_shapes=[
            pltpu.VMEM((4, D), BF16),
            pltpu.VMEM((4, 8), jnp.int32),
            pltpu.VMEM((4, 8), F32),
            pltpu.SemaphoreType.DMA((3,)),
        ],
        compiler_params=pltpu.CompilerParams(vmem_limit_bytes=4 * MIB),
        name="pack",
    )(expert, in_hbm(tokens), in_hbm(ids), in_hbm(weights))


def expert_lanes(expert, shape, dim):
    lane = lax.broadcasted_iota(jnp.int32, shape, dim)
    return (lane < 64) & (lane % 32 == expert)


def block_columns(refs, start, size):
    if len(refs) == 1:
        return refs[0][:, start : start + size]
    if start < CUT:
        return refs[0][:, start : start + size]
    return refs[1][:, start - CUT : start - CUT + size]


def select_kernel(pieces, loads, expert_ref, *refs):
    refs = list(refs)
    blocks = [[refs.pop(0) for _ in range(n)] for n in pieces]
    sources = [refs.pop(0) for _ in range(loads)]
    del refs[0]
    mine_ref, sent_ref = refs[:2]
    targets = refs[2 : 2 + loads]
    pick, sems = refs[2 + loads :]
    copies = [pltpu.make_async_copy(sources[i], targets[i], sems.at[i]) for i in range(loads)]
    for copy in copies:
        copy.start()
    own = expert_ref[0]
    turn = lax.broadcasted_iota(jnp.int32, (8, EXT), 0)
    experts = jnp.where(turn == 0, own, own ^ 1)
    wanted = jnp.where(expert_lanes(experts, (8, EXT), 1) & (turn < 2), 1.0, 0.0).astype(BF16)
    ext = jnp.concatenate([block_columns(block, HALF, EXT) for block in blocks], axis=0)
    route = lax.dot_general(wanted, ext, (((1,), (1,)), ((), ())), preferred_element_type=F32)
    chosen = route > 0
    first = lax.broadcasted_iota(jnp.int32, (PART, PART), 0)
    second = lax.broadcasted_iota(jnp.int32, (PART, PART), 1)
    earlier = jnp.where((first // 4 == second // 4) & (first < second), 1.0, 0.0).astype(BF16)
    rank = jnp.dot(jnp.where(chosen, 1.0, 0.0).astype(BF16), earlier, preferred_element_type=F32)
    column = lax.broadcasted_iota(jnp.int32, (8, PART), 1)
    place = jnp.where(chosen, column // 8 * 2 + rank.astype(jnp.int32), -1)
    row = lax.broadcasted_iota(jnp.int32, (SEL, PART), 0)
    is_left = lax.broadcasted_iota(jnp.int32, (SEL, PART), 1) % 8 < 4
    for e in range(2):
        hit = place[e : e + 1, :] == row
        pick[e * SEL : (e + 1) * SEL, :] = jnp.where(hit & is_left, 1.0, 0.0).astype(BF16)
        pick[(2 + e) * SEL : (3 + e) * SEL, :] = jnp.where(hit & ~is_left, 1.0, 0.0).astype(BF16)
    for n in range(0, HALF, 512):
        x = jnp.concatenate([block_columns(block, n, 512) for block in blocks], axis=0)
        value = jnp.dot(pick[...], x, preferred_element_type=F32).astype(BF16)
        mine_ref[:, n : n + 512] = value[:SEL]
        sent_ref[:, n : n + 512] = value[SEL : 2 * SEL]
        mine_ref[:, HALF + n : HALF + n + 512] = value[2 * SEL : 3 * SEL]
        sent_ref[:, HALF + n : HALF + n + 512] = value[3 * SEL :]
    value = jnp.dot(pick[: 2 * SEL, :], ext, preferred_element_type=F32).astype(BF16)
    mine_ref[:, D:] = value[:SEL]
    sent_ref[:, D:] = value[SEL:]
    for copy in copies:
        copy.wait()


def select(expert, blocks, after, loads=()):
    arrays = [piece for block in blocks for piece in block]
    return pl.pallas_call(
        functools.partial(select_kernel, tuple(len(block) for block in blocks), len(loads)),
        out_shape=[jax.ShapeDtypeStruct((SEL, D + EXT), BF16)] * 2
        + [jax.ShapeDtypeStruct(load.shape, load.dtype) for load in loads],
        in_specs=[SMEM] + [VMEM] * len(arrays) + [HBM] * len(loads) + [ANY],
        out_specs=[VMEM] * (2 + len(loads)),
        scratch_shapes=[pltpu.VMEM((PART, PART), BF16), pltpu.SemaphoreType.DMA((2,))],
        compiler_params=SMALL,
        cost_estimate=BRIEF,
        name="select",
    )(expert, *arrays, *[in_hbm(load) for load in loads], after)


DEPTH = 1792


def load_kernel(source_ref, after_ref, out_ref, sem):
    del after_ref
    copy = pltpu.make_async_copy(source_ref, out_ref, sem)
    copy.start()
    copy.wait()


def load(source, after):
    return pl.pallas_call(
        load_kernel,
        out_shape=jax.ShapeDtypeStruct(source.shape, source.dtype),
        in_specs=[HBM, ANY],
        out_specs=VMEM,
        scratch_shapes=[pltpu.SemaphoreType.DMA],
        compiler_params=SMALL,
        cost_estimate=BRIEF,
        name="load",
    )(in_hbm(source), after)


def hidden_kernel(expert_ref, mine_ref, theirs_ref, gate_ref, up_ref, after_ref, hidden, gate_sum, up_sum):
    del after_ref
    for i in range(0, D, DEPTH):
        block = slice(i, i + DEPTH)
        x = jnp.concatenate([mine_ref[:, block], theirs_ref[:, block]], axis=0)
        gate = jnp.dot(x, gate_ref[0, block, :], preferred_element_type=F32)
        up = jnp.dot(x, up_ref[0, block, :], preferred_element_type=F32)
        gate_sum[...] = gate if i == 0 else gate_sum[...] + gate
        up_sum[...] = up if i == 0 else up_sum[...] + up
    lanes = expert_lanes(expert_ref[0], (2 * SEL, EXT), 1)
    route = jnp.concatenate([mine_ref[:, D:], theirs_ref[:, D:]], axis=0).astype(F32)
    scale = jnp.sum(jnp.where(lanes, route, 0.0), axis=1, keepdims=True)
    v = gate_sum[...]
    hidden[...] = (v / (1.0 + jnp.exp(-v)) * up_sum[...] * scale).astype(BF16)


def hidden_units(expert, mine, theirs, gate, up, after):
    return pl.pallas_call(
        hidden_kernel,
        out_shape=jax.ShapeDtypeStruct((2 * SEL, 512), BF16),
        in_specs=[SMEM, VMEM, VMEM, VMEM, VMEM, ANY],
        out_specs=VMEM,
        scratch_shapes=[pltpu.VMEM((2 * SEL, 512), F32)] * 2,
        compiler_params=SMALL,
        cost_estimate=BRIEF,
        name="hidden",
    )(expert, mine, theirs, gate, up, after)


def down_kernel(part, hidden_ref, down_ref, after_ref, out_ref):
    del after_ref
    for n in range(0, D, 1024):
        block = slice(n, n + 1024)
        rows = hidden_ref[part * SEL : (part + 1) * SEL, :]
        out_ref[:, block] = jnp.dot(rows, down_ref[0, :, block], preferred_element_type=F32).astype(BF16)


def down_rows(part, hidden, down, after):
    return pl.pallas_call(
        functools.partial(down_kernel, part),
        out_shape=jax.ShapeDtypeStruct((SEL, D), BF16),
        in_specs=[VMEM, VMEM, ANY],
        out_specs=VMEM,
        compiler_params=SMALL,
        cost_estimate=BRIEF,
        name="down",
    )(hidden, down, after)


def spread_kernel(expert_ref, *refs):
    refs = list(refs)
    exts = [refs.pop(0) for _ in range(4)]
    mine_ref, theirs_ref = refs[:2]
    outs = [refs[3 + i] for i in range(4)]
    place_scr = refs[7]
    own = expert_ref[0]
    turn = lax.broadcasted_iota(jnp.int32, (EXT, EXT), 1)
    experts = jnp.where(turn == 0, own, own ^ 1)
    wanted = jnp.where(expert_lanes(experts, (EXT, EXT), 0) & (turn < 2), 1.0, 0.0).astype(BF16)
    ext = jnp.concatenate([ref[:, ref.shape[1] - EXT :] for ref in exts], axis=0)
    chosen = jnp.dot(ext, wanted, preferred_element_type=F32) > 0
    first = lax.broadcasted_iota(jnp.int32, (PART, PART), 0)
    second = lax.broadcasted_iota(jnp.int32, (PART, PART), 1)
    earlier = jnp.where((first // 4 == second // 4) & (second < first), 1.0, 0.0).astype(BF16)
    rank = jnp.dot(earlier, jnp.where(chosen, 1.0, 0.0).astype(BF16), preferred_element_type=F32)
    token = lax.broadcasted_iota(jnp.int32, (PART, EXT), 0)
    place = jnp.where(chosen, token // 8 * 2 + rank.astype(jnp.int32), -1)
    column = lax.broadcasted_iota(jnp.int32, (PART, 2 * SEL), 1)
    hit = jnp.where(column < SEL, place[:, 0:1], place[:, 1:2]) == column % SEL
    is_left = lax.broadcasted_iota(jnp.int32, (PART, 2 * SEL), 0) % 8 < 4
    place_scr[:, : 2 * SEL] = jnp.where(hit & is_left, 1.0, 0.0).astype(BF16)
    place_scr[:, 2 * SEL :] = jnp.where(hit & ~is_left, 1.0, 0.0).astype(BF16)
    for n in range(0, HALF, 512):
        left, right = slice(n, n + 512), slice(HALF + n, HALF + n + 512)
        y = jnp.concatenate([mine_ref[:, left], theirs_ref[:, left], mine_ref[:, right], theirs_ref[:, right]], axis=0)
        value = jnp.dot(place_scr[...], y, preferred_element_type=F32).astype(BF16)
        for i in range(4):
            outs[i][:, left] = value[i * BLOCK : (i + 1) * BLOCK]


def spread(expert, blocks, mine, theirs, after):
    exts = [block[-1] for block in blocks]
    return pl.pallas_call(
        spread_kernel,
        out_shape=[jax.ShapeDtypeStruct((BLOCK, HALF), BF16)] * 4,
        in_specs=[SMEM] + [VMEM] * 6 + [ANY],
        out_specs=[VMEM] * 4,
        scratch_shapes=[pltpu.VMEM((PART, 4 * SEL), BF16)],
        compiler_params=SMALL,
        cost_estimate=BRIEF,
        name="spread",
    )(expert, *exts, mine, theirs, after)


def add(*terms):
    total = terms[0].astype(F32)
    for term in terms[1:]:
        total += term.astype(F32)
    return total.astype(BF16)


def finish_kernel(parts_ref, out_ref):
    total = parts_ref[0].astype(F32)
    for i in range(1, 8):
        total += parts_ref[i].astype(F32)
    out_ref[:, :HALF] = total[:4].astype(BF16)
    out_ref[:, HALF:] = total[4:].astype(BF16)


def finish(parts):
    return pl.pallas_call(
        finish_kernel,
        out_shape=jax.ShapeDtypeStruct((4, D), BF16),
        in_specs=[VMEM],
        out_specs=VMEM,
        compiler_params=SMALL,
        name="finish",
    )(parts)


def body(tokens, ids, weights, gate, up, down):
    expert = lax.axis_index("dev").astype(jnp.int32).reshape(1)
    own = swap_near(pack(expert, tokens, ids, weights)).reshape(BLOCK, WIDE)
    x, y, z = swap_far(own, 0), swap_far(own, 1), swap_far(own, 2)
    xy, yz, zx = swap_far(y, 0), swap_far(z, 1), swap_far(x, 2)
    near = ((x,), (y,), (z,), (own,))
    up = load(up, own)
    mine_near, sent = select(expert, near, up)
    xy, yz, zx, sent = lax.optimization_barrier((xy, yz, zx, sent))
    got_near = to_sibling(sent)
    far = ((xy,), (zx,), (yz,), (swap_far(yz[:, :CUT], 0), swap_far(xy[:, CUT:], 2)))
    hidden_near = hidden_units(expert, mine_near, got_near, gate, up, own)
    mine_far, sent = select(expert, far, hidden_near)
    got_far = to_sibling(sent)
    theirs = down_rows(1, hidden_near, down, mine_far)
    returned_near = to_sibling(theirs)
    result_near = down_rows(0, hidden_near, down, theirs)
    hidden_far = hidden_units(expert, mine_far, got_far, gate, up, result_near)
    theirs = down_rows(1, hidden_far, down, own)
    returned = to_sibling(theirs)
    result = down_rows(0, hidden_far, down, theirs)
    y_xy, y_zx, y_yz, y_xyz = spread(expert, far, result, returned, own)
    at_yz = swap_far(y_xyz, 0)
    at_y, at_x = swap_far(y_xy, 0), swap_far(y_zx, 2)
    y_x, y_y, y_z, y_own = spread(expert, near, result_near, returned_near, y_xyz)
    at_z = swap_far(add(y_yz, at_yz), 1)
    total = add(
        y_own,
        swap_far(add(y_x, at_x), 0),
        swap_far(add(y_y, at_y), 1),
        swap_far(add(y_z, at_z), 2),
    )
    return finish(swap_near(total.reshape(8, 8, HALF)))


def solution(mesh):
    in_specs = (
        P(AXES, None),
        P(AXES, None),
        P(AXES, None),
        P("dev", None, "grp"),
        P("dev", None, "grp"),
        P("dev", "grp", None),
    )
    return jax.shard_map(body, mesh=mesh, in_specs=in_specs, out_specs=P(AXES, None), check_vma=False)
```

time: 103 us -> 100 us (0.971)
  Pallas kernels: 23.9 us -> 18.3 us
  waiting for transfers between devices: 29.6 us -> 34.1 us
  local copies, waits for them, and re-layouts: 2.2 us -> 0.05 us
    pallas_call x12 -> x10, Pallas kernels: 20 us -> 13.6 us  [the longest x4 5.52 us: down_rows(): pl.pallas_call(functools.partial(down_kernel, part), out_shape=jax.ShapeD...]
    ppermute x14 -> x15, waiting for transfers between devices: 28.5 us -> 31.9 us  [swap_far(): return lax.ppermute(values, AXES, FAR[axis])]
    unnamed x14 -> x8, local copies, waits for them, and re-layouts: 2.2 us -> 0.02 us
    ppermute x14 -> x15, starting transfers between devices: 3.2 us -> 4.76 us  [swap_far(): return lax.ppermute(values, AXES, FAR[axis])]
    ppermute x4, starting transfers between devices: 6.29 us -> 5.14 us  [to_sibling(): return lax.ppermute(values, 'dev', [(i, i ^ 1) for i in range(32)])]
    ppermute x4, waiting for transfers between devices: 1.07 us -> 2.19 us  [to_sibling(): return lax.ppermute(values, 'dev', [(i, i ^ 1) for i in range(32)])]
  transfers between devices with their start and end apart: 18 -> 19, of which waited for: 11 -> 14; matrix products, arithmetic and copies ran while one was open for 0% -> 0% of each run, Pallas kernels for 17% -> 12%
where the time goes in v4:
time: 100 us; the launch traced here: 99 us
  blocking collectives  35.7 us (36%)
  waiting for transfers between devices  34.1 us (34%)
  Pallas kernels  18.3 us (18%)
  starting transfers between devices  9.9 us (10%)
    all_to_all x2, blocking collectives, swap_near(): lax.all_to_all(values, AXES, 0, 0, axis_index_groups=NEAR, tiled=True)  35.7 us
    ppermute x15, waiting for transfers between devices, swap_far(): return lax.ppermute(values, AXES, FAR[axis])  31.9 us
    pallas_call x4, Pallas kernels, down_rows(): pl.pallas_call(functools.partial(down_kernel, part), out_shape=jax.ShapeD...  5.52 us
    ppermute x4, starting transfers between devices, to_sibling(): return lax.ppermute(values, 'dev', [(i, i ^ 1) for i in range(32)])  5.14 us
    ppermute x15, starting transfers between devices, swap_far(): return lax.ppermute(values, AXES, FAR[axis])  4.76 us
    pallas_call x2, Pallas kernels, hidden_units(): pl.pallas_call(hidden_kernel, out_shape=jax.ShapeDtypeStruct((2 * SEL, 51...  4.12 us
    pallas_call x1, Pallas kernels, load(): pl.pallas_call(load_kernel, out_shape=jax.ShapeDtypeStruct(source.shape,...  3.09 us
    ppermute x4, waiting for transfers between devices, to_sibling(): return lax.ppermute(values, 'dev', [(i, i ^ 1) for i in range(32)])  2.19 us
  transfers between devices with their start and end apart: 19, of which 14 were waited for; matrix products, arithmetic and copies ran while one was open for 0% of the time, Pallas kernels for 12%

profile of v4, /device:TPU:1, one launch (start us, length us, event | category | flops | bytes accessed | tf_op | source)
XLA Modules:
  0.0 99.0 jit_solution(17208302707805343048)
XLA Ops:
  0.0 0.9 pack.1
  1.0 21.2 %all_to_all.10 = bf16[8,8,3712]{2,1,0:T(8,128)(2,1)S(1)} all-to-all(bf16[8,8,3712]{2,1,0:T(8,128)(2,1)S(1)} %pack.1), channel_id=1, replica_groups={{0,2,8,10,32,34,40,42},{1,7,25,31,97,103,121,127},{3,5,27,29,99,101,123..., dimensions={0} | all-to-all | bytes 950272 | tf_op jit(solution)/shard_map/all_to_all | solution.py:71
  22.2 7.4 %collective-permute-done.1.refs_1_ = bf16[64,3712]{1,0:T(8,128)(2,1)S(1)} collective-permute-done((bf16[64,3712]{1,0:T(8,128)(2,1)S(1)}, bf16[64,3712]{1,0:T(8,128)(2,1)S(1)}, u32[]{:S(2)}, u32[]{:S(2)}) %collective-permute-start.1) | collective-permute-done | bytes 475168 | tf_op jit(solution)/shard_map/ppermute | solution.py:75
  29.6 1.8 %collective-permute-start.4 = (bf16[64,3712]{1,0:T(8,128)(2,1)S(1)}, bf16[64,3712]{1,0:T(8,128)(2,1)S(1)}, u32[]{:S(2)}, u32[]{:S(2)}) collective-permute-start(bf16[64,3712]{1,0:T(8,128)(2,1)S(1)} %collective-permute-done.2.refs_2_), channel_id=1, source_target_pairs={{0,24},{1,9},{2,26},{3,11},{4,28},{5,13},{6,30},{7,15},{8,16},{9,1... | collective-permute-start | bytes 1425416 | tf_op jit(solution)/shard_map/ppermute | solution.py:75
  31.4 3.1 %load.1.refs_4_.up_ref = bf16[1,7168,512]{2,1,0:T(8,128)(2,1)S(1)} custom-call(bf16[1,7168,512]{2,1,0:T(8,128)(2,1)} %source_ref.1, bf16[64,3712]{1,0:T(8,128)(2,1)S(1)} %bitcast.11), custom_call_target="tpu_custom_call" | custom-call | flops 1000 | bytes 1000 | tf_op jit(solution)/shard_map/load/pallas_call | solution.py:208
  34.5 0.9 select.2
  35.4 2.0 %collective-permute-done.3.refs_0_ = bf16[64,3712]{1,0:T(8,128)(2,1)S(1)} collective-permute-done((bf16[64,3712]{1,0:T(8,128)(2,1)S(1)}, bf16[64,3712]{1,0:T(8,128)(2,1)S(1)}, u32[]{:S(2)}, u32[]{:S(2)}) %collective-permute-start.3) | collective-permute-done | bytes 475168 | tf_op jit(solution)/shard_map/ppermute | solution.py:75
  37.7 1.5 %collective-permute-done.5.refs_1_ = bf16[64,3712]{1,0:T(8,128)(2,1)S(1)} collective-permute-done((bf16[64,3712]{1,0:T(8,128)(2,1)S(1)}, bf16[64,3712]{1,0:T(8,128)(2,1)S(1)}, u32[]{:S(2)}, u32[]{:S(2)}) %collective-permute-start.5) | collective-permute-done | bytes 475168 | tf_op jit(solution)/shard_map/ppermute | solution.py:75
  39.2 0.8 collective-permute-start.6
  40.5 1.6 %collective-permute-done.6.theirs_ref = bf16[64,7296]{1,0:T(8,128)(2,1)S(1)} collective-permute-done((bf16[64,7296]{1,0:T(8,128)(2,1)S(1)}, bf16[64,7296]{1,0:T(8,128)(2,1)S(1)}, u32[]{:S(2)}, u32[]{:S(2)}) %collective-permute-start.6) | collective-permute-done | bytes 933920 | tf_op jit(solution)/shard_map/ppermute | solution.py:79
  42.2 2.1 %hidden.2.refs_5_.hidden_ref = bf16[128,512]{1,0:T(8,128)(2,1)S(1)} custom-call(s32[1]{0:T(128)} %bitcast.expert_ref, bf16[64,7296]{1,0:T(8,128)(2,1)S(1)} %get-tuple-element.21.mine_ref, bf16[64,7296]{1,0:T(8,128)(2,1)S(1)} %collective-permute-done.6.theirs_ref, bf16[1,7168,512]{2,1,0:T(8,128)(2,1)S(1)} %bitcast.7, ...), custom_call_target="tpu_custom_call" | custom-call | flops 1000 | bytes 1000 | tf_op jit(solution)/shard_map/hidden/pallas_call | solution.py:237
  44.2 1.3 %collective-permute-done.8.refs_4_.refs_3_ = bf16[64,1664]{1,0:T(8,128)(2,1)S(1)} collective-permute-done((bf16[64,1664]{1,0:T(8,128)(2,1)S(1)}, bf16[64,1664]{1,0:T(8,128)(2,1)S(1)}, u32[]{:S(2)}, u32[]{:S(2)}) %collective-permute-start.8) | collective-permute-done | bytes 213024 | tf_op jit(solution)/shard_map/ppermute | solution.py:75
  45.7 0.9 select.3
  46.6 3.7 %collective-permute-start.10 = (bf16[64,7296]{1,0:T(8,128)(2,1)S(1)}, bf16[64,7296]{1,0:T(8,128)(2,1)S(1)}, u32[]{:S(2)}, u32[]{:S(2)}) collective-permute-start(bf16[64,7296]{1,0:T(8,128)(2,1)S(1)} %get-tuple-element.28), channel_id=1, source_target_pairs={{0,1},{1,0},{2,3},{3,2},{4,5},{5,4},{6,7},{7,6},{8,9},{9,8},{10,11... | collective-permute-start | bytes 2801672 | tf_op jit(solution)/shard_map/ppermute | solution.py:79
  50.3 1.4 %down.4.after_ref = bf16[64,7168]{1,0:T(8,128)(2,1)S(1)} custom-call(bf16[128,512]{1,0:T(8,128)(2,1)S(1)} %hidden.2.refs_5_.hidden_ref, bf16[1,512,7168]{2,1,0:T(8,128)(2,1)S(1)} %bitcast.5, bf16[64,7296]{1,0:T(8,128)(2,1)S(1)} %get-tuple-element.27.after_ref.mine_ref), custom_call_target="tpu_custom_call" | custom-call | flops 1000 | bytes 1000 | tf_op jit(solution)/shard_map/down/pallas_call | solution.py:258
  51.7 1.4 %down.5.after_ref.refs_4_ = bf16[64,7168]{1,0:T(8,128)(2,1)S(1)} custom-call(bf16[128,512]{1,0:T(8,128)(2,1)S(1)} %hidden.2.refs_5_.hidden_ref, bf16[1,512,7168]{2,1,0:T(8,128)(2,1)S(1)} %bitcast.5, bf16[64,7168]{1,0:T(8,128)(2,1)S(1)} %down.4.after_ref), custom_call_target="tpu_custom_call" | custom-call | flops 1000 | bytes 1000 | tf_op jit(solution)/shard_map/down/pallas_call | solution.py:258
  53.1 2.1 %hidden.3.hidden_ref = bf16[128,512]{1,0:T(8,128)(2,1)S(1)} custom-call(s32[1]{0:T(128)} %bitcast.expert_ref, bf16[64,7296]{1,0:T(8,128)(2,1)S(1)} %get-tuple-element.27.after_ref.mine_ref, bf16[64,7296]{1,0:T(8,128)(2,1)S(1)} %collective-permute-done.10.theirs_ref, bf16[1,7168,512]{2,1,0:T(8,128)(2,1)S(1)} %bitcast.7, ...), custom_call_target="tpu_custom_call" | custom-call | flops 1000 | bytes 1000 | tf_op jit(solution)/shard_map/hidden/pallas_call | solution.py:237
  55.2 1.4 %down.6.after_ref = bf16[64,7168]{1,0:T(8,128)(2,1)S(1)} custom-call(bf16[128,512]{1,0:T(8,128)(2,1)S(1)} %hidden.3.hidden_ref, bf16[1,512,7168]{2,1,0:T(8,128)(2,1)S(1)} %bitcast.5, bf16[64,3712]{1,0:T(8,128)(2,1)S(1)} %bitcast.14), custom_call_target="tpu_custom_call" | custom-call | flops 1000 | bytes 1000 | tf_op jit(solution)/shard_map/down/pallas_call | solution.py:258
  56.7 0.5 collective-permute-start.9
  57.1 1.4 %down.7.refs_4_ = bf16[64,7168]{1,0:T(8,128)(2,1)S(1)} custom-call(bf16[128,512]{1,0:T(8,128)(2,1)S(1)} %hidden.3.hidden_ref, bf16[1,512,7168]{2,1,0:T(8,128)(2,1)S(1)} %bitcast.5, bf16[64,7168]{1,0:T(8,128)(2,1)S(1)} %down.6.after_ref), custom_call_target="tpu_custom_call" | custom-call | flops 1000 | bytes 1000 | tf_op jit(solution)/shard_map/down/pallas_call | solution.py:258
  58.5 0.6 collective-permute-done.11.refs_5_
  59.1 1.1 %spread.2 = (bf16[64,3584]{1,0:T(8,128)(2,1)S(1)}, bf16[64,3584]{1,0:T(8,128)(2,1)S(1)}, bf16[64,3584]{1,0:T(8,128)(2,1)S(1)}, bf16[64,3584]{1,0:T(8,128)(2,1)S(1)}) custom-call(s32[1]{0:T(128)} %bitcast.expert_ref, bf16[64,3712]{1,0:T(8,128)(2,1)S(1)} %collective-permute-done.3.refs_0_, bf16[64,3712]{1,0:T(8,128)(2,1)S(1)} %collective-permute-done.5.refs_1_, ...), custom_call_target="tpu_custom_call" | custom-call | flops 1000 | bytes 1000 | tf_op jit(solution)/shard_map/spread/pallas_call | solution.py:302
  60.3 1.5 %collective-permute-start.14 = (bf16[64,3584]{1,0:T(8,128)(2,1)S(1)}, bf16[64,3584]{1,0:T(8,128)(2,1)S(1)}, u32[]{:S(2)}, u32[]{:S(2)}) collective-permute-start(bf16[64,3584]{1,0:T(8,128)(2,1)S(1)} %get-tuple-element.34), channel_id=1, source_target_pairs={{0,96},{1,33},{2,98},{3,35},{4,100},{5,37},{6,102},{7,39},{8,104},... | collective-permute-start | bytes 1376264 | tf_op jit(solution)/shard_map/ppermute | solution.py:75
  61.7 1.1 %spread.3 = (bf16[64,3584]{1,0:T(8,128)(2,1)S(1)}, bf16[64,3584]{1,0:T(8,128)(2,1)S(1)}, bf16[64,3584]{1,0:T(8,128)(2,1)S(1)}, bf16[64,3584]{1,0:T(8,128)(2,1)S(1)}) custom-call(s32[1]{0:T(128)} %bitcast.expert_ref, bf16[64,3712]{1,0:T(8,128)(2,1)S(1)} %collective-permute-done.refs_0_, bf16[64,3712]{1,0:T(8,128)(2,1)S(1)} %collective-permute-done.1.refs_1_, ...), custom_call_target="tpu_custom_call" | custom-call | flops 1000 | bytes 1000 | tf_op jit(solution)/shard_map/spread/pallas_call | solution.py:302
  62.8 5.1 %collective-permute-done.16 = bf16[64,3584]{1,0:T(8,128)(2,1)S(1)} collective-permute-done((bf16[64,3584]{1,0:T(8,128)(2,1)S(1)}, bf16[64,3584]{1,0:T(8,128)(2,1)S(1)}, u32[]{:S(2)}, u32[]{:S(2)}) %collective-permute-start.16) | collective-permute-done | bytes 458784 | tf_op jit(solution)/shard_map/ppermute | solution.py:75
  68.4 4.4 %collective-permute-done.14 = bf16[64,3584]{1,0:T(8,128)(2,1)S(1)} collective-permute-done((bf16[64,3584]{1,0:T(8,128)(2,1)S(1)}, bf16[64,3584]{1,0:T(8,128)(2,1)S(1)}, u32[]{:S(2)}, u32[]{:S(2)}) %collective-permute-start.14) | collective-permute-done | bytes 458784 | tf_op jit(solution)/shard_map/ppermute | solution.py:75
  73.5 2.2 %collective-permute-done.17 = bf16[64,3584]{1,0:T(8,128)(2,1)S(1)} collective-permute-done((bf16[64,3584]{1,0:T(8,128)(2,1)S(1)}, bf16[64,3584]{1,0:T(8,128)(2,1)S(1)}, u32[]{:S(2)}, u32[]{:S(2)}) %collective-permute-start.17) | collective-permute-done | bytes 458784 | tf_op jit(solution)/shard_map/ppermute | solution.py:75
  75.9 4.7 %collective-permute-done.15 = bf16[64,3584]{1,0:T(8,128)(2,1)S(1)} collective-permute-done((bf16[64,3584]{1,0:T(8,128)(2,1)S(1)}, bf16[64,3584]{1,0:T(8,128)(2,1)S(1)}, u32[]{:S(2)}, u32[]{:S(2)}) %collective-permute-start.15) | collective-permute-done | bytes 458784 | tf_op jit(solution)/shard_map/ppermute | solution.py:75
  80.6 0.5 collective-permute-done.13
  81.1 2.4 %collective-permute-done.18 = bf16[64,3584]{1,0:T(8,128)(2,1)S(1)} collective-permute-done((bf16[64,3584]{1,0:T(8,128)(2,1)S(1)}, bf16[64,3584]{1,0:T(8,128)(2,1)S(1)}, u32[]{:S(2)}, u32[]{:S(2)}) %collective-permute-start.18) | collective-permute-done | bytes 458784 | tf_op jit(solution)/shard_map/ppermute | solution.py:75
  83.7 14.5 %all_to_all.11.parts_ref = bf16[8,8,3584]{2,1,0:T(8,128)(2,1)S(1)} all-to-all(bf16[8,8,3584]{2,1,0:T(8,128)(2,1)S(1)} %fusion), channel_id=1, replica_groups={{0,2,8,10,32,34,40,42},{1,7,25,31,97,103,121,127},{3,5,27,29,99,101,123..., dimensions={0} | all-to-all | bytes 917504 | tf_op jit(solution)/shard_map/all_to_all | solution.py:71
  98.3 0.7 finish.1
  (38 shorter events, 2.8 us)
Async XLA Ops:
  1.0 41.2 %slice-start.2 = ((s8[7340032]{0:T(1024)(128)(4,1)}), s8[4194304]{0:T(1024)(128)(4,1)S(1)}, s32[]{:S(2)}) async-start(s8[7340032]{0:T(1024)(128)(4,1)} %bitcast.6), calls=%async_computation.4 | async-start | bytes 8388608
  22.1 20.0 %slice-start.3 = ((s8[7340032]{0:T(1024)(128)(4,1)}), s8[3145728]{0:T(1024)(128)(4,1)S(1)}, s32[]{:S(2)}) async-start(s8[7340032]{0:T(1024)(128)(4,1)} %bitcast.6), calls=%async_computation.5 | async-start | bytes 6291456
  22.1 7.5 %collective-permute-start.1 = (bf16[64,3712]{1,0:T(8,128)(2,1)S(1)}, bf16[64,3712]{1,0:T(8,128)(2,1)S(1)}, u32[]{:S(2)}, u32[]{:S(2)}) collective-permute-start(bf16[64,3712]{1,0:T(8,128)(2,1)S(1)} %bitcast.8), channel_id=1, source_target_pairs={{0,24},{1,9},{2,26},{3,11},{4,28},{5,13},{6,30},{7,15},{8,16},{9,1... | collective-permute-start | bytes 1425416 | tf_op jit(solution)/shard_map/ppermute | solution.py:75
  22.1 7.5 %collective-permute-start.2 = (bf16[64,3712]{1,0:T(8,128)(2,1)S(1)}, bf16[64,3712]{1,0:T(8,128)(2,1)S(1)}, u32[]{:S(2)}, u32[]{:S(2)}) collective-permute-start(bf16[64,3712]{1,0:T(8,128)(2,1)S(1)} %bitcast.9), channel_id=1, source_target_pairs={{0,6},{1,3},{2,4},{3,1},{4,2},{5,7},{6,0},{7,5},{8,14},{9,11},{10,... | collective-permute-start | bytes 1425416 | tf_op jit(solution)/shard_map/ppermute | solution.py:75
  22.1 9.3 %collective-permute-start = (bf16[64,3712]{1,0:T(8,128)(2,1)S(1)}, bf16[64,3712]{1,0:T(8,128)(2,1)S(1)}, u32[]{:S(2)}, u32[]{:S(2)}) collective-permute-start(bf16[64,3712]{1,0:T(8,128)(2,1)S(1)} %bitcast.10), channel_id=1, source_target_pairs={{0,96},{1,33},{2,98},{3,35},{4,100},{5,37},{6,102},{7,39},{8,104},... | collective-permute-start | bytes 1425416 | tf_op jit(solution)/shard_map/ppermute | solution.py:75
  29.6 7.8 %collective-permute-start.3 = (bf16[64,3712]{1,0:T(8,128)(2,1)S(1)}, bf16[64,3712]{1,0:T(8,128)(2,1)S(1)}, u32[]{:S(2)}, u32[]{:S(2)}) collective-permute-start(bf16[64,3712]{1,0:T(8,128)(2,1)S(1)} %collective-permute-done.1.refs_1_), channel_id=1, source_target_pairs={{0,96},{1,33},{2,98},{3,35},{4,100},{5,37},{6,102},{7,39},{8,104},... | collective-permute-start | bytes 1425416 | tf_op jit(solution)/shard_map/ppermute | solution.py:75
  29.6 8.1 %collective-permute-start.4 = (bf16[64,3712]{1,0:T(8,128)(2,1)S(1)}, bf16[64,3712]{1,0:T(8,128)(2,1)S(1)}, u32[]{:S(2)}, u32[]{:S(2)}) collective-permute-start(bf16[64,3712]{1,0:T(8,128)(2,1)S(1)} %collective-permute-done.2.refs_2_), channel_id=1, source_target_pairs={{0,24},{1,9},{2,26},{3,11},{4,28},{5,13},{6,30},{7,15},{8,16},{9,1... | collective-permute-start | bytes 1425416 | tf_op jit(solution)/shard_map/ppermute | solution.py:75
  31.4 7.8 %collective-permute-start.5 = (bf16[64,3712]{1,0:T(8,128)(2,1)S(1)}, bf16[64,3712]{1,0:T(8,128)(2,1)S(1)}, u32[]{:S(2)}, u32[]{:S(2)}) collective-permute-start(bf16[64,3712]{1,0:T(8,128)(2,1)S(1)} %collective-permute-done.refs_0_), channel_id=1, source_target_pairs={{0,6},{1,3},{2,4},{3,1},{4,2},{5,7},{6,0},{7,5},{8,14},{9,11},{10,... | collective-permute-start | bytes 1425416 | tf_op jit(solution)/shard_map/ppermute | solution.py:75
  39.2 3.0 %collective-permute-start.6 = (bf16[64,7296]{1,0:T(8,128)(2,1)S(1)}, bf16[64,7296]{1,0:T(8,128)(2,1)S(1)}, u32[]{:S(2)}, u32[]{:S(2)}) collective-permute-start(bf16[64,7296]{1,0:T(8,128)(2,1)S(1)} %get-tuple-element.23), channel_id=1, source_target_pairs={{0,1},{1,0},{2,3},{3,2},{4,5},{5,4},{6,7},{7,6},{8,9},{9,8},{10,11... | collective-permute-start | bytes 2801672 | tf_op jit(solution)/shard_map/ppermute | solution.py:79
  40.0 10.3 %slice-start = ((s8[7340032]{0:T(1024)(128)(4,1)}), s8[4194304]{0:T(1024)(128)(4,1)S(1)}, s32[]{:S(2)}) async-start(s8[7340032]{0:T(1024)(128)(4,1)} %bitcast.4), calls=%async_computation.2 | async-start | bytes 8388608
  40.1 5.6 %collective-permute-start.7 = (bf16[64,2048]{1,0:T(8,128)(2,1)S(1)}, bf16[64,2048]{1,0:T(8,128)(2,1)S(1)}, u32[]{:S(2)}, u32[]{:S(2)}) collective-permute-start(bf16[64,2048]{1,0:T(8,128)(2,1)S(1)} %slice.6), channel_id=1, source_target_pairs={{0,96},{1,33},{2,98},{3,35},{4,100},{5,37},{6,102},{7,39},{8,104},... | collective-permute-start | bytes 786440 | tf_op jit(solution)/shard_map/ppermute | solution.py:75
  40.5 5.1 %collective-permute-start.8 = (bf16[64,1664]{1,0:T(8,128)(2,1)S(1)}, bf16[64,1664]{1,0:T(8,128)(2,1)S(1)}, u32[]{:S(2)}, u32[]{:S(2)}) collective-permute-start(bf16[64,1664]{1,0:T(8,128)(2,1)S(1)} %slice.7), channel_id=1, source_target_pairs={{0,6},{1,3},{2,4},{3,1},{4,2},{5,7},{6,0},{7,5},{8,14},{9,11},{10,... | collective-permute-start | bytes 638984 | tf_op jit(solution)/shard_map/ppermute | solution.py:75
  42.2 8.1 %slice-start.1 = ((s8[7340032]{0:T(1024)(128)(4,1)}), s8[3145728]{0:T(1024)(128)(4,1)S(1)}, s32[]{:S(2)}) async-start(s8[7340032]{0:T(1024)(128)(4,1)} %bitcast.4), calls=%async_computation.3 | async-start | bytes 6291456
  46.6 6.5 %collective-permute-start.10 = (bf16[64,7296]{1,0:T(8,128)(2,1)S(1)}, bf16[64,7296]{1,0:T(8,128)(2,1)S(1)}, u32[]{:S(2)}, u32[]{:S(2)}) collective-permute-start(bf16[64,7296]{1,0:T(8,128)(2,1)S(1)} %get-tuple-element.28), channel_id=1, source_target_pairs={{0,1},{1,0},{2,3},{3,2},{4,5},{5,4},{6,7},{7,6},{8,9},{9,8},{10,11... | collective-permute-start | bytes 2801672 | tf_op jit(solution)/shard_map/ppermute | solution.py:79
  56.6 2.6 %collective-permute-start.11 = (bf16[64,7168]{1,0:T(8,128)(2,1)S(1)}, bf16[64,7168]{1,0:T(8,128)(2,1)S(1)}, u32[]{:S(2)}, u32[]{:S(2)}) collective-permute-start(bf16[64,7168]{1,0:T(8,128)(2,1)S(1)} %down.6.after_ref), channel_id=1, source_target_pairs={{0,1},{1,0},{2,3},{3,2},{4,5},{5,4},{6,7},{7,6},{8,9},{9,8},{10,11... | collective-permute-start | bytes 2752520 | tf_op jit(solution)/shard_map/ppermute | solution.py:79
  56.7 5.1 %collective-permute-start.9 = (bf16[64,7168]{1,0:T(8,128)(2,1)S(1)}, bf16[64,7168]{1,0:T(8,128)(2,1)S(1)}, u32[]{:S(2)}, u32[]{:S(2)}) collective-permute-start(bf16[64,7168]{1,0:T(8,128)(2,1)S(1)} %down.4.after_ref), channel_id=1, source_target_pairs={{0,1},{1,0},{2,3},{3,2},{4,5},{5,4},{6,7},{7,6},{8,9},{9,8},{10,11... | collective-permute-start | bytes 2752520 | tf_op jit(solution)/shard_map/ppermute | solution.py:79
  60.2 7.7 %collective-permute-start.16 = (bf16[64,3584]{1,0:T(8,128)(2,1)S(1)}, bf16[64,3584]{1,0:T(8,128)(2,1)S(1)}, u32[]{:S(2)}, u32[]{:S(2)}) collective-permute-start(bf16[64,3584]{1,0:T(8,128)(2,1)S(1)} %get-tuple-element.29.refs_6_), channel_id=1, source_target_pairs={{0,96},{1,33},{2,98},{3,35},{4,100},{5,37},{6,102},{7,39},{8,104},... | collective-permute-start | bytes 1376264 | tf_op jit(solution)/shard_map/ppermute | solution.py:75
  60.3 12.5 %collective-permute-start.14 = (bf16[64,3584]{1,0:T(8,128)(2,1)S(1)}, bf16[64,3584]{1,0:T(8,128)(2,1)S(1)}, u32[]{:S(2)}, u32[]{:S(2)}) collective-permute-start(bf16[64,3584]{1,0:T(8,128)(2,1)S(1)} %get-tuple-element.34), channel_id=1, source_target_pairs={{0,96},{1,33},{2,98},{3,35},{4,100},{5,37},{6,102},{7,39},{8,104},... | collective-permute-start | bytes 1376264 | tf_op jit(solution)/shard_map/ppermute | solution.py:75
  61.7 11.6 %collective-permute-start.12 = (bf16[64,3584]{1,0:T(8,128)(2,1)S(1)}, bf16[64,3584]{1,0:T(8,128)(2,1)S(1)}, u32[]{:S(2)}, u32[]{:S(2)}) collective-permute-start(bf16[64,3584]{1,0:T(8,128)(2,1)S(1)} %get-tuple-element.32), channel_id=1, source_target_pairs={{0,6},{1,3},{2,4},{3,1},{4,2},{5,7},{6,0},{7,5},{8,14},{9,11},{10,... | collective-permute-start | bytes 1376264 | tf_op jit(solution)/shard_map/ppermute | solution.py:75
  68.0 7.7 %collective-permute-start.17 = (bf16[64,3584]{1,0:T(8,128)(2,1)S(1)}, bf16[64,3584]{1,0:T(8,128)(2,1)S(1)}, u32[]{:S(2)}, u32[]{:S(2)}) collective-permute-start(bf16[64,3584]{1,0:T(8,128)(2,1)S(1)} %add_convert_fusion.2), channel_id=1, source_target_pairs={{0,24},{1,9},{2,26},{3,11},{4,28},{5,13},{6,30},{7,15},{8,16},{9,1... | collective-permute-start | bytes 1376264 | tf_op jit(solution)/shard_map/ppermute | solution.py:75
  72.9 7.7 %collective-permute-start.15 = (bf16[64,3584]{1,0:T(8,128)(2,1)S(1)}, bf16[64,3584]{1,0:T(8,128)(2,1)S(1)}, u32[]{:S(2)}, u32[]{:S(2)}) collective-permute-start(bf16[64,3584]{1,0:T(8,128)(2,1)S(1)} %add_convert_fusion.3), channel_id=1, source_target_pairs={{0,24},{1,9},{2,26},{3,11},{4,28},{5,13},{6,30},{7,15},{8,16},{9,1... | collective-permute-start | bytes 1376264 | tf_op jit(solution)/shard_map/ppermute | solution.py:75
  73.4 7.7 %collective-permute-start.13 = (bf16[64,3584]{1,0:T(8,128)(2,1)S(1)}, bf16[64,3584]{1,0:T(8,128)(2,1)S(1)}, u32[]{:S(2)}, u32[]{:S(2)}) collective-permute-start(bf16[64,3584]{1,0:T(8,128)(2,1)S(1)} %add_convert_fusion.4), channel_id=1, source_target_pairs={{0,96},{1,33},{2,98},{3,35},{4,100},{5,37},{6,102},{7,39},{8,104},... | collective-permute-start | bytes 1376264 | tf_op jit(solution)/shard_map/ppermute | solution.py:75
  75.8 7.7 %collective-permute-start.18 = (bf16[64,3584]{1,0:T(8,128)(2,1)S(1)}, bf16[64,3584]{1,0:T(8,128)(2,1)S(1)}, u32[]{:S(2)}, u32[]{:S(2)}) collective-permute-start(bf16[64,3584]{1,0:T(8,128)(2,1)S(1)} %add_convert_fusion.1), channel_id=1, source_target_pairs={{0,6},{1,3},{2,4},{3,1},{4,2},{5,7},{6,0},{7,5},{8,14},{9,11},{10,... | collective-permute-start | bytes 1376264 | tf_op jit(solution)/shard_map/ppermute | solution.py:75

commit v5 on v4

--- a/solution.py
+++ b/solution.py
@@ -23,9 +23,10 @@
 HBM = pl.BlockSpec(memory_space=pltpu.HBM)
 ANY = pl.BlockSpec(memory_space=pl.ANY)
 SMALL = pltpu.CompilerParams(vmem_limit_bytes=8 * MIB)
-CUT = 2048
-
-
+
+
+DEPTH = 1792
+MIDDLE = D // 2
 BRIEF = pl.CostEstimate(flops=1000, bytes_accessed=1000, transcendentals=0)
 
 
@@ -51,20 +52,21 @@
     return groups
 
 
-def far_pairs(axis):
+def far_pairs(*axes):
     pairs = []
     for z in range(4):
         for x in range(4):
             for y in range(4):
                 for c in range(2):
                     at = [z, x, y]
-                    at[axis] ^= 1 if c else 3
+                    for axis in axes:
+                        at[axis] ^= 1 if c else 3
                     pairs.append((flat(z, x, y, c), flat(*at, c)))
     return pairs
 
 
 NEAR = near_groups()
-FAR = [far_pairs(axis) for axis in range(3)]
+FAR = [far_pairs(0), far_pairs(1), far_pairs(2), far_pairs(0, 1, 2)]
 
 
 def swap_near(values):
@@ -127,30 +129,22 @@
     return (lane < 64) & (lane % 32 == expert)
 
 
-def block_columns(refs, start, size):
-    if len(refs) == 1:
-        return refs[0][:, start : start + size]
-    if start < CUT:
-        return refs[0][:, start : start + size]
-    return refs[1][:, start - CUT : start - CUT + size]
-
-
-def select_kernel(pieces, loads, expert_ref, *refs):
+def select_kernel(loads, expert_ref, *refs):
     refs = list(refs)
-    blocks = [[refs.pop(0) for _ in range(n)] for n in pieces]
+    blocks = [refs.pop(0) for _ in range(4)]
     sources = [refs.pop(0) for _ in range(loads)]
     del refs[0]
     mine_ref, sent_ref = refs[:2]
     targets = refs[2 : 2 + loads]
-    pick, sems = refs[2 + loads :]
-    copies = [pltpu.make_async_copy(sources[i], targets[i], sems.at[i]) for i in range(loads)]
+    pick, sem = refs[2 + loads :]
+    copies = [pltpu.make_async_copy(a.at[:, :MIDDLE, :], b, sem) for a, b in zip(sources, targets)]
     for copy in copies:
         copy.start()
     own = expert_ref[0]
     turn = lax.broadcasted_iota(jnp.int32, (8, EXT), 0)
     experts = jnp.where(turn == 0, own, own ^ 1)
     wanted = jnp.where(expert_lanes(experts, (8, EXT), 1) & (turn < 2), 1.0, 0.0).astype(BF16)
-    ext = jnp.concatenate([block_columns(block, HALF, EXT) for block in blocks], axis=0)
+    ext = jnp.concatenate([ref[:, HALF:] for ref in blocks], axis=0)
     route = lax.dot_general(wanted, ext, (((1,), (1,)), ((), ())), preferred_element_type=F32)
     chosen = route > 0
     first = lax.broadcasted_iota(jnp.int32, (PART, PART), 0)
@@ -166,7 +160,7 @@
         pick[e * SEL : (e + 1) * SEL, :] = jnp.where(hit & is_left, 1.0, 0.0).astype(BF16)
         pick[(2 + e) * SEL : (3 + e) * SEL, :] = jnp.where(hit & ~is_left, 1.0, 0.0).astype(BF16)
     for n in range(0, HALF, 512):
-        x = jnp.concatenate([block_columns(block, n, 512) for block in blocks], axis=0)
+        x = jnp.concatenate([ref[:, n : n + 512] for ref in blocks], axis=0)
         value = jnp.dot(pick[...], x, preferred_element_type=F32).astype(BF16)
         mine_ref[:, n : n + 512] = value[:SEL]
         sent_ref[:, n : n + 512] = value[SEL : 2 * SEL]
@@ -180,86 +174,77 @@
 
 
 def select(expert, blocks, after, loads=()):
-    arrays = [piece for block in blocks for piece in block]
-    return pl.pallas_call(
-        functools.partial(select_kernel, tuple(len(block) for block in blocks), len(loads)),
+    return pl.pallas_call(
+        functools.partial(select_kernel, len(loads)),
         out_shape=[jax.ShapeDtypeStruct((SEL, D + EXT), BF16)] * 2
-        + [jax.ShapeDtypeStruct(load.shape, load.dtype) for load in loads],
-        in_specs=[SMEM] + [VMEM] * len(arrays) + [HBM] * len(loads) + [ANY],
+        + [jax.ShapeDtypeStruct((1, MIDDLE, 512), BF16) for _ in loads],
+        in_specs=[SMEM] + [VMEM] * 4 + [HBM] * len(loads) + [ANY],
         out_specs=[VMEM] * (2 + len(loads)),
-        scratch_shapes=[pltpu.VMEM((PART, PART), BF16), pltpu.SemaphoreType.DMA((2,))],
+        scratch_shapes=[pltpu.VMEM((PART, PART), BF16), pltpu.SemaphoreType.DMA],
         compiler_params=SMALL,
         cost_estimate=BRIEF,
         name="select",
-    )(expert, *arrays, *[in_hbm(load) for load in loads], after)
-
-
-DEPTH = 1792
-
-
-def load_kernel(source_ref, after_ref, out_ref, sem):
+    )(expert, *blocks, *[in_hbm(load) for load in loads], after)
+
+
+def hidden_kernel(streams, expert_ref, mine_ref, theirs_ref, gate_ref, first_ref, rest_ref, after_ref, *refs):
     del after_ref
-    copy = pltpu.make_async_copy(source_ref, out_ref, sem)
-    copy.start()
-    copy.wait()
-
-
-def load(source, after):
-    return pl.pallas_call(
-        load_kernel,
-        out_shape=jax.ShapeDtypeStruct(source.shape, source.dtype),
-        in_specs=[HBM, ANY],
-        out_specs=VMEM,
-        scratch_shapes=[pltpu.SemaphoreType.DMA],
-        compiler_params=SMALL,
-        cost_estimate=BRIEF,
-        name="load",
-    )(in_hbm(source), after)
-
-
-def hidden_kernel(expert_ref, mine_ref, theirs_ref, gate_ref, up_ref, after_ref, hidden, gate_sum, up_sum):
-    del after_ref
+    if streams:
+        hidden, second_ref, gate_sum, up_sum, sem = refs
+        copy = pltpu.make_async_copy(rest_ref.at[:, MIDDLE:, :], second_ref, sem)
+        copy.start()
+    else:
+        hidden, gate_sum, up_sum = refs
+        second_ref = rest_ref
+
+    def rows(block):
+        return jnp.concatenate([mine_ref[:, block], theirs_ref[:, block]], axis=0)
+
     for i in range(0, D, DEPTH):
         block = slice(i, i + DEPTH)
-        x = jnp.concatenate([mine_ref[:, block], theirs_ref[:, block]], axis=0)
-        gate = jnp.dot(x, gate_ref[0, block, :], preferred_element_type=F32)
-        up = jnp.dot(x, up_ref[0, block, :], preferred_element_type=F32)
+        gate = jnp.dot(rows(block), gate_ref[0, block, :], preferred_element_type=F32)
         gate_sum[...] = gate if i == 0 else gate_sum[...] + gate
+    for i in range(0, D, DEPTH):
+        if streams and i == MIDDLE:
+            copy.wait()
+        ref, start = (first_ref, i) if i < MIDDLE else (second_ref, i - MIDDLE)
+        up = jnp.dot(rows(slice(i, i + DEPTH)), ref[0, start : start + DEPTH, :], preferred_element_type=F32)
         up_sum[...] = up if i == 0 else up_sum[...] + up
     lanes = expert_lanes(expert_ref[0], (2 * SEL, EXT), 1)
-    route = jnp.concatenate([mine_ref[:, D:], theirs_ref[:, D:]], axis=0).astype(F32)
-    scale = jnp.sum(jnp.where(lanes, route, 0.0), axis=1, keepdims=True)
+    scale = jnp.sum(jnp.where(lanes, rows(slice(D, D + EXT)).astype(F32), 0.0), axis=1, keepdims=True)
     v = gate_sum[...]
     hidden[...] = (v / (1.0 + jnp.exp(-v)) * up_sum[...] * scale).astype(BF16)
 
 
-def hidden_units(expert, mine, theirs, gate, up, after):
-    return pl.pallas_call(
-        hidden_kernel,
-        out_shape=jax.ShapeDtypeStruct((2 * SEL, 512), BF16),
-        in_specs=[SMEM, VMEM, VMEM, VMEM, VMEM, ANY],
-        out_specs=VMEM,
-        scratch_shapes=[pltpu.VMEM((2 * SEL, 512), F32)] * 2,
+def hidden_units(expert, mine, theirs, gate, first, rest, after, streams):
+    half = jax.ShapeDtypeStruct((1, MIDDLE, 512), BF16)
+    return pl.pallas_call(
+        functools.partial(hidden_kernel, streams),
+        out_shape=[jax.ShapeDtypeStruct((2 * SEL, 512), BF16)] + [half] * streams,
+        in_specs=[SMEM, VMEM, VMEM, VMEM, VMEM, HBM if streams else VMEM, ANY],
+        out_specs=[VMEM] * (1 + streams),
+        scratch_shapes=[pltpu.VMEM((2 * SEL, 512), F32)] * 2 + [pltpu.SemaphoreType.DMA] * streams,
         compiler_params=SMALL,
         cost_estimate=BRIEF,
         name="hidden",
-    )(expert, mine, theirs, gate, up, after)
-
-
-def down_kernel(part, hidden_ref, down_ref, after_ref, out_ref):
+    )(expert, mine, theirs, gate, first, in_hbm(rest) if streams else rest, after)
+
+
+def down_kernel(hidden_ref, down_ref, after_ref, mine_ref, theirs_ref):
     del after_ref
     for n in range(0, D, 1024):
         block = slice(n, n + 1024)
-        rows = hidden_ref[part * SEL : (part + 1) * SEL, :]
-        out_ref[:, block] = jnp.dot(rows, down_ref[0, :, block], preferred_element_type=F32).astype(BF16)
-
-
-def down_rows(part, hidden, down, after):
-    return pl.pallas_call(
-        functools.partial(down_kernel, part),
-        out_shape=jax.ShapeDtypeStruct((SEL, D), BF16),
+        value = jnp.dot(hidden_ref[...], down_ref[0, :, block], preferred_element_type=F32).astype(BF16)
+        mine_ref[:, block] = value[:SEL]
+        theirs_ref[:, block] = value[SEL:]
+
+
+def down_rows(hidden, down, after):
+    return pl.pallas_call(
+        down_kernel,
+        out_shape=[jax.ShapeDtypeStruct((SEL, D), BF16)] * 2,
         in_specs=[VMEM, VMEM, ANY],
-        out_specs=VMEM,
+        out_specs=[VMEM, VMEM],
         compiler_params=SMALL,
         cost_estimate=BRIEF,
         name="down",
@@ -276,7 +261,7 @@
     turn = lax.broadcasted_iota(jnp.int32, (EXT, EXT), 1)
     experts = jnp.where(turn == 0, own, own ^ 1)
     wanted = jnp.where(expert_lanes(experts, (EXT, EXT), 0) & (turn < 2), 1.0, 0.0).astype(BF16)
-    ext = jnp.concatenate([ref[:, ref.shape[1] - EXT :] for ref in exts], axis=0)
+    ext = jnp.concatenate([ref[:, HALF:] for ref in exts], axis=0)
     chosen = jnp.dot(ext, wanted, preferred_element_type=F32) > 0
     first = lax.broadcasted_iota(jnp.int32, (PART, PART), 0)
     second = lax.broadcasted_iota(jnp.int32, (PART, PART), 1)
@@ -298,7 +283,6 @@
 
 
 def spread(expert, blocks, mine, theirs, after):
-    exts = [block[-1] for block in blocks]
     return pl.pallas_call(
         spread_kernel,
         out_shape=[jax.ShapeDtypeStruct((BLOCK, HALF), BF16)] * 4,
@@ -308,7 +292,7 @@
         compiler_params=SMALL,
         cost_estimate=BRIEF,
         name="spread",
-    )(expert, *exts, mine, theirs, after)
+    )(expert, *blocks, mine, theirs, after)
 
 
 def add(*terms):
@@ -341,33 +325,31 @@
     expert = lax.axis_index("dev").astype(jnp.int32).reshape(1)
     own = swap_near(pack(expert, tokens, ids, weights)).reshape(BLOCK, WIDE)
     x, y, z = swap_far(own, 0), swap_far(own, 1), swap_far(own, 2)
+    xyz = swap_far(own, 3)
     xy, yz, zx = swap_far(y, 0), swap_far(z, 1), swap_far(x, 2)
-    near = ((x,), (y,), (z,), (own,))
-    up = load(up, own)
-    mine_near, sent = select(expert, near, up)
-    xy, yz, zx, sent = lax.optimization_barrier((xy, yz, zx, sent))
+    near = (x, y, z, own)
+    mine_near, sent, up_first = select(expert, near, own, (up,))
+    xy, yz, zx, xyz, sent = lax.optimization_barrier((xy, yz, zx, xyz, sent))
     got_near = to_sibling(sent)
-    far = ((xy,), (zx,), (yz,), (swap_far(yz[:, :CUT], 0), swap_far(xy[:, CUT:], 2)))
-    hidden_near = hidden_units(expert, mine_near, got_near, gate, up, own)
-    mine_far, sent = select(expert, far, hidden_near)
+    far = (xy, zx, yz, xyz)
+    mine_far, sent = select(expert, far, own)
     got_far = to_sibling(sent)
-    theirs = down_rows(1, hidden_near, down, mine_far)
+    hidden_near, up_second = hidden_units(expert, mine_near, got_near, gate, up_first, up, mine_far, 1)
+    result_near, theirs = down_rows(hidden_near, down, own)
     returned_near = to_sibling(theirs)
-    result_near = down_rows(0, hidden_near, down, theirs)
-    hidden_far = hidden_units(expert, mine_far, got_far, gate, up, result_near)
-    theirs = down_rows(1, hidden_far, down, own)
+    (hidden_far,) = hidden_units(expert, mine_far, got_far, gate, up_first, up_second, result_near, 0)
+    result, theirs = down_rows(hidden_far, down, own)
     returned = to_sibling(theirs)
-    result = down_rows(0, hidden_far, down, theirs)
-    y_xy, y_zx, y_yz, y_xyz = spread(expert, far, result, returned, own)
-    at_yz = swap_far(y_xyz, 0)
-    at_y, at_x = swap_far(y_xy, 0), swap_far(y_zx, 2)
-    y_x, y_y, y_z, y_own = spread(expert, near, result_near, returned_near, y_xyz)
-    at_z = swap_far(add(y_yz, at_yz), 1)
+    y_x, y_y, y_z, y_own = spread(expert, near, result_near, returned_near, result)
+    y_xy, y_zx, y_yz, y_xyz = spread(expert, far, result, returned, y_own)
+    at_y, at_z, at_x = swap_far(y_xy, 0), swap_far(y_yz, 1), swap_far(y_zx, 2)
+    at_own = swap_far(y_xyz, 3)
     total = add(
         y_own,
         swap_far(add(y_x, at_x), 0),
         swap_far(add(y_y, at_y), 1),
         swap_far(add(y_z, at_z), 2),
+        at_own,
     )
     return finish(swap_near(total.reshape(8, 8, HALF)))
 

time: 100 us -> 93.6 us (0.936)
  waiting for transfers between devices: 34.1 us -> 28.3 us
  Pallas kernels: 18.3 us -> 14.8 us
  starting transfers between devices: 9.9 us -> 12.9 us
    ppermute x15 -> x14, starting transfers between devices: 4.76 us -> 11.6 us  [swap_far(): return lax.ppermute(values, AXES, FAR[axis])]
    ppermute x15 -> x14, waiting for transfers between devices: 31.9 us -> 26 us  [swap_far(): return lax.ppermute(values, AXES, FAR[axis])]
    ppermute x4, starting transfers between devices: 5.14 us -> 1.29 us  [to_sibling(): return lax.ppermute(values, 'dev', [(i, i ^ 1) for i in range(32)])]
    pallas_call x9 -> x6, Pallas kernels: 14.6 us -> 10.9 us  [the longest x2 4.94 us: hidden_units(): pl.pallas_call(functools.partial(hidden_kernel, streams), out_shape=[jax....]
  transfers between devices with their start and end apart: 19 -> 18, of which waited for: 14 -> 10; matrix products, arithmetic and copies ran while one was open for 0% -> 0% of each run, Pallas kernels for 12% -> 13%
where the time goes in v5:
time: 93.6 us; the launch traced here: 93.4 us
  blocking collectives  36.5 us (39%)
  waiting for transfers between devices  28.3 us (30%)
  Pallas kernels  14.8 us (16%)
  starting transfers between devices  12.9 us (14%)
    all_to_all x2, blocking collectives, swap_near(): lax.all_to_all(values, AXES, 0, 0, axis_index_groups=NEAR, tiled=True)  36.5 us
    ppermute x14, waiting for transfers between devices, swap_far(): return lax.ppermute(values, AXES, FAR[axis])  26 us
    ppermute x14, starting transfers between devices, swap_far(): return lax.ppermute(values, AXES, FAR[axis])  11.6 us
    pallas_call x2, Pallas kernels, hidden_units(): pl.pallas_call(functools.partial(hidden_kernel, streams), out_shape=[jax....  4.94 us
    pallas_call x2, Pallas kernels, select(): pl.pallas_call(functools.partial(select_kernel, len(loads)), out_shape=[j...  3.66 us
    ppermute x4, waiting for transfers between devices, to_sibling(): return lax.ppermute(values, 'dev', [(i, i ^ 1) for i in range(32)])  2.36 us
    pallas_call x2, Pallas kernels, down_rows(): pl.pallas_call(down_kernel, out_shape=[jax.ShapeDtypeStruct((SEL, D), BF1...  2.27 us
    pallas_call x2, Pallas kernels, spread(): pl.pallas_call(spread_kernel, out_shape=[jax.ShapeDtypeStruct((BLOCK, HAL...  2.13 us
  transfers between devices with their start and end apart: 18, of which 10 were waited for; matrix products, arithmetic and copies ran while one was open for 0% of the time, Pallas kernels for 13%

profile of v5, /device:TPU:1, one launch (start us, length us, event | category | flops | bytes accessed | tf_op | source)
XLA Modules:
  0.0 93.4 jit_solution(4778484168759086929)
XLA Ops:
  0.0 1.1 %pack.1 = bf16[8,8,3712]{2,1,0:T(8,128)(2,1)S(1)} custom-call(s32[1]{0:T(128)} %bitcast.expert_ref, bf16[4,7168]{1,0:T(4,128)(2,1)} %tokens_hbm.1, s32[4,8]{1,0:T(4,128)} %ids_hbm.1, f32[4,8]{1,0:T(4,128)} %weights_hbm.1), custom_call_target="tpu_custom_call" | custom-call | tf_op jit(solution)/shard_map/pack/pallas_call | solution.py:111
  1.1 20.9 %all_to_all.10 = bf16[8,8,3712]{2,1,0:T(8,128)(2,1)S(1)} all-to-all(bf16[8,8,3712]{2,1,0:T(8,128)(2,1)S(1)} %pack.1), channel_id=1, replica_groups={{0,2,8,10,32,34,40,42},{1,7,25,31,97,103,121,127},{3,5,27,29,99,101,123..., dimensions={0} | all-to-all | bytes 950272 | tf_op jit(solution)/shard_map/all_to_all | solution.py:73
  22.1 3.7 %collective-permute-start.6 = (bf16[64,3712]{1,0:T(8,128)(2,1)S(1)}, bf16[64,3712]{1,0:T(8,128)(2,1)S(1)}, u32[]{:S(2)}, u32[]{:S(2)}) collective-permute-start(bf16[64,3712]{1,0:T(8,128)(2,1)S(1)} %bitcast.11), channel_id=1, source_target_pairs={{0,126},{1,43},{2,124},{3,41},{4,122},{5,47},{6,120},{7,45},{8,118... | collective-permute-start | bytes 1425416 | tf_op jit(solution)/shard_map/ppermute | solution.py:77
  25.9 3.7 %collective-permute-done.2.refs_2_ = bf16[64,3712]{1,0:T(8,128)(2,1)S(1)} collective-permute-done((bf16[64,3712]{1,0:T(8,128)(2,1)S(1)}, bf16[64,3712]{1,0:T(8,128)(2,1)S(1)}, u32[]{:S(2)}, u32[]{:S(2)}) %collective-permute-start.2) | collective-permute-done | bytes 475168 | tf_op jit(solution)/shard_map/ppermute | solution.py:77
  29.5 5.5 %collective-permute-done.refs_0_ = bf16[64,3712]{1,0:T(8,128)(2,1)S(1)} collective-permute-done((bf16[64,3712]{1,0:T(8,128)(2,1)S(1)}, bf16[64,3712]{1,0:T(8,128)(2,1)S(1)}, u32[]{:S(2)}, u32[]{:S(2)}) %collective-permute-start) | collective-permute-done | bytes 475168 | tf_op jit(solution)/shard_map/ppermute | solution.py:77
  35.0 1.4 %collective-permute-start.5 = (bf16[64,3712]{1,0:T(8,128)(2,1)S(1)}, bf16[64,3712]{1,0:T(8,128)(2,1)S(1)}, u32[]{:S(2)}, u32[]{:S(2)}) collective-permute-start(bf16[64,3712]{1,0:T(8,128)(2,1)S(1)} %collective-permute-done.refs_0_), channel_id=1, source_target_pairs={{0,6},{1,3},{2,4},{3,1},{4,2},{5,7},{6,0},{7,5},{8,14},{9,11},{10,... | collective-permute-start | bytes 1425416 | tf_op jit(solution)/shard_map/ppermute | solution.py:77
  36.4 2.8 %select.2 = (bf16[64,7296]{1,0:T(8,128)(2,1)S(1)}, bf16[64,7296]{1,0:T(8,128)(2,1)S(1)}, bf16[1,3584,512]{2,1,0:T(8,128)(2,1)S(1)}) custom-call(s32[1]{0:T(128)} %bitcast.expert_ref, bf16[64,3712]{1,0:T(8,128)(2,1)S(1)} %collective-permute-done.refs_0_, bf16[64,3712]{1,0:T(8,128)(2,1)S(1)} %collective-permute-done.1.refs_1_, ...), custom_call_target="tpu_custom_call" | custom-call | flops 1000 | bytes 1000 | tf_op jit(solution)/shard_map/select/pallas_call | solution.py:177
  39.2 0.9 collective-permute-done.4.refs_2_
  40.2 2.6 %collective-permute-done.5.refs_1_ = bf16[64,3712]{1,0:T(8,128)(2,1)S(1)} collective-permute-done((bf16[64,3712]{1,0:T(8,128)(2,1)S(1)}, bf16[64,3712]{1,0:T(8,128)(2,1)S(1)}, u32[]{:S(2)}, u32[]{:S(2)}) %collective-permute-start.5) | collective-permute-done | bytes 475168 | tf_op jit(solution)/shard_map/ppermute | solution.py:77
  42.8 0.5 collective-permute-start.7
  43.3 0.9 select.3
  44.3 1.1 %collective-permute-done.7.theirs_ref = bf16[64,7296]{1,0:T(8,128)(2,1)S(1)} collective-permute-done((bf16[64,7296]{1,0:T(8,128)(2,1)S(1)}, bf16[64,7296]{1,0:T(8,128)(2,1)S(1)}, u32[]{:S(2)}, u32[]{:S(2)}) %collective-permute-start.7) | collective-permute-done | bytes 933920 | tf_op jit(solution)/shard_map/ppermute | solution.py:81
  45.5 2.9 %hidden.2 = (bf16[128,512]{1,0:T(8,128)(2,1)S(1)}, bf16[1,3584,512]{2,1,0:T(8,128)(2,1)S(1)}) custom-call(s32[1]{0:T(128)} %bitcast.expert_ref, bf16[64,7296]{1,0:T(8,128)(2,1)S(1)} %get-tuple-element.29.mine_ref, bf16[64,7296]{1,0:T(8,128)(2,1)S(1)} %collective-permute-done.7.theirs_ref, bf16[1,7168,512]{2,1,0:T(8,128)(2,1)S(1)} %bitcast.5, ...), custom_call_target="tpu_custom_call" | custom-call | flops 1000 | bytes 1000 | tf_op jit(solution)/shard_map/hidden/pallas_call | solution.py:221
  48.5 1.1 %down.2 = (bf16[64,7168]{1,0:T(8,128)(2,1)S(1)}, bf16[64,7168]{1,0:T(8,128)(2,1)S(1)}) custom-call(bf16[128,512]{1,0:T(8,128)(2,1)S(1)} %get-tuple-element.38.hidden_ref, bf16[1,512,7168]{2,1,0:T(8,128)(2,1)S(1)} %bitcast.7, bf16[64,3712]{1,0:T(8,128)(2,1)S(1)} %bitcast.15), custom_call_target="tpu_custom_call" | custom-call | flops 1000 | bytes 1000 | tf_op jit(solution)/shard_map/down/pallas_call | solution.py:243
  49.6 0.4 collective-permute-start.8
  50.1 2.1 %hidden.3.hidden_ref = bf16[128,512]{1,0:T(8,128)(2,1)S(1)} custom-call(s32[1]{0:T(128)} %bitcast.expert_ref, bf16[64,7296]{1,0:T(8,128)(2,1)S(1)} %get-tuple-element.37.after_ref.mine_ref, bf16[64,7296]{1,0:T(8,128)(2,1)S(1)} %collective-permute-done.9.theirs_ref, bf16[1,7168,512]{2,1,0:T(8,128)(2,1)S(1)} %bitcast.5, ...), custom_call_target="tpu_custom_call" | custom-call | flops 1000 | bytes 1000 | tf_op jit(solution)/shard_map/hidden/pallas_call | solution.py:221
  52.1 1.1 %down.3 = (bf16[64,7168]{1,0:T(8,128)(2,1)S(1)}, bf16[64,7168]{1,0:T(8,128)(2,1)S(1)}) custom-call(bf16[128,512]{1,0:T(8,128)(2,1)S(1)} %hidden.3.hidden_ref, bf16[1,512,7168]{2,1,0:T(8,128)(2,1)S(1)} %bitcast.7, bf16[64,3712]{1,0:T(8,128)(2,1)S(1)} %bitcast.16), custom_call_target="tpu_custom_call" | custom-call | flops 1000 | bytes 1000 | tf_op jit(solution)/shard_map/down/pallas_call | solution.py:243
  53.5 1.1 %spread.2 = (bf16[64,3584]{1,0:T(8,128)(2,1)S(1)}, bf16[64,3584]{1,0:T(8,128)(2,1)S(1)}, bf16[64,3584]{1,0:T(8,128)(2,1)S(1)}, bf16[64,3584]{1,0:T(8,128)(2,1)S(1)}) custom-call(s32[1]{0:T(128)} %bitcast.expert_ref, bf16[64,3712]{1,0:T(8,128)(2,1)S(1)} %collective-permute-done.refs_0_, bf16[64,3712]{1,0:T(8,128)(2,1)S(1)} %collective-permute-done.1.refs_1_, ...), custom_call_target="tpu_custom_call" | custom-call | flops 1000 | bytes 1000 | tf_op jit(solution)/shard_map/spread/pallas_call | solution.py:286
  54.6 1.2 %collective-permute-done.10.refs_5_ = bf16[64,7168]{1,0:T(8,128)(2,1)S(1)} collective-permute-done((bf16[64,7168]{1,0:T(8,128)(2,1)S(1)}, bf16[64,7168]{1,0:T(8,128)(2,1)S(1)}, u32[]{:S(2)}, u32[]{:S(2)}) %collective-permute-start.10) | collective-permute-done | bytes 917536 | tf_op jit(solution)/shard_map/ppermute | solution.py:81
  55.8 1.1 %spread.3 = (bf16[64,3584]{1,0:T(8,128)(2,1)S(1)}, bf16[64,3584]{1,0:T(8,128)(2,1)S(1)}, bf16[64,3584]{1,0:T(8,128)(2,1)S(1)}, bf16[64,3584]{1,0:T(8,128)(2,1)S(1)}) custom-call(s32[1]{0:T(128)} %bitcast.expert_ref, bf16[64,3712]{1,0:T(8,128)(2,1)S(1)} %collective-permute-done.3.refs_0_, bf16[64,3712]{1,0:T(8,128)(2,1)S(1)} %collective-permute-done.5.refs_1_, ...), custom_call_target="tpu_custom_call" | custom-call | flops 1000 | bytes 1000 | tf_op jit(solution)/shard_map/spread/pallas_call | solution.py:286
  56.9 0.8 collective-permute-start.11
  57.8 1.4 %collective-permute-start.15 = (bf16[64,3584]{1,0:T(8,128)(2,1)S(1)}, bf16[64,3584]{1,0:T(8,128)(2,1)S(1)}, u32[]{:S(2)}, u32[]{:S(2)}) collective-permute-start(bf16[64,3584]{1,0:T(8,128)(2,1)S(1)} %get-tuple-element.51), channel_id=1, source_target_pairs={{0,24},{1,9},{2,26},{3,11},{4,28},{5,13},{6,30},{7,15},{8,16},{9,1... | collective-permute-start | bytes 1376264 | tf_op jit(solution)/shard_map/ppermute | solution.py:77
  59.2 1.7 %collective-permute-start.17 = (bf16[64,3584]{1,0:T(8,128)(2,1)S(1)}, bf16[64,3584]{1,0:T(8,128)(2,1)S(1)}, u32[]{:S(2)}, u32[]{:S(2)}) collective-permute-start(bf16[64,3584]{1,0:T(8,128)(2,1)S(1)} %get-tuple-element.52), channel_id=1, source_target_pairs={{0,126},{1,43},{2,124},{3,41},{4,122},{5,47},{6,120},{7,45},{8,118... | collective-permute-start | bytes 1376264 | tf_op jit(solution)/shard_map/ppermute | solution.py:77
  60.8 3.8 %collective-permute-done.11 = bf16[64,3584]{1,0:T(8,128)(2,1)S(1)} collective-permute-done((bf16[64,3584]{1,0:T(8,128)(2,1)S(1)}, bf16[64,3584]{1,0:T(8,128)(2,1)S(1)}, u32[]{:S(2)}, u32[]{:S(2)}) %collective-permute-start.11) | collective-permute-done | bytes 458784 | tf_op jit(solution)/shard_map/ppermute | solution.py:77
  64.7 0.6 collective-permute-start.12
  65.5 1.5 %collective-permute-start.14 = (bf16[64,3584]{1,0:T(8,128)(2,1)S(1)}, bf16[64,3584]{1,0:T(8,128)(2,1)S(1)}, u32[]{:S(2)}, u32[]{:S(2)}) collective-permute-start(bf16[64,3584]{1,0:T(8,128)(2,1)S(1)} %add_convert_fusion.2), channel_id=1, source_target_pairs={{0,24},{1,9},{2,26},{3,11},{4,28},{5,13},{6,30},{7,15},{8,16},{9,1... | collective-permute-start | bytes 1376264 | tf_op jit(solution)/shard_map/ppermute | solution.py:77
  67.1 0.4 collective-permute-start.16
  67.4 4.4 %collective-permute-done.17 = bf16[64,3584]{1,0:T(8,128)(2,1)S(1)} collective-permute-done((bf16[64,3584]{1,0:T(8,128)(2,1)S(1)}, bf16[64,3584]{1,0:T(8,128)(2,1)S(1)}, u32[]{:S(2)}, u32[]{:S(2)}) %collective-permute-start.17) | collective-permute-done | bytes 458784 | tf_op jit(solution)/shard_map/ppermute | solution.py:77
  71.8 5.0 %collective-permute-done.12 = bf16[64,3584]{1,0:T(8,128)(2,1)S(1)} collective-permute-done((bf16[64,3584]{1,0:T(8,128)(2,1)S(1)}, bf16[64,3584]{1,0:T(8,128)(2,1)S(1)}, u32[]{:S(2)}, u32[]{:S(2)}) %collective-permute-start.12) | collective-permute-done | bytes 458784 | tf_op jit(solution)/shard_map/ppermute | solution.py:77
  76.8 0.3 fusion
  77.1 15.6 %all_to_all.11.parts_ref = bf16[8,8,3584]{2,1,0:T(8,128)(2,1)S(1)} all-to-all(bf16[8,8,3584]{2,1,0:T(8,128)(2,1)S(1)} %fusion), channel_id=1, replica_groups={{0,2,8,10,32,34,40,42},{1,7,25,31,97,103,121,127},{3,5,27,29,99,101,123..., dimensions={0} | all-to-all | bytes 917504 | tf_op jit(solution)/shard_map/all_to_all | solution.py:73
  92.7 0.7 finish.1
  (30 shorter events, 1.2 us)
Async XLA Ops:
  0.0 45.5 %slice-start = ((s8[7340032]{0:T(1024)(128)(4,1)}), s8[3145728]{0:T(1024)(128)(4,1)S(1)}, s32[]{:S(2)}) async-start(s8[7340032]{0:T(1024)(128)(4,1)} %bitcast.4), calls=%async_computation.2 | async-start | bytes 6291456
  22.0 23.4 %slice-start.1 = ((s8[7340032]{0:T(1024)(128)(4,1)}), s8[4194304]{0:T(1024)(128)(4,1)S(1)}, s32[]{:S(2)}) async-start(s8[7340032]{0:T(1024)(128)(4,1)} %bitcast.4), calls=%async_computation.3 | async-start | bytes 8388608
  22.0 7.5 %collective-permute-start.2 = (bf16[64,3712]{1,0:T(8,128)(2,1)S(1)}, bf16[64,3712]{1,0:T(8,128)(2,1)S(1)}, u32[]{:S(2)}, u32[]{:S(2)}) collective-permute-start(bf16[64,3712]{1,0:T(8,128)(2,1)S(1)} %bitcast.8), channel_id=1, source_target_pairs={{0,6},{1,3},{2,4},{3,1},{4,2},{5,7},{6,0},{7,5},{8,14},{9,11},{10,... | collective-permute-start | bytes 1425416 | tf_op jit(solution)/shard_map/ppermute | solution.py:77
  22.0 7.5 %collective-permute-start.1 = (bf16[64,3712]{1,0:T(8,128)(2,1)S(1)}, bf16[64,3712]{1,0:T(8,128)(2,1)S(1)}, u32[]{:S(2)}, u32[]{:S(2)}) collective-permute-start(bf16[64,3712]{1,0:T(8,128)(2,1)S(1)} %bitcast.9), channel_id=1, source_target_pairs={{0,24},{1,9},{2,26},{3,11},{4,28},{5,13},{6,30},{7,15},{8,16},{9,1... | collective-permute-start | bytes 1425416 | tf_op jit(solution)/shard_map/ppermute | solution.py:77
  22.0 13.0 %collective-permute-start = (bf16[64,3712]{1,0:T(8,128)(2,1)S(1)}, bf16[64,3712]{1,0:T(8,128)(2,1)S(1)}, u32[]{:S(2)}, u32[]{:S(2)}) collective-permute-start(bf16[64,3712]{1,0:T(8,128)(2,1)S(1)} %bitcast.10), channel_id=1, source_target_pairs={{0,96},{1,33},{2,98},{3,35},{4,100},{5,37},{6,102},{7,39},{8,104},... | collective-permute-start | bytes 1425416 | tf_op jit(solution)/shard_map/ppermute | solution.py:77
  22.1 17.0 %collective-permute-start.6 = (bf16[64,3712]{1,0:T(8,128)(2,1)S(1)}, bf16[64,3712]{1,0:T(8,128)(2,1)S(1)}, u32[]{:S(2)}, u32[]{:S(2)}) collective-permute-start(bf16[64,3712]{1,0:T(8,128)(2,1)S(1)} %bitcast.11), channel_id=1, source_target_pairs={{0,126},{1,43},{2,124},{3,41},{4,122},{5,47},{6,120},{7,45},{8,118... | collective-permute-start | bytes 1425416 | tf_op jit(solution)/shard_map/ppermute | solution.py:77
  29.5 10.5 %collective-permute-start.4 = (bf16[64,3712]{1,0:T(8,128)(2,1)S(1)}, bf16[64,3712]{1,0:T(8,128)(2,1)S(1)}, u32[]{:S(2)}, u32[]{:S(2)}) collective-permute-start(bf16[64,3712]{1,0:T(8,128)(2,1)S(1)} %collective-permute-done.2.refs_2_), channel_id=1, source_target_pairs={{0,24},{1,9},{2,26},{3,11},{4,28},{5,13},{6,30},{7,15},{8,16},{9,1... | collective-permute-start | bytes 1425416 | tf_op jit(solution)/shard_map/ppermute | solution.py:77
  29.5 10.6 %collective-permute-start.3 = (bf16[64,3712]{1,0:T(8,128)(2,1)S(1)}, bf16[64,3712]{1,0:T(8,128)(2,1)S(1)}, u32[]{:S(2)}, u32[]{:S(2)}) collective-permute-start(bf16[64,3712]{1,0:T(8,128)(2,1)S(1)} %collective-permute-done.1.refs_1_), channel_id=1, source_target_pairs={{0,96},{1,33},{2,98},{3,35},{4,100},{5,37},{6,102},{7,39},{8,104},... | collective-permute-start | bytes 1425416 | tf_op jit(solution)/shard_map/ppermute | solution.py:77
  35.0 7.8 %collective-permute-start.5 = (bf16[64,3712]{1,0:T(8,128)(2,1)S(1)}, bf16[64,3712]{1,0:T(8,128)(2,1)S(1)}, u32[]{:S(2)}, u32[]{:S(2)}) collective-permute-start(bf16[64,3712]{1,0:T(8,128)(2,1)S(1)} %collective-permute-done.refs_0_), channel_id=1, source_target_pairs={{0,6},{1,3},{2,4},{3,1},{4,2},{5,7},{6,0},{7,5},{8,14},{9,11},{10,... | collective-permute-start | bytes 1425416 | tf_op jit(solution)/shard_map/ppermute | solution.py:77
  42.8 2.7 %collective-permute-start.7 = (bf16[64,7296]{1,0:T(8,128)(2,1)S(1)}, bf16[64,7296]{1,0:T(8,128)(2,1)S(1)}, u32[]{:S(2)}, u32[]{:S(2)}) collective-permute-start(bf16[64,7296]{1,0:T(8,128)(2,1)S(1)} %get-tuple-element.31), channel_id=1, source_target_pairs={{0,1},{1,0},{2,3},{3,2},{4,5},{5,4},{6,7},{7,6},{8,9},{9,8},{10,11... | collective-permute-start | bytes 2801672 | tf_op jit(solution)/shard_map/ppermute | solution.py:81
  43.3 5.0 %slice-start.2 = ((s8[7340032]{0:T(1024)(128)(4,1)}), s8[4194304]{0:T(1024)(128)(4,1)S(1)}, s32[]{:S(2)}) async-start(s8[7340032]{0:T(1024)(128)(4,1)} %bitcast.6), calls=%async_computation.4 | async-start | bytes 8388608
  44.3 5.8 %collective-permute-start.9 = (bf16[64,7296]{1,0:T(8,128)(2,1)S(1)}, bf16[64,7296]{1,0:T(8,128)(2,1)S(1)}, u32[]{:S(2)}, u32[]{:S(2)}) collective-permute-start(bf16[64,7296]{1,0:T(8,128)(2,1)S(1)} %get-tuple-element.41), channel_id=1, source_target_pairs={{0,1},{1,0},{2,3},{3,2},{4,5},{5,4},{6,7},{7,6},{8,9},{9,8},{10,11... | collective-permute-start | bytes 2801672 | tf_op jit(solution)/shard_map/ppermute | solution.py:81
  45.5 3.0 %slice-start.3 = ((s8[7340032]{0:T(1024)(128)(4,1)}), s8[3145728]{0:T(1024)(128)(4,1)S(1)}, s32[]{:S(2)}) async-start(s8[7340032]{0:T(1024)(128)(4,1)} %bitcast.6), calls=%async_computation.5 | async-start | bytes 6291456
  49.6 3.9 %collective-permute-start.8 = (bf16[64,7168]{1,0:T(8,128)(2,1)S(1)}, bf16[64,7168]{1,0:T(8,128)(2,1)S(1)}, u32[]{:S(2)}, u32[]{:S(2)}) collective-permute-start(bf16[64,7168]{1,0:T(8,128)(2,1)S(1)} %get-tuple-element.40), channel_id=1, source_target_pairs={{0,1},{1,0},{2,3},{3,2},{4,5},{5,4},{6,7},{7,6},{8,9},{9,8},{10,11... | collective-permute-start | bytes 2752520 | tf_op jit(solution)/shard_map/ppermute | solution.py:81
  53.3 2.6 %collective-permute-start.10 = (bf16[64,7168]{1,0:T(8,128)(2,1)S(1)}, bf16[64,7168]{1,0:T(8,128)(2,1)S(1)}, u32[]{:S(2)}, u32[]{:S(2)}) collective-permute-start(bf16[64,7168]{1,0:T(8,128)(2,1)S(1)} %get-tuple-element.46), channel_id=1, source_target_pairs={{0,1},{1,0},{2,3},{3,2},{4,5},{5,4},{6,7},{7,6},{8,9},{9,8},{10,11... | collective-permute-start | bytes 2752520 | tf_op jit(solution)/shard_map/ppermute | solution.py:81
  56.9 7.7 %collective-permute-start.11 = (bf16[64,3584]{1,0:T(8,128)(2,1)S(1)}, bf16[64,3584]{1,0:T(8,128)(2,1)S(1)}, u32[]{:S(2)}, u32[]{:S(2)}) collective-permute-start(bf16[64,3584]{1,0:T(8,128)(2,1)S(1)} %get-tuple-element.47), channel_id=1, source_target_pairs={{0,6},{1,3},{2,4},{3,1},{4,2},{5,7},{6,0},{7,5},{8,14},{9,11},{10,... | collective-permute-start | bytes 1376264 | tf_op jit(solution)/shard_map/ppermute | solution.py:77
  57.7 7.7 %collective-permute-start.13 = (bf16[64,3584]{1,0:T(8,128)(2,1)S(1)}, bf16[64,3584]{1,0:T(8,128)(2,1)S(1)}, u32[]{:S(2)}, u32[]{:S(2)}) collective-permute-start(bf16[64,3584]{1,0:T(8,128)(2,1)S(1)} %get-tuple-element.49), channel_id=1, source_target_pairs={{0,96},{1,33},{2,98},{3,35},{4,100},{5,37},{6,102},{7,39},{8,104},... | collective-permute-start | bytes 1376264 | tf_op jit(solution)/shard_map/ppermute | solution.py:77
  57.8 9.2 %collective-permute-start.15 = (bf16[64,3584]{1,0:T(8,128)(2,1)S(1)}, bf16[64,3584]{1,0:T(8,128)(2,1)S(1)}, u32[]{:S(2)}, u32[]{:S(2)}) collective-permute-start(bf16[64,3584]{1,0:T(8,128)(2,1)S(1)} %get-tuple-element.51), channel_id=1, source_target_pairs={{0,24},{1,9},{2,26},{3,11},{4,28},{5,13},{6,30},{7,15},{8,16},{9,1... | collective-permute-start | bytes 1376264 | tf_op jit(solution)/shard_map/ppermute | solution.py:77
  59.2 12.6 %collective-permute-start.17 = (bf16[64,3584]{1,0:T(8,128)(2,1)S(1)}, bf16[64,3584]{1,0:T(8,128)(2,1)S(1)}, u32[]{:S(2)}, u32[]{:S(2)}) collective-permute-start(bf16[64,3584]{1,0:T(8,128)(2,1)S(1)} %get-tuple-element.52), channel_id=1, source_target_pairs={{0,126},{1,43},{2,124},{3,41},{4,122},{5,47},{6,120},{7,45},{8,118... | collective-permute-start | bytes 1376264 | tf_op jit(solution)/shard_map/ppermute | solution.py:77
  64.7 12.1 %collective-permute-start.12 = (bf16[64,3584]{1,0:T(8,128)(2,1)S(1)}, bf16[64,3584]{1,0:T(8,128)(2,1)S(1)}, u32[]{:S(2)}, u32[]{:S(2)}) collective-permute-start(bf16[64,3584]{1,0:T(8,128)(2,1)S(1)} %add_convert_fusion.3), channel_id=1, source_target_pairs={{0,96},{1,33},{2,98},{3,35},{4,100},{5,37},{6,102},{7,39},{8,104},... | collective-permute-start | bytes 1376264 | tf_op jit(solution)/shard_map/ppermute | solution.py:77
  65.5 11.3 %collective-permute-start.14 = (bf16[64,3584]{1,0:T(8,128)(2,1)S(1)}, bf16[64,3584]{1,0:T(8,128)(2,1)S(1)}, u32[]{:S(2)}, u32[]{:S(2)}) collective-permute-start(bf16[64,3584]{1,0:T(8,128)(2,1)S(1)} %add_convert_fusion.2), channel_id=1, source_target_pairs={{0,24},{1,9},{2,26},{3,11},{4,28},{5,13},{6,30},{7,15},{8,16},{9,1... | collective-permute-start | bytes 1376264 | tf_op jit(solution)/shard_map/ppermute | solution.py:77
  67.1 9.7 %collective-permute-start.16 = (bf16[64,3584]{1,0:T(8,128)(2,1)S(1)}, bf16[64,3584]{1,0:T(8,128)(2,1)S(1)}, u32[]{:S(2)}, u32[]{:S(2)}) collective-permute-start(bf16[64,3584]{1,0:T(8,128)(2,1)S(1)} %add_convert_fusion.1), channel_id=1, source_target_pairs={{0,6},{1,3},{2,4},{3,1},{4,2},{5,7},{6,0},{7,5},{8,14},{9,11},{10,... | collective-permute-start | bytes 1376264 | tf_op jit(solution)/shard_map/ppermute | solution.py:77

commit v6 on v5

--- a/solution.py
+++ b/solution.py
@@ -25,8 +25,8 @@
 SMALL = pltpu.CompilerParams(vmem_limit_bytes=8 * MIB)
 
 
-DEPTH = 1792
 MIDDLE = D // 2
+CUTS = ((0, MIDDLE), (MIDDLE, D))
 BRIEF = pl.CostEstimate(flops=1000, bytes_accessed=1000, transcendentals=0)
 
 
@@ -66,7 +66,7 @@
 
 
 NEAR = near_groups()
-FAR = [far_pairs(0), far_pairs(1), far_pairs(2), far_pairs(0, 1, 2)]
+FAR = [far_pairs(0), far_pairs(1), far_pairs(2), far_pairs(0, 1, 2), far_pairs(0, 1)]
 
 
 def swap_near(values):
@@ -75,6 +75,10 @@
 
 def swap_far(values, axis):
     return lax.ppermute(values, AXES, FAR[axis])
+
+
+def both_cores(values):
+    return lax.all_gather(values, "dev", axis_index_groups=[[i, i + 1] for i in range(0, 32, 2)])
 
 
 def to_sibling(values):
@@ -134,9 +138,8 @@
     blocks = [refs.pop(0) for _ in range(4)]
     sources = [refs.pop(0) for _ in range(loads)]
     del refs[0]
-    mine_ref, sent_ref = refs[:2]
-    targets = refs[2 : 2 + loads]
-    pick, sem = refs[2 + loads :]
+    mine_ref, sent_refs, targets = refs[0], refs[1:3], refs[3 : 3 + loads]
+    pick, sem = refs[3 + loads :]
     copies = [pltpu.make_async_copy(a.at[:, :MIDDLE, :], b, sem) for a, b in zip(sources, targets)]
     for copy in copies:
         copy.start()
@@ -159,16 +162,17 @@
         hit = place[e : e + 1, :] == row
         pick[e * SEL : (e + 1) * SEL, :] = jnp.where(hit & is_left, 1.0, 0.0).astype(BF16)
         pick[(2 + e) * SEL : (3 + e) * SEL, :] = jnp.where(hit & ~is_left, 1.0, 0.0).astype(BF16)
+
     for n in range(0, HALF, 512):
         x = jnp.concatenate([ref[:, n : n + 512] for ref in blocks], axis=0)
         value = jnp.dot(pick[...], x, preferred_element_type=F32).astype(BF16)
         mine_ref[:, n : n + 512] = value[:SEL]
-        sent_ref[:, n : n + 512] = value[SEL : 2 * SEL]
+        sent_refs[0][:, n : n + 512] = value[SEL : 2 * SEL]
         mine_ref[:, HALF + n : HALF + n + 512] = value[2 * SEL : 3 * SEL]
-        sent_ref[:, HALF + n : HALF + n + 512] = value[3 * SEL :]
+        sent_refs[1][:, n : n + 512] = value[3 * SEL :]
     value = jnp.dot(pick[: 2 * SEL, :], ext, preferred_element_type=F32).astype(BF16)
     mine_ref[:, D:] = value[:SEL]
-    sent_ref[:, D:] = value[SEL:]
+    sent_refs[1][:, HALF:] = value[SEL:]
     for copy in copies:
         copy.wait()
 
@@ -176,10 +180,11 @@
 def select(expert, blocks, after, loads=()):
     return pl.pallas_call(
         functools.partial(select_kernel, len(loads)),
-        out_shape=[jax.ShapeDtypeStruct((SEL, D + EXT), BF16)] * 2
+        out_shape=[jax.ShapeDtypeStruct((SEL, D + EXT), BF16)]
+        + [jax.ShapeDtypeStruct((SEL, high - low + EXT * (high == D)), BF16) for low, high in CUTS]
         + [jax.ShapeDtypeStruct((1, MIDDLE, 512), BF16) for _ in loads],
         in_specs=[SMEM] + [VMEM] * 4 + [HBM] * len(loads) + [ANY],
-        out_specs=[VMEM] * (2 + len(loads)),
+        out_specs=[VMEM] * (3 + len(loads)),
         scratch_shapes=[pltpu.VMEM((PART, PART), BF16), pltpu.SemaphoreType.DMA],
         compiler_params=SMALL,
         cost_estimate=BRIEF,
@@ -187,7 +192,7 @@
     )(expert, *blocks, *[in_hbm(load) for load in loads], after)
 
 
-def hidden_kernel(streams, expert_ref, mine_ref, theirs_ref, gate_ref, first_ref, rest_ref, after_ref, *refs):
+def hidden_kernel(streams, expert_ref, mine_ref, a_ref, b_ref, gate_ref, first_ref, rest_ref, after_ref, *refs):
     del after_ref
     if streams:
         hidden, second_ref, gate_sum, up_sum, sem = refs
@@ -197,37 +202,39 @@
         hidden, gate_sum, up_sum = refs
         second_ref = rest_ref
 
-    def rows(block):
-        return jnp.concatenate([mine_ref[:, block], theirs_ref[:, block]], axis=0)
-
-    for i in range(0, D, DEPTH):
-        block = slice(i, i + DEPTH)
-        gate = jnp.dot(rows(block), gate_ref[0, block, :], preferred_element_type=F32)
-        gate_sum[...] = gate if i == 0 else gate_sum[...] + gate
-    for i in range(0, D, DEPTH):
-        if streams and i == MIDDLE:
+    def rows(piece, low, high):
+        start = CUTS[piece][0]
+        theirs_ref, block = (a_ref, b_ref)[piece], slice(low - start, high - start)
+        theirs = theirs_ref[1 - expert_ref[0] % 2, :, block] if streams else theirs_ref[:, block]
+        return jnp.concatenate([mine_ref[:, low:high], theirs], axis=0)
+
+    for piece, (low, high) in enumerate(CUTS):
+        gate = jnp.dot(rows(piece, low, high), gate_ref[0, low:high, :], preferred_element_type=F32)
+        gate_sum[...] = gate if low == 0 else gate_sum[...] + gate
+    for piece, (low, high) in enumerate(CUTS):
+        if streams and low == MIDDLE:
             copy.wait()
-        ref, start = (first_ref, i) if i < MIDDLE else (second_ref, i - MIDDLE)
-        up = jnp.dot(rows(slice(i, i + DEPTH)), ref[0, start : start + DEPTH, :], preferred_element_type=F32)
-        up_sum[...] = up if i == 0 else up_sum[...] + up
+        ref, start = (first_ref, 0) if low < MIDDLE else (second_ref, MIDDLE)
+        up = jnp.dot(rows(piece, low, high), ref[0, low - start : high - start, :], preferred_element_type=F32)
+        up_sum[...] = up if low == 0 else up_sum[...] + up
     lanes = expert_lanes(expert_ref[0], (2 * SEL, EXT), 1)
-    scale = jnp.sum(jnp.where(lanes, rows(slice(D, D + EXT)).astype(F32), 0.0), axis=1, keepdims=True)
+    scale = jnp.sum(jnp.where(lanes, rows(1, D, D + EXT).astype(F32), 0.0), axis=1, keepdims=True)
     v = gate_sum[...]
     hidden[...] = (v / (1.0 + jnp.exp(-v)) * up_sum[...] * scale).astype(BF16)
 
 
 def hidden_units(expert, mine, theirs, gate, first, rest, after, streams):
-    half = jax.ShapeDtypeStruct((1, MIDDLE, 512), BF16)
+    second = jax.ShapeDtypeStruct((1, D - MIDDLE, 512), BF16)
     return pl.pallas_call(
         functools.partial(hidden_kernel, streams),
-        out_shape=[jax.ShapeDtypeStruct((2 * SEL, 512), BF16)] + [half] * streams,
-        in_specs=[SMEM, VMEM, VMEM, VMEM, VMEM, HBM if streams else VMEM, ANY],
+        out_shape=[jax.ShapeDtypeStruct((2 * SEL, 512), BF16)] + [second] * streams,
+        in_specs=[SMEM] + [VMEM] * 5 + [HBM if streams else VMEM, ANY],
         out_specs=[VMEM] * (1 + streams),
         scratch_shapes=[pltpu.VMEM((2 * SEL, 512), F32)] * 2 + [pltpu.SemaphoreType.DMA] * streams,
         compiler_params=SMALL,
         cost_estimate=BRIEF,
         name="hidden",
-    )(expert, mine, theirs, gate, first, in_hbm(rest) if streams else rest, after)
+    )(expert, mine, *theirs, gate, first, in_hbm(rest) if streams else rest, after)
 
 
 def down_kernel(hidden_ref, down_ref, after_ref, mine_ref, theirs_ref):
@@ -325,23 +332,23 @@
     expert = lax.axis_index("dev").astype(jnp.int32).reshape(1)
     own = swap_near(pack(expert, tokens, ids, weights)).reshape(BLOCK, WIDE)
     x, y, z = swap_far(own, 0), swap_far(own, 1), swap_far(own, 2)
-    xyz = swap_far(own, 3)
     xy, yz, zx = swap_far(y, 0), swap_far(z, 1), swap_far(x, 2)
+    xyz = swap_far(z, 4)
     near = (x, y, z, own)
-    mine_near, sent, up_first = select(expert, near, own, (up,))
-    xy, yz, zx, xyz, sent = lax.optimization_barrier((xy, yz, zx, xyz, sent))
-    got_near = to_sibling(sent)
+    mine_near, *sent, up_first = select(expert, near, own, (up,))
+    got_near = [both_cores(piece) for piece in sent]
+    hidden_near, up_second = hidden_units(expert, mine_near, got_near, gate, up_first, up, own, 1)
+    result_near, theirs = down_rows(hidden_near, down, own)
+    xy, yz, zx, xyz, theirs = lax.optimization_barrier((xy, yz, zx, xyz, theirs))
     far = (xy, zx, yz, xyz)
-    mine_far, sent = select(expert, far, own)
-    got_far = to_sibling(sent)
-    hidden_near, up_second = hidden_units(expert, mine_near, got_near, gate, up_first, up, mine_far, 1)
-    result_near, theirs = down_rows(hidden_near, down, own)
     returned_near = to_sibling(theirs)
-    (hidden_far,) = hidden_units(expert, mine_far, got_far, gate, up_first, up_second, result_near, 0)
+    mine_far, *sent = select(expert, far, result_near)
+    got_far = [to_sibling(piece) for piece in sent]
+    y_x, y_y, y_z, y_own = spread(expert, near, result_near, returned_near, mine_far)
+    (hidden_far,) = hidden_units(expert, mine_far, got_far, gate, up_first, up_second, y_own, 0)
     result, theirs = down_rows(hidden_far, down, own)
     returned = to_sibling(theirs)
-    y_x, y_y, y_z, y_own = spread(expert, near, result_near, returned_near, result)
-    y_xy, y_zx, y_yz, y_xyz = spread(expert, far, result, returned, y_own)
+    y_xy, y_zx, y_yz, y_xyz = spread(expert, far, result, returned, own)
     at_y, at_z, at_x = swap_far(y_xy, 0), swap_far(y_yz, 1), swap_far(y_zx, 2)
     at_own = swap_far(y_xyz, 3)
     total = add(

time: 93.6 us -> 98.5 us (1.052)
  the two profiles are of different devices: /device:TPU:1 before, /device:TPU:0 now
where the time goes in v6:
time: 98.5 us; the launch traced here: 98.3 us
  starting transfers between devices  30.9 us (31%)
  blocking collectives  28.6 us (29%)
  waiting for transfers between devices  23.8 us (24%)
  Pallas kernels  14.1 us (14%)
    ppermute x14, starting transfers between devices, swap_far(): return lax.ppermute(values, AXES, FAR[axis])  29.8 us
    all_to_all x2, blocking collectives, swap_near(): lax.all_to_all(values, AXES, 0, 0, axis_index_groups=NEAR, tiled=True)  23.6 us
    ppermute x14, waiting for transfers between devices, swap_far(): return lax.ppermute(values, AXES, FAR[axis])  20.4 us
    all_gather x2, blocking collectives, both_cores(): lax.all_gather(values, 'dev', axis_index_groups=[[i, i + 1] for i in rang...  5.07 us
    pallas_call x2, Pallas kernels, hidden_units(): pl.pallas_call(functools.partial(hidden_kernel, streams), out_shape=[jax....  4.95 us
    ppermute x4, waiting for transfers between devices, to_sibling(): return lax.ppermute(values, 'dev', [(i, i ^ 1) for i in range(32)])  3.39 us
    pallas_call x2, Pallas kernels, select(): pl.pallas_call(functools.partial(select_kernel, len(loads)), out_shape=[j...  2.96 us
    pallas_call x2, Pallas kernels, down_rows(): pl.pallas_call(down_kernel, out_shape=[jax.ShapeDtypeStruct((SEL, D), BF1...  2.27 us
  transfers between devices with their start and end apart: 18, of which 9 were waited for; matrix products, arithmetic and copies ran while one was open for 0% of the time, Pallas kernels for 8%

profile of v6, /device:TPU:0, one launch (start us, length us, event | category | flops | bytes accessed | tf_op | source)
XLA Modules:
  0.0 98.3 jit_solution(12420017015022218828)
XLA Ops:
  0.0 1.1 %pack.1 = bf16[8,8,3712]{2,1,0:T(8,128)(2,1)S(1)} custom-call(s32[1]{0:T(128)} %bitcast.expert_ref, bf16[4,7168]{1,0:T(4,128)(2,1)} %tokens_hbm.1, s32[4,8]{1,0:T(4,128)} %ids_hbm.1, f32[4,8]{1,0:T(4,128)} %weights_hbm.1), custom_call_target="tpu_custom_call" | custom-call | tf_op jit(solution)/shard_map/pack/pallas_call | solution.py:115
  1.1 13.1 %all_to_all.10 = bf16[8,8,3712]{2,1,0:T(8,128)(2,1)S(1)} all-to-all(bf16[8,8,3712]{2,1,0:T(8,128)(2,1)S(1)} %pack.1), channel_id=1, replica_groups={{0,2,8,10,32,34,40,42},{1,7,25,31,97,103,121,127},{3,5,27,29,99,101,123..., dimensions={0} | all-to-all | bytes 950272 | tf_op jit(solution)/shard_map/all_to_all | solution.py:73
  14.2 1.5 %collective-permute-start.1 = (bf16[64,3712]{1,0:T(8,128)(2,1)S(1)}, bf16[64,3712]{1,0:T(8,128)(2,1)S(1)}, u32[]{:S(2)}, u32[]{:S(2)}) collective-permute-start(bf16[64,3712]{1,0:T(8,128)(2,1)S(1)} %bitcast.6), channel_id=1, source_target_pairs={{0,24},{1,9},{2,26},{3,11},{4,28},{5,13},{6,30},{7,15},{8,16},{9,1... | collective-permute-start | bytes 1425416 | tf_op jit(solution)/shard_map/ppermute | solution.py:77
  15.8 2.3 %collective-permute-start.2 = (bf16[64,3712]{1,0:T(8,128)(2,1)S(1)}, bf16[64,3712]{1,0:T(8,128)(2,1)S(1)}, u32[]{:S(2)}, u32[]{:S(2)}) collective-permute-start(bf16[64,3712]{1,0:T(8,128)(2,1)S(1)} %bitcast.7), channel_id=1, source_target_pairs={{0,6},{1,3},{2,4},{3,1},{4,2},{5,7},{6,0},{7,5},{8,14},{9,11},{10,... | collective-permute-start | bytes 1425416 | tf_op jit(solution)/shard_map/ppermute | solution.py:77
  18.1 2.7 %collective-permute-start = (bf16[64,3712]{1,0:T(8,128)(2,1)S(1)}, bf16[64,3712]{1,0:T(8,128)(2,1)S(1)}, u32[]{:S(2)}, u32[]{:S(2)}) collective-permute-start(bf16[64,3712]{1,0:T(8,128)(2,1)S(1)} %bitcast.8), channel_id=1, source_target_pairs={{0,96},{1,33},{2,98},{3,35},{4,100},{5,37},{6,102},{7,39},{8,104},... | collective-permute-start | bytes 1425416 | tf_op jit(solution)/shard_map/ppermute | solution.py:77
  20.8 3.4 %collective-permute-done.1.refs_1_ = bf16[64,3712]{1,0:T(8,128)(2,1)S(1)} collective-permute-done((bf16[64,3712]{1,0:T(8,128)(2,1)S(1)}, bf16[64,3712]{1,0:T(8,128)(2,1)S(1)}, u32[]{:S(2)}, u32[]{:S(2)}) %collective-permute-start.1) | collective-permute-done | bytes 475168 | tf_op jit(solution)/shard_map/ppermute | solution.py:77
  24.1 2.7 %collective-permute-start.3 = (bf16[64,3712]{1,0:T(8,128)(2,1)S(1)}, bf16[64,3712]{1,0:T(8,128)(2,1)S(1)}, u32[]{:S(2)}, u32[]{:S(2)}) collective-permute-start(bf16[64,3712]{1,0:T(8,128)(2,1)S(1)} %collective-permute-done.1.refs_1_), channel_id=1, source_target_pairs={{0,96},{1,33},{2,98},{3,35},{4,100},{5,37},{6,102},{7,39},{8,104},... | collective-permute-start | bytes 1425416 | tf_op jit(solution)/shard_map/ppermute | solution.py:77
  26.8 1.8 %collective-permute-start.4 = (bf16[64,3712]{1,0:T(8,128)(2,1)S(1)}, bf16[64,3712]{1,0:T(8,128)(2,1)S(1)}, u32[]{:S(2)}, u32[]{:S(2)}) collective-permute-start(bf16[64,3712]{1,0:T(8,128)(2,1)S(1)} %collective-permute-done.2.refs_2_), channel_id=1, source_target_pairs={{0,24},{1,9},{2,26},{3,11},{4,28},{5,13},{6,30},{7,15},{8,16},{9,1... | collective-permute-start | bytes 1425416 | tf_op jit(solution)/shard_map/ppermute | solution.py:77
  28.6 2.0 %collective-permute-start.5 = (bf16[64,3712]{1,0:T(8,128)(2,1)S(1)}, bf16[64,3712]{1,0:T(8,128)(2,1)S(1)}, u32[]{:S(2)}, u32[]{:S(2)}) collective-permute-start(bf16[64,3712]{1,0:T(8,128)(2,1)S(1)} %collective-permute-done.refs_0_), channel_id=1, source_target_pairs={{0,6},{1,3},{2,4},{3,1},{4,2},{5,7},{6,0},{7,5},{8,14},{9,11},{10,... | collective-permute-start | bytes 1425416 | tf_op jit(solution)/shard_map/ppermute | solution.py:77
  30.6 2.7 %collective-permute-start.6 = (bf16[64,3712]{1,0:T(8,128)(2,1)S(1)}, bf16[64,3712]{1,0:T(8,128)(2,1)S(1)}, u32[]{:S(2)}, u32[]{:S(2)}) collective-permute-start(bf16[64,3712]{1,0:T(8,128)(2,1)S(1)} %collective-permute-done.2.refs_2_), channel_id=1, source_target_pairs={{0,120},{1,41},{2,122},{3,43},{4,124},{5,45},{6,126},{7,47},{8,112... | collective-permute-start | bytes 1425416 | tf_op jit(solution)/shard_map/ppermute | solution.py:77
  33.3 2.0 %select.2 = (bf16[64,7296]{1,0:T(8,128)(2,1)S(1)}, bf16[64,3584]{1,0:T(8,128)(2,1)S(1)}, bf16[64,3712]{1,0:T(8,128)(2,1)S(1)}, bf16[1,3584,512]{2,1,0:T(8,128)(2,1)S(1)}) custom-call(s32[1]{0:T(128)} %bitcast.expert_ref, bf16[64,3712]{1,0:T(8,128)(2,1)S(1)} %collective-permute-done.refs_0_, bf16[64,3712]{1,0:T(8,128)(2,1)S(1)} %collective-permute-done.1.refs_1_, ...), custom_call_target="tpu_custom_call" | custom-call | flops 1000 | bytes 1000 | tf_op jit(solution)/shard_map/select/pallas_call | solution.py:181
  35.4 2.5 %all-gather = bf16[128,3584]{1,0:T(8,128)(2,1)S(1)} all-gather(bf16[64,3584]{1,0:T(8,128)(2,1)S(1)} %get-tuple-element.32), channel_id=2, replica_groups={{0,1},{2,3},{4,5},{6,7},{8,9},{10,11},{12,13},{14,15},{16,17},{18,19},{..., dimensions={0}, use_global_device_ids=true | all-gather | bytes 1376256 | tf_op jit(solution)/shard_map/all_gather | solution.py:81
  37.8 2.6 %all-gather.1 = bf16[128,3712]{1,0:T(8,128)(2,1)S(1)} all-gather(bf16[64,3712]{1,0:T(8,128)(2,1)S(1)} %get-tuple-element.33), channel_id=3, replica_groups={{0,1},{2,3},{4,5},{6,7},{8,9},{10,11},{12,13},{14,15},{16,17},{18,19},{..., dimensions={0}, use_global_device_ids=true | all-gather | bytes 1425408 | tf_op jit(solution)/shard_map/all_gather | solution.py:81
  40.4 2.9 %hidden.2 = (bf16[128,512]{1,0:T(8,128)(2,1)S(1)}, bf16[1,3584,512]{2,1,0:T(8,128)(2,1)S(1)}) custom-call(s32[1]{0:T(128)} %bitcast.expert_ref, bf16[64,7296]{1,0:T(8,128)(2,1)S(1)} %get-tuple-element.31.mine_ref, bf16[2,64,3584]{2,1,0:T(8,128)(2,1)S(1)} %bitcast.21, bf16[2,64,3712]{2,1,0:T(8,128)(2,1)S(1)} %bitcast.20, bf16[1,7168,512]{2,1,0:T(8,128)(2,1)S(1)} %bitcast.17, ...), custom_call_target="tpu_custom_call" | custom-call | flops 1000 | bytes 1000 | tf_op jit(solution)/shard_map/hidden/pallas_call | solution.py:228
  43.4 1.1 %down.2 = (bf16[64,7168]{1,0:T(8,128)(2,1)S(1)}, bf16[64,7168]{1,0:T(8,128)(2,1)S(1)}) custom-call(bf16[128,512]{1,0:T(8,128)(2,1)S(1)} %get-tuple-element.35.hidden_ref, bf16[1,512,7168]{2,1,0:T(8,128)(2,1)S(1)} %bitcast.19, bf16[64,3712]{1,0:T(8,128)(2,1)S(1)} %bitcast.12), custom_call_target="tpu_custom_call" | custom-call | flops 1000 | bytes 1000 | tf_op jit(solution)/shard_map/down/pallas_call | solution.py:250
  48.5 2.1 %hidden.3.hidden_ref = bf16[128,512]{1,0:T(8,128)(2,1)S(1)} custom-call(s32[1]{0:T(128)} %bitcast.expert_ref, bf16[64,7296]{1,0:T(8,128)(2,1)S(1)} %get-tuple-element.43.refs_6_.mine_ref, bf16[64,3584]{1,0:T(8,128)(2,1)S(1)} %collective-permute-done.8.a_ref, bf16[64,3712]{1,0:T(8,128)(2,1)S(1)} %collective-permute-done.9.b_ref, ...), custom_call_target="tpu_custom_call" | custom-call | flops 1000 | bytes 1000 | tf_op jit(solution)/shard_map/hidden/pallas_call | solution.py:228
  50.6 1.1 %down.3 = (bf16[64,7168]{1,0:T(8,128)(2,1)S(1)}, bf16[64,7168]{1,0:T(8,128)(2,1)S(1)}) custom-call(bf16[128,512]{1,0:T(8,128)(2,1)S(1)} %hidden.3.hidden_ref, bf16[1,512,7168]{2,1,0:T(8,128)(2,1)S(1)} %bitcast.19, bf16[64,3712]{1,0:T(8,128)(2,1)S(1)} %bitcast.14), custom_call_target="tpu_custom_call" | custom-call | flops 1000 | bytes 1000 | tf_op jit(solution)/shard_map/down/pallas_call | solution.py:250
  52.0 2.3 %collective-permute-done.10.refs_5_ = bf16[64,7168]{1,0:T(8,128)(2,1)S(1)} collective-permute-done((bf16[64,7168]{1,0:T(8,128)(2,1)S(1)}, bf16[64,7168]{1,0:T(8,128)(2,1)S(1)}, u32[]{:S(2)}, u32[]{:S(2)}) %collective-permute-start.10) | collective-permute-done | bytes 917536 | tf_op jit(solution)/shard_map/ppermute | solution.py:85
  54.3 1.1 %spread.3 = (bf16[64,3584]{1,0:T(8,128)(2,1)S(1)}, bf16[64,3584]{1,0:T(8,128)(2,1)S(1)}, bf16[64,3584]{1,0:T(8,128)(2,1)S(1)}, bf16[64,3584]{1,0:T(8,128)(2,1)S(1)}) custom-call(s32[1]{0:T(128)} %bitcast.expert_ref, bf16[64,3712]{1,0:T(8,128)(2,1)S(1)} %collective-permute-done.3.refs_0_, bf16[64,3712]{1,0:T(8,128)(2,1)S(1)} %collective-permute-done.5.refs_1_, ...), custom_call_target="tpu_custom_call" | custom-call | flops 1000 | bytes 1000 | tf_op jit(solution)/shard_map/spread/pallas_call | solution.py:293
  55.4 1.5 %collective-permute-start.15 = (bf16[64,3584]{1,0:T(8,128)(2,1)S(1)}, bf16[64,3584]{1,0:T(8,128)(2,1)S(1)}, u32[]{:S(2)}, u32[]{:S(2)}) collective-permute-start(bf16[64,3584]{1,0:T(8,128)(2,1)S(1)} %get-tuple-element.55), channel_id=1, source_target_pairs={{0,24},{1,9},{2,26},{3,11},{4,28},{5,13},{6,30},{7,15},{8,16},{9,1... | collective-permute-start | bytes 1376264 | tf_op jit(solution)/shard_map/ppermute | solution.py:77
  56.8 3.5 %collective-permute-start.17 = (bf16[64,3584]{1,0:T(8,128)(2,1)S(1)}, bf16[64,3584]{1,0:T(8,128)(2,1)S(1)}, u32[]{:S(2)}, u32[]{:S(2)}) collective-permute-start(bf16[64,3584]{1,0:T(8,128)(2,1)S(1)} %get-tuple-element.56), channel_id=1, source_target_pairs={{0,126},{1,43},{2,124},{3,41},{4,122},{5,47},{6,120},{7,45},{8,118... | collective-permute-start | bytes 1376264 | tf_op jit(solution)/shard_map/ppermute | solution.py:77
  60.4 1.8 %collective-permute-start.13 = (bf16[64,3584]{1,0:T(8,128)(2,1)S(1)}, bf16[64,3584]{1,0:T(8,128)(2,1)S(1)}, u32[]{:S(2)}, u32[]{:S(2)}) collective-permute-start(bf16[64,3584]{1,0:T(8,128)(2,1)S(1)} %get-tuple-element.53), channel_id=1, source_target_pairs={{0,96},{1,33},{2,98},{3,35},{4,100},{5,37},{6,102},{7,39},{8,104},... | collective-permute-start | bytes 1376264 | tf_op jit(solution)/shard_map/ppermute | solution.py:77
  62.2 2.0 %collective-permute-start.11 = (bf16[64,3584]{1,0:T(8,128)(2,1)S(1)}, bf16[64,3584]{1,0:T(8,128)(2,1)S(1)}, u32[]{:S(2)}, u32[]{:S(2)}) collective-permute-start(bf16[64,3584]{1,0:T(8,128)(2,1)S(1)} %get-tuple-element.51), channel_id=1, source_target_pairs={{0,6},{1,3},{2,4},{3,1},{4,2},{5,7},{6,0},{7,5},{8,14},{9,11},{10,... | collective-permute-start | bytes 1376264 | tf_op jit(solution)/shard_map/ppermute | solution.py:77
  64.2 1.1 %collective-permute-done.15 = bf16[64,3584]{1,0:T(8,128)(2,1)S(1)} collective-permute-done((bf16[64,3584]{1,0:T(8,128)(2,1)S(1)}, bf16[64,3584]{1,0:T(8,128)(2,1)S(1)}, u32[]{:S(2)}, u32[]{:S(2)}) %collective-permute-start.15) | collective-permute-done | bytes 458784 | tf_op jit(solution)/shard_map/ppermute | solution.py:77
  65.4 1.3 %collective-permute-start.16 = (bf16[64,3584]{1,0:T(8,128)(2,1)S(1)}, bf16[64,3584]{1,0:T(8,128)(2,1)S(1)}, u32[]{:S(2)}, u32[]{:S(2)}) collective-permute-start(bf16[64,3584]{1,0:T(8,128)(2,1)S(1)} %add_convert_fusion.1), channel_id=1, source_target_pairs={{0,6},{1,3},{2,4},{3,1},{4,2},{5,7},{6,0},{7,5},{8,14},{9,11},{10,... | collective-permute-start | bytes 1376264 | tf_op jit(solution)/shard_map/ppermute | solution.py:77
  66.7 8.2 %collective-permute-done.13 = bf16[64,3584]{1,0:T(8,128)(2,1)S(1)} collective-permute-done((bf16[64,3584]{1,0:T(8,128)(2,1)S(1)}, bf16[64,3584]{1,0:T(8,128)(2,1)S(1)}, u32[]{:S(2)}, u32[]{:S(2)}) %collective-permute-start.13) | collective-permute-done | bytes 458784 | tf_op jit(solution)/shard_map/ppermute | solution.py:77
  75.1 1.9 %collective-permute-start.14 = (bf16[64,3584]{1,0:T(8,128)(2,1)S(1)}, bf16[64,3584]{1,0:T(8,128)(2,1)S(1)}, u32[]{:S(2)}, u32[]{:S(2)}) collective-permute-start(bf16[64,3584]{1,0:T(8,128)(2,1)S(1)} %add_convert_fusion.2), channel_id=1, source_target_pairs={{0,24},{1,9},{2,26},{3,11},{4,28},{5,13},{6,30},{7,15},{8,16},{9,1... | collective-permute-start | bytes 1376264 | tf_op jit(solution)/shard_map/ppermute | solution.py:77
  77.1 2.1 %collective-permute-start.12 = (bf16[64,3584]{1,0:T(8,128)(2,1)S(1)}, bf16[64,3584]{1,0:T(8,128)(2,1)S(1)}, u32[]{:S(2)}, u32[]{:S(2)}) collective-permute-start(bf16[64,3584]{1,0:T(8,128)(2,1)S(1)} %add_convert_fusion.3), channel_id=1, source_target_pairs={{0,96},{1,33},{2,98},{3,35},{4,100},{5,37},{6,102},{7,39},{8,104},... | collective-permute-start | bytes 1376264 | tf_op jit(solution)/shard_map/ppermute | solution.py:77
  79.2 1.5 %collective-permute-done.16 = bf16[64,3584]{1,0:T(8,128)(2,1)S(1)} collective-permute-done((bf16[64,3584]{1,0:T(8,128)(2,1)S(1)}, bf16[64,3584]{1,0:T(8,128)(2,1)S(1)}, u32[]{:S(2)}, u32[]{:S(2)}) %collective-permute-start.16) | collective-permute-done | bytes 458784 | tf_op jit(solution)/shard_map/ppermute | solution.py:77
  80.7 4.1 %collective-permute-done.14 = bf16[64,3584]{1,0:T(8,128)(2,1)S(1)} collective-permute-done((bf16[64,3584]{1,0:T(8,128)(2,1)S(1)}, bf16[64,3584]{1,0:T(8,128)(2,1)S(1)}, u32[]{:S(2)}, u32[]{:S(2)}) %collective-permute-start.14) | collective-permute-done | bytes 458784 | tf_op jit(solution)/shard_map/ppermute | solution.py:77
  84.8 2.0 %collective-permute-done.12 = bf16[64,3584]{1,0:T(8,128)(2,1)S(1)} collective-permute-done((bf16[64,3584]{1,0:T(8,128)(2,1)S(1)}, bf16[64,3584]{1,0:T(8,128)(2,1)S(1)}, u32[]{:S(2)}, u32[]{:S(2)}) %collective-permute-start.12) | collective-permute-done | bytes 458784 | tf_op jit(solution)/shard_map/ppermute | solution.py:77
  87.2 10.4 %all_to_all.11.parts_ref = bf16[8,8,3584]{2,1,0:T(8,128)(2,1)S(1)} all-to-all(bf16[8,8,3584]{2,1,0:T(8,128)(2,1)S(1)} %fusion), channel_id=1, replica_groups={{0,2,8,10,32,34,40,42},{1,7,25,31,97,103,121,127},{3,5,27,29,99,101,123..., dimensions={0} | all-to-all | bytes 917504 | tf_op jit(solution)/shard_map/all_to_all | solution.py:73
  (32 shorter events, 5.6 us)
Async XLA Ops:
  0.0 40.4 %slice-start = ((s8[7340032]{0:T(1024)(128)(4,1)}), s8[3145728]{0:T(1024)(128)(4,1)S(1)}, s32[]{:S(2)}) async-start(s8[7340032]{0:T(1024)(128)(4,1)} %bitcast.16), calls=%async_computation.2 | async-start | bytes 6291456
  14.2 26.2 %slice-start.1 = ((s8[7340032]{0:T(1024)(128)(4,1)}), s8[4194304]{0:T(1024)(128)(4,1)S(1)}, s32[]{:S(2)}) async-start(s8[7340032]{0:T(1024)(128)(4,1)} %bitcast.16), calls=%async_computation.3 | async-start | bytes 8388608
  14.2 9.9 %collective-permute-start.1 = (bf16[64,3712]{1,0:T(8,128)(2,1)S(1)}, bf16[64,3712]{1,0:T(8,128)(2,1)S(1)}, u32[]{:S(2)}, u32[]{:S(2)}) collective-permute-start(bf16[64,3712]{1,0:T(8,128)(2,1)S(1)} %bitcast.6), channel_id=1, source_target_pairs={{0,24},{1,9},{2,26},{3,11},{4,28},{5,13},{6,30},{7,15},{8,16},{9,1... | collective-permute-start | bytes 1425416 | tf_op jit(solution)/shard_map/ppermute | solution.py:77
  15.8 11.0 %collective-permute-start.2 = (bf16[64,3712]{1,0:T(8,128)(2,1)S(1)}, bf16[64,3712]{1,0:T(8,128)(2,1)S(1)}, u32[]{:S(2)}, u32[]{:S(2)}) collective-permute-start(bf16[64,3712]{1,0:T(8,128)(2,1)S(1)} %bitcast.7), channel_id=1, source_target_pairs={{0,6},{1,3},{2,4},{3,1},{4,2},{5,7},{6,0},{7,5},{8,14},{9,11},{10,... | collective-permute-start | bytes 1425416 | tf_op jit(solution)/shard_map/ppermute | solution.py:77
  18.1 10.6 %collective-permute-start = (bf16[64,3712]{1,0:T(8,128)(2,1)S(1)}, bf16[64,3712]{1,0:T(8,128)(2,1)S(1)}, u32[]{:S(2)}, u32[]{:S(2)}) collective-permute-start(bf16[64,3712]{1,0:T(8,128)(2,1)S(1)} %bitcast.8), channel_id=1, source_target_pairs={{0,96},{1,33},{2,98},{3,35},{4,100},{5,37},{6,102},{7,39},{8,104},... | collective-permute-start | bytes 1425416 | tf_op jit(solution)/shard_map/ppermute | solution.py:77
  24.1 20.5 %collective-permute-start.3 = (bf16[64,3712]{1,0:T(8,128)(2,1)S(1)}, bf16[64,3712]{1,0:T(8,128)(2,1)S(1)}, u32[]{:S(2)}, u32[]{:S(2)}) collective-permute-start(bf16[64,3712]{1,0:T(8,128)(2,1)S(1)} %collective-permute-done.1.refs_1_), channel_id=1, source_target_pairs={{0,96},{1,33},{2,98},{3,35},{4,100},{5,37},{6,102},{7,39},{8,104},... | collective-permute-start | bytes 1425416 | tf_op jit(solution)/shard_map/ppermute | solution.py:77
  26.8 17.8 %collective-permute-start.4 = (bf16[64,3712]{1,0:T(8,128)(2,1)S(1)}, bf16[64,3712]{1,0:T(8,128)(2,1)S(1)}, u32[]{:S(2)}, u32[]{:S(2)}) collective-permute-start(bf16[64,3712]{1,0:T(8,128)(2,1)S(1)} %collective-permute-done.2.refs_2_), channel_id=1, source_target_pairs={{0,24},{1,9},{2,26},{3,11},{4,28},{5,13},{6,30},{7,15},{8,16},{9,1... | collective-permute-start | bytes 1425416 | tf_op jit(solution)/shard_map/ppermute | solution.py:77
  28.6 16.0 %collective-permute-start.5 = (bf16[64,3712]{1,0:T(8,128)(2,1)S(1)}, bf16[64,3712]{1,0:T(8,128)(2,1)S(1)}, u32[]{:S(2)}, u32[]{:S(2)}) collective-permute-start(bf16[64,3712]{1,0:T(8,128)(2,1)S(1)} %collective-permute-done.refs_0_), channel_id=1, source_target_pairs={{0,6},{1,3},{2,4},{3,1},{4,2},{5,7},{6,0},{7,5},{8,14},{9,11},{10,... | collective-permute-start | bytes 1425416 | tf_op jit(solution)/shard_map/ppermute | solution.py:77
  30.6 14.0 %collective-permute-start.6 = (bf16[64,3712]{1,0:T(8,128)(2,1)S(1)}, bf16[64,3712]{1,0:T(8,128)(2,1)S(1)}, u32[]{:S(2)}, u32[]{:S(2)}) collective-permute-start(bf16[64,3712]{1,0:T(8,128)(2,1)S(1)} %collective-permute-done.2.refs_2_), channel_id=1, source_target_pairs={{0,120},{1,41},{2,122},{3,43},{4,124},{5,45},{6,126},{7,47},{8,112... | collective-permute-start | bytes 1425416 | tf_op jit(solution)/shard_map/ppermute | solution.py:77
  37.8 5.5 %slice-start.2 = ((s8[7340032]{0:T(1024)(128)(4,1)}), s8[4194304]{0:T(1024)(128)(4,1)S(1)}, s32[]{:S(2)}) async-start(s8[7340032]{0:T(1024)(128)(4,1)} %bitcast.18), calls=%async_computation.4 | async-start | bytes 8388608
  40.4 3.0 %slice-start.3 = ((s8[7340032]{0:T(1024)(128)(4,1)}), s8[3145728]{0:T(1024)(128)(4,1)S(1)}, s32[]{:S(2)}) async-start(s8[7340032]{0:T(1024)(128)(4,1)} %bitcast.18), calls=%async_computation.5 | async-start | bytes 6291456
  44.6 2.6 %collective-permute-start.7 = (bf16[64,7168]{1,0:T(8,128)(2,1)S(1)}, bf16[64,7168]{1,0:T(8,128)(2,1)S(1)}, u32[]{:S(2)}, u32[]{:S(2)}) collective-permute-start(bf16[64,7168]{1,0:T(8,128)(2,1)S(1)} %get-tuple-element.38), channel_id=1, source_target_pairs={{0,1},{1,0},{2,3},{3,2},{4,5},{5,4},{6,7},{7,6},{8,9},{9,8},{10,11... | collective-permute-start | bytes 2752520 | tf_op jit(solution)/shard_map/ppermute | solution.py:85
  45.7 2.8 %collective-permute-start.9 = (bf16[64,3712]{1,0:T(8,128)(2,1)S(1)}, bf16[64,3712]{1,0:T(8,128)(2,1)S(1)}, u32[]{:S(2)}, u32[]{:S(2)}) collective-permute-start(bf16[64,3712]{1,0:T(8,128)(2,1)S(1)} %get-tuple-element.47), channel_id=1, source_target_pairs={{0,1},{1,0},{2,3},{3,2},{4,5},{5,4},{6,7},{7,6},{8,9},{9,8},{10,11... | collective-permute-start | bytes 1425416 | tf_op jit(solution)/shard_map/ppermute | solution.py:85
  46.2 2.3 %collective-permute-start.8 = (bf16[64,3584]{1,0:T(8,128)(2,1)S(1)}, bf16[64,3584]{1,0:T(8,128)(2,1)S(1)}, u32[]{:S(2)}, u32[]{:S(2)}) collective-permute-start(bf16[64,3584]{1,0:T(8,128)(2,1)S(1)} %get-tuple-element.46), channel_id=1, source_target_pairs={{0,1},{1,0},{2,3},{3,2},{4,5},{5,4},{6,7},{7,6},{8,9},{9,8},{10,11... | collective-permute-start | bytes 1376264 | tf_op jit(solution)/shard_map/ppermute | solution.py:85
  51.7 2.6 %collective-permute-start.10 = (bf16[64,7168]{1,0:T(8,128)(2,1)S(1)}, bf16[64,7168]{1,0:T(8,128)(2,1)S(1)}, u32[]{:S(2)}, u32[]{:S(2)}) collective-permute-start(bf16[64,7168]{1,0:T(8,128)(2,1)S(1)} %get-tuple-element.50), channel_id=1, source_target_pairs={{0,1},{1,0},{2,3},{3,2},{4,5},{5,4},{6,7},{7,6},{8,9},{9,8},{10,11... | collective-permute-start | bytes 2752520 | tf_op jit(solution)/shard_map/ppermute | solution.py:85
  55.4 9.9 %collective-permute-start.15 = (bf16[64,3584]{1,0:T(8,128)(2,1)S(1)}, bf16[64,3584]{1,0:T(8,128)(2,1)S(1)}, u32[]{:S(2)}, u32[]{:S(2)}) collective-permute-start(bf16[64,3584]{1,0:T(8,128)(2,1)S(1)} %get-tuple-element.55), channel_id=1, source_target_pairs={{0,24},{1,9},{2,26},{3,11},{4,28},{5,13},{6,30},{7,15},{8,16},{9,1... | collective-permute-start | bytes 1376264 | tf_op jit(solution)/shard_map/ppermute | solution.py:77
  56.8 22.4 %collective-permute-start.17 = (bf16[64,3584]{1,0:T(8,128)(2,1)S(1)}, bf16[64,3584]{1,0:T(8,128)(2,1)S(1)}, u32[]{:S(2)}, u32[]{:S(2)}) collective-permute-start(bf16[64,3584]{1,0:T(8,128)(2,1)S(1)} %get-tuple-element.56), channel_id=1, source_target_pairs={{0,126},{1,43},{2,124},{3,41},{4,122},{5,47},{6,120},{7,45},{8,118... | collective-permute-start | bytes 1376264 | tf_op jit(solution)/shard_map/ppermute | solution.py:77
  60.4 14.6 %collective-permute-start.13 = (bf16[64,3584]{1,0:T(8,128)(2,1)S(1)}, bf16[64,3584]{1,0:T(8,128)(2,1)S(1)}, u32[]{:S(2)}, u32[]{:S(2)}) collective-permute-start(bf16[64,3584]{1,0:T(8,128)(2,1)S(1)} %get-tuple-element.53), channel_id=1, source_target_pairs={{0,96},{1,33},{2,98},{3,35},{4,100},{5,37},{6,102},{7,39},{8,104},... | collective-permute-start | bytes 1376264 | tf_op jit(solution)/shard_map/ppermute | solution.py:77
  62.2 14.8 %collective-permute-start.11 = (bf16[64,3584]{1,0:T(8,128)(2,1)S(1)}, bf16[64,3584]{1,0:T(8,128)(2,1)S(1)}, u32[]{:S(2)}, u32[]{:S(2)}) collective-permute-start(bf16[64,3584]{1,0:T(8,128)(2,1)S(1)} %get-tuple-element.51), channel_id=1, source_target_pairs={{0,6},{1,3},{2,4},{3,1},{4,2},{5,7},{6,0},{7,5},{8,14},{9,11},{10,... | collective-permute-start | bytes 1376264 | tf_op jit(solution)/shard_map/ppermute | solution.py:77
  65.4 15.3 %collective-permute-start.16 = (bf16[64,3584]{1,0:T(8,128)(2,1)S(1)}, bf16[64,3584]{1,0:T(8,128)(2,1)S(1)}, u32[]{:S(2)}, u32[]{:S(2)}) collective-permute-start(bf16[64,3584]{1,0:T(8,128)(2,1)S(1)} %add_convert_fusion.1), channel_id=1, source_target_pairs={{0,6},{1,3},{2,4},{3,1},{4,2},{5,7},{6,0},{7,5},{8,14},{9,11},{10,... | collective-permute-start | bytes 1376264 | tf_op jit(solution)/shard_map/ppermute | solution.py:77
  75.1 9.8 %collective-permute-start.14 = (bf16[64,3584]{1,0:T(8,128)(2,1)S(1)}, bf16[64,3584]{1,0:T(8,128)(2,1)S(1)}, u32[]{:S(2)}, u32[]{:S(2)}) collective-permute-start(bf16[64,3584]{1,0:T(8,128)(2,1)S(1)} %add_convert_fusion.2), channel_id=1, source_target_pairs={{0,24},{1,9},{2,26},{3,11},{4,28},{5,13},{6,30},{7,15},{8,16},{9,1... | collective-permute-start | bytes 1376264 | tf_op jit(solution)/shard_map/ppermute | solution.py:77
  77.1 9.8 %collective-permute-start.12 = (bf16[64,3584]{1,0:T(8,128)(2,1)S(1)}, bf16[64,3584]{1,0:T(8,128)(2,1)S(1)}, u32[]{:S(2)}, u32[]{:S(2)}) collective-permute-start(bf16[64,3584]{1,0:T(8,128)(2,1)S(1)} %add_convert_fusion.3), channel_id=1, source_target_pairs={{0,96},{1,33},{2,98},{3,35},{4,100},{5,37},{6,102},{7,39},{8,104},... | collective-permute-start | bytes 1376264 | tf_op jit(solution)/shard_map/ppermute | solution.py:77

commit v7 on v6

--- a/solution.py
+++ b/solution.py
@@ -77,8 +77,8 @@
     return lax.ppermute(values, AXES, FAR[axis])
 
 
-def both_cores(values):
-    return lax.all_gather(values, "dev", axis_index_groups=[[i, i + 1] for i in range(0, 32, 2)])
+def swap_cores(values):
+    return lax.all_to_all(values, "dev", 0, 0, axis_index_groups=[[i, i + 1] for i in range(0, 32, 2)], tiled=True)
 
 
 def to_sibling(values):
@@ -138,9 +138,13 @@
     blocks = [refs.pop(0) for _ in range(4)]
     sources = [refs.pop(0) for _ in range(loads)]
     del refs[0]
-    mine_ref, sent_refs, targets = refs[0], refs[1:3], refs[3 : 3 + loads]
-    pick, sem = refs[3 + loads :]
-    copies = [pltpu.make_async_copy(a.at[:, :MIDDLE, :], b, sem) for a, b in zip(sources, targets)]
+    pick, sem = refs[-2:]
+    if loads:
+        core = expert_ref[0] % 2
+        mine_ref, left_ref, right_ref = refs[0].at[core], refs[0].at[1 - core, :, :HALF], refs[0].at[1 - core, :, HALF:]
+    else:
+        mine_ref, left_ref, right_ref = refs[:3]
+    copies = [pltpu.make_async_copy(a.at[:, :MIDDLE, :], b, sem) for a, b in zip(sources, refs[1 : 1 + loads])]
     for copy in copies:
         copy.start()
     own = expert_ref[0]
@@ -167,24 +171,26 @@
         x = jnp.concatenate([ref[:, n : n + 512] for ref in blocks], axis=0)
         value = jnp.dot(pick[...], x, preferred_element_type=F32).astype(BF16)
         mine_ref[:, n : n + 512] = value[:SEL]
-        sent_refs[0][:, n : n + 512] = value[SEL : 2 * SEL]
+        left_ref[:, n : n + 512] = value[SEL : 2 * SEL]
         mine_ref[:, HALF + n : HALF + n + 512] = value[2 * SEL : 3 * SEL]
-        sent_refs[1][:, n : n + 512] = value[3 * SEL :]
+        right_ref[:, n : n + 512] = value[3 * SEL :]
     value = jnp.dot(pick[: 2 * SEL, :], ext, preferred_element_type=F32).astype(BF16)
     mine_ref[:, D:] = value[:SEL]
-    sent_refs[1][:, HALF:] = value[SEL:]
+    right_ref[:, HALF:] = value[SEL:]
     for copy in copies:
         copy.wait()
 
 
 def select(expert, blocks, after, loads=()):
+    if loads:
+        shapes = [(2, SEL, D + EXT)] + [(1, MIDDLE, 512) for _ in loads]
+    else:
+        shapes = [(SEL, D + EXT), (SEL, HALF), (SEL, HALF + EXT)]
     return pl.pallas_call(
         functools.partial(select_kernel, len(loads)),
-        out_shape=[jax.ShapeDtypeStruct((SEL, D + EXT), BF16)]
-        + [jax.ShapeDtypeStruct((SEL, high - low + EXT * (high == D)), BF16) for low, high in CUTS]
-        + [jax.ShapeDtypeStruct((1, MIDDLE, 512), BF16) for _ in loads],
+        out_shape=[jax.ShapeDtypeStruct(shape, BF16) for shape in shapes],
         in_specs=[SMEM] + [VMEM] * 4 + [HBM] * len(loads) + [ANY],
-        out_specs=[VMEM] * (3 + len(loads)),
+        out_specs=[VMEM] * len(shapes),
         scratch_shapes=[pltpu.VMEM((PART, PART), BF16), pltpu.SemaphoreType.DMA],
         compiler_params=SMALL,
         cost_estimate=BRIEF,
@@ -192,21 +198,24 @@
     )(expert, *blocks, *[in_hbm(load) for load in loads], after)
 
 
-def hidden_kernel(streams, expert_ref, mine_ref, a_ref, b_ref, gate_ref, first_ref, rest_ref, after_ref, *refs):
-    del after_ref
+def hidden_kernel(streams, expert_ref, *refs):
+    refs = list(refs)
+    row_refs = [refs.pop(0) for _ in range(1 if streams else 3)]
+    gate_ref, first_ref, rest_ref = refs[:3]
     if streams:
-        hidden, second_ref, gate_sum, up_sum, sem = refs
+        hidden, second_ref, gate_sum, up_sum, sem = refs[4:]
         copy = pltpu.make_async_copy(rest_ref.at[:, MIDDLE:, :], second_ref, sem)
         copy.start()
     else:
-        hidden, gate_sum, up_sum = refs
+        hidden, gate_sum, up_sum = refs[4:]
         second_ref = rest_ref
+    core = expert_ref[0] % 2
 
     def rows(piece, low, high):
+        if streams:
+            return jnp.concatenate([row_refs[0][core, :, low:high], row_refs[0][1 - core, :, low:high]], axis=0)
         start = CUTS[piece][0]
-        theirs_ref, block = (a_ref, b_ref)[piece], slice(low - start, high - start)
-        theirs = theirs_ref[1 - expert_ref[0] % 2, :, block] if streams else theirs_ref[:, block]
-        return jnp.concatenate([mine_ref[:, low:high], theirs], axis=0)
+        return jnp.concatenate([row_refs[0][:, low:high], row_refs[1 + piece][:, low - start : high - start]], axis=0)
 
     for piece, (low, high) in enumerate(CUTS):
         gate = jnp.dot(rows(piece, low, high), gate_ref[0, low:high, :], preferred_element_type=F32)
@@ -223,18 +232,18 @@
     hidden[...] = (v / (1.0 + jnp.exp(-v)) * up_sum[...] * scale).astype(BF16)
 
 
-def hidden_units(expert, mine, theirs, gate, first, rest, after, streams):
+def hidden_units(expert, rows, gate, first, rest, after, streams):
     second = jax.ShapeDtypeStruct((1, D - MIDDLE, 512), BF16)
     return pl.pallas_call(
         functools.partial(hidden_kernel, streams),
         out_shape=[jax.ShapeDtypeStruct((2 * SEL, 512), BF16)] + [second] * streams,
-        in_specs=[SMEM] + [VMEM] * 5 + [HBM if streams else VMEM, ANY],
+        in_specs=[SMEM] + [VMEM] * (len(rows) + 2) + [HBM if streams else VMEM, ANY],
         out_specs=[VMEM] * (1 + streams),
         scratch_shapes=[pltpu.VMEM((2 * SEL, 512), F32)] * 2 + [pltpu.SemaphoreType.DMA] * streams,
         compiler_params=SMALL,
         cost_estimate=BRIEF,
         name="hidden",
-    )(expert, mine, *theirs, gate, first, in_hbm(rest) if streams else rest, after)
+    )(expert, *rows, gate, first, in_hbm(rest) if streams else rest, after)
 
 
 def down_kernel(hidden_ref, down_ref, after_ref, mine_ref, theirs_ref):
@@ -258,44 +267,47 @@
     )(hidden, down, after)
 
 
-def spread_kernel(expert_ref, *refs):
-    refs = list(refs)
-    exts = [refs.pop(0) for _ in range(4)]
-    mine_ref, theirs_ref = refs[:2]
-    outs = [refs[3 + i] for i in range(4)]
-    place_scr = refs[7]
+def spread_kernel(first, expert_ref, *refs):
+    count = (len(refs) - 4) // 2
+    exts, outs = refs[:count], refs[count + 3 : -1]
+    mine_ref, theirs_ref = refs[count : count + 2]
+    place_scr = refs[-1]
+    part, sel = count * BLOCK, count * BLOCK // 4
     own = expert_ref[0]
     turn = lax.broadcasted_iota(jnp.int32, (EXT, EXT), 1)
     experts = jnp.where(turn == 0, own, own ^ 1)
     wanted = jnp.where(expert_lanes(experts, (EXT, EXT), 0) & (turn < 2), 1.0, 0.0).astype(BF16)
     ext = jnp.concatenate([ref[:, HALF:] for ref in exts], axis=0)
     chosen = jnp.dot(ext, wanted, preferred_element_type=F32) > 0
-    first = lax.broadcasted_iota(jnp.int32, (PART, PART), 0)
-    second = lax.broadcasted_iota(jnp.int32, (PART, PART), 1)
-    earlier = jnp.where((first // 4 == second // 4) & (second < first), 1.0, 0.0).astype(BF16)
+    row = lax.broadcasted_iota(jnp.int32, (part, part), 0)
+    other = lax.broadcasted_iota(jnp.int32, (part, part), 1)
+    earlier = jnp.where((row // 4 == other // 4) & (other < row), 1.0, 0.0).astype(BF16)
     rank = jnp.dot(earlier, jnp.where(chosen, 1.0, 0.0).astype(BF16), preferred_element_type=F32)
-    token = lax.broadcasted_iota(jnp.int32, (PART, EXT), 0)
+    token = lax.broadcasted_iota(jnp.int32, (part, EXT), 0)
     place = jnp.where(chosen, token // 8 * 2 + rank.astype(jnp.int32), -1)
-    column = lax.broadcasted_iota(jnp.int32, (PART, 2 * SEL), 1)
-    hit = jnp.where(column < SEL, place[:, 0:1], place[:, 1:2]) == column % SEL
-    is_left = lax.broadcasted_iota(jnp.int32, (PART, 2 * SEL), 0) % 8 < 4
-    place_scr[:, : 2 * SEL] = jnp.where(hit & is_left, 1.0, 0.0).astype(BF16)
-    place_scr[:, 2 * SEL :] = jnp.where(hit & ~is_left, 1.0, 0.0).astype(BF16)
+    column = lax.broadcasted_iota(jnp.int32, (part, 4 * sel), 1)
+    hit = jnp.where(column // sel % 2 == 0, place[:, 0:1], place[:, 1:2]) == column % sel
+    is_left = lax.broadcasted_iota(jnp.int32, (part, 4 * sel), 0) % 8 < 4
+    place_scr[...] = jnp.where(hit & (is_left == (column < 2 * sel)), 1.0, 0.0).astype(BF16)
+    rows = slice(first * BLOCK // 4, first * BLOCK // 4 + sel)
     for n in range(0, HALF, 512):
         left, right = slice(n, n + 512), slice(HALF + n, HALF + n + 512)
-        y = jnp.concatenate([mine_ref[:, left], theirs_ref[:, left], mine_ref[:, right], theirs_ref[:, right]], axis=0)
+        y = jnp.concatenate(
+            [mine_ref[rows, left], theirs_ref[rows, left], mine_ref[rows, right], theirs_ref[rows, right]], axis=0
+        )
         value = jnp.dot(place_scr[...], y, preferred_element_type=F32).astype(BF16)
-        for i in range(4):
+        for i in range(count):
             outs[i][:, left] = value[i * BLOCK : (i + 1) * BLOCK]
 
 
-def spread(expert, blocks, mine, theirs, after):
-    return pl.pallas_call(
-        spread_kernel,
-        out_shape=[jax.ShapeDtypeStruct((BLOCK, HALF), BF16)] * 4,
-        in_specs=[SMEM] + [VMEM] * 6 + [ANY],
-        out_specs=[VMEM] * 4,
-        scratch_shapes=[pltpu.VMEM((PART, 4 * SEL), BF16)],
+def spread(expert, blocks, mine, theirs, after, first=0):
+    count = len(blocks)
+    return pl.pallas_call(
+        functools.partial(spread_kernel, first),
+        out_shape=[jax.ShapeDtypeStruct((BLOCK, HALF), BF16)] * count,
+        in_specs=[SMEM] + [VMEM] * (count + 2) + [ANY],
+        out_specs=[VMEM] * count,
+        scratch_shapes=[pltpu.VMEM((count * BLOCK, count * BLOCK), BF16)],
         compiler_params=SMALL,
         cost_estimate=BRIEF,
         name="spread",
@@ -335,28 +347,27 @@
     xy, yz, zx = swap_far(y, 0), swap_far(z, 1), swap_far(x, 2)
     xyz = swap_far(z, 4)
     near = (x, y, z, own)
-    mine_near, *sent, up_first = select(expert, near, own, (up,))
-    got_near = [both_cores(piece) for piece in sent]
-    hidden_near, up_second = hidden_units(expert, mine_near, got_near, gate, up_first, up, own, 1)
+    pair, up_first = select(expert, near, own, (up,))
+    hidden_near, up_second = hidden_units(expert, [swap_cores(pair)], gate, up_first, up, own, 1)
     result_near, theirs = down_rows(hidden_near, down, own)
     xy, yz, zx, xyz, theirs = lax.optimization_barrier((xy, yz, zx, xyz, theirs))
     far = (xy, zx, yz, xyz)
     returned_near = to_sibling(theirs)
     mine_far, *sent = select(expert, far, result_near)
-    got_far = [to_sibling(piece) for piece in sent]
+    rows = [mine_far] + [to_sibling(piece) for piece in sent]
     y_x, y_y, y_z, y_own = spread(expert, near, result_near, returned_near, mine_far)
-    (hidden_far,) = hidden_units(expert, mine_far, got_far, gate, up_first, up_second, y_own, 0)
+    (hidden_far,) = hidden_units(expert, rows, gate, up_first, up_second, y_own, 0)
     result, theirs = down_rows(hidden_far, down, own)
     returned = to_sibling(theirs)
     y_xy, y_zx, y_yz, y_xyz = spread(expert, far, result, returned, own)
+    at_own = swap_far(y_xyz, 3)
     at_y, at_z, at_x = swap_far(y_xy, 0), swap_far(y_yz, 1), swap_far(y_zx, 2)
-    at_own = swap_far(y_xyz, 3)
     total = add(
+        at_own,
         y_own,
         swap_far(add(y_x, at_x), 0),
         swap_far(add(y_y, at_y), 1),
         swap_far(add(y_z, at_z), 2),
-        at_own,
     )
     return finish(swap_near(total.reshape(8, 8, HALF)))
 

time: 98.5 us -> 95.5 us (0.970)
  the two profiles are of different devices: /device:TPU:0 before, /device:TPU:1 now
where the time goes in v7:
time: 95.5 us; the launch traced here: 94.9 us
  blocking collectives  43.2 us (45%)
  waiting for transfers between devices  26.2 us (27%)
  Pallas kernels  13.8 us (14%)
  starting transfers between devices  10.8 us (11%)
    all_to_all x2, blocking collectives, swap_near(): lax.all_to_all(values, AXES, 0, 0, axis_index_groups=NEAR, tiled=True)  35.8 us
    ppermute x14, waiting for transfers between devices, swap_far(): return lax.ppermute(values, AXES, FAR[axis])  23.1 us
    ppermute x14, starting transfers between devices, swap_far(): return lax.ppermute(values, AXES, FAR[axis])  9.3 us
    all_to_all x1, blocking collectives, swap_cores(): lax.all_to_all(values, 'dev', 0, 0, axis_index_groups=[[i, i + 1] for i i...  7.36 us
    pallas_call x2, Pallas kernels, hidden_units(): pl.pallas_call(functools.partial(hidden_kernel, streams), out_shape=[jax....  4.92 us
    ppermute x4, waiting for transfers between devices, to_sibling(): return lax.ppermute(values, 'dev', [(i, i ^ 1) for i in range(32)])  3.08 us
    pallas_call x2, Pallas kernels, select(): pl.pallas_call(functools.partial(select_kernel, len(loads)), out_shape=[j...  2.96 us
    pallas_call x2, Pallas kernels, down_rows(): pl.pallas_call(down_kernel, out_shape=[jax.ShapeDtypeStruct((SEL, D), BF1...  2.26 us
  transfers between devices with their start and end apart: 18, of which 9 were waited for; matrix products, arithmetic and copies ran while one was open for 0% of the time, Pallas kernels for 8%

profile of v7, /device:TPU:1, one launch (start us, length us, event | category | flops | bytes accessed | tf_op | source)
XLA Modules:
  0.0 94.9 jit_solution(14116723835741782806)
XLA Ops:
  0.0 0.9 pack.1
  1.0 21.2 %all_to_all.15 = bf16[8,8,3712]{2,1,0:T(8,128)(2,1)S(1)} all-to-all(bf16[8,8,3712]{2,1,0:T(8,128)(2,1)S(1)} %pack.1), channel_id=1, replica_groups={{0,2,8,10,32,34,40,42},{1,7,25,31,97,103,121,127},{3,5,27,29,99,101,123..., dimensions={0} | all-to-all | bytes 950272 | tf_op jit(solution)/shard_map/all_to_all | solution.py:73
  22.2 7.4 %collective-permute-done.refs_1_ = bf16[64,3712]{1,0:T(8,128)(2,1)S(1)} collective-permute-done((bf16[64,3712]{1,0:T(8,128)(2,1)S(1)}, bf16[64,3712]{1,0:T(8,128)(2,1)S(1)}, u32[]{:S(2)}, u32[]{:S(2)}) %collective-permute-start) | collective-permute-done | bytes 475168 | tf_op jit(solution)/shard_map/ppermute | solution.py:77
  29.6 1.8 %collective-permute-start.3 = (bf16[64,3712]{1,0:T(8,128)(2,1)S(1)}, bf16[64,3712]{1,0:T(8,128)(2,1)S(1)}, u32[]{:S(2)}, u32[]{:S(2)}) collective-permute-start(bf16[64,3712]{1,0:T(8,128)(2,1)S(1)} %collective-permute-done.2.refs_2_), channel_id=1, source_target_pairs={{0,24},{1,9},{2,26},{3,11},{4,28},{5,13},{6,30},{7,15},{8,16},{9,1... | collective-permute-start | bytes 1425416 | tf_op jit(solution)/shard_map/ppermute | solution.py:77
  31.4 1.2 %collective-permute-start.6 = (bf16[64,3712]{1,0:T(8,128)(2,1)S(1)}, bf16[64,3712]{1,0:T(8,128)(2,1)S(1)}, u32[]{:S(2)}, u32[]{:S(2)}) collective-permute-start(bf16[64,3712]{1,0:T(8,128)(2,1)S(1)} %collective-permute-done.2.refs_2_), channel_id=1, source_target_pairs={{0,120},{1,41},{2,122},{3,43},{4,124},{5,45},{6,126},{7,47},{8,112... | collective-permute-start | bytes 1425416 | tf_op jit(solution)/shard_map/ppermute | solution.py:77
  32.6 2.1 %select.2 = (bf16[2,64,7296]{2,1,0:T(8,128)(2,1)S(1)}, bf16[1,3584,512]{2,1,0:T(8,128)(2,1)S(1)}) custom-call(s32[1]{0:T(128)} %bitcast.expert_ref, bf16[64,3712]{1,0:T(8,128)(2,1)S(1)} %collective-permute-done.4.refs_0_, bf16[64,3712]{1,0:T(8,128)(2,1)S(1)} %collective-permute-done.refs_1_, bf16[64,3712]{1,0:T(8,128)(2,1)S(1)} %collective-permute-done.2.refs_2_, ...), custom_call_target="tpu_custom_call" | custom-call | flops 1000 | bytes 1000 | tf_op jit(solution)/shard_map/select/pallas_call | solution.py:189
  34.7 7.4 %all_to_all.16.refs_0_ = bf16[2,64,7296]{2,1,0:T(8,128)(2,1)S(1)} all-to-all(bf16[2,64,7296]{2,1,0:T(8,128)(2,1)S(1)} %get-tuple-element.29), channel_id=1, replica_groups={{0,1},{2,3},{4,5},{6,7},{8,9},{10,11},{12,13},{14,15},{16,17},{18,19},{..., dimensions={0} | all-to-all | bytes 3735552 | tf_op jit(solution)/shard_map/all_to_all | solution.py:81
  42.0 2.9 %hidden.2 = (bf16[128,512]{1,0:T(8,128)(2,1)S(1)}, bf16[1,3584,512]{2,1,0:T(8,128)(2,1)S(1)}) custom-call(s32[1]{0:T(128)} %bitcast.expert_ref, bf16[2,64,7296]{2,1,0:T(8,128)(2,1)S(1)} %all_to_all.16.refs_0_, bf16[1,7168,512]{2,1,0:T(8,128)(2,1)S(1)} %bitcast.15, bf16[1,3584,512]{2,1,0:T(8,128)(2,1)S(1)} %get-tuple-element.30.refs_2_.refs_4_, ...), custom_call_target="tpu_custom_call" | custom-call | flops 1000 | bytes 1000 | tf_op jit(solution)/shard_map/hidden/pallas_call | solution.py:237
  45.0 1.1 %down.2 = (bf16[64,7168]{1,0:T(8,128)(2,1)S(1)}, bf16[64,7168]{1,0:T(8,128)(2,1)S(1)}) custom-call(bf16[128,512]{1,0:T(8,128)(2,1)S(1)} %get-tuple-element.31.hidden_ref, bf16[1,512,7168]{2,1,0:T(8,128)(2,1)S(1)} %bitcast.17, bf16[64,3712]{1,0:T(8,128)(2,1)S(1)} %bitcast.10), custom_call_target="tpu_custom_call" | custom-call | flops 1000 | bytes 1000 | tf_op jit(solution)/shard_map/down/pallas_call | solution.py:259
  46.2 0.5 collective-permute-start.9
  46.7 0.9 select.3
  47.8 0.4 collective-permute-start.7
  48.2 0.6 collective-permute-done.9.refs_5_
  48.8 1.0 %spread.2 = (bf16[64,3584]{1,0:T(8,128)(2,1)S(1)}, bf16[64,3584]{1,0:T(8,128)(2,1)S(1)}, bf16[64,3584]{1,0:T(8,128)(2,1)S(1)}, bf16[64,3584]{1,0:T(8,128)(2,1)S(1)}) custom-call(s32[1]{0:T(128)} %bitcast.expert_ref, bf16[64,3712]{1,0:T(8,128)(2,1)S(1)} %collective-permute-done.4.refs_0_, bf16[64,3712]{1,0:T(8,128)(2,1)S(1)} %collective-permute-done.refs_1_, ...), custom_call_target="tpu_custom_call" | custom-call | flops 1000 | bytes 1000 | tf_op jit(solution)/shard_map/spread/pallas_call | solution.py:305
  49.8 0.3 collective-permute-done.7.refs_1_
  50.2 2.1 %hidden.3.hidden_ref = bf16[128,512]{1,0:T(8,128)(2,1)S(1)} custom-call(s32[1]{0:T(128)} %bitcast.expert_ref, bf16[64,7296]{1,0:T(8,128)(2,1)S(1)} %get-tuple-element.38.refs_6_.refs_0_, bf16[64,3584]{1,0:T(8,128)(2,1)S(1)} %collective-permute-done.7.refs_1_, bf16[64,3712]{1,0:T(8,128)(2,1)S(1)} %collective-permute-done.8.refs_2_, ...), custom_call_target="tpu_custom_call" | custom-call | flops 1000 | bytes 1000 | tf_op jit(solution)/shard_map/hidden/pallas_call | solution.py:237
  52.2 1.1 %down.3 = (bf16[64,7168]{1,0:T(8,128)(2,1)S(1)}, bf16[64,7168]{1,0:T(8,128)(2,1)S(1)}) custom-call(bf16[128,512]{1,0:T(8,128)(2,1)S(1)} %hidden.3.hidden_ref, bf16[1,512,7168]{2,1,0:T(8,128)(2,1)S(1)} %bitcast.17, bf16[64,3712]{1,0:T(8,128)(2,1)S(1)} %bitcast.12), custom_call_target="tpu_custom_call" | custom-call | flops 1000 | bytes 1000 | tf_op jit(solution)/shard_map/down/pallas_call | solution.py:259
  53.4 0.4 collective-permute-start.10
  53.8 2.1 %collective-permute-done.10.refs_5_ = bf16[64,7168]{1,0:T(8,128)(2,1)S(1)} collective-permute-done((bf16[64,7168]{1,0:T(8,128)(2,1)S(1)}, bf16[64,7168]{1,0:T(8,128)(2,1)S(1)}, u32[]{:S(2)}, u32[]{:S(2)}) %collective-permute-start.10) | collective-permute-done | bytes 917536 | tf_op jit(solution)/shard_map/ppermute | solution.py:85
  55.9 1.0 %spread.3 = (bf16[64,3584]{1,0:T(8,128)(2,1)S(1)}, bf16[64,3584]{1,0:T(8,128)(2,1)S(1)}, bf16[64,3584]{1,0:T(8,128)(2,1)S(1)}, bf16[64,3584]{1,0:T(8,128)(2,1)S(1)}) custom-call(s32[1]{0:T(128)} %bitcast.expert_ref, bf16[64,3712]{1,0:T(8,128)(2,1)S(1)} %collective-permute-done.1.refs_0_, bf16[64,3712]{1,0:T(8,128)(2,1)S(1)} %collective-permute-done.5.refs_1_, ...), custom_call_target="tpu_custom_call" | custom-call | flops 1000 | bytes 1000 | tf_op jit(solution)/shard_map/spread/pallas_call | solution.py:305
  57.2 0.6 collective-permute-start.14
  57.9 3.1 %collective-permute-start.11 = (bf16[64,3584]{1,0:T(8,128)(2,1)S(1)}, bf16[64,3584]{1,0:T(8,128)(2,1)S(1)}, u32[]{:S(2)}, u32[]{:S(2)}) collective-permute-start(bf16[64,3584]{1,0:T(8,128)(2,1)S(1)} %get-tuple-element.46), channel_id=1, source_target_pairs={{0,126},{1,43},{2,124},{3,41},{4,122},{5,47},{6,120},{7,45},{8,118... | collective-permute-start | bytes 1376264 | tf_op jit(solution)/shard_map/ppermute | solution.py:77
  61.0 3.8 %collective-permute-done.16 = bf16[64,3584]{1,0:T(8,128)(2,1)S(1)} collective-permute-done((bf16[64,3584]{1,0:T(8,128)(2,1)S(1)}, bf16[64,3584]{1,0:T(8,128)(2,1)S(1)}, u32[]{:S(2)}, u32[]{:S(2)}) %collective-permute-start.16) | collective-permute-done | bytes 458784 | tf_op jit(solution)/shard_map/ppermute | solution.py:77
  65.0 4.8 %collective-permute-done.14 = bf16[64,3584]{1,0:T(8,128)(2,1)S(1)} collective-permute-done((bf16[64,3584]{1,0:T(8,128)(2,1)S(1)}, bf16[64,3584]{1,0:T(8,128)(2,1)S(1)}, u32[]{:S(2)}, u32[]{:S(2)}) %collective-permute-start.14) | collective-permute-done | bytes 458784 | tf_op jit(solution)/shard_map/ppermute | solution.py:77
  70.0 1.5 %collective-permute-start.15 = (bf16[64,3584]{1,0:T(8,128)(2,1)S(1)}, bf16[64,3584]{1,0:T(8,128)(2,1)S(1)}, u32[]{:S(2)}, u32[]{:S(2)}) collective-permute-start(bf16[64,3584]{1,0:T(8,128)(2,1)S(1)} %add_convert_fusion.2), channel_id=1, source_target_pairs={{0,24},{1,9},{2,26},{3,11},{4,28},{5,13},{6,30},{7,15},{8,16},{9,1... | collective-permute-start | bytes 1376264 | tf_op jit(solution)/shard_map/ppermute | solution.py:77
  71.5 0.6 collective-permute-start.13
  72.2 3.2 %collective-permute-done.17 = bf16[64,3584]{1,0:T(8,128)(2,1)S(1)} collective-permute-done((bf16[64,3584]{1,0:T(8,128)(2,1)S(1)}, bf16[64,3584]{1,0:T(8,128)(2,1)S(1)}, u32[]{:S(2)}, u32[]{:S(2)}) %collective-permute-start.17) | collective-permute-done | bytes 458784 | tf_op jit(solution)/shard_map/ppermute | solution.py:77
  75.3 2.3 %collective-permute-done.15 = bf16[64,3584]{1,0:T(8,128)(2,1)S(1)} collective-permute-done((bf16[64,3584]{1,0:T(8,128)(2,1)S(1)}, bf16[64,3584]{1,0:T(8,128)(2,1)S(1)}, u32[]{:S(2)}, u32[]{:S(2)}) %collective-permute-start.15) | collective-permute-done | bytes 458784 | tf_op jit(solution)/shard_map/ppermute | solution.py:77
  77.7 1.6 %collective-permute-done.13 = bf16[64,3584]{1,0:T(8,128)(2,1)S(1)} collective-permute-done((bf16[64,3584]{1,0:T(8,128)(2,1)S(1)}, bf16[64,3584]{1,0:T(8,128)(2,1)S(1)}, u32[]{:S(2)}, u32[]{:S(2)}) %collective-permute-start.13) | collective-permute-done | bytes 458784 | tf_op jit(solution)/shard_map/ppermute | solution.py:77
  79.2 0.3 fusion
  79.5 14.7 %all_to_all.17.parts_ref = bf16[8,8,3584]{2,1,0:T(8,128)(2,1)S(1)} all-to-all(bf16[8,8,3584]{2,1,0:T(8,128)(2,1)S(1)} %fusion), channel_id=1, replica_groups={{0,2,8,10,32,34,40,42},{1,7,25,31,97,103,121,127},{3,5,27,29,99,101,123..., dimensions={0} | all-to-all | bytes 917504 | tf_op jit(solution)/shard_map/all_to_all | solution.py:73
  94.2 0.7 finish.1
  (31 shorter events, 1.2 us)
Async XLA Ops:
  1.0 41.1 %slice-start = ((s8[7340032]{0:T(1024)(128)(4,1)}), s8[4194304]{0:T(1024)(128)(4,1)S(1)}, s32[]{:S(2)}) async-start(s8[7340032]{0:T(1024)(128)(4,1)} %bitcast.14), calls=%async_computation.3 | async-start | bytes 8388608
  22.1 19.9 %slice-start.1 = ((s8[7340032]{0:T(1024)(128)(4,1)}), s8[3145728]{0:T(1024)(128)(4,1)S(1)}, s32[]{:S(2)}) async-start(s8[7340032]{0:T(1024)(128)(4,1)} %bitcast.14), calls=%async_computation.4 | async-start | bytes 6291456
  22.1 7.5 %collective-permute-start = (bf16[64,3712]{1,0:T(8,128)(2,1)S(1)}, bf16[64,3712]{1,0:T(8,128)(2,1)S(1)}, u32[]{:S(2)}, u32[]{:S(2)}) collective-permute-start(bf16[64,3712]{1,0:T(8,128)(2,1)S(1)} %bitcast.4), channel_id=1, source_target_pairs={{0,24},{1,9},{2,26},{3,11},{4,28},{5,13},{6,30},{7,15},{8,16},{9,1... | collective-permute-start | bytes 1425416 | tf_op jit(solution)/shard_map/ppermute | solution.py:77
  22.1 7.5 %collective-permute-start.2 = (bf16[64,3712]{1,0:T(8,128)(2,1)S(1)}, bf16[64,3712]{1,0:T(8,128)(2,1)S(1)}, u32[]{:S(2)}, u32[]{:S(2)}) collective-permute-start(bf16[64,3712]{1,0:T(8,128)(2,1)S(1)} %bitcast.5), channel_id=1, source_target_pairs={{0,6},{1,3},{2,4},{3,1},{4,2},{5,7},{6,0},{7,5},{8,14},{9,11},{10,... | collective-permute-start | bytes 1425416 | tf_op jit(solution)/shard_map/ppermute | solution.py:77
  22.1 9.3 %collective-permute-start.4 = (bf16[64,3712]{1,0:T(8,128)(2,1)S(1)}, bf16[64,3712]{1,0:T(8,128)(2,1)S(1)}, u32[]{:S(2)}, u32[]{:S(2)}) collective-permute-start(bf16[64,3712]{1,0:T(8,128)(2,1)S(1)} %bitcast.6), channel_id=1, source_target_pairs={{0,96},{1,33},{2,98},{3,35},{4,100},{5,37},{6,102},{7,39},{8,104},... | collective-permute-start | bytes 1425416 | tf_op jit(solution)/shard_map/ppermute | solution.py:77
  29.6 16.5 %collective-permute-start.1 = (bf16[64,3712]{1,0:T(8,128)(2,1)S(1)}, bf16[64,3712]{1,0:T(8,128)(2,1)S(1)}, u32[]{:S(2)}, u32[]{:S(2)}) collective-permute-start(bf16[64,3712]{1,0:T(8,128)(2,1)S(1)} %collective-permute-done.refs_1_), channel_id=1, source_target_pairs={{0,96},{1,33},{2,98},{3,35},{4,100},{5,37},{6,102},{7,39},{8,104},... | collective-permute-start | bytes 1425416 | tf_op jit(solution)/shard_map/ppermute | solution.py:77
  29.6 16.5 %collective-permute-start.3 = (bf16[64,3712]{1,0:T(8,128)(2,1)S(1)}, bf16[64,3712]{1,0:T(8,128)(2,1)S(1)}, u32[]{:S(2)}, u32[]{:S(2)}) collective-permute-start(bf16[64,3712]{1,0:T(8,128)(2,1)S(1)} %collective-permute-done.2.refs_2_), channel_id=1, source_target_pairs={{0,24},{1,9},{2,26},{3,11},{4,28},{5,13},{6,30},{7,15},{8,16},{9,1... | collective-permute-start | bytes 1425416 | tf_op jit(solution)/shard_map/ppermute | solution.py:77
  31.4 14.8 %collective-permute-start.5 = (bf16[64,3712]{1,0:T(8,128)(2,1)S(1)}, bf16[64,3712]{1,0:T(8,128)(2,1)S(1)}, u32[]{:S(2)}, u32[]{:S(2)}) collective-permute-start(bf16[64,3712]{1,0:T(8,128)(2,1)S(1)} %collective-permute-done.4.refs_0_), channel_id=1, source_target_pairs={{0,6},{1,3},{2,4},{3,1},{4,2},{5,7},{6,0},{7,5},{8,14},{9,11},{10,... | collective-permute-start | bytes 1425416 | tf_op jit(solution)/shard_map/ppermute | solution.py:77
  31.4 14.8 %collective-permute-start.6 = (bf16[64,3712]{1,0:T(8,128)(2,1)S(1)}, bf16[64,3712]{1,0:T(8,128)(2,1)S(1)}, u32[]{:S(2)}, u32[]{:S(2)}) collective-permute-start(bf16[64,3712]{1,0:T(8,128)(2,1)S(1)} %collective-permute-done.2.refs_2_), channel_id=1, source_target_pairs={{0,120},{1,41},{2,122},{3,43},{4,124},{5,45},{6,126},{7,47},{8,112... | collective-permute-start | bytes 1425416 | tf_op jit(solution)/shard_map/ppermute | solution.py:77
  34.6 10.3 %slice-start.2 = ((s8[7340032]{0:T(1024)(128)(4,1)}), s8[4194304]{0:T(1024)(128)(4,1)S(1)}, s32[]{:S(2)}) async-start(s8[7340032]{0:T(1024)(128)(4,1)} %bitcast.16), calls=%async_computation.5 | async-start | bytes 8388608
  42.0 3.0 %slice-start.3 = ((s8[7340032]{0:T(1024)(128)(4,1)}), s8[3145728]{0:T(1024)(128)(4,1)S(1)}, s32[]{:S(2)}) async-start(s8[7340032]{0:T(1024)(128)(4,1)} %bitcast.16), calls=%async_computation.6 | async-start | bytes 6291456
  46.2 2.6 %collective-permute-start.9 = (bf16[64,7168]{1,0:T(8,128)(2,1)S(1)}, bf16[64,7168]{1,0:T(8,128)(2,1)S(1)}, u32[]{:S(2)}, u32[]{:S(2)}) collective-permute-start(bf16[64,7168]{1,0:T(8,128)(2,1)S(1)} %get-tuple-element.42), channel_id=1, source_target_pairs={{0,1},{1,0},{2,3},{3,2},{4,5},{5,4},{6,7},{7,6},{8,9},{9,8},{10,11... | collective-permute-start | bytes 2752520 | tf_op jit(solution)/shard_map/ppermute | solution.py:85
  47.6 2.6 %collective-permute-start.8 = (bf16[64,3712]{1,0:T(8,128)(2,1)S(1)}, bf16[64,3712]{1,0:T(8,128)(2,1)S(1)}, u32[]{:S(2)}, u32[]{:S(2)}) collective-permute-start(bf16[64,3712]{1,0:T(8,128)(2,1)S(1)} %get-tuple-element.40), channel_id=1, source_target_pairs={{0,1},{1,0},{2,3},{3,2},{4,5},{5,4},{6,7},{7,6},{8,9},{9,8},{10,11... | collective-permute-start | bytes 1425416 | tf_op jit(solution)/shard_map/ppermute | solution.py:85
  47.8 2.4 %collective-permute-start.7 = (bf16[64,3584]{1,0:T(8,128)(2,1)S(1)}, bf16[64,3584]{1,0:T(8,128)(2,1)S(1)}, u32[]{:S(2)}, u32[]{:S(2)}) collective-permute-start(bf16[64,3584]{1,0:T(8,128)(2,1)S(1)} %get-tuple-element.39), channel_id=1, source_target_pairs={{0,1},{1,0},{2,3},{3,2},{4,5},{5,4},{6,7},{7,6},{8,9},{9,8},{10,11... | collective-permute-start | bytes 1376264 | tf_op jit(solution)/shard_map/ppermute | solution.py:85
  53.4 2.6 %collective-permute-start.10 = (bf16[64,7168]{1,0:T(8,128)(2,1)S(1)}, bf16[64,7168]{1,0:T(8,128)(2,1)S(1)}, u32[]{:S(2)}, u32[]{:S(2)}) collective-permute-start(bf16[64,7168]{1,0:T(8,128)(2,1)S(1)} %get-tuple-element.45), channel_id=1, source_target_pairs={{0,1},{1,0},{2,3},{3,2},{4,5},{5,4},{6,7},{7,6},{8,9},{9,8},{10,11... | collective-permute-start | bytes 2752520 | tf_op jit(solution)/shard_map/ppermute | solution.py:85
  57.0 7.9 %collective-permute-start.16 = (bf16[64,3584]{1,0:T(8,128)(2,1)S(1)}, bf16[64,3584]{1,0:T(8,128)(2,1)S(1)}, u32[]{:S(2)}, u32[]{:S(2)}) collective-permute-start(bf16[64,3584]{1,0:T(8,128)(2,1)S(1)} %get-tuple-element.52), channel_id=1, source_target_pairs={{0,24},{1,9},{2,26},{3,11},{4,28},{5,13},{6,30},{7,15},{8,16},{9,1... | collective-permute-start | bytes 1376264 | tf_op jit(solution)/shard_map/ppermute | solution.py:77
  57.2 12.6 %collective-permute-start.14 = (bf16[64,3584]{1,0:T(8,128)(2,1)S(1)}, bf16[64,3584]{1,0:T(8,128)(2,1)S(1)}, u32[]{:S(2)}, u32[]{:S(2)}) collective-permute-start(bf16[64,3584]{1,0:T(8,128)(2,1)S(1)} %get-tuple-element.50), channel_id=1, source_target_pairs={{0,96},{1,33},{2,98},{3,35},{4,100},{5,37},{6,102},{7,39},{8,104},... | collective-permute-start | bytes 1376264 | tf_op jit(solution)/shard_map/ppermute | solution.py:77
  57.9 13.5 %collective-permute-start.12 = (bf16[64,3584]{1,0:T(8,128)(2,1)S(1)}, bf16[64,3584]{1,0:T(8,128)(2,1)S(1)}, u32[]{:S(2)}, u32[]{:S(2)}) collective-permute-start(bf16[64,3584]{1,0:T(8,128)(2,1)S(1)} %get-tuple-element.48), channel_id=1, source_target_pairs={{0,6},{1,3},{2,4},{3,1},{4,2},{5,7},{6,0},{7,5},{8,14},{9,11},{10,... | collective-permute-start | bytes 1376264 | tf_op jit(solution)/shard_map/ppermute | solution.py:77
  57.9 14.3 %collective-permute-start.11 = (bf16[64,3584]{1,0:T(8,128)(2,1)S(1)}, bf16[64,3584]{1,0:T(8,128)(2,1)S(1)}, u32[]{:S(2)}, u32[]{:S(2)}) collective-permute-start(bf16[64,3584]{1,0:T(8,128)(2,1)S(1)} %get-tuple-element.46), channel_id=1, source_target_pairs={{0,126},{1,43},{2,124},{3,41},{4,122},{5,47},{6,120},{7,45},{8,118... | collective-permute-start | bytes 1376264 | tf_op jit(solution)/shard_map/ppermute | solution.py:77
  64.9 10.4 %collective-permute-start.17 = (bf16[64,3584]{1,0:T(8,128)(2,1)S(1)}, bf16[64,3584]{1,0:T(8,128)(2,1)S(1)}, u32[]{:S(2)}, u32[]{:S(2)}) collective-permute-start(bf16[64,3584]{1,0:T(8,128)(2,1)S(1)} %add_convert_fusion.1), channel_id=1, source_target_pairs={{0,6},{1,3},{2,4},{3,1},{4,2},{5,7},{6,0},{7,5},{8,14},{9,11},{10,... | collective-permute-start | bytes 1376264 | tf_op jit(solution)/shard_map/ppermute | solution.py:77
  70.0 7.7 %collective-permute-start.15 = (bf16[64,3584]{1,0:T(8,128)(2,1)S(1)}, bf16[64,3584]{1,0:T(8,128)(2,1)S(1)}, u32[]{:S(2)}, u32[]{:S(2)}) collective-permute-start(bf16[64,3584]{1,0:T(8,128)(2,1)S(1)} %add_convert_fusion.2), channel_id=1, source_target_pairs={{0,24},{1,9},{2,26},{3,11},{4,28},{5,13},{6,30},{7,15},{8,16},{9,1... | collective-permute-start | bytes 1376264 | tf_op jit(solution)/shard_map/ppermute | solution.py:77
  71.5 7.7 %collective-permute-start.13 = (bf16[64,3584]{1,0:T(8,128)(2,1)S(1)}, bf16[64,3584]{1,0:T(8,128)(2,1)S(1)}, u32[]{:S(2)}, u32[]{:S(2)}) collective-permute-start(bf16[64,3584]{1,0:T(8,128)(2,1)S(1)} %add_convert_fusion.3), channel_id=1, source_target_pairs={{0,96},{1,33},{2,98},{3,35},{4,100},{5,37},{6,102},{7,39},{8,104},... | collective-permute-start | bytes 1376264 | tf_op jit(solution)/shard_map/ppermute | solution.py:77

commit v8 on v7

--- a/solution.py
+++ b/solution.py
@@ -25,8 +25,8 @@
 SMALL = pltpu.CompilerParams(vmem_limit_bytes=8 * MIB)
 
 
-MIDDLE = D // 2
-CUTS = ((0, MIDDLE), (MIDDLE, D))
+MIDDLE = 2560
+CUTS = ((0, 2560), (2560, 5120), (5120, D))
 BRIEF = pl.CostEstimate(flops=1000, bytes_accessed=1000, transcendentals=0)
 
 
@@ -58,10 +58,10 @@
         for x in range(4):
             for y in range(4):
                 for c in range(2):
-                    at = [z, x, y]
+                    at = [x, z, y]
                     for axis in axes:
                         at[axis] ^= 1 if c else 3
-                    pairs.append((flat(z, x, y, c), flat(*at, c)))
+                    pairs.append((flat(z, x, y, c), flat(at[1], at[0], at[2], c)))
     return pairs
 
 
@@ -75,10 +75,6 @@
 
 def swap_far(values, axis):
     return lax.ppermute(values, AXES, FAR[axis])
-
-
-def swap_cores(values):
-    return lax.all_to_all(values, "dev", 0, 0, axis_index_groups=[[i, i + 1] for i in range(0, 32, 2)], tiled=True)
 
 
 def to_sibling(values):
@@ -138,13 +134,9 @@
     blocks = [refs.pop(0) for _ in range(4)]
     sources = [refs.pop(0) for _ in range(loads)]
     del refs[0]
-    pick, sem = refs[-2:]
-    if loads:
-        core = expert_ref[0] % 2
-        mine_ref, left_ref, right_ref = refs[0].at[core], refs[0].at[1 - core, :, :HALF], refs[0].at[1 - core, :, HALF:]
-    else:
-        mine_ref, left_ref, right_ref = refs[:3]
-    copies = [pltpu.make_async_copy(a.at[:, :MIDDLE, :], b, sem) for a, b in zip(sources, refs[1 : 1 + loads])]
+    mine_ref, sent_refs, targets = refs[0], refs[1:4], refs[4 : 4 + loads]
+    pick, sem = refs[4 + loads :]
+    copies = [pltpu.make_async_copy(a.at[:, :MIDDLE, :], b, sem) for a, b in zip(sources, targets)]
     for copy in copies:
         copy.start()
     own = expert_ref[0]
@@ -167,30 +159,38 @@
         pick[e * SEL : (e + 1) * SEL, :] = jnp.where(hit & is_left, 1.0, 0.0).astype(BF16)
         pick[(2 + e) * SEL : (3 + e) * SEL, :] = jnp.where(hit & ~is_left, 1.0, 0.0).astype(BF16)
 
+
+    def put_sent(start, value):
+        low = 0
+        while low < value.shape[1]:
+            piece = min((start + low) // MIDDLE, 2)
+            at = start + low - CUTS[piece][0]
+            size = min(value.shape[1] - low, sent_refs[piece].shape[1] - at)
+            sent_refs[piece][:, at : at + size] = value[:, low : low + size]
+            low += size
+
     for n in range(0, HALF, 512):
         x = jnp.concatenate([ref[:, n : n + 512] for ref in blocks], axis=0)
         value = jnp.dot(pick[...], x, preferred_element_type=F32).astype(BF16)
         mine_ref[:, n : n + 512] = value[:SEL]
-        left_ref[:, n : n + 512] = value[SEL : 2 * SEL]
+        put_sent(n, value[SEL : 2 * SEL])
         mine_ref[:, HALF + n : HALF + n + 512] = value[2 * SEL : 3 * SEL]
-        right_ref[:, n : n + 512] = value[3 * SEL :]
+        put_sent(HALF + n, value[3 * SEL :])
     value = jnp.dot(pick[: 2 * SEL, :], ext, preferred_element_type=F32).astype(BF16)
     mine_ref[:, D:] = value[:SEL]
-    right_ref[:, HALF:] = value[SEL:]
+    put_sent(D, value[SEL:])
     for copy in copies:
         copy.wait()
 
 
 def select(expert, blocks, after, loads=()):
-    if loads:
-        shapes = [(2, SEL, D + EXT)] + [(1, MIDDLE, 512) for _ in loads]
-    else:
-        shapes = [(SEL, D + EXT), (SEL, HALF), (SEL, HALF + EXT)]
     return pl.pallas_call(
         functools.partial(select_kernel, len(loads)),
-        out_shape=[jax.ShapeDtypeStruct(shape, BF16) for shape in shapes],
+        out_shape=[jax.ShapeDtypeStruct((SEL, D + EXT), BF16)]
+        + [jax.ShapeDtypeStruct((SEL, high - low + EXT * (high == D)), BF16) for low, high in CUTS]
+        + [jax.ShapeDtypeStruct((1, MIDDLE, 512), BF16) for _ in loads],
         in_specs=[SMEM] + [VMEM] * 4 + [HBM] * len(loads) + [ANY],
-        out_specs=[VMEM] * len(shapes),
+        out_specs=[VMEM] * (4 + len(loads)),
         scratch_shapes=[pltpu.VMEM((PART, PART), BF16), pltpu.SemaphoreType.DMA],
         compiler_params=SMALL,
         cost_estimate=BRIEF,
@@ -198,24 +198,20 @@
     )(expert, *blocks, *[in_hbm(load) for load in loads], after)
 
 
-def hidden_kernel(streams, expert_ref, *refs):
-    refs = list(refs)
-    row_refs = [refs.pop(0) for _ in range(1 if streams else 3)]
-    gate_ref, first_ref, rest_ref = refs[:3]
+def hidden_kernel(streams, expert_ref, mine_ref, a_ref, b_ref, c_ref, gate_ref, first_ref, rest_ref, after_ref, *refs):
+    del after_ref
     if streams:
-        hidden, second_ref, gate_sum, up_sum, sem = refs[4:]
+        hidden, second_ref, gate_sum, up_sum, sem = refs
         copy = pltpu.make_async_copy(rest_ref.at[:, MIDDLE:, :], second_ref, sem)
         copy.start()
     else:
-        hidden, gate_sum, up_sum = refs[4:]
+        hidden, gate_sum, up_sum = refs
         second_ref = rest_ref
-    core = expert_ref[0] % 2
 
     def rows(piece, low, high):
-        if streams:
-            return jnp.concatenate([row_refs[0][core, :, low:high], row_refs[0][1 - core, :, low:high]], axis=0)
         start = CUTS[piece][0]
-        return jnp.concatenate([row_refs[0][:, low:high], row_refs[1 + piece][:, low - start : high - start]], axis=0)
+        theirs_ref = (a_ref, b_ref, c_ref)[piece]
+        return jnp.concatenate([mine_ref[:, low:high], theirs_ref[:, low - start : high - start]], axis=0)
 
     for piece, (low, high) in enumerate(CUTS):
         gate = jnp.dot(rows(piece, low, high), gate_ref[0, low:high, :], preferred_element_type=F32)
@@ -227,23 +223,23 @@
         up = jnp.dot(rows(piece, low, high), ref[0, low - start : high - start, :], preferred_element_type=F32)
         up_sum[...] = up if low == 0 else up_sum[...] + up
     lanes = expert_lanes(expert_ref[0], (2 * SEL, EXT), 1)
-    scale = jnp.sum(jnp.where(lanes, rows(1, D, D + EXT).astype(F32), 0.0), axis=1, keepdims=True)
+    scale = jnp.sum(jnp.where(lanes, rows(2, D, D + EXT).astype(F32), 0.0), axis=1, keepdims=True)
     v = gate_sum[...]
     hidden[...] = (v / (1.0 + jnp.exp(-v)) * up_sum[...] * scale).astype(BF16)
 
 
-def hidden_units(expert, rows, gate, first, rest, after, streams):
+def hidden_units(expert, mine, theirs, gate, first, rest, after, streams):
     second = jax.ShapeDtypeStruct((1, D - MIDDLE, 512), BF16)
     return pl.pallas_call(
         functools.partial(hidden_kernel, streams),
         out_shape=[jax.ShapeDtypeStruct((2 * SEL, 512), BF16)] + [second] * streams,
-        in_specs=[SMEM] + [VMEM] * (len(rows) + 2) + [HBM if streams else VMEM, ANY],
+        in_specs=[SMEM] + [VMEM] * 6 + [HBM if streams else VMEM, ANY],
         out_specs=[VMEM] * (1 + streams),
         scratch_shapes=[pltpu.VMEM((2 * SEL, 512), F32)] * 2 + [pltpu.SemaphoreType.DMA] * streams,
         compiler_params=SMALL,
         cost_estimate=BRIEF,
         name="hidden",
-    )(expert, *rows, gate, first, in_hbm(rest) if streams else rest, after)
+    )(expert, mine, *theirs, gate, first, in_hbm(rest) if streams else rest, after)
 
 
 def down_kernel(hidden_ref, down_ref, after_ref, mine_ref, theirs_ref):
@@ -347,16 +343,18 @@
     xy, yz, zx = swap_far(y, 0), swap_far(z, 1), swap_far(x, 2)
     xyz = swap_far(z, 4)
     near = (x, y, z, own)
-    pair, up_first = select(expert, near, own, (up,))
-    hidden_near, up_second = hidden_units(expert, [swap_cores(pair)], gate, up_first, up, own, 1)
+    mine_near, *sent, up_first = select(expert, near, own, (up,))
+    xy, yz, *sent = lax.optimization_barrier((xy, yz, *sent))
+    got_near = [to_sibling(piece) for piece in sent]
+    hidden_near, up_second = hidden_units(expert, mine_near, got_near, gate, up_first, up, own, 1)
     result_near, theirs = down_rows(hidden_near, down, own)
     xy, yz, zx, xyz, theirs = lax.optimization_barrier((xy, yz, zx, xyz, theirs))
     far = (xy, zx, yz, xyz)
     returned_near = to_sibling(theirs)
     mine_far, *sent = select(expert, far, result_near)
-    rows = [mine_far] + [to_sibling(piece) for piece in sent]
+    got_far = [to_sibling(piece) for piece in sent]
     y_x, y_y, y_z, y_own = spread(expert, near, result_near, returned_near, mine_far)
-    (hidden_far,) = hidden_units(expert, rows, gate, up_first, up_second, y_own, 0)
+    (hidden_far,) = hidden_units(expert, mine_far, got_far, gate, up_first, up_second, y_own, 0)
     result, theirs = down_rows(hidden_far, down, own)
     returned = to_sibling(theirs)
     y_xy, y_zx, y_yz, y_xyz = spread(expert, far, result, returned, own)

time: 95.5 us -> 99.6 us (1.043)
  waiting for transfers between devices: 26.2 us -> 36.2 us
  blocking collectives: 43.2 us -> 37.1 us
    ppermute x14, waiting for transfers between devices: 23.1 us -> 31.2 us  [swap_far(): return lax.ppermute(values, AXES, FAR[axis])]
    all_to_all x1 -> x0, blocking collectives: 7.36 us -> none  [swap_cores(): lax.all_to_all(values, 'dev', 0, 0, axis_index_groups=[[i, i + 1] for i i...]
    ppermute x4 -> x8, waiting for transfers between devices: 3.08 us -> 5.01 us  [to_sibling(): return lax.ppermute(values, 'dev', [(i, i ^ 1) for i in range(32)])]
    all_to_all x2, blocking collectives: 35.8 us -> 37.1 us  [swap_near(): lax.all_to_all(values, AXES, 0, 0, axis_index_groups=NEAR, tiled=True)]
    ppermute x4 -> x8, starting transfers between devices: 1.47 us -> 2.15 us  [to_sibling(): return lax.ppermute(values, 'dev', [(i, i ^ 1) for i in range(32)])]
  transfers between devices with their start and end apart: 18 -> 22, of which waited for: 9 -> 12; matrix products, arithmetic and copies ran while one was open for 0% -> 0% of each run, Pallas kernels for 8% -> 8%
where the time goes in v8:
time: 99.6 us; the launch traced here: 99.4 us
  blocking collectives  37.1 us (37%)
  waiting for transfers between devices  36.2 us (36%)
  Pallas kernels  14.3 us (14%)
  starting transfers between devices  11 us (11%)
    all_to_all x2, blocking collectives, swap_near(): lax.all_to_all(values, AXES, 0, 0, axis_index_groups=NEAR, tiled=True)  37.1 us
    ppermute x14, waiting for transfers between devices, swap_far(): return lax.ppermute(values, AXES, FAR[axis])  31.2 us
    ppermute x14, starting transfers between devices, swap_far(): return lax.ppermute(values, AXES, FAR[axis])  8.87 us
    pallas_call x2, Pallas kernels, hidden_units(): pl.pallas_call(functools.partial(hidden_kernel, streams), out_shape=[jax....  5.36 us
    ppermute x8, waiting for transfers between devices, to_sibling(): return lax.ppermute(values, 'dev', [(i, i ^ 1) for i in range(32)])  5.01 us
    pallas_call x2, Pallas kernels, select(): pl.pallas_call(functools.partial(select_kernel, len(loads)), out_shape=[j...  2.81 us
    pallas_call x2, Pallas kernels, down_rows(): pl.pallas_call(down_kernel, out_shape=[jax.ShapeDtypeStruct((SEL, D), BF1...  2.26 us
    ppermute x8, starting transfers between devices, to_sibling(): return lax.ppermute(values, 'dev', [(i, i ^ 1) for i in range(32)])  2.15 us
  transfers between devices with their start and end apart: 22, of which 12 were waited for; matrix products, arithmetic and copies ran while one was open for 0% of the time, Pallas kernels for 8%

profile of v8, /device:TPU:1, one launch (start us, length us, event | category | flops | bytes accessed | tf_op | source)
XLA Modules:
  0.0 99.4 jit_solution(14608739612493658941)
XLA Ops:
  0.0 1.1 %pack.1 = bf16[8,8,3712]{2,1,0:T(8,128)(2,1)S(1)} custom-call(s32[1]{0:T(128)} %bitcast.expert_ref, bf16[4,7168]{1,0:T(4,128)(2,1)} %tokens_hbm.1, s32[4,8]{1,0:T(4,128)} %ids_hbm.1, f32[4,8]{1,0:T(4,128)} %weights_hbm.1), custom_call_target="tpu_custom_call" | custom-call | tf_op jit(solution)/shard_map/pack/pallas_call | solution.py:111
  1.1 21.2 %all_to_all.10 = bf16[8,8,3712]{2,1,0:T(8,128)(2,1)S(1)} all-to-all(bf16[8,8,3712]{2,1,0:T(8,128)(2,1)S(1)} %pack.1), channel_id=1, replica_groups={{0,2,8,10,32,34,40,42},{1,7,25,31,97,103,121,127},{3,5,27,29,99,101,123..., dimensions={0} | all-to-all | bytes 950272 | tf_op jit(solution)/shard_map/all_to_all | solution.py:73
  22.3 7.5 %collective-permute-done.refs_1_ = bf16[64,3712]{1,0:T(8,128)(2,1)S(1)} collective-permute-done((bf16[64,3712]{1,0:T(8,128)(2,1)S(1)}, bf16[64,3712]{1,0:T(8,128)(2,1)S(1)}, u32[]{:S(2)}, u32[]{:S(2)}) %collective-permute-start) | collective-permute-done | bytes 475168 | tf_op jit(solution)/shard_map/ppermute | solution.py:77
  29.8 1.8 %collective-permute-start.3 = (bf16[64,3712]{1,0:T(8,128)(2,1)S(1)}, bf16[64,3712]{1,0:T(8,128)(2,1)S(1)}, u32[]{:S(2)}, u32[]{:S(2)}) collective-permute-start(bf16[64,3712]{1,0:T(8,128)(2,1)S(1)} %collective-permute-done.2.refs_2_), channel_id=1, source_target_pairs={{0,96},{1,33},{2,98},{3,35},{4,100},{5,37},{6,102},{7,39},{8,104},... | collective-permute-start | bytes 1425416 | tf_op jit(solution)/shard_map/ppermute | solution.py:77
  31.6 1.2 %collective-permute-start.6 = (bf16[64,3712]{1,0:T(8,128)(2,1)S(1)}, bf16[64,3712]{1,0:T(8,128)(2,1)S(1)}, u32[]{:S(2)}, u32[]{:S(2)}) collective-permute-start(bf16[64,3712]{1,0:T(8,128)(2,1)S(1)} %collective-permute-done.2.refs_2_), channel_id=1, source_target_pairs={{0,120},{1,41},{2,122},{3,43},{4,124},{5,45},{6,126},{7,47},{8,112... | collective-permute-start | bytes 1425416 | tf_op jit(solution)/shard_map/ppermute | solution.py:77
  32.8 1.9 %select.2 = (bf16[64,7296]{1,0:T(8,128)(2,1)S(1)}, bf16[64,2560]{1,0:T(8,128)(2,1)S(1)}, bf16[64,2560]{1,0:T(8,128)(2,1)S(1)}, bf16[64,2176]{1,0:T(8,128)(2,1)S(1)}, bf16[1,2560,512]{2,1,0:T(8,128)(2,1)S(1)}) custom-call(s32[1]{0:T(128)} %bitcast.expert_ref, bf16[64,3712]{1,0:T(8,128)(2,1)S(1)} %collective-permute-done.4.refs_0_, ...), custom_call_target="tpu_custom_call" | custom-call | flops 1000 | bytes 1000 | tf_op jit(solution)/shard_map/select/pallas_call | solution.py:187
  34.7 2.9 %collective-permute-done.1.refs_0_ = bf16[64,3712]{1,0:T(8,128)(2,1)S(1)} collective-permute-done((bf16[64,3712]{1,0:T(8,128)(2,1)S(1)}, bf16[64,3712]{1,0:T(8,128)(2,1)S(1)}, u32[]{:S(2)}, u32[]{:S(2)}) %collective-permute-start.1) | collective-permute-done | bytes 475168 | tf_op jit(solution)/shard_map/ppermute | solution.py:77
  37.6 5.4 %collective-permute-done.3.refs_2_ = bf16[64,3712]{1,0:T(8,128)(2,1)S(1)} collective-permute-done((bf16[64,3712]{1,0:T(8,128)(2,1)S(1)}, bf16[64,3712]{1,0:T(8,128)(2,1)S(1)}, u32[]{:S(2)}, u32[]{:S(2)}) %collective-permute-start.3) | collective-permute-done | bytes 475168 | tf_op jit(solution)/shard_map/ppermute | solution.py:77
  43.0 0.5 collective-permute-start.8
  43.5 2.0 %collective-permute-done.9.c_ref = bf16[64,2176]{1,0:T(8,128)(2,1)S(1)} collective-permute-done((bf16[64,2176]{1,0:T(8,128)(2,1)S(1)}, bf16[64,2176]{1,0:T(8,128)(2,1)S(1)}, u32[]{:S(2)}, u32[]{:S(2)}) %collective-permute-start.9) | collective-permute-done | bytes 278560 | tf_op jit(solution)/shard_map/ppermute | solution.py:81
  45.5 3.3 %hidden.2 = (bf16[128,512]{1,0:T(8,128)(2,1)S(1)}, bf16[1,4608,512]{2,1,0:T(8,128)(2,1)S(1)}) custom-call(s32[1]{0:T(128)} %bitcast.expert_ref, bf16[64,7296]{1,0:T(8,128)(2,1)S(1)} %get-tuple-element.43.mine_ref, bf16[64,2560]{1,0:T(8,128)(2,1)S(1)} %collective-permute-done.7.a_ref, bf16[64,2560]{1,0:T(8,128)(2,1)S(1)} %collective-permute-done.8.b_ref, ...), custom_call_target="tpu_custom_call" | custom-call | flops 1000 | bytes 1000 | tf_op jit(solution)/shard_map/hidden/pallas_call | solution.py:233
  48.9 1.1 %down.2 = (bf16[64,7168]{1,0:T(8,128)(2,1)S(1)}, bf16[64,7168]{1,0:T(8,128)(2,1)S(1)}) custom-call(bf16[128,512]{1,0:T(8,128)(2,1)S(1)} %get-tuple-element.48.hidden_ref, bf16[1,512,7168]{2,1,0:T(8,128)(2,1)S(1)} %bitcast.15, bf16[64,3712]{1,0:T(8,128)(2,1)S(1)} %bitcast.10), custom_call_target="tpu_custom_call" | custom-call | flops 1000 | bytes 1000 | tf_op jit(solution)/shard_map/down/pallas_call | solution.py:255
  50.2 0.9 select.3
  51.1 0.5 collective-permute-start.10
  52.1 0.5 collective-permute-done.13.refs_5_
  52.6 1.0 %spread.2 = (bf16[64,3584]{1,0:T(8,128)(2,1)S(1)}, bf16[64,3584]{1,0:T(8,128)(2,1)S(1)}, bf16[64,3584]{1,0:T(8,128)(2,1)S(1)}, bf16[64,3584]{1,0:T(8,128)(2,1)S(1)}) custom-call(s32[1]{0:T(128)} %bitcast.expert_ref, bf16[64,3712]{1,0:T(8,128)(2,1)S(1)} %collective-permute-done.4.refs_0_, bf16[64,3712]{1,0:T(8,128)(2,1)S(1)} %collective-permute-done.refs_1_, ...), custom_call_target="tpu_custom_call" | custom-call | flops 1000 | bytes 1000 | tf_op jit(solution)/shard_map/spread/pallas_call | solution.py:301
  53.9 2.1 %hidden.3.hidden_ref = bf16[128,512]{1,0:T(8,128)(2,1)S(1)} custom-call(s32[1]{0:T(128)} %bitcast.expert_ref, bf16[64,7296]{1,0:T(8,128)(2,1)S(1)} %get-tuple-element.55.refs_6_.mine_ref, bf16[64,2560]{1,0:T(8,128)(2,1)S(1)} %collective-permute-done.10.a_ref, bf16[64,2560]{1,0:T(8,128)(2,1)S(1)} %collective-permute-done.11.b_ref, ...), custom_call_target="tpu_custom_call" | custom-call | flops 1000 | bytes 1000 | tf_op jit(solution)/shard_map/hidden/pallas_call | solution.py:233
  56.0 1.1 %down.3 = (bf16[64,7168]{1,0:T(8,128)(2,1)S(1)}, bf16[64,7168]{1,0:T(8,128)(2,1)S(1)}) custom-call(bf16[128,512]{1,0:T(8,128)(2,1)S(1)} %hidden.3.hidden_ref, bf16[1,512,7168]{2,1,0:T(8,128)(2,1)S(1)} %bitcast.15, bf16[64,3712]{1,0:T(8,128)(2,1)S(1)} %bitcast.12), custom_call_target="tpu_custom_call" | custom-call | flops 1000 | bytes 1000 | tf_op jit(solution)/shard_map/down/pallas_call | solution.py:255
  57.1 0.5 collective-permute-start.14
  57.6 2.3 %collective-permute-done.14.refs_5_ = bf16[64,7168]{1,0:T(8,128)(2,1)S(1)} collective-permute-done((bf16[64,7168]{1,0:T(8,128)(2,1)S(1)}, bf16[64,7168]{1,0:T(8,128)(2,1)S(1)}, u32[]{:S(2)}, u32[]{:S(2)}) %collective-permute-start.14) | collective-permute-done | bytes 917536 | tf_op jit(solution)/shard_map/ppermute | solution.py:81
  59.9 1.0 %spread.3 = (bf16[64,3584]{1,0:T(8,128)(2,1)S(1)}, bf16[64,3584]{1,0:T(8,128)(2,1)S(1)}, bf16[64,3584]{1,0:T(8,128)(2,1)S(1)}, bf16[64,3584]{1,0:T(8,128)(2,1)S(1)}) custom-call(s32[1]{0:T(128)} %bitcast.expert_ref, bf16[64,3712]{1,0:T(8,128)(2,1)S(1)} %collective-permute-done.1.refs_0_, bf16[64,3712]{1,0:T(8,128)(2,1)S(1)} %collective-permute-done.5.refs_1_, ...), custom_call_target="tpu_custom_call" | custom-call | flops 1000 | bytes 1000 | tf_op jit(solution)/shard_map/spread/pallas_call | solution.py:301
  60.9 1.2 %collective-permute-start.20 = (bf16[64,3584]{1,0:T(8,128)(2,1)S(1)}, bf16[64,3584]{1,0:T(8,128)(2,1)S(1)}, u32[]{:S(2)}, u32[]{:S(2)}) collective-permute-start(bf16[64,3584]{1,0:T(8,128)(2,1)S(1)} %get-tuple-element.70), channel_id=1, source_target_pairs={{0,96},{1,33},{2,98},{3,35},{4,100},{5,37},{6,102},{7,39},{8,104},... | collective-permute-start | bytes 1376264 | tf_op jit(solution)/shard_map/ppermute | solution.py:77
  62.1 2.7 %collective-permute-start.15 = (bf16[64,3584]{1,0:T(8,128)(2,1)S(1)}, bf16[64,3584]{1,0:T(8,128)(2,1)S(1)}, u32[]{:S(2)}, u32[]{:S(2)}) collective-permute-start(bf16[64,3584]{1,0:T(8,128)(2,1)S(1)} %get-tuple-element.64), channel_id=1, source_target_pairs={{0,126},{1,43},{2,124},{3,41},{4,122},{5,47},{6,120},{7,45},{8,118... | collective-permute-start | bytes 1376264 | tf_op jit(solution)/shard_map/ppermute | solution.py:77
  64.8 3.8 %collective-permute-done.20 = bf16[64,3584]{1,0:T(8,128)(2,1)S(1)} collective-permute-done((bf16[64,3584]{1,0:T(8,128)(2,1)S(1)}, bf16[64,3584]{1,0:T(8,128)(2,1)S(1)}, u32[]{:S(2)}, u32[]{:S(2)}) %collective-permute-start.20) | collective-permute-done | bytes 458784 | tf_op jit(solution)/shard_map/ppermute | solution.py:77
  68.8 1.0 collective-permute-done.18
  69.9 0.4 collective-permute-start.19
  70.3 4.4 %collective-permute-done.16 = bf16[64,3584]{1,0:T(8,128)(2,1)S(1)} collective-permute-done((bf16[64,3584]{1,0:T(8,128)(2,1)S(1)}, bf16[64,3584]{1,0:T(8,128)(2,1)S(1)}, u32[]{:S(2)}, u32[]{:S(2)}) %collective-permute-start.16) | collective-permute-done | bytes 458784 | tf_op jit(solution)/shard_map/ppermute | solution.py:77
  74.8 1.5 %collective-permute-start.17 = (bf16[64,3584]{1,0:T(8,128)(2,1)S(1)}, bf16[64,3584]{1,0:T(8,128)(2,1)S(1)}, u32[]{:S(2)}, u32[]{:S(2)}) collective-permute-start(bf16[64,3584]{1,0:T(8,128)(2,1)S(1)} %add_convert_fusion.3), channel_id=1, source_target_pairs={{0,24},{1,9},{2,26},{3,11},{4,28},{5,13},{6,30},{7,15},{8,16},{9,1... | collective-permute-start | bytes 1376264 | tf_op jit(solution)/shard_map/ppermute | solution.py:77
  76.4 3.2 %collective-permute-done.21 = bf16[64,3584]{1,0:T(8,128)(2,1)S(1)} collective-permute-done((bf16[64,3584]{1,0:T(8,128)(2,1)S(1)}, bf16[64,3584]{1,0:T(8,128)(2,1)S(1)}, u32[]{:S(2)}, u32[]{:S(2)}) %collective-permute-start.21) | collective-permute-done | bytes 458784 | tf_op jit(solution)/shard_map/ppermute | solution.py:77
  79.6 2.9 %collective-permute-done.17 = bf16[64,3584]{1,0:T(8,128)(2,1)S(1)} collective-permute-done((bf16[64,3584]{1,0:T(8,128)(2,1)S(1)}, bf16[64,3584]{1,0:T(8,128)(2,1)S(1)}, u32[]{:S(2)}, u32[]{:S(2)}) %collective-permute-start.17) | collective-permute-done | bytes 458784 | tf_op jit(solution)/shard_map/ppermute | solution.py:77
  82.8 16.0 %all_to_all.11.parts_ref = bf16[8,8,3584]{2,1,0:T(8,128)(2,1)S(1)} all-to-all(bf16[8,8,3584]{2,1,0:T(8,128)(2,1)S(1)} %fusion), channel_id=1, replica_groups={{0,2,8,10,32,34,40,42},{1,7,25,31,97,103,121,127},{3,5,27,29,99,101,123..., dimensions={0} | all-to-all | bytes 917504 | tf_op jit(solution)/shard_map/all_to_all | solution.py:73
  98.8 0.7 finish.1
  (35 shorter events, 1.8 us)
Async XLA Ops:
  0.0 45.5 %copy-start = (bf16[1,7168,512]{2,1,0:T(8,128)(2,1)S(1)}, bf16[1,7168,512]{2,1,0:T(8,128)(2,1)}, u32[]{:S(2)}) copy-start(bf16[1,7168,512]{2,1,0:T(8,128)(2,1)} %gate_ref.3) | copy-start | bytes 22020100
  22.3 7.5 %collective-permute-start = (bf16[64,3712]{1,0:T(8,128)(2,1)S(1)}, bf16[64,3712]{1,0:T(8,128)(2,1)S(1)}, u32[]{:S(2)}, u32[]{:S(2)}) collective-permute-start(bf16[64,3712]{1,0:T(8,128)(2,1)S(1)} %bitcast.4), channel_id=1, source_target_pairs={{0,96},{1,33},{2,98},{3,35},{4,100},{5,37},{6,102},{7,39},{8,104},... | collective-permute-start | bytes 1425416 | tf_op jit(solution)/shard_map/ppermute | solution.py:77
  22.3 7.5 %collective-permute-start.2 = (bf16[64,3712]{1,0:T(8,128)(2,1)S(1)}, bf16[64,3712]{1,0:T(8,128)(2,1)S(1)}, u32[]{:S(2)}, u32[]{:S(2)}) collective-permute-start(bf16[64,3712]{1,0:T(8,128)(2,1)S(1)} %bitcast.5), channel_id=1, source_target_pairs={{0,6},{1,3},{2,4},{3,1},{4,2},{5,7},{6,0},{7,5},{8,14},{9,11},{10,... | collective-permute-start | bytes 1425416 | tf_op jit(solution)/shard_map/ppermute | solution.py:77
  22.3 9.3 %collective-permute-start.4 = (bf16[64,3712]{1,0:T(8,128)(2,1)S(1)}, bf16[64,3712]{1,0:T(8,128)(2,1)S(1)}, u32[]{:S(2)}, u32[]{:S(2)}) collective-permute-start(bf16[64,3712]{1,0:T(8,128)(2,1)S(1)} %bitcast.6), channel_id=1, source_target_pairs={{0,24},{1,9},{2,26},{3,11},{4,28},{5,13},{6,30},{7,15},{8,16},{9,1... | collective-permute-start | bytes 1425416 | tf_op jit(solution)/shard_map/ppermute | solution.py:77
  29.8 7.8 %collective-permute-start.1 = (bf16[64,3712]{1,0:T(8,128)(2,1)S(1)}, bf16[64,3712]{1,0:T(8,128)(2,1)S(1)}, u32[]{:S(2)}, u32[]{:S(2)}) collective-permute-start(bf16[64,3712]{1,0:T(8,128)(2,1)S(1)} %collective-permute-done.refs_1_), channel_id=1, source_target_pairs={{0,24},{1,9},{2,26},{3,11},{4,28},{5,13},{6,30},{7,15},{8,16},{9,1... | collective-permute-start | bytes 1425416 | tf_op jit(solution)/shard_map/ppermute | solution.py:77
  29.8 13.2 %collective-permute-start.3 = (bf16[64,3712]{1,0:T(8,128)(2,1)S(1)}, bf16[64,3712]{1,0:T(8,128)(2,1)S(1)}, u32[]{:S(2)}, u32[]{:S(2)}) collective-permute-start(bf16[64,3712]{1,0:T(8,128)(2,1)S(1)} %collective-permute-done.2.refs_2_), channel_id=1, source_target_pairs={{0,96},{1,33},{2,98},{3,35},{4,100},{5,37},{6,102},{7,39},{8,104},... | collective-permute-start | bytes 1425416 | tf_op jit(solution)/shard_map/ppermute | solution.py:77
  31.6 18.4 %collective-permute-start.5 = (bf16[64,3712]{1,0:T(8,128)(2,1)S(1)}, bf16[64,3712]{1,0:T(8,128)(2,1)S(1)}, u32[]{:S(2)}, u32[]{:S(2)}) collective-permute-start(bf16[64,3712]{1,0:T(8,128)(2,1)S(1)} %collective-permute-done.4.refs_0_), channel_id=1, source_target_pairs={{0,6},{1,3},{2,4},{3,1},{4,2},{5,7},{6,0},{7,5},{8,14},{9,11},{10,... | collective-permute-start | bytes 1425416 | tf_op jit(solution)/shard_map/ppermute | solution.py:77
  31.6 18.4 %collective-permute-start.6 = (bf16[64,3712]{1,0:T(8,128)(2,1)S(1)}, bf16[64,3712]{1,0:T(8,128)(2,1)S(1)}, u32[]{:S(2)}, u32[]{:S(2)}) collective-permute-start(bf16[64,3712]{1,0:T(8,128)(2,1)S(1)} %collective-permute-done.2.refs_2_), channel_id=1, source_target_pairs={{0,120},{1,41},{2,122},{3,43},{4,124},{5,45},{6,126},{7,47},{8,112... | collective-permute-start | bytes 1425416 | tf_op jit(solution)/shard_map/ppermute | solution.py:77
  32.8 16.1 %slice-start = ((s8[7340032]{0:T(1024)(128)(4,1)}), s8[4194304]{0:T(1024)(128)(4,1)S(1)}, s32[]{:S(2)}) async-start(s8[7340032]{0:T(1024)(128)(4,1)} %bitcast.14), calls=%async_computation.2 | async-start | bytes 8388608
  43.0 2.5 %collective-permute-start.7 = (bf16[64,2560]{1,0:T(8,128)(2,1)S(1)}, bf16[64,2560]{1,0:T(8,128)(2,1)S(1)}, u32[]{:S(2)}, u32[]{:S(2)}) collective-permute-start(bf16[64,2560]{1,0:T(8,128)(2,1)S(1)} %get-tuple-element.44), channel_id=1, source_target_pairs={{0,1},{1,0},{2,3},{3,2},{4,5},{5,4},{6,7},{7,6},{8,9},{9,8},{10,11... | collective-permute-start | bytes 983048 | tf_op jit(solution)/shard_map/ppermute | solution.py:81
  43.0 2.5 %collective-permute-start.8 = (bf16[64,2560]{1,0:T(8,128)(2,1)S(1)}, bf16[64,2560]{1,0:T(8,128)(2,1)S(1)}, u32[]{:S(2)}, u32[]{:S(2)}) collective-permute-start(bf16[64,2560]{1,0:T(8,128)(2,1)S(1)} %get-tuple-element.45), channel_id=1, source_target_pairs={{0,1},{1,0},{2,3},{3,2},{4,5},{5,4},{6,7},{7,6},{8,9},{9,8},{10,11... | collective-permute-start | bytes 983048 | tf_op jit(solution)/shard_map/ppermute | solution.py:81
  43.5 2.0 %collective-permute-start.9 = (bf16[64,2176]{1,0:T(8,128)(2,1)S(1)}, bf16[64,2176]{1,0:T(8,128)(2,1)S(1)}, u32[]{:S(2)}, u32[]{:S(2)}) collective-permute-start(bf16[64,2176]{1,0:T(8,128)(2,1)S(1)} %get-tuple-element.46), channel_id=1, source_target_pairs={{0,1},{1,0},{2,3},{3,2},{4,5},{5,4},{6,7},{7,6},{8,9},{9,8},{10,11... | collective-permute-start | bytes 835592 | tf_op jit(solution)/shard_map/ppermute | solution.py:81
  45.5 3.3 %slice-start.1 = ((s8[7340032]{0:T(1024)(128)(4,1)}), s8[3145728]{0:T(1024)(128)(4,1)S(1)}, s32[]{:S(2)}) async-start(s8[7340032]{0:T(1024)(128)(4,1)} %bitcast.14), calls=%async_computation.3 | async-start | bytes 6291456
  50.0 2.6 %collective-permute-start.13 = (bf16[64,7168]{1,0:T(8,128)(2,1)S(1)}, bf16[64,7168]{1,0:T(8,128)(2,1)S(1)}, u32[]{:S(2)}, u32[]{:S(2)}) collective-permute-start(bf16[64,7168]{1,0:T(8,128)(2,1)S(1)} %get-tuple-element.60), channel_id=1, source_target_pairs={{0,1},{1,0},{2,3},{3,2},{4,5},{5,4},{6,7},{7,6},{8,9},{9,8},{10,11... | collective-permute-start | bytes 2752520 | tf_op jit(solution)/shard_map/ppermute | solution.py:81
  51.1 2.8 %collective-permute-start.10 = (bf16[64,2560]{1,0:T(8,128)(2,1)S(1)}, bf16[64,2560]{1,0:T(8,128)(2,1)S(1)}, u32[]{:S(2)}, u32[]{:S(2)}) collective-permute-start(bf16[64,2560]{1,0:T(8,128)(2,1)S(1)} %get-tuple-element.56), channel_id=1, source_target_pairs={{0,1},{1,0},{2,3},{3,2},{4,5},{5,4},{6,7},{7,6},{8,9},{9,8},{10,11... | collective-permute-start | bytes 983048 | tf_op jit(solution)/shard_map/ppermute | solution.py:81
  51.6 2.3 %collective-permute-start.11 = (bf16[64,2560]{1,0:T(8,128)(2,1)S(1)}, bf16[64,2560]{1,0:T(8,128)(2,1)S(1)}, u32[]{:S(2)}, u32[]{:S(2)}) collective-permute-start(bf16[64,2560]{1,0:T(8,128)(2,1)S(1)} %get-tuple-element.57), channel_id=1, source_target_pairs={{0,1},{1,0},{2,3},{3,2},{4,5},{5,4},{6,7},{7,6},{8,9},{9,8},{10,11... | collective-permute-start | bytes 983048 | tf_op jit(solution)/shard_map/ppermute | solution.py:81
  51.7 2.2 %collective-permute-start.12 = (bf16[64,2176]{1,0:T(8,128)(2,1)S(1)}, bf16[64,2176]{1,0:T(8,128)(2,1)S(1)}, u32[]{:S(2)}, u32[]{:S(2)}) collective-permute-start(bf16[64,2176]{1,0:T(8,128)(2,1)S(1)} %get-tuple-element.58), channel_id=1, source_target_pairs={{0,1},{1,0},{2,3},{3,2},{4,5},{5,4},{6,7},{7,6},{8,9},{9,8},{10,11... | collective-permute-start | bytes 835592 | tf_op jit(solution)/shard_map/ppermute | solution.py:81
  57.1 2.7 %collective-permute-start.14 = (bf16[64,7168]{1,0:T(8,128)(2,1)S(1)}, bf16[64,7168]{1,0:T(8,128)(2,1)S(1)}, u32[]{:S(2)}, u32[]{:S(2)}) collective-permute-start(bf16[64,7168]{1,0:T(8,128)(2,1)S(1)} %get-tuple-element.63), channel_id=1, source_target_pairs={{0,1},{1,0},{2,3},{3,2},{4,5},{5,4},{6,7},{7,6},{8,9},{9,8},{10,11... | collective-permute-start | bytes 2752520 | tf_op jit(solution)/shard_map/ppermute | solution.py:81
  60.9 7.7 %collective-permute-start.20 = (bf16[64,3584]{1,0:T(8,128)(2,1)S(1)}, bf16[64,3584]{1,0:T(8,128)(2,1)S(1)}, u32[]{:S(2)}, u32[]{:S(2)}) collective-permute-start(bf16[64,3584]{1,0:T(8,128)(2,1)S(1)} %get-tuple-element.70), channel_id=1, source_target_pairs={{0,96},{1,33},{2,98},{3,35},{4,100},{5,37},{6,102},{7,39},{8,104},... | collective-permute-start | bytes 1376264 | tf_op jit(solution)/shard_map/ppermute | solution.py:77
  62.1 7.6 %collective-permute-start.18 = (bf16[64,3584]{1,0:T(8,128)(2,1)S(1)}, bf16[64,3584]{1,0:T(8,128)(2,1)S(1)}, u32[]{:S(2)}, u32[]{:S(2)}) collective-permute-start(bf16[64,3584]{1,0:T(8,128)(2,1)S(1)} %get-tuple-element.68), channel_id=1, source_target_pairs={{0,24},{1,9},{2,26},{3,11},{4,28},{5,13},{6,30},{7,15},{8,16},{9,1... | collective-permute-start | bytes 1376264 | tf_op jit(solution)/shard_map/ppermute | solution.py:77
  62.1 12.5 %collective-permute-start.16 = (bf16[64,3584]{1,0:T(8,128)(2,1)S(1)}, bf16[64,3584]{1,0:T(8,128)(2,1)S(1)}, u32[]{:S(2)}, u32[]{:S(2)}) collective-permute-start(bf16[64,3584]{1,0:T(8,128)(2,1)S(1)} %get-tuple-element.66), channel_id=1, source_target_pairs={{0,6},{1,3},{2,4},{3,1},{4,2},{5,7},{6,0},{7,5},{8,14},{9,11},{10,... | collective-permute-start | bytes 1376264 | tf_op jit(solution)/shard_map/ppermute | solution.py:77
  62.1 14.2 %collective-permute-start.15 = (bf16[64,3584]{1,0:T(8,128)(2,1)S(1)}, bf16[64,3584]{1,0:T(8,128)(2,1)S(1)}, u32[]{:S(2)}, u32[]{:S(2)}) collective-permute-start(bf16[64,3584]{1,0:T(8,128)(2,1)S(1)} %get-tuple-element.64), channel_id=1, source_target_pairs={{0,126},{1,43},{2,124},{3,41},{4,122},{5,47},{6,120},{7,45},{8,118... | collective-permute-start | bytes 1376264 | tf_op jit(solution)/shard_map/ppermute | solution.py:77
  68.7 10.9 %collective-permute-start.21 = (bf16[64,3584]{1,0:T(8,128)(2,1)S(1)}, bf16[64,3584]{1,0:T(8,128)(2,1)S(1)}, u32[]{:S(2)}, u32[]{:S(2)}) collective-permute-start(bf16[64,3584]{1,0:T(8,128)(2,1)S(1)} %add_convert_fusion.1), channel_id=1, source_target_pairs={{0,6},{1,3},{2,4},{3,1},{4,2},{5,7},{6,0},{7,5},{8,14},{9,11},{10,... | collective-permute-start | bytes 1376264 | tf_op jit(solution)/shard_map/ppermute | solution.py:77
  69.9 9.7 %collective-permute-start.19 = (bf16[64,3584]{1,0:T(8,128)(2,1)S(1)}, bf16[64,3584]{1,0:T(8,128)(2,1)S(1)}, u32[]{:S(2)}, u32[]{:S(2)}) collective-permute-start(bf16[64,3584]{1,0:T(8,128)(2,1)S(1)} %add_convert_fusion.2), channel_id=1, source_target_pairs={{0,96},{1,33},{2,98},{3,35},{4,100},{5,37},{6,102},{7,39},{8,104},... | collective-permute-start | bytes 1376264 | tf_op jit(solution)/shard_map/ppermute | solution.py:77
  74.8 7.7 %collective-permute-start.17 = (bf16[64,3584]{1,0:T(8,128)(2,1)S(1)}, bf16[64,3584]{1,0:T(8,128)(2,1)S(1)}, u32[]{:S(2)}, u32[]{:S(2)}) collective-permute-start(bf16[64,3584]{1,0:T(8,128)(2,1)S(1)} %add_convert_fusion.3), channel_id=1, source_target_pairs={{0,24},{1,9},{2,26},{3,11},{4,28},{5,13},{6,30},{7,15},{8,16},{9,1... | collective-permute-start | bytes 1376264 | tf_op jit(solution)/shard_map/ppermute | solution.py:77

commit v9 on v5

--- a/solution.py
+++ b/solution.py
@@ -58,10 +58,10 @@
         for x in range(4):
             for y in range(4):
                 for c in range(2):
-                    at = [z, x, y]
+                    at = [x, y, z]
                     for axis in axes:
                         at[axis] ^= 1 if c else 3
-                    pairs.append((flat(z, x, y, c), flat(*at, c)))
+                    pairs.append((flat(z, x, y, c), flat(at[2], at[0], at[1], c)))
     return pairs
 
 
@@ -342,7 +342,7 @@
     returned = to_sibling(theirs)
     y_x, y_y, y_z, y_own = spread(expert, near, result_near, returned_near, result)
     y_xy, y_zx, y_yz, y_xyz = spread(expert, far, result, returned, y_own)
-    at_y, at_z, at_x = swap_far(y_xy, 0), swap_far(y_yz, 1), swap_far(y_zx, 2)
+    at_y, at_x, at_z = swap_far(y_yz, 2), swap_far(y_xy, 1), swap_far(y_zx, 0)
     at_own = swap_far(y_xyz, 3)
     total = add(
         y_own,

time: 93.6 us -> 92.6 us (0.989)
  transfers between devices with their start and end apart: 18 -> 18, of which waited for: 10 -> 12; matrix products, arithmetic and copies ran while one was open for 0% -> 0% of each run, Pallas kernels for 13% -> 13%
where the time goes in v9:
time: 92.6 us; the launch traced here: 92.4 us
  blocking collectives  36.5 us (39%)
  waiting for transfers between devices  27.8 us (30%)
  Pallas kernels  14.8 us (16%)
  starting transfers between devices  12.5 us (13%)
    all_to_all x2, blocking collectives, swap_near(): lax.all_to_all(values, AXES, 0, 0, axis_index_groups=NEAR, tiled=True)  36.5 us
    ppermute x14, waiting for transfers between devices, swap_far(): return lax.ppermute(values, AXES, FAR[axis])  25.8 us
    ppermute x14, starting transfers between devices, swap_far(): return lax.ppermute(values, AXES, FAR[axis])  11.2 us
    pallas_call x2, Pallas kernels, hidden_units(): pl.pallas_call(functools.partial(hidden_kernel, streams), out_shape=[jax....  4.93 us
    pallas_call x2, Pallas kernels, select(): pl.pallas_call(functools.partial(select_kernel, len(loads)), out_shape=[j...  3.66 us
    pallas_call x2, Pallas kernels, down_rows(): pl.pallas_call(down_kernel, out_shape=[jax.ShapeDtypeStruct((SEL, D), BF1...  2.26 us
    pallas_call x2, Pallas kernels, spread(): pl.pallas_call(spread_kernel, out_shape=[jax.ShapeDtypeStruct((BLOCK, HAL...  2.13 us
    ppermute x4, waiting for transfers between devices, to_sibling(): return lax.ppermute(values, 'dev', [(i, i ^ 1) for i in range(32)])  2.02 us
  transfers between devices with their start and end apart: 18, of which 12 were waited for; matrix products, arithmetic and copies ran while one was open for 0% of the time, Pallas kernels for 13%

profile of v9, /device:TPU:1, one launch (start us, length us, event | category | flops | bytes accessed | tf_op | source)
XLA Modules:
  0.0 92.4 jit_solution(7404054307231403231)
XLA Ops:
  0.0 1.1 %pack.1 = bf16[8,8,3712]{2,1,0:T(8,128)(2,1)S(1)} custom-call(s32[1]{0:T(128)} %bitcast.expert_ref, bf16[4,7168]{1,0:T(4,128)(2,1)} %tokens_hbm.1, s32[4,8]{1,0:T(4,128)} %ids_hbm.1, f32[4,8]{1,0:T(4,128)} %weights_hbm.1), custom_call_target="tpu_custom_call" | custom-call | tf_op jit(solution)/shard_map/pack/pallas_call | solution.py:111
  1.1 20.9 %all_to_all.10 = bf16[8,8,3712]{2,1,0:T(8,128)(2,1)S(1)} all-to-all(bf16[8,8,3712]{2,1,0:T(8,128)(2,1)S(1)} %pack.1), channel_id=1, replica_groups={{0,2,8,10,32,34,40,42},{1,7,25,31,97,103,121,127},{3,5,27,29,99,101,123..., dimensions={0} | all-to-all | bytes 950272 | tf_op jit(solution)/shard_map/all_to_all | solution.py:73
  22.1 3.7 %collective-permute-start.6 = (bf16[64,3712]{1,0:T(8,128)(2,1)S(1)}, bf16[64,3712]{1,0:T(8,128)(2,1)S(1)}, u32[]{:S(2)}, u32[]{:S(2)}) collective-permute-start(bf16[64,3712]{1,0:T(8,128)(2,1)S(1)} %bitcast.11), channel_id=1, source_target_pairs={{0,126},{1,43},{2,124},{3,41},{4,122},{5,47},{6,120},{7,45},{8,118... | collective-permute-start | bytes 1425416 | tf_op jit(solution)/shard_map/ppermute | solution.py:77
  25.9 3.7 %collective-permute-done.2.refs_2_ = bf16[64,3712]{1,0:T(8,128)(2,1)S(1)} collective-permute-done((bf16[64,3712]{1,0:T(8,128)(2,1)S(1)}, bf16[64,3712]{1,0:T(8,128)(2,1)S(1)}, u32[]{:S(2)}, u32[]{:S(2)}) %collective-permute-start.2) | collective-permute-done | bytes 475168 | tf_op jit(solution)/shard_map/ppermute | solution.py:77
  29.6 1.7 %collective-permute-start.5 = (bf16[64,3712]{1,0:T(8,128)(2,1)S(1)}, bf16[64,3712]{1,0:T(8,128)(2,1)S(1)}, u32[]{:S(2)}, u32[]{:S(2)}) collective-permute-start(bf16[64,3712]{1,0:T(8,128)(2,1)S(1)} %collective-permute-done.refs_0_), channel_id=1, source_target_pairs={{0,96},{1,33},{2,98},{3,35},{4,100},{5,37},{6,102},{7,39},{8,104},... | collective-permute-start | bytes 1425416 | tf_op jit(solution)/shard_map/ppermute | solution.py:77
  31.3 2.8 %select.2 = (bf16[64,7296]{1,0:T(8,128)(2,1)S(1)}, bf16[64,7296]{1,0:T(8,128)(2,1)S(1)}, bf16[1,3584,512]{2,1,0:T(8,128)(2,1)S(1)}) custom-call(s32[1]{0:T(128)} %bitcast.expert_ref, bf16[64,3712]{1,0:T(8,128)(2,1)S(1)} %collective-permute-done.refs_0_, bf16[64,3712]{1,0:T(8,128)(2,1)S(1)} %collective-permute-done.1.refs_1_, ...), custom_call_target="tpu_custom_call" | custom-call | flops 1000 | bytes 1000 | tf_op jit(solution)/shard_map/select/pallas_call | solution.py:177
  34.1 3.1 %collective-permute-done.6.refs_3_ = bf16[64,3712]{1,0:T(8,128)(2,1)S(1)} collective-permute-done((bf16[64,3712]{1,0:T(8,128)(2,1)S(1)}, bf16[64,3712]{1,0:T(8,128)(2,1)S(1)}, u32[]{:S(2)}, u32[]{:S(2)}) %collective-permute-start.6) | collective-permute-done | bytes 475168 | tf_op jit(solution)/shard_map/ppermute | solution.py:77
  37.2 3.9 %collective-permute-done.4.refs_2_ = bf16[64,3712]{1,0:T(8,128)(2,1)S(1)} collective-permute-done((bf16[64,3712]{1,0:T(8,128)(2,1)S(1)}, bf16[64,3712]{1,0:T(8,128)(2,1)S(1)}, u32[]{:S(2)}, u32[]{:S(2)}) %collective-permute-start.4) | collective-permute-done | bytes 475168 | tf_op jit(solution)/shard_map/ppermute | solution.py:77
  41.1 1.1 %collective-permute-done.5.refs_1_ = bf16[64,3712]{1,0:T(8,128)(2,1)S(1)} collective-permute-done((bf16[64,3712]{1,0:T(8,128)(2,1)S(1)}, bf16[64,3712]{1,0:T(8,128)(2,1)S(1)}, u32[]{:S(2)}, u32[]{:S(2)}) %collective-permute-start.5) | collective-permute-done | bytes 475168 | tf_op jit(solution)/shard_map/ppermute | solution.py:77
  42.1 0.9 select.3
  43.0 0.6 collective-permute-start.9
  43.6 1.0 %collective-permute-done.7.theirs_ref = bf16[64,7296]{1,0:T(8,128)(2,1)S(1)} collective-permute-done((bf16[64,7296]{1,0:T(8,128)(2,1)S(1)}, bf16[64,7296]{1,0:T(8,128)(2,1)S(1)}, u32[]{:S(2)}, u32[]{:S(2)}) %collective-permute-start.7) | collective-permute-done | bytes 933920 | tf_op jit(solution)/shard_map/ppermute | solution.py:81
  44.6 2.9 %hidden.2 = (bf16[128,512]{1,0:T(8,128)(2,1)S(1)}, bf16[1,3584,512]{2,1,0:T(8,128)(2,1)S(1)}) custom-call(s32[1]{0:T(128)} %bitcast.expert_ref, bf16[64,7296]{1,0:T(8,128)(2,1)S(1)} %get-tuple-element.29.mine_ref, bf16[64,7296]{1,0:T(8,128)(2,1)S(1)} %collective-permute-done.7.theirs_ref, bf16[1,7168,512]{2,1,0:T(8,128)(2,1)S(1)} %bitcast.5, ...), custom_call_target="tpu_custom_call" | custom-call | flops 1000 | bytes 1000 | tf_op jit(solution)/shard_map/hidden/pallas_call | solution.py:221
  47.6 1.1 %down.2 = (bf16[64,7168]{1,0:T(8,128)(2,1)S(1)}, bf16[64,7168]{1,0:T(8,128)(2,1)S(1)}) custom-call(bf16[128,512]{1,0:T(8,128)(2,1)S(1)} %get-tuple-element.38.hidden_ref, bf16[1,512,7168]{2,1,0:T(8,128)(2,1)S(1)} %bitcast.7, bf16[64,3712]{1,0:T(8,128)(2,1)S(1)} %bitcast.15), custom_call_target="tpu_custom_call" | custom-call | flops 1000 | bytes 1000 | tf_op jit(solution)/shard_map/down/pallas_call | solution.py:243
  49.0 2.1 %hidden.3.hidden_ref = bf16[128,512]{1,0:T(8,128)(2,1)S(1)} custom-call(s32[1]{0:T(128)} %bitcast.expert_ref, bf16[64,7296]{1,0:T(8,128)(2,1)S(1)} %get-tuple-element.37.after_ref.mine_ref, bf16[64,7296]{1,0:T(8,128)(2,1)S(1)} %collective-permute-done.9.theirs_ref, bf16[1,7168,512]{2,1,0:T(8,128)(2,1)S(1)} %bitcast.5, ...), custom_call_target="tpu_custom_call" | custom-call | flops 1000 | bytes 1000 | tf_op jit(solution)/shard_map/hidden/pallas_call | solution.py:221
  51.1 1.1 %down.3 = (bf16[64,7168]{1,0:T(8,128)(2,1)S(1)}, bf16[64,7168]{1,0:T(8,128)(2,1)S(1)}) custom-call(bf16[128,512]{1,0:T(8,128)(2,1)S(1)} %hidden.3.hidden_ref, bf16[1,512,7168]{2,1,0:T(8,128)(2,1)S(1)} %bitcast.7, bf16[64,3712]{1,0:T(8,128)(2,1)S(1)} %bitcast.16), custom_call_target="tpu_custom_call" | custom-call | flops 1000 | bytes 1000 | tf_op jit(solution)/shard_map/down/pallas_call | solution.py:243
  52.2 0.5 collective-permute-start.10
  52.7 1.1 %spread.2 = (bf16[64,3584]{1,0:T(8,128)(2,1)S(1)}, bf16[64,3584]{1,0:T(8,128)(2,1)S(1)}, bf16[64,3584]{1,0:T(8,128)(2,1)S(1)}, bf16[64,3584]{1,0:T(8,128)(2,1)S(1)}) custom-call(s32[1]{0:T(128)} %bitcast.expert_ref, bf16[64,3712]{1,0:T(8,128)(2,1)S(1)} %collective-permute-done.refs_0_, bf16[64,3712]{1,0:T(8,128)(2,1)S(1)} %collective-permute-done.1.refs_1_, ...), custom_call_target="tpu_custom_call" | custom-call | flops 1000 | bytes 1000 | tf_op jit(solution)/shard_map/spread/pallas_call | solution.py:286
  53.7 1.0 %collective-permute-done.10.refs_5_ = bf16[64,7168]{1,0:T(8,128)(2,1)S(1)} collective-permute-done((bf16[64,7168]{1,0:T(8,128)(2,1)S(1)}, bf16[64,7168]{1,0:T(8,128)(2,1)S(1)}, u32[]{:S(2)}, u32[]{:S(2)}) %collective-permute-start.10) | collective-permute-done | bytes 917536 | tf_op jit(solution)/shard_map/ppermute | solution.py:81
  54.8 1.1 %spread.3 = (bf16[64,3584]{1,0:T(8,128)(2,1)S(1)}, bf16[64,3584]{1,0:T(8,128)(2,1)S(1)}, bf16[64,3584]{1,0:T(8,128)(2,1)S(1)}, bf16[64,3584]{1,0:T(8,128)(2,1)S(1)}) custom-call(s32[1]{0:T(128)} %bitcast.expert_ref, bf16[64,3712]{1,0:T(8,128)(2,1)S(1)} %collective-permute-done.3.refs_0_, bf16[64,3712]{1,0:T(8,128)(2,1)S(1)} %collective-permute-done.5.refs_1_, ...), custom_call_target="tpu_custom_call" | custom-call | flops 1000 | bytes 1000 | tf_op jit(solution)/shard_map/spread/pallas_call | solution.py:286
  56.0 0.5 collective-permute-start.13
  56.6 3.2 %collective-permute-start.17 = (bf16[64,3584]{1,0:T(8,128)(2,1)S(1)}, bf16[64,3584]{1,0:T(8,128)(2,1)S(1)}, u32[]{:S(2)}, u32[]{:S(2)}) collective-permute-start(bf16[64,3584]{1,0:T(8,128)(2,1)S(1)} %get-tuple-element.52), channel_id=1, source_target_pairs={{0,126},{1,43},{2,124},{3,41},{4,122},{5,47},{6,120},{7,45},{8,118... | collective-permute-start | bytes 1376264 | tf_op jit(solution)/shard_map/ppermute | solution.py:77
  59.8 3.8 %collective-permute-done.11 = bf16[64,3584]{1,0:T(8,128)(2,1)S(1)} collective-permute-done((bf16[64,3584]{1,0:T(8,128)(2,1)S(1)}, bf16[64,3584]{1,0:T(8,128)(2,1)S(1)}, u32[]{:S(2)}, u32[]{:S(2)}) %collective-permute-start.11) | collective-permute-done | bytes 458784 | tf_op jit(solution)/shard_map/ppermute | solution.py:77
  63.9 1.3 %collective-permute-start.14 = (bf16[64,3584]{1,0:T(8,128)(2,1)S(1)}, bf16[64,3584]{1,0:T(8,128)(2,1)S(1)}, u32[]{:S(2)}, u32[]{:S(2)}) collective-permute-start(bf16[64,3584]{1,0:T(8,128)(2,1)S(1)} %add_convert_fusion.2), channel_id=1, source_target_pairs={{0,6},{1,3},{2,4},{3,1},{4,2},{5,7},{6,0},{7,5},{8,14},{9,11},{10,... | collective-permute-start | bytes 1376264 | tf_op jit(solution)/shard_map/ppermute | solution.py:77
  65.3 0.4 collective-permute-start.16
  65.7 5.1 %collective-permute-done.17 = bf16[64,3584]{1,0:T(8,128)(2,1)S(1)} collective-permute-done((bf16[64,3584]{1,0:T(8,128)(2,1)S(1)}, bf16[64,3584]{1,0:T(8,128)(2,1)S(1)}, u32[]{:S(2)}, u32[]{:S(2)}) %collective-permute-start.17) | collective-permute-done | bytes 458784 | tf_op jit(solution)/shard_map/ppermute | solution.py:77
  70.7 3.3 %collective-permute-done.12 = bf16[64,3584]{1,0:T(8,128)(2,1)S(1)} collective-permute-done((bf16[64,3584]{1,0:T(8,128)(2,1)S(1)}, bf16[64,3584]{1,0:T(8,128)(2,1)S(1)}, u32[]{:S(2)}, u32[]{:S(2)}) %collective-permute-start.12) | collective-permute-done | bytes 458784 | tf_op jit(solution)/shard_map/ppermute | solution.py:77
  74.0 0.8 collective-permute-done.14
  74.8 1.0 %collective-permute-done.16 = bf16[64,3584]{1,0:T(8,128)(2,1)S(1)} collective-permute-done((bf16[64,3584]{1,0:T(8,128)(2,1)S(1)}, bf16[64,3584]{1,0:T(8,128)(2,1)S(1)}, u32[]{:S(2)}, u32[]{:S(2)}) %collective-permute-start.16) | collective-permute-done | bytes 458784 | tf_op jit(solution)/shard_map/ppermute | solution.py:77
  75.8 0.3 fusion
  76.1 15.6 %all_to_all.11.parts_ref = bf16[8,8,3584]{2,1,0:T(8,128)(2,1)S(1)} all-to-all(bf16[8,8,3584]{2,1,0:T(8,128)(2,1)S(1)} %fusion), channel_id=1, replica_groups={{0,2,8,10,32,34,40,42},{1,7,25,31,97,103,121,127},{3,5,27,29,99,101,123..., dimensions={0} | all-to-all | bytes 917504 | tf_op jit(solution)/shard_map/all_to_all | solution.py:73
  91.7 0.7 finish.1
  (30 shorter events, 1.3 us)
Async XLA Ops:
  0.0 44.6 %slice-start = ((s8[7340032]{0:T(1024)(128)(4,1)}), s8[3145728]{0:T(1024)(128)(4,1)S(1)}, s32[]{:S(2)}) async-start(s8[7340032]{0:T(1024)(128)(4,1)} %bitcast.4), calls=%async_computation.2 | async-start | bytes 6291456
  22.0 22.6 %slice-start.1 = ((s8[7340032]{0:T(1024)(128)(4,1)}), s8[4194304]{0:T(1024)(128)(4,1)S(1)}, s32[]{:S(2)}) async-start(s8[7340032]{0:T(1024)(128)(4,1)} %bitcast.4), calls=%async_computation.3 | async-start | bytes 8388608
  22.0 7.5 %collective-permute-start.2 = (bf16[64,3712]{1,0:T(8,128)(2,1)S(1)}, bf16[64,3712]{1,0:T(8,128)(2,1)S(1)}, u32[]{:S(2)}, u32[]{:S(2)}) collective-permute-start(bf16[64,3712]{1,0:T(8,128)(2,1)S(1)} %bitcast.8), channel_id=1, source_target_pairs={{0,96},{1,33},{2,98},{3,35},{4,100},{5,37},{6,102},{7,39},{8,104},... | collective-permute-start | bytes 1425416 | tf_op jit(solution)/shard_map/ppermute | solution.py:77
  22.0 7.5 %collective-permute-start.1 = (bf16[64,3712]{1,0:T(8,128)(2,1)S(1)}, bf16[64,3712]{1,0:T(8,128)(2,1)S(1)}, u32[]{:S(2)}, u32[]{:S(2)}) collective-permute-start(bf16[64,3712]{1,0:T(8,128)(2,1)S(1)} %bitcast.9), channel_id=1, source_target_pairs={{0,6},{1,3},{2,4},{3,1},{4,2},{5,7},{6,0},{7,5},{8,14},{9,11},{10,... | collective-permute-start | bytes 1425416 | tf_op jit(solution)/shard_map/ppermute | solution.py:77
  22.1 7.6 %collective-permute-start = (bf16[64,3712]{1,0:T(8,128)(2,1)S(1)}, bf16[64,3712]{1,0:T(8,128)(2,1)S(1)}, u32[]{:S(2)}, u32[]{:S(2)}) collective-permute-start(bf16[64,3712]{1,0:T(8,128)(2,1)S(1)} %bitcast.10), channel_id=1, source_target_pairs={{0,24},{1,9},{2,26},{3,11},{4,28},{5,13},{6,30},{7,15},{8,16},{9,1... | collective-permute-start | bytes 1425416 | tf_op jit(solution)/shard_map/ppermute | solution.py:77
  22.1 15.0 %collective-permute-start.6 = (bf16[64,3712]{1,0:T(8,128)(2,1)S(1)}, bf16[64,3712]{1,0:T(8,128)(2,1)S(1)}, u32[]{:S(2)}, u32[]{:S(2)}) collective-permute-start(bf16[64,3712]{1,0:T(8,128)(2,1)S(1)} %bitcast.11), channel_id=1, source_target_pairs={{0,126},{1,43},{2,124},{3,41},{4,122},{5,47},{6,120},{7,45},{8,118... | collective-permute-start | bytes 1425416 | tf_op jit(solution)/shard_map/ppermute | solution.py:77
  29.5 11.5 %collective-permute-start.4 = (bf16[64,3712]{1,0:T(8,128)(2,1)S(1)}, bf16[64,3712]{1,0:T(8,128)(2,1)S(1)}, u32[]{:S(2)}, u32[]{:S(2)}) collective-permute-start(bf16[64,3712]{1,0:T(8,128)(2,1)S(1)} %collective-permute-done.2.refs_2_), channel_id=1, source_target_pairs={{0,6},{1,3},{2,4},{3,1},{4,2},{5,7},{6,0},{7,5},{8,14},{9,11},{10,... | collective-permute-start | bytes 1425416 | tf_op jit(solution)/shard_map/ppermute | solution.py:77
  29.6 11.5 %collective-permute-start.3 = (bf16[64,3712]{1,0:T(8,128)(2,1)S(1)}, bf16[64,3712]{1,0:T(8,128)(2,1)S(1)}, u32[]{:S(2)}, u32[]{:S(2)}) collective-permute-start(bf16[64,3712]{1,0:T(8,128)(2,1)S(1)} %collective-permute-done.1.refs_1_), channel_id=1, source_target_pairs={{0,24},{1,9},{2,26},{3,11},{4,28},{5,13},{6,30},{7,15},{8,16},{9,1... | collective-permute-start | bytes 1425416 | tf_op jit(solution)/shard_map/ppermute | solution.py:77
  29.6 12.5 %collective-permute-start.5 = (bf16[64,3712]{1,0:T(8,128)(2,1)S(1)}, bf16[64,3712]{1,0:T(8,128)(2,1)S(1)}, u32[]{:S(2)}, u32[]{:S(2)}) collective-permute-start(bf16[64,3712]{1,0:T(8,128)(2,1)S(1)} %collective-permute-done.refs_0_), channel_id=1, source_target_pairs={{0,96},{1,33},{2,98},{3,35},{4,100},{5,37},{6,102},{7,39},{8,104},... | collective-permute-start | bytes 1425416 | tf_op jit(solution)/shard_map/ppermute | solution.py:77
  42.1 2.5 %collective-permute-start.7 = (bf16[64,7296]{1,0:T(8,128)(2,1)S(1)}, bf16[64,7296]{1,0:T(8,128)(2,1)S(1)}, u32[]{:S(2)}, u32[]{:S(2)}) collective-permute-start(bf16[64,7296]{1,0:T(8,128)(2,1)S(1)} %get-tuple-element.31), channel_id=1, source_target_pairs={{0,1},{1,0},{2,3},{3,2},{4,5},{5,4},{6,7},{7,6},{8,9},{9,8},{10,11... | collective-permute-start | bytes 2801672 | tf_op jit(solution)/shard_map/ppermute | solution.py:81
  42.1 5.4 %slice-start.2 = ((s8[7340032]{0:T(1024)(128)(4,1)}), s8[4194304]{0:T(1024)(128)(4,1)S(1)}, s32[]{:S(2)}) async-start(s8[7340032]{0:T(1024)(128)(4,1)} %bitcast.6), calls=%async_computation.4 | async-start | bytes 8388608
  43.0 6.0 %collective-permute-start.9 = (bf16[64,7296]{1,0:T(8,128)(2,1)S(1)}, bf16[64,7296]{1,0:T(8,128)(2,1)S(1)}, u32[]{:S(2)}, u32[]{:S(2)}) collective-permute-start(bf16[64,7296]{1,0:T(8,128)(2,1)S(1)} %get-tuple-element.41), channel_id=1, source_target_pairs={{0,1},{1,0},{2,3},{3,2},{4,5},{5,4},{6,7},{7,6},{8,9},{9,8},{10,11... | collective-permute-start | bytes 2801672 | tf_op jit(solution)/shard_map/ppermute | solution.py:81
  44.6 3.0 %slice-start.3 = ((s8[7340032]{0:T(1024)(128)(4,1)}), s8[3145728]{0:T(1024)(128)(4,1)S(1)}, s32[]{:S(2)}) async-start(s8[7340032]{0:T(1024)(128)(4,1)} %bitcast.6), calls=%async_computation.5 | async-start | bytes 6291456
  48.8 3.9 %collective-permute-start.8 = (bf16[64,7168]{1,0:T(8,128)(2,1)S(1)}, bf16[64,7168]{1,0:T(8,128)(2,1)S(1)}, u32[]{:S(2)}, u32[]{:S(2)}) collective-permute-start(bf16[64,7168]{1,0:T(8,128)(2,1)S(1)} %get-tuple-element.40), channel_id=1, source_target_pairs={{0,1},{1,0},{2,3},{3,2},{4,5},{5,4},{6,7},{7,6},{8,9},{9,8},{10,11... | collective-permute-start | bytes 2752520 | tf_op jit(solution)/shard_map/ppermute | solution.py:81
  52.2 2.6 %collective-permute-start.10 = (bf16[64,7168]{1,0:T(8,128)(2,1)S(1)}, bf16[64,7168]{1,0:T(8,128)(2,1)S(1)}, u32[]{:S(2)}, u32[]{:S(2)}) collective-permute-start(bf16[64,7168]{1,0:T(8,128)(2,1)S(1)} %get-tuple-element.46), channel_id=1, source_target_pairs={{0,1},{1,0},{2,3},{3,2},{4,5},{5,4},{6,7},{7,6},{8,9},{9,8},{10,11... | collective-permute-start | bytes 2752520 | tf_op jit(solution)/shard_map/ppermute | solution.py:81
  55.8 7.7 %collective-permute-start.11 = (bf16[64,3584]{1,0:T(8,128)(2,1)S(1)}, bf16[64,3584]{1,0:T(8,128)(2,1)S(1)}, u32[]{:S(2)}, u32[]{:S(2)}) collective-permute-start(bf16[64,3584]{1,0:T(8,128)(2,1)S(1)} %get-tuple-element.47), channel_id=1, source_target_pairs={{0,6},{1,3},{2,4},{3,1},{4,2},{5,7},{6,0},{7,5},{8,14},{9,11},{10,... | collective-permute-start | bytes 1376264 | tf_op jit(solution)/shard_map/ppermute | solution.py:77
  56.0 7.8 %collective-permute-start.13 = (bf16[64,3584]{1,0:T(8,128)(2,1)S(1)}, bf16[64,3584]{1,0:T(8,128)(2,1)S(1)}, u32[]{:S(2)}, u32[]{:S(2)}) collective-permute-start(bf16[64,3584]{1,0:T(8,128)(2,1)S(1)} %get-tuple-element.49), channel_id=1, source_target_pairs={{0,96},{1,33},{2,98},{3,35},{4,100},{5,37},{6,102},{7,39},{8,104},... | collective-permute-start | bytes 1376264 | tf_op jit(solution)/shard_map/ppermute | solution.py:77
  56.5 8.7 %collective-permute-start.15 = (bf16[64,3584]{1,0:T(8,128)(2,1)S(1)}, bf16[64,3584]{1,0:T(8,128)(2,1)S(1)}, u32[]{:S(2)}, u32[]{:S(2)}) collective-permute-start(bf16[64,3584]{1,0:T(8,128)(2,1)S(1)} %get-tuple-element.51), channel_id=1, source_target_pairs={{0,24},{1,9},{2,26},{3,11},{4,28},{5,13},{6,30},{7,15},{8,16},{9,1... | collective-permute-start | bytes 1376264 | tf_op jit(solution)/shard_map/ppermute | solution.py:77
  56.6 14.2 %collective-permute-start.17 = (bf16[64,3584]{1,0:T(8,128)(2,1)S(1)}, bf16[64,3584]{1,0:T(8,128)(2,1)S(1)}, u32[]{:S(2)}, u32[]{:S(2)}) collective-permute-start(bf16[64,3584]{1,0:T(8,128)(2,1)S(1)} %get-tuple-element.52), channel_id=1, source_target_pairs={{0,126},{1,43},{2,124},{3,41},{4,122},{5,47},{6,120},{7,45},{8,118... | collective-permute-start | bytes 1376264 | tf_op jit(solution)/shard_map/ppermute | solution.py:77
  63.7 10.3 %collective-permute-start.12 = (bf16[64,3584]{1,0:T(8,128)(2,1)S(1)}, bf16[64,3584]{1,0:T(8,128)(2,1)S(1)}, u32[]{:S(2)}, u32[]{:S(2)}) collective-permute-start(bf16[64,3584]{1,0:T(8,128)(2,1)S(1)} %add_convert_fusion.3), channel_id=1, source_target_pairs={{0,24},{1,9},{2,26},{3,11},{4,28},{5,13},{6,30},{7,15},{8,16},{9,1... | collective-permute-start | bytes 1376264 | tf_op jit(solution)/shard_map/ppermute | solution.py:77
  63.9 10.9 %collective-permute-start.14 = (bf16[64,3584]{1,0:T(8,128)(2,1)S(1)}, bf16[64,3584]{1,0:T(8,128)(2,1)S(1)}, u32[]{:S(2)}, u32[]{:S(2)}) collective-permute-start(bf16[64,3584]{1,0:T(8,128)(2,1)S(1)} %add_convert_fusion.2), channel_id=1, source_target_pairs={{0,6},{1,3},{2,4},{3,1},{4,2},{5,7},{6,0},{7,5},{8,14},{9,11},{10,... | collective-permute-start | bytes 1376264 | tf_op jit(solution)/shard_map/ppermute | solution.py:77
  65.3 10.5 %collective-permute-start.16 = (bf16[64,3584]{1,0:T(8,128)(2,1)S(1)}, bf16[64,3584]{1,0:T(8,128)(2,1)S(1)}, u32[]{:S(2)}, u32[]{:S(2)}) collective-permute-start(bf16[64,3584]{1,0:T(8,128)(2,1)S(1)} %add_convert_fusion.1), channel_id=1, source_target_pairs={{0,96},{1,33},{2,98},{3,35},{4,100},{5,37},{6,102},{7,39},{8,104},... | collective-permute-start | bytes 1376264 | tf_op jit(solution)/shard_map/ppermute | solution.py:77

commit v10 on v9

--- a/solution.py
+++ b/solution.py
@@ -25,8 +25,9 @@
 SMALL = pltpu.CompilerParams(vmem_limit_bytes=8 * MIB)
 
 
-DEPTH = 1792
-MIDDLE = D // 2
+STEPS = ((0, 2560), (2560, 5120), (5120, D))
+THREE = (0, 2560, 5120)
+ONE = (0,)
 BRIEF = pl.CostEstimate(flops=1000, bytes_accessed=1000, transcendentals=0)
 
 
@@ -58,10 +59,10 @@
         for x in range(4):
             for y in range(4):
                 for c in range(2):
-                    at = [x, y, z]
+                    at = [x, z, y]
                     for axis in axes:
                         at[axis] ^= 1 if c else 3
-                    pairs.append((flat(z, x, y, c), flat(at[2], at[0], at[1], c)))
+                    pairs.append((flat(z, x, y, c), flat(at[1], at[0], at[2], c)))
     return pairs
 
 
@@ -129,15 +130,14 @@
     return (lane < 64) & (lane % 32 == expert)
 
 
-def select_kernel(loads, expert_ref, *refs):
+def select_kernel(starts, loads, expert_ref, *refs):
     refs = list(refs)
     blocks = [refs.pop(0) for _ in range(4)]
     sources = [refs.pop(0) for _ in range(loads)]
     del refs[0]
-    mine_ref, sent_ref = refs[:2]
-    targets = refs[2 : 2 + loads]
-    pick, sem = refs[2 + loads :]
-    copies = [pltpu.make_async_copy(a.at[:, :MIDDLE, :], b, sem) for a, b in zip(sources, targets)]
+    mine_ref, sent_refs, targets = refs[0], refs[1 : 1 + len(starts)], refs[1 + len(starts) : -2]
+    pick, sem = refs[-2:]
+    copies = [pltpu.make_async_copy(a, b, sem) for a, b in zip(sources, targets)]
     for copy in copies:
         copy.start()
     own = expert_ref[0]
@@ -159,27 +159,38 @@
         hit = place[e : e + 1, :] == row
         pick[e * SEL : (e + 1) * SEL, :] = jnp.where(hit & is_left, 1.0, 0.0).astype(BF16)
         pick[(2 + e) * SEL : (3 + e) * SEL, :] = jnp.where(hit & ~is_left, 1.0, 0.0).astype(BF16)
+
+    def put_sent(column, value):
+        done = 0
+        while done < value.shape[1]:
+            piece = max(i for i, start in enumerate(starts) if start <= column + done)
+            at = column + done - starts[piece]
+            size = min(value.shape[1] - done, sent_refs[piece].shape[1] - at)
+            sent_refs[piece][:, at : at + size] = value[:, done : done + size]
+            done += size
+
     for n in range(0, HALF, 512):
         x = jnp.concatenate([ref[:, n : n + 512] for ref in blocks], axis=0)
         value = jnp.dot(pick[...], x, preferred_element_type=F32).astype(BF16)
         mine_ref[:, n : n + 512] = value[:SEL]
-        sent_ref[:, n : n + 512] = value[SEL : 2 * SEL]
+        put_sent(n, value[SEL : 2 * SEL])
         mine_ref[:, HALF + n : HALF + n + 512] = value[2 * SEL : 3 * SEL]
-        sent_ref[:, HALF + n : HALF + n + 512] = value[3 * SEL :]
+        put_sent(HALF + n, value[3 * SEL :])
     value = jnp.dot(pick[: 2 * SEL, :], ext, preferred_element_type=F32).astype(BF16)
     mine_ref[:, D:] = value[:SEL]
-    sent_ref[:, D:] = value[SEL:]
+    put_sent(D, value[SEL:])
     for copy in copies:
         copy.wait()
 
 
-def select(expert, blocks, after, loads=()):
-    return pl.pallas_call(
-        functools.partial(select_kernel, len(loads)),
-        out_shape=[jax.ShapeDtypeStruct((SEL, D + EXT), BF16)] * 2
-        + [jax.ShapeDtypeStruct((1, MIDDLE, 512), BF16) for _ in loads],
+def select(expert, blocks, after, starts, loads=()):
+    widths = [end - start for start, end in zip(starts, starts[1:] + (D + EXT,))]
+    return pl.pallas_call(
+        functools.partial(select_kernel, starts, len(loads)),
+        out_shape=[jax.ShapeDtypeStruct((SEL, width), BF16) for width in [D + EXT] + widths]
+        + [jax.ShapeDtypeStruct(load.shape, load.dtype) for load in loads],
         in_specs=[SMEM] + [VMEM] * 4 + [HBM] * len(loads) + [ANY],
-        out_specs=[VMEM] * (2 + len(loads)),
+        out_specs=[VMEM] * (1 + len(starts) + len(loads)),
         scratch_shapes=[pltpu.VMEM((PART, PART), BF16), pltpu.SemaphoreType.DMA],
         compiler_params=SMALL,
         cost_estimate=BRIEF,
@@ -187,47 +198,39 @@
     )(expert, *blocks, *[in_hbm(load) for load in loads], after)
 
 
-def hidden_kernel(streams, expert_ref, mine_ref, theirs_ref, gate_ref, first_ref, rest_ref, after_ref, *refs):
-    del after_ref
-    if streams:
-        hidden, second_ref, gate_sum, up_sum, sem = refs
-        copy = pltpu.make_async_copy(rest_ref.at[:, MIDDLE:, :], second_ref, sem)
-        copy.start()
-    else:
-        hidden, gate_sum, up_sum = refs
-        second_ref = rest_ref
-
-    def rows(block):
-        return jnp.concatenate([mine_ref[:, block], theirs_ref[:, block]], axis=0)
-
-    for i in range(0, D, DEPTH):
-        block = slice(i, i + DEPTH)
-        gate = jnp.dot(rows(block), gate_ref[0, block, :], preferred_element_type=F32)
-        gate_sum[...] = gate if i == 0 else gate_sum[...] + gate
-    for i in range(0, D, DEPTH):
-        if streams and i == MIDDLE:
-            copy.wait()
-        ref, start = (first_ref, i) if i < MIDDLE else (second_ref, i - MIDDLE)
-        up = jnp.dot(rows(slice(i, i + DEPTH)), ref[0, start : start + DEPTH, :], preferred_element_type=F32)
-        up_sum[...] = up if i == 0 else up_sum[...] + up
+def hidden_kernel(starts, expert_ref, mine_ref, *refs):
+    theirs_refs = refs[: len(starts)]
+    gate_ref, up_ref = refs[len(starts) : len(starts) + 2]
+    hidden, gate_sum, up_sum = refs[len(starts) + 3 :]
+
+    def rows(low, high):
+        piece = max(i for i, start in enumerate(starts) if start <= low)
+        theirs = theirs_refs[piece][:, low - starts[piece] : high - starts[piece]]
+        return jnp.concatenate([mine_ref[:, low:high], theirs], axis=0)
+
+    for low, high in STEPS:
+        x = rows(low, high)
+        gate = jnp.dot(x, gate_ref[0, low:high, :], preferred_element_type=F32)
+        up = jnp.dot(x, up_ref[0, low:high, :], preferred_element_type=F32)
+        gate_sum[...] = gate if low == 0 else gate_sum[...] + gate
+        up_sum[...] = up if low == 0 else up_sum[...] + up
     lanes = expert_lanes(expert_ref[0], (2 * SEL, EXT), 1)
-    scale = jnp.sum(jnp.where(lanes, rows(slice(D, D + EXT)).astype(F32), 0.0), axis=1, keepdims=True)
+    scale = jnp.sum(jnp.where(lanes, rows(D, D + EXT).astype(F32), 0.0), axis=1, keepdims=True)
     v = gate_sum[...]
     hidden[...] = (v / (1.0 + jnp.exp(-v)) * up_sum[...] * scale).astype(BF16)
 
 
-def hidden_units(expert, mine, theirs, gate, first, rest, after, streams):
-    half = jax.ShapeDtypeStruct((1, MIDDLE, 512), BF16)
-    return pl.pallas_call(
-        functools.partial(hidden_kernel, streams),
-        out_shape=[jax.ShapeDtypeStruct((2 * SEL, 512), BF16)] + [half] * streams,
-        in_specs=[SMEM, VMEM, VMEM, VMEM, VMEM, HBM if streams else VMEM, ANY],
-        out_specs=[VMEM] * (1 + streams),
-        scratch_shapes=[pltpu.VMEM((2 * SEL, 512), F32)] * 2 + [pltpu.SemaphoreType.DMA] * streams,
+def hidden_units(expert, mine, theirs, gate, up, after, starts):
+    return pl.pallas_call(
+        functools.partial(hidden_kernel, starts),
+        out_shape=jax.ShapeDtypeStruct((2 * SEL, 512), BF16),
+        in_specs=[SMEM] + [VMEM] * (3 + len(starts)) + [ANY],
+        out_specs=VMEM,
+        scratch_shapes=[pltpu.VMEM((2 * SEL, 512), F32)] * 2,
         compiler_params=SMALL,
         cost_estimate=BRIEF,
         name="hidden",
-    )(expert, mine, theirs, gate, first, in_hbm(rest) if streams else rest, after)
+    )(expert, mine, *theirs, gate, up, after)
 
 
 def down_kernel(hidden_ref, down_ref, after_ref, mine_ref, theirs_ref):
@@ -328,21 +331,22 @@
     xyz = swap_far(own, 3)
     xy, yz, zx = swap_far(y, 0), swap_far(z, 1), swap_far(x, 2)
     near = (x, y, z, own)
-    mine_near, sent, up_first = select(expert, near, own, (up,))
-    xy, yz, zx, xyz, sent = lax.optimization_barrier((xy, yz, zx, xyz, sent))
-    got_near = to_sibling(sent)
+    mine_near, *sent, up = select(expert, near, own, THREE, (up,))
+    xyz, yz, *sent = lax.optimization_barrier((xyz, yz, *sent))
+    got_near = [to_sibling(piece) for piece in sent]
+    xy, zx, *got_near = lax.optimization_barrier((xy, zx, *got_near))
     far = (xy, zx, yz, xyz)
-    mine_far, sent = select(expert, far, own)
-    got_far = to_sibling(sent)
-    hidden_near, up_second = hidden_units(expert, mine_near, got_near, gate, up_first, up, mine_far, 1)
+    mine_far, sent = select(expert, far, own, ONE)
+    got_far = [to_sibling(sent)]
+    hidden_near = hidden_units(expert, mine_near, got_near, gate, up, mine_far, THREE)
     result_near, theirs = down_rows(hidden_near, down, own)
     returned_near = to_sibling(theirs)
-    (hidden_far,) = hidden_units(expert, mine_far, got_far, gate, up_first, up_second, result_near, 0)
+    hidden_far = hidden_units(expert, mine_far, got_far, gate, up, result_near, ONE)
     result, theirs = down_rows(hidden_far, down, own)
     returned = to_sibling(theirs)
     y_x, y_y, y_z, y_own = spread(expert, near, result_near, returned_near, result)
     y_xy, y_zx, y_yz, y_xyz = spread(expert, far, result, returned, y_own)
-    at_y, at_x, at_z = swap_far(y_yz, 2), swap_far(y_xy, 1), swap_far(y_zx, 0)
+    at_x, at_y, at_z = swap_far(y_xy, 1), swap_far(y_yz, 2), swap_far(y_zx, 0)
     at_own = swap_far(y_xyz, 3)
     total = add(
         y_own,

time: 92.6 us -> 92.6 us (level)
    ppermute x4 -> x6, waiting for transfers between devices: 2.02 us -> 3.12 us  [to_sibling(): return lax.ppermute(values, 'dev', [(i, i ^ 1) for i in range(32)])]
  transfers between devices with their start and end apart: 18 -> 20, of which waited for: 12 -> 10; matrix products, arithmetic and copies ran while one was open for 0% -> 0% of each run, Pallas kernels for 13% -> 12%
where the time goes in v10:
time: 92.6 us; the launch traced here: 92.4 us
  blocking collectives  35.8 us (39%)
  waiting for transfers between devices  28.7 us (31%)
  Pallas kernels  14.5 us (16%)
  starting transfers between devices  12.5 us (13%)
    all_to_all x2, blocking collectives, swap_near(): lax.all_to_all(values, AXES, 0, 0, axis_index_groups=NEAR, tiled=True)  35.8 us
    ppermute x14, waiting for transfers between devices, swap_far(): return lax.ppermute(values, AXES, FAR[axis])  25.5 us
    ppermute x14, starting transfers between devices, swap_far(): return lax.ppermute(values, AXES, FAR[axis])  10.9 us
    pallas_call x2, Pallas kernels, hidden_units(): pl.pallas_call(functools.partial(hidden_kernel, starts), out_shape=jax.Sh...  4.15 us
    pallas_call x2, Pallas kernels, select(): pl.pallas_call(functools.partial(select_kernel, starts, len(loads)), out_...  4 us
    ppermute x6, waiting for transfers between devices, to_sibling(): return lax.ppermute(values, 'dev', [(i, i ^ 1) for i in range(32)])  3.12 us
    pallas_call x2, Pallas kernels, down_rows(): pl.pallas_call(down_kernel, out_shape=[jax.ShapeDtypeStruct((SEL, D), BF1...  2.38 us
    pallas_call x2, Pallas kernels, spread(): pl.pallas_call(spread_kernel, out_shape=[jax.ShapeDtypeStruct((BLOCK, HAL...  2.14 us
  transfers between devices with their start and end apart: 20, of which 10 were waited for; matrix products, arithmetic and copies ran while one was open for 0% of the time, Pallas kernels for 12%

profile of v10, /device:TPU:1, one launch (start us, length us, event | category | flops | bytes accessed | tf_op | source)
XLA Modules:
  0.0 92.4 jit_solution(12997721231398144806)
XLA Ops:
  0.0 1.1 %pack.1 = bf16[8,8,3712]{2,1,0:T(8,128)(2,1)S(1)} custom-call(s32[1]{0:T(128)} %bitcast.expert_ref, bf16[4,7168]{1,0:T(4,128)(2,1)} %tokens_hbm.1, s32[4,8]{1,0:T(4,128)} %ids_hbm.1, f32[4,8]{1,0:T(4,128)} %weights_hbm.1), custom_call_target="tpu_custom_call" | custom-call | tf_op jit(solution)/shard_map/pack/pallas_call | solution.py:112
  1.1 21.0 %all_to_all.10 = bf16[8,8,3712]{2,1,0:T(8,128)(2,1)S(1)} all-to-all(bf16[8,8,3712]{2,1,0:T(8,128)(2,1)S(1)} %pack.1), channel_id=1, replica_groups={{0,2,8,10,32,34,40,42},{1,7,25,31,97,103,121,127},{3,5,27,29,99,101,123..., dimensions={0} | all-to-all | bytes 950272 | tf_op jit(solution)/shard_map/all_to_all | solution.py:74
  22.2 3.7 %collective-permute-start.5 = (bf16[64,3712]{1,0:T(8,128)(2,1)S(1)}, bf16[64,3712]{1,0:T(8,128)(2,1)S(1)}, u32[]{:S(2)}, u32[]{:S(2)}) collective-permute-start(bf16[64,3712]{1,0:T(8,128)(2,1)S(1)} %bitcast.11), channel_id=1, source_target_pairs={{0,126},{1,43},{2,124},{3,41},{4,122},{5,47},{6,120},{7,45},{8,118... | collective-permute-start | bytes 1425416 | tf_op jit(solution)/shard_map/ppermute | solution.py:78
  26.0 3.7 %collective-permute-done.2.refs_2_ = bf16[64,3712]{1,0:T(8,128)(2,1)S(1)} collective-permute-done((bf16[64,3712]{1,0:T(8,128)(2,1)S(1)}, bf16[64,3712]{1,0:T(8,128)(2,1)S(1)}, u32[]{:S(2)}, u32[]{:S(2)}) %collective-permute-start.2) | collective-permute-done | bytes 475168 | tf_op jit(solution)/shard_map/ppermute | solution.py:78
  29.7 1.7 %collective-permute-start.4 = (bf16[64,3712]{1,0:T(8,128)(2,1)S(1)}, bf16[64,3712]{1,0:T(8,128)(2,1)S(1)}, u32[]{:S(2)}, u32[]{:S(2)}) collective-permute-start(bf16[64,3712]{1,0:T(8,128)(2,1)S(1)} %collective-permute-done.refs_0_), channel_id=1, source_target_pairs={{0,6},{1,3},{2,4},{3,1},{4,2},{5,7},{6,0},{7,5},{8,14},{9,11},{10,... | collective-permute-start | bytes 1425416 | tf_op jit(solution)/shard_map/ppermute | solution.py:78
  31.4 3.1 %select.2 = (bf16[64,7296]{1,0:T(8,128)(2,1)S(1)}, bf16[64,2560]{1,0:T(8,128)(2,1)S(1)}, bf16[64,2560]{1,0:T(8,128)(2,1)S(1)}, bf16[64,2176]{1,0:T(8,128)(2,1)S(1)}, bf16[1,7168,512]{2,1,0:T(8,128)(2,1)S(1)}) custom-call(s32[1]{0:T(128)} %bitcast.expert_ref, bf16[64,3712]{1,0:T(8,128)(2,1)S(1)} %collective-permute-done.refs_0_, ...), custom_call_target="tpu_custom_call" | custom-call | flops 1000 | bytes 1000 | tf_op jit(solution)/shard_map/select/pallas_call | solution.py:188
  34.5 2.7 %collective-permute-done.5.refs_3_ = bf16[64,3712]{1,0:T(8,128)(2,1)S(1)} collective-permute-done((bf16[64,3712]{1,0:T(8,128)(2,1)S(1)}, bf16[64,3712]{1,0:T(8,128)(2,1)S(1)}, u32[]{:S(2)}, u32[]{:S(2)}) %collective-permute-start.5) | collective-permute-done | bytes 475168 | tf_op jit(solution)/shard_map/ppermute | solution.py:78
  37.2 4.9 %collective-permute-done.6.refs_2_ = bf16[64,3712]{1,0:T(8,128)(2,1)S(1)} collective-permute-done((bf16[64,3712]{1,0:T(8,128)(2,1)S(1)}, bf16[64,3712]{1,0:T(8,128)(2,1)S(1)}, u32[]{:S(2)}, u32[]{:S(2)}) %collective-permute-start.6) | collective-permute-done | bytes 475168 | tf_op jit(solution)/shard_map/ppermute | solution.py:78
  42.2 0.5 collective-permute-start.8
  42.7 2.0 %collective-permute-done.9.refs_2_ = bf16[64,2176]{1,0:T(8,128)(2,1)S(1)} collective-permute-done((bf16[64,2176]{1,0:T(8,128)(2,1)S(1)}, bf16[64,2176]{1,0:T(8,128)(2,1)S(1)}, u32[]{:S(2)}, u32[]{:S(2)}) %collective-permute-start.9) | collective-permute-done | bytes 278560 | tf_op jit(solution)/shard_map/ppermute | solution.py:82
  44.7 0.9 select.3
  45.6 0.2 collective-permute-start.11
  45.8 2.1 %hidden.2.hidden_ref = bf16[128,512]{1,0:T(8,128)(2,1)S(1)} custom-call(s32[1]{0:T(128)} %bitcast.expert_ref, bf16[64,7296]{1,0:T(8,128)(2,1)S(1)} %get-tuple-element.34.mine_ref, bf16[64,2560]{1,0:T(8,128)(2,1)S(1)} %collective-permute-done.7.refs_0_, bf16[64,2560]{1,0:T(8,128)(2,1)S(1)} %collective-permute-done.8.refs_1_, ...), custom_call_target="tpu_custom_call" | custom-call | flops 1000 | bytes 1000 | tf_op jit(solution)/shard_map/hidden/pallas_call | solution.py:224
  47.9 0.2 slice-done.3
  48.1 1.1 %down.2 = (bf16[64,7168]{1,0:T(8,128)(2,1)S(1)}, bf16[64,7168]{1,0:T(8,128)(2,1)S(1)}) custom-call(bf16[128,512]{1,0:T(8,128)(2,1)S(1)} %hidden.2.hidden_ref, bf16[1,512,7168]{2,1,0:T(8,128)(2,1)S(1)} %bitcast.7, bf16[64,3712]{1,0:T(8,128)(2,1)S(1)} %bitcast.15), custom_call_target="tpu_custom_call" | custom-call | flops 1000 | bytes 1000 | tf_op jit(solution)/shard_map/down/pallas_call | solution.py:246
  49.2 0.3 collective-permute-start.10
  49.5 2.1 %hidden.3.hidden_ref = bf16[128,512]{1,0:T(8,128)(2,1)S(1)} custom-call(s32[1]{0:T(128)} %bitcast.expert_ref, bf16[64,7296]{1,0:T(8,128)(2,1)S(1)} %get-tuple-element.49.refs_5_.mine_ref, bf16[64,7296]{1,0:T(8,128)(2,1)S(1)} %collective-permute-done.11.refs_0_, bf16[1,7168,512]{2,1,0:T(8,128)(2,1)S(1)} %bitcast.5, ...), custom_call_target="tpu_custom_call" | custom-call | flops 1000 | bytes 1000 | tf_op jit(solution)/shard_map/hidden/pallas_call | solution.py:224
  51.6 1.3 %down.3 = (bf16[64,7168]{1,0:T(8,128)(2,1)S(1)}, bf16[64,7168]{1,0:T(8,128)(2,1)S(1)}) custom-call(bf16[128,512]{1,0:T(8,128)(2,1)S(1)} %hidden.3.hidden_ref, bf16[1,512,7168]{2,1,0:T(8,128)(2,1)S(1)} %bitcast.7, bf16[64,3712]{1,0:T(8,128)(2,1)S(1)} %bitcast.16), custom_call_target="tpu_custom_call" | custom-call | flops 1000 | bytes 1000 | tf_op jit(solution)/shard_map/down/pallas_call | solution.py:246
  52.9 0.5 collective-permute-start.12
  53.4 1.1 %spread.2 = (bf16[64,3584]{1,0:T(8,128)(2,1)S(1)}, bf16[64,3584]{1,0:T(8,128)(2,1)S(1)}, bf16[64,3584]{1,0:T(8,128)(2,1)S(1)}, bf16[64,3584]{1,0:T(8,128)(2,1)S(1)}) custom-call(s32[1]{0:T(128)} %bitcast.expert_ref, bf16[64,3712]{1,0:T(8,128)(2,1)S(1)} %collective-permute-done.refs_0_, bf16[64,3712]{1,0:T(8,128)(2,1)S(1)} %collective-permute-done.1.refs_1_, ...), custom_call_target="tpu_custom_call" | custom-call | flops 1000 | bytes 1000 | tf_op jit(solution)/shard_map/spread/pallas_call | solution.py:289
  54.5 1.1 %collective-permute-done.12.refs_5_ = bf16[64,7168]{1,0:T(8,128)(2,1)S(1)} collective-permute-done((bf16[64,7168]{1,0:T(8,128)(2,1)S(1)}, bf16[64,7168]{1,0:T(8,128)(2,1)S(1)}, u32[]{:S(2)}, u32[]{:S(2)}) %collective-permute-start.12) | collective-permute-done | bytes 917536 | tf_op jit(solution)/shard_map/ppermute | solution.py:82
  55.6 1.1 %spread.3 = (bf16[64,3584]{1,0:T(8,128)(2,1)S(1)}, bf16[64,3584]{1,0:T(8,128)(2,1)S(1)}, bf16[64,3584]{1,0:T(8,128)(2,1)S(1)}, bf16[64,3584]{1,0:T(8,128)(2,1)S(1)}) custom-call(s32[1]{0:T(128)} %bitcast.expert_ref, bf16[64,3712]{1,0:T(8,128)(2,1)S(1)} %collective-permute-done.3.refs_0_, bf16[64,3712]{1,0:T(8,128)(2,1)S(1)} %collective-permute-done.4.refs_1_, ...), custom_call_target="tpu_custom_call" | custom-call | flops 1000 | bytes 1000 | tf_op jit(solution)/shard_map/spread/pallas_call | solution.py:289
  57.0 3.6 %collective-permute-start.19 = (bf16[64,3584]{1,0:T(8,128)(2,1)S(1)}, bf16[64,3584]{1,0:T(8,128)(2,1)S(1)}, u32[]{:S(2)}, u32[]{:S(2)}) collective-permute-start(bf16[64,3584]{1,0:T(8,128)(2,1)S(1)} %get-tuple-element.62), channel_id=1, source_target_pairs={{0,126},{1,43},{2,124},{3,41},{4,122},{5,47},{6,120},{7,45},{8,118... | collective-permute-start | bytes 1376264 | tf_op jit(solution)/shard_map/ppermute | solution.py:78
  60.6 3.8 %collective-permute-done.13 = bf16[64,3584]{1,0:T(8,128)(2,1)S(1)} collective-permute-done((bf16[64,3584]{1,0:T(8,128)(2,1)S(1)}, bf16[64,3584]{1,0:T(8,128)(2,1)S(1)}, u32[]{:S(2)}, u32[]{:S(2)}) %collective-permute-start.13) | collective-permute-done | bytes 458784 | tf_op jit(solution)/shard_map/ppermute | solution.py:78
  64.6 0.1 add_convert_fusion.2
  64.7 1.3 %collective-permute-start.16 = (bf16[64,3584]{1,0:T(8,128)(2,1)S(1)}, bf16[64,3584]{1,0:T(8,128)(2,1)S(1)}, u32[]{:S(2)}, u32[]{:S(2)}) collective-permute-start(bf16[64,3584]{1,0:T(8,128)(2,1)S(1)} %add_convert_fusion.2), channel_id=1, source_target_pairs={{0,96},{1,33},{2,98},{3,35},{4,100},{5,37},{6,102},{7,39},{8,104},... | collective-permute-start | bytes 1376264 | tf_op jit(solution)/shard_map/ppermute | solution.py:78
  66.3 5.4 %collective-permute-done.19 = bf16[64,3584]{1,0:T(8,128)(2,1)S(1)} collective-permute-done((bf16[64,3584]{1,0:T(8,128)(2,1)S(1)}, bf16[64,3584]{1,0:T(8,128)(2,1)S(1)}, u32[]{:S(2)}, u32[]{:S(2)}) %collective-permute-start.19) | collective-permute-done | bytes 458784 | tf_op jit(solution)/shard_map/ppermute | solution.py:78
  71.7 2.7 %collective-permute-done.14 = bf16[64,3584]{1,0:T(8,128)(2,1)S(1)} collective-permute-done((bf16[64,3584]{1,0:T(8,128)(2,1)S(1)}, bf16[64,3584]{1,0:T(8,128)(2,1)S(1)}, u32[]{:S(2)}, u32[]{:S(2)}) %collective-permute-start.14) | collective-permute-done | bytes 458784 | tf_op jit(solution)/shard_map/ppermute | solution.py:78
  74.4 2.2 %collective-permute-done.16 = bf16[64,3584]{1,0:T(8,128)(2,1)S(1)} collective-permute-done((bf16[64,3584]{1,0:T(8,128)(2,1)S(1)}, bf16[64,3584]{1,0:T(8,128)(2,1)S(1)}, u32[]{:S(2)}, u32[]{:S(2)}) %collective-permute-start.16) | collective-permute-done | bytes 458784 | tf_op jit(solution)/shard_map/ppermute | solution.py:78
  76.6 0.3 fusion
  76.9 14.7 %all_to_all.11.parts_ref = bf16[8,8,3584]{2,1,0:T(8,128)(2,1)S(1)} all-to-all(bf16[8,8,3584]{2,1,0:T(8,128)(2,1)S(1)} %fusion), channel_id=1, replica_groups={{0,2,8,10,32,34,40,42},{1,7,25,31,97,103,121,127},{3,5,27,29,99,101,123..., dimensions={0} | all-to-all | bytes 917504 | tf_op jit(solution)/shard_map/all_to_all | solution.py:74
  91.7 0.7 finish.1
  (34 shorter events, 0.9 us)
Async XLA Ops:
  0.0 45.8 %slice-start = ((s8[7340032]{0:T(1024)(128)(4,1)}), s8[3145728]{0:T(1024)(128)(4,1)S(1)}, s32[]{:S(2)}) async-start(s8[7340032]{0:T(1024)(128)(4,1)} %bitcast.4), calls=%async_computation.2 | async-start | bytes 6291456
  22.1 23.7 %slice-start.1 = ((s8[7340032]{0:T(1024)(128)(4,1)}), s8[4194304]{0:T(1024)(128)(4,1)S(1)}, s32[]{:S(2)}) async-start(s8[7340032]{0:T(1024)(128)(4,1)} %bitcast.4), calls=%async_computation.3 | async-start | bytes 8388608
  22.1 7.5 %collective-permute-start.2 = (bf16[64,3712]{1,0:T(8,128)(2,1)S(1)}, bf16[64,3712]{1,0:T(8,128)(2,1)S(1)}, u32[]{:S(2)}, u32[]{:S(2)}) collective-permute-start(bf16[64,3712]{1,0:T(8,128)(2,1)S(1)} %bitcast.8), channel_id=1, source_target_pairs={{0,6},{1,3},{2,4},{3,1},{4,2},{5,7},{6,0},{7,5},{8,14},{9,11},{10,... | collective-permute-start | bytes 1425416 | tf_op jit(solution)/shard_map/ppermute | solution.py:78
  22.1 7.5 %collective-permute-start.1 = (bf16[64,3712]{1,0:T(8,128)(2,1)S(1)}, bf16[64,3712]{1,0:T(8,128)(2,1)S(1)}, u32[]{:S(2)}, u32[]{:S(2)}) collective-permute-start(bf16[64,3712]{1,0:T(8,128)(2,1)S(1)} %bitcast.9), channel_id=1, source_target_pairs={{0,96},{1,33},{2,98},{3,35},{4,100},{5,37},{6,102},{7,39},{8,104},... | collective-permute-start | bytes 1425416 | tf_op jit(solution)/shard_map/ppermute | solution.py:78
  22.1 7.6 %collective-permute-start = (bf16[64,3712]{1,0:T(8,128)(2,1)S(1)}, bf16[64,3712]{1,0:T(8,128)(2,1)S(1)}, u32[]{:S(2)}, u32[]{:S(2)}) collective-permute-start(bf16[64,3712]{1,0:T(8,128)(2,1)S(1)} %bitcast.10), channel_id=1, source_target_pairs={{0,24},{1,9},{2,26},{3,11},{4,28},{5,13},{6,30},{7,15},{8,16},{9,1... | collective-permute-start | bytes 1425416 | tf_op jit(solution)/shard_map/ppermute | solution.py:78
  22.2 15.0 %collective-permute-start.5 = (bf16[64,3712]{1,0:T(8,128)(2,1)S(1)}, bf16[64,3712]{1,0:T(8,128)(2,1)S(1)}, u32[]{:S(2)}, u32[]{:S(2)}) collective-permute-start(bf16[64,3712]{1,0:T(8,128)(2,1)S(1)} %bitcast.11), channel_id=1, source_target_pairs={{0,126},{1,43},{2,124},{3,41},{4,122},{5,47},{6,120},{7,45},{8,118... | collective-permute-start | bytes 1425416 | tf_op jit(solution)/shard_map/ppermute | solution.py:78
  29.6 12.5 %collective-permute-start.6 = (bf16[64,3712]{1,0:T(8,128)(2,1)S(1)}, bf16[64,3712]{1,0:T(8,128)(2,1)S(1)}, u32[]{:S(2)}, u32[]{:S(2)}) collective-permute-start(bf16[64,3712]{1,0:T(8,128)(2,1)S(1)} %collective-permute-done.2.refs_2_), channel_id=1, source_target_pairs={{0,96},{1,33},{2,98},{3,35},{4,100},{5,37},{6,102},{7,39},{8,104},... | collective-permute-start | bytes 1425416 | tf_op jit(solution)/shard_map/ppermute | solution.py:78
  29.6 13.1 %collective-permute-start.3 = (bf16[64,3712]{1,0:T(8,128)(2,1)S(1)}, bf16[64,3712]{1,0:T(8,128)(2,1)S(1)}, u32[]{:S(2)}, u32[]{:S(2)}) collective-permute-start(bf16[64,3712]{1,0:T(8,128)(2,1)S(1)} %collective-permute-done.1.refs_1_), channel_id=1, source_target_pairs={{0,24},{1,9},{2,26},{3,11},{4,28},{5,13},{6,30},{7,15},{8,16},{9,1... | collective-permute-start | bytes 1425416 | tf_op jit(solution)/shard_map/ppermute | solution.py:78
  29.7 13.0 %collective-permute-start.4 = (bf16[64,3712]{1,0:T(8,128)(2,1)S(1)}, bf16[64,3712]{1,0:T(8,128)(2,1)S(1)}, u32[]{:S(2)}, u32[]{:S(2)}) collective-permute-start(bf16[64,3712]{1,0:T(8,128)(2,1)S(1)} %collective-permute-done.refs_0_), channel_id=1, source_target_pairs={{0,6},{1,3},{2,4},{3,1},{4,2},{5,7},{6,0},{7,5},{8,14},{9,11},{10,... | collective-permute-start | bytes 1425416 | tf_op jit(solution)/shard_map/ppermute | solution.py:78
  42.2 2.5 %collective-permute-start.7 = (bf16[64,2560]{1,0:T(8,128)(2,1)S(1)}, bf16[64,2560]{1,0:T(8,128)(2,1)S(1)}, u32[]{:S(2)}, u32[]{:S(2)}) collective-permute-start(bf16[64,2560]{1,0:T(8,128)(2,1)S(1)} %get-tuple-element.38), channel_id=1, source_target_pairs={{0,1},{1,0},{2,3},{3,2},{4,5},{5,4},{6,7},{7,6},{8,9},{9,8},{10,11... | collective-permute-start | bytes 983048 | tf_op jit(solution)/shard_map/ppermute | solution.py:82
  42.2 2.5 %collective-permute-start.8 = (bf16[64,2560]{1,0:T(8,128)(2,1)S(1)}, bf16[64,2560]{1,0:T(8,128)(2,1)S(1)}, u32[]{:S(2)}, u32[]{:S(2)}) collective-permute-start(bf16[64,2560]{1,0:T(8,128)(2,1)S(1)} %get-tuple-element.39), channel_id=1, source_target_pairs={{0,1},{1,0},{2,3},{3,2},{4,5},{5,4},{6,7},{7,6},{8,9},{9,8},{10,11... | collective-permute-start | bytes 983048 | tf_op jit(solution)/shard_map/ppermute | solution.py:82
  42.7 2.0 %collective-permute-start.9 = (bf16[64,2176]{1,0:T(8,128)(2,1)S(1)}, bf16[64,2176]{1,0:T(8,128)(2,1)S(1)}, u32[]{:S(2)}, u32[]{:S(2)}) collective-permute-start(bf16[64,2176]{1,0:T(8,128)(2,1)S(1)} %get-tuple-element.40), channel_id=1, source_target_pairs={{0,1},{1,0},{2,3},{3,2},{4,5},{5,4},{6,7},{7,6},{8,9},{9,8},{10,11... | collective-permute-start | bytes 835592 | tf_op jit(solution)/shard_map/ppermute | solution.py:82
  44.7 3.2 %slice-start.2 = ((s8[7340032]{0:T(1024)(128)(4,1)}), s8[4194304]{0:T(1024)(128)(4,1)S(1)}, s32[]{:S(2)}) async-start(s8[7340032]{0:T(1024)(128)(4,1)} %bitcast.6), calls=%async_computation.4 | async-start | bytes 8388608
  45.6 3.9 %collective-permute-start.11 = (bf16[64,7296]{1,0:T(8,128)(2,1)S(1)}, bf16[64,7296]{1,0:T(8,128)(2,1)S(1)}, u32[]{:S(2)}, u32[]{:S(2)}) collective-permute-start(bf16[64,7296]{1,0:T(8,128)(2,1)S(1)} %get-tuple-element.52), channel_id=1, source_target_pairs={{0,1},{1,0},{2,3},{3,2},{4,5},{5,4},{6,7},{7,6},{8,9},{9,8},{10,11... | collective-permute-start | bytes 2801672 | tf_op jit(solution)/shard_map/ppermute | solution.py:82
  45.8 2.3 %slice-start.3 = ((s8[7340032]{0:T(1024)(128)(4,1)}), s8[3145728]{0:T(1024)(128)(4,1)S(1)}, s32[]{:S(2)}) async-start(s8[7340032]{0:T(1024)(128)(4,1)} %bitcast.6), calls=%async_computation.5 | async-start | bytes 6291456
  49.2 4.2 %collective-permute-start.10 = (bf16[64,7168]{1,0:T(8,128)(2,1)S(1)}, bf16[64,7168]{1,0:T(8,128)(2,1)S(1)}, u32[]{:S(2)}, u32[]{:S(2)}) collective-permute-start(bf16[64,7168]{1,0:T(8,128)(2,1)S(1)} %get-tuple-element.51), channel_id=1, source_target_pairs={{0,1},{1,0},{2,3},{3,2},{4,5},{5,4},{6,7},{7,6},{8,9},{9,8},{10,11... | collective-permute-start | bytes 2752520 | tf_op jit(solution)/shard_map/ppermute | solution.py:82
  52.9 2.7 %collective-permute-start.12 = (bf16[64,7168]{1,0:T(8,128)(2,1)S(1)}, bf16[64,7168]{1,0:T(8,128)(2,1)S(1)}, u32[]{:S(2)}, u32[]{:S(2)}) collective-permute-start(bf16[64,7168]{1,0:T(8,128)(2,1)S(1)} %get-tuple-element.56), channel_id=1, source_target_pairs={{0,1},{1,0},{2,3},{3,2},{4,5},{5,4},{6,7},{7,6},{8,9},{9,8},{10,11... | collective-permute-start | bytes 2752520 | tf_op jit(solution)/shard_map/ppermute | solution.py:82
  56.7 7.7 %collective-permute-start.13 = (bf16[64,3584]{1,0:T(8,128)(2,1)S(1)}, bf16[64,3584]{1,0:T(8,128)(2,1)S(1)}, u32[]{:S(2)}, u32[]{:S(2)}) collective-permute-start(bf16[64,3584]{1,0:T(8,128)(2,1)S(1)} %get-tuple-element.57), channel_id=1, source_target_pairs={{0,96},{1,33},{2,98},{3,35},{4,100},{5,37},{6,102},{7,39},{8,104},... | collective-permute-start | bytes 1376264 | tf_op jit(solution)/shard_map/ppermute | solution.py:78
  56.8 7.8 %collective-permute-start.15 = (bf16[64,3584]{1,0:T(8,128)(2,1)S(1)}, bf16[64,3584]{1,0:T(8,128)(2,1)S(1)}, u32[]{:S(2)}, u32[]{:S(2)}) collective-permute-start(bf16[64,3584]{1,0:T(8,128)(2,1)S(1)} %get-tuple-element.59), channel_id=1, source_target_pairs={{0,6},{1,3},{2,4},{3,1},{4,2},{5,7},{6,0},{7,5},{8,14},{9,11},{10,... | collective-permute-start | bytes 1376264 | tf_op jit(solution)/shard_map/ppermute | solution.py:78
  56.9 9.2 %collective-permute-start.17 = (bf16[64,3584]{1,0:T(8,128)(2,1)S(1)}, bf16[64,3584]{1,0:T(8,128)(2,1)S(1)}, u32[]{:S(2)}, u32[]{:S(2)}) collective-permute-start(bf16[64,3584]{1,0:T(8,128)(2,1)S(1)} %get-tuple-element.61), channel_id=1, source_target_pairs={{0,24},{1,9},{2,26},{3,11},{4,28},{5,13},{6,30},{7,15},{8,16},{9,1... | collective-permute-start | bytes 1376264 | tf_op jit(solution)/shard_map/ppermute | solution.py:78
  57.0 14.7 %collective-permute-start.19 = (bf16[64,3584]{1,0:T(8,128)(2,1)S(1)}, bf16[64,3584]{1,0:T(8,128)(2,1)S(1)}, u32[]{:S(2)}, u32[]{:S(2)}) collective-permute-start(bf16[64,3584]{1,0:T(8,128)(2,1)S(1)} %get-tuple-element.62), channel_id=1, source_target_pairs={{0,126},{1,43},{2,124},{3,41},{4,122},{5,47},{6,120},{7,45},{8,118... | collective-permute-start | bytes 1376264 | tf_op jit(solution)/shard_map/ppermute | solution.py:78
  64.5 9.9 %collective-permute-start.14 = (bf16[64,3584]{1,0:T(8,128)(2,1)S(1)}, bf16[64,3584]{1,0:T(8,128)(2,1)S(1)}, u32[]{:S(2)}, u32[]{:S(2)}) collective-permute-start(bf16[64,3584]{1,0:T(8,128)(2,1)S(1)} %add_convert_fusion.3), channel_id=1, source_target_pairs={{0,24},{1,9},{2,26},{3,11},{4,28},{5,13},{6,30},{7,15},{8,16},{9,1... | collective-permute-start | bytes 1376264 | tf_op jit(solution)/shard_map/ppermute | solution.py:78
  64.7 11.9 %collective-permute-start.16 = (bf16[64,3584]{1,0:T(8,128)(2,1)S(1)}, bf16[64,3584]{1,0:T(8,128)(2,1)S(1)}, u32[]{:S(2)}, u32[]{:S(2)}) collective-permute-start(bf16[64,3584]{1,0:T(8,128)(2,1)S(1)} %add_convert_fusion.2), channel_id=1, source_target_pairs={{0,96},{1,33},{2,98},{3,35},{4,100},{5,37},{6,102},{7,39},{8,104},... | collective-permute-start | bytes 1376264 | tf_op jit(solution)/shard_map/ppermute | solution.py:78
  66.2 10.4 %collective-permute-start.18 = (bf16[64,3584]{1,0:T(8,128)(2,1)S(1)}, bf16[64,3584]{1,0:T(8,128)(2,1)S(1)}, u32[]{:S(2)}, u32[]{:S(2)}) collective-permute-start(bf16[64,3584]{1,0:T(8,128)(2,1)S(1)} %add_convert_fusion.1), channel_id=1, source_target_pairs={{0,6},{1,3},{2,4},{3,1},{4,2},{5,7},{6,0},{7,5},{8,14},{9,11},{10,... | collective-permute-start | bytes 1376264 | tf_op jit(solution)/shard_map/ppermute | solution.py:78

commit v11 on v10

--- a/solution.py
+++ b/solution.py
@@ -25,8 +25,8 @@
 SMALL = pltpu.CompilerParams(vmem_limit_bytes=8 * MIB)
 
 
-STEPS = ((0, 2560), (2560, 5120), (5120, D))
-THREE = (0, 2560, 5120)
+STEPS = ((0, HALF), (HALF, D))
+TWO = (0, HALF)
 ONE = (0,)
 BRIEF = pl.CostEstimate(flops=1000, bytes_accessed=1000, transcendentals=0)
 
@@ -76,6 +76,10 @@
 
 def swap_far(values, axis):
     return lax.ppermute(values, AXES, FAR[axis])
+
+
+def both_cores(values):
+    return lax.all_gather(values, "dev", axis_index_groups=[[i, i + 1] for i in range(0, 32, 2)])
 
 
 def to_sibling(values):
@@ -205,7 +209,11 @@
 
     def rows(low, high):
         piece = max(i for i, start in enumerate(starts) if start <= low)
-        theirs = theirs_refs[piece][:, low - starts[piece] : high - starts[piece]]
+        columns = slice(low - starts[piece], high - starts[piece])
+        if len(starts) > 1:
+            theirs = theirs_refs[piece][1 - expert_ref[0] % 2, :, columns]
+        else:
+            theirs = theirs_refs[piece][:, columns]
         return jnp.concatenate([mine_ref[:, low:high], theirs], axis=0)
 
     for low, high in STEPS:
@@ -331,23 +339,22 @@
     xyz = swap_far(own, 3)
     xy, yz, zx = swap_far(y, 0), swap_far(z, 1), swap_far(x, 2)
     near = (x, y, z, own)
-    mine_near, *sent, up = select(expert, near, own, THREE, (up,))
-    xyz, yz, *sent = lax.optimization_barrier((xyz, yz, *sent))
-    got_near = [to_sibling(piece) for piece in sent]
-    xy, zx, *got_near = lax.optimization_barrier((xy, zx, *got_near))
+    mine_near, *sent, up = select(expert, near, own, TWO, (up,))
+    got_near = [both_cores(piece) for piece in sent]
+    xy, yz, zx, xyz, *got_near = lax.optimization_barrier((xy, yz, zx, xyz, *got_near))
     far = (xy, zx, yz, xyz)
     mine_far, sent = select(expert, far, own, ONE)
     got_far = [to_sibling(sent)]
-    hidden_near = hidden_units(expert, mine_near, got_near, gate, up, mine_far, THREE)
-    result_near, theirs = down_rows(hidden_near, down, own)
-    returned_near = to_sibling(theirs)
-    hidden_far = hidden_units(expert, mine_far, got_far, gate, up, result_near, ONE)
+    hidden_near = hidden_units(expert, mine_near, got_near, gate, up, mine_far, TWO)
+    hidden_far = hidden_units(expert, mine_far, got_far, gate, up, hidden_near, ONE)
     result, theirs = down_rows(hidden_far, down, own)
     returned = to_sibling(theirs)
-    y_x, y_y, y_z, y_own = spread(expert, near, result_near, returned_near, result)
-    y_xy, y_zx, y_yz, y_xyz = spread(expert, far, result, returned, y_own)
+    result_near, theirs = down_rows(hidden_near, down, result)
+    returned_near = to_sibling(theirs)
+    y_xy, y_zx, y_yz, y_xyz = spread(expert, far, result, returned, result_near)
     at_x, at_y, at_z = swap_far(y_xy, 1), swap_far(y_yz, 2), swap_far(y_zx, 0)
     at_own = swap_far(y_xyz, 3)
+    y_x, y_y, y_z, y_own = spread(expert, near, result_near, returned_near, y_xyz)
     total = add(
         y_own,
         swap_far(add(y_x, at_x), 0),

time: 92.6 us -> 88.2 us (0.952)
  waiting for transfers between devices: 28.7 us -> 20.8 us
  blocking collectives: 35.8 us -> 40.9 us
  starting transfers between devices: 12.5 us -> 11.3 us
    ppermute x14, waiting for transfers between devices: 25.5 us -> 19.7 us  [swap_far(): return lax.ppermute(values, AXES, FAR[axis])]
    all_gather x0 -> x2, blocking collectives: none -> 5.22 us  [both_cores(): lax.all_gather(values, 'dev', axis_index_groups=[[i, i + 1] for i in rang...]
    ppermute x6 -> x3, waiting for transfers between devices: 3.12 us -> 1.11 us  [to_sibling(): return lax.ppermute(values, 'dev', [(i, i ^ 1) for i in range(32)])]
  transfers between devices with their start and end apart: 20 -> 17, of which waited for: 10 -> 11; matrix products, arithmetic and copies ran while one was open for 0% -> 0% of each run, Pallas kernels for 12% -> 10%
where the time goes in v11:
time: 88.2 us; the launch traced here: 87.9 us
  blocking collectives  40.9 us (46%)
  waiting for transfers between devices  20.8 us (24%)
  Pallas kernels  14.2 us (16%)
  starting transfers between devices  11.3 us (13%)
    all_to_all x2, blocking collectives, swap_near(): lax.all_to_all(values, AXES, 0, 0, axis_index_groups=NEAR, tiled=True)  35.6 us
    ppermute x14, waiting for transfers between devices, swap_far(): return lax.ppermute(values, AXES, FAR[axis])  19.7 us
    ppermute x14, starting transfers between devices, swap_far(): return lax.ppermute(values, AXES, FAR[axis])  10.6 us
    all_gather x2, blocking collectives, both_cores(): lax.all_gather(values, 'dev', axis_index_groups=[[i, i + 1] for i in rang...  5.22 us
    pallas_call x2, Pallas kernels, hidden_units(): pl.pallas_call(functools.partial(hidden_kernel, starts), out_shape=jax.Sh...  4.12 us
    pallas_call x2, Pallas kernels, select(): pl.pallas_call(functools.partial(select_kernel, starts, len(loads)), out_...  4.01 us
    pallas_call x2, Pallas kernels, down_rows(): pl.pallas_call(down_kernel, out_shape=[jax.ShapeDtypeStruct((SEL, D), BF1...  2.28 us
    pallas_call x2, Pallas kernels, spread(): pl.pallas_call(spread_kernel, out_shape=[jax.ShapeDtypeStruct((BLOCK, HAL...  2.11 us
  transfers between devices with their start and end apart: 17, of which 11 were waited for; matrix products, arithmetic and copies ran while one was open for 0% of the time, Pallas kernels for 10%

profile of v11, /device:TPU:1, one launch (start us, length us, event | category | flops | bytes accessed | tf_op | source)
XLA Modules:
  0.0 87.9 jit_solution(11435144239475143611)
XLA Ops:
  0.0 0.9 %pack.1 = bf16[8,8,3712]{2,1,0:T(8,128)(2,1)S(1)} custom-call(s32[1]{0:T(128)} %bitcast.expert_ref, bf16[4,7168]{1,0:T(4,128)(2,1)} %tokens_hbm.1, s32[4,8]{1,0:T(4,128)} %ids_hbm.1, f32[4,8]{1,0:T(4,128)} %weights_hbm.1), custom_call_target="tpu_custom_call" | custom-call | tf_op jit(solution)/shard_map/pack/pallas_call | solution.py:116
  1.0 21.0 %all_to_all.10 = bf16[8,8,3712]{2,1,0:T(8,128)(2,1)S(1)} all-to-all(bf16[8,8,3712]{2,1,0:T(8,128)(2,1)S(1)} %pack.1), channel_id=1, replica_groups={{0,2,8,10,32,34,40,42},{1,7,25,31,97,103,121,127},{3,5,27,29,99,101,123..., dimensions={0} | all-to-all | bytes 950272 | tf_op jit(solution)/shard_map/all_to_all | solution.py:74
  22.2 3.6 %collective-permute-start.6 = (bf16[64,3712]{1,0:T(8,128)(2,1)S(1)}, bf16[64,3712]{1,0:T(8,128)(2,1)S(1)}, u32[]{:S(2)}, u32[]{:S(2)}) collective-permute-start(bf16[64,3712]{1,0:T(8,128)(2,1)S(1)} %bitcast.13), channel_id=1, source_target_pairs={{0,126},{1,43},{2,124},{3,41},{4,122},{5,47},{6,120},{7,45},{8,118... | collective-permute-start | bytes 1425416 | tf_op jit(solution)/shard_map/ppermute | solution.py:78
  25.8 3.7 %collective-permute-done.2.refs_2_ = bf16[64,3712]{1,0:T(8,128)(2,1)S(1)} collective-permute-done((bf16[64,3712]{1,0:T(8,128)(2,1)S(1)}, bf16[64,3712]{1,0:T(8,128)(2,1)S(1)}, u32[]{:S(2)}, u32[]{:S(2)}) %collective-permute-start.2) | collective-permute-done | bytes 475168 | tf_op jit(solution)/shard_map/ppermute | solution.py:78
  29.6 0.4 collective-permute-done.refs_0_
  29.9 1.3 %collective-permute-start.5 = (bf16[64,3712]{1,0:T(8,128)(2,1)S(1)}, bf16[64,3712]{1,0:T(8,128)(2,1)S(1)}, u32[]{:S(2)}, u32[]{:S(2)}) collective-permute-start(bf16[64,3712]{1,0:T(8,128)(2,1)S(1)} %collective-permute-done.refs_0_), channel_id=1, source_target_pairs={{0,6},{1,3},{2,4},{3,1},{4,2},{5,7},{6,0},{7,5},{8,14},{9,11},{10,... | collective-permute-start | bytes 1425416 | tf_op jit(solution)/shard_map/ppermute | solution.py:78
  31.2 3.1 %select.2 = (bf16[64,7296]{1,0:T(8,128)(2,1)S(1)}, bf16[64,3584]{1,0:T(8,128)(2,1)S(1)}, bf16[64,3712]{1,0:T(8,128)(2,1)S(1)}, bf16[1,7168,512]{2,1,0:T(8,128)(2,1)S(1)}) custom-call(s32[1]{0:T(128)} %bitcast.expert_ref, bf16[64,3712]{1,0:T(8,128)(2,1)S(1)} %collective-permute-done.refs_0_, bf16[64,3712]{1,0:T(8,128)(2,1)S(1)} %collective-permute-done.1.refs_1_, ...), custom_call_target="tpu_custom_call" | custom-call | flops 1000 | bytes 1000 | tf_op jit(solution)/shard_map/select/pallas_call | solution.py:192
  34.3 2.7 %all-gather = bf16[128,3584]{1,0:T(8,128)(2,1)S(1)} all-gather(bf16[64,3584]{1,0:T(8,128)(2,1)S(1)} %get-tuple-element.30), channel_id=2, replica_groups={{0,1},{2,3},{4,5},{6,7},{8,9},{10,11},{12,13},{14,15},{16,17},{18,19},{..., dimensions={0}, use_global_device_ids=true | all-gather | bytes 1376256 | tf_op jit(solution)/shard_map/all_gather | solution.py:82
  37.1 2.5 %all-gather.1 = bf16[128,3712]{1,0:T(8,128)(2,1)S(1)} all-gather(bf16[64,3712]{1,0:T(8,128)(2,1)S(1)} %get-tuple-element.31), channel_id=3, replica_groups={{0,1},{2,3},{4,5},{6,7},{8,9},{10,11},{12,13},{14,15},{16,17},{18,19},{..., dimensions={0}, use_global_device_ids=true | all-gather | bytes 1425408 | tf_op jit(solution)/shard_map/all_gather | solution.py:82
  39.6 2.5 %collective-permute-done.4.refs_2_ = bf16[64,3712]{1,0:T(8,128)(2,1)S(1)} collective-permute-done((bf16[64,3712]{1,0:T(8,128)(2,1)S(1)}, bf16[64,3712]{1,0:T(8,128)(2,1)S(1)}, u32[]{:S(2)}, u32[]{:S(2)}) %collective-permute-start.4) | collective-permute-done | bytes 475168 | tf_op jit(solution)/shard_map/ppermute | solution.py:78
  42.0 0.9 %select.3 = (bf16[64,7296]{1,0:T(8,128)(2,1)S(1)}, bf16[64,7296]{1,0:T(8,128)(2,1)S(1)}) custom-call(s32[1]{0:T(128)} %bitcast.expert_ref, bf16[64,3712]{1,0:T(8,128)(2,1)S(1)} %collective-permute-done.3.refs_0_, bf16[64,3712]{1,0:T(8,128)(2,1)S(1)} %collective-permute-done.5.refs_1_, bf16[64,3712]{1,0:T(8,128)(2,1)S(1)} %collective-permute-done.4.refs_2_, ...), custom_call_target="tpu_custom_call" | custom-call | flops 1000 | bytes 1000 | tf_op jit(solution)/shard_map/select/pallas_call | solution.py:192
  43.1 2.1 %hidden.2.refs_3_.hidden_ref = bf16[128,512]{1,0:T(8,128)(2,1)S(1)} custom-call(s32[1]{0:T(128)} %bitcast.expert_ref, bf16[64,7296]{1,0:T(8,128)(2,1)S(1)} %get-tuple-element.29.mine_ref, bf16[2,64,3584]{2,1,0:T(8,128)(2,1)S(1)} %bitcast.20, bf16[2,64,3712]{2,1,0:T(8,128)(2,1)S(1)} %bitcast.19, bf16[1,7168,512]{2,1,0:T(8,128)(2,1)S(1)} %bitcast.7, ...), custom_call_target="tpu_custom_call" | custom-call | flops 1000 | bytes 1000 | tf_op jit(solution)/shard_map/hidden/pallas_call | solution.py:232
  45.2 0.4 collective-permute-done.7.refs_0_
  45.5 2.1 %hidden.3.hidden_ref = bf16[128,512]{1,0:T(8,128)(2,1)S(1)} custom-call(s32[1]{0:T(128)} %bitcast.expert_ref, bf16[64,7296]{1,0:T(8,128)(2,1)S(1)} %get-tuple-element.39.refs_4_.mine_ref, bf16[64,7296]{1,0:T(8,128)(2,1)S(1)} %collective-permute-done.7.refs_0_, bf16[1,7168,512]{2,1,0:T(8,128)(2,1)S(1)} %bitcast.7, ...), custom_call_target="tpu_custom_call" | custom-call | flops 1000 | bytes 1000 | tf_op jit(solution)/shard_map/hidden/pallas_call | solution.py:232
  47.6 1.1 %down.2 = (bf16[64,7168]{1,0:T(8,128)(2,1)S(1)}, bf16[64,7168]{1,0:T(8,128)(2,1)S(1)}) custom-call(bf16[128,512]{1,0:T(8,128)(2,1)S(1)} %hidden.3.hidden_ref, bf16[1,512,7168]{2,1,0:T(8,128)(2,1)S(1)} %bitcast.9, bf16[64,3712]{1,0:T(8,128)(2,1)S(1)} %bitcast.17), custom_call_target="tpu_custom_call" | custom-call | flops 1000 | bytes 1000 | tf_op jit(solution)/shard_map/down/pallas_call | solution.py:254
  48.8 0.2 collective-permute-start.9
  49.0 1.1 %down.3 = (bf16[64,7168]{1,0:T(8,128)(2,1)S(1)}, bf16[64,7168]{1,0:T(8,128)(2,1)S(1)}) custom-call(bf16[128,512]{1,0:T(8,128)(2,1)S(1)} %hidden.2.refs_3_.hidden_ref, bf16[1,512,7168]{2,1,0:T(8,128)(2,1)S(1)} %bitcast.9, bf16[64,7168]{1,0:T(8,128)(2,1)S(1)} %get-tuple-element.41.after_ref.refs_4_), custom_call_target="tpu_custom_call" | custom-call | flops 1000 | bytes 1000 | tf_op jit(solution)/shard_map/down/pallas_call | solution.py:254
  50.1 0.4 collective-permute-start.8
  50.6 0.7 collective-permute-done.9.refs_5_
  51.3 1.1 %spread.2 = (bf16[64,3584]{1,0:T(8,128)(2,1)S(1)}, bf16[64,3584]{1,0:T(8,128)(2,1)S(1)}, bf16[64,3584]{1,0:T(8,128)(2,1)S(1)}, bf16[64,3584]{1,0:T(8,128)(2,1)S(1)}) custom-call(s32[1]{0:T(128)} %bitcast.expert_ref, bf16[64,3712]{1,0:T(8,128)(2,1)S(1)} %collective-permute-done.3.refs_0_, bf16[64,3712]{1,0:T(8,128)(2,1)S(1)} %collective-permute-done.5.refs_1_, ...), custom_call_target="tpu_custom_call" | custom-call | flops 1000 | bytes 1000 | tf_op jit(solution)/shard_map/spread/pallas_call | solution.py:297
  52.4 0.4 collective-permute-start.10
  52.8 0.3 collective-permute-start.12
  53.1 3.2 %collective-permute-start.16 = (bf16[64,3584]{1,0:T(8,128)(2,1)S(1)}, bf16[64,3584]{1,0:T(8,128)(2,1)S(1)}, u32[]{:S(2)}, u32[]{:S(2)}) collective-permute-start(bf16[64,3584]{1,0:T(8,128)(2,1)S(1)} %get-tuple-element.45.refs_6_), channel_id=1, source_target_pairs={{0,126},{1,43},{2,124},{3,41},{4,122},{5,47},{6,120},{7,45},{8,118... | collective-permute-start | bytes 1376264 | tf_op jit(solution)/shard_map/ppermute | solution.py:78
  56.3 1.1 %spread.3 = (bf16[64,3584]{1,0:T(8,128)(2,1)S(1)}, bf16[64,3584]{1,0:T(8,128)(2,1)S(1)}, bf16[64,3584]{1,0:T(8,128)(2,1)S(1)}, bf16[64,3584]{1,0:T(8,128)(2,1)S(1)}) custom-call(s32[1]{0:T(128)} %bitcast.expert_ref, bf16[64,3712]{1,0:T(8,128)(2,1)S(1)} %collective-permute-done.refs_0_, bf16[64,3712]{1,0:T(8,128)(2,1)S(1)} %collective-permute-done.1.refs_1_, ...), custom_call_target="tpu_custom_call" | custom-call | flops 1000 | bytes 1000 | tf_op jit(solution)/shard_map/spread/pallas_call | solution.py:297
  57.4 2.7 %collective-permute-done.10 = bf16[64,3584]{1,0:T(8,128)(2,1)S(1)} collective-permute-done((bf16[64,3584]{1,0:T(8,128)(2,1)S(1)}, bf16[64,3584]{1,0:T(8,128)(2,1)S(1)}, u32[]{:S(2)}, u32[]{:S(2)}) %collective-permute-start.10) | collective-permute-done | bytes 458784 | tf_op jit(solution)/shard_map/ppermute | solution.py:78
  60.5 1.3 %collective-permute-start.13 = (bf16[64,3584]{1,0:T(8,128)(2,1)S(1)}, bf16[64,3584]{1,0:T(8,128)(2,1)S(1)}, u32[]{:S(2)}, u32[]{:S(2)}) collective-permute-start(bf16[64,3584]{1,0:T(8,128)(2,1)S(1)} %add_convert_fusion.2), channel_id=1, source_target_pairs={{0,96},{1,33},{2,98},{3,35},{4,100},{5,37},{6,102},{7,39},{8,104},... | collective-permute-start | bytes 1376264 | tf_op jit(solution)/shard_map/ppermute | solution.py:78
  62.0 5.4 %collective-permute-done.16 = bf16[64,3584]{1,0:T(8,128)(2,1)S(1)} collective-permute-done((bf16[64,3584]{1,0:T(8,128)(2,1)S(1)}, bf16[64,3584]{1,0:T(8,128)(2,1)S(1)}, u32[]{:S(2)}, u32[]{:S(2)}) %collective-permute-start.16) | collective-permute-done | bytes 458784 | tf_op jit(solution)/shard_map/ppermute | solution.py:78
  67.4 3.2 %collective-permute-done.11 = bf16[64,3584]{1,0:T(8,128)(2,1)S(1)} collective-permute-done((bf16[64,3584]{1,0:T(8,128)(2,1)S(1)}, bf16[64,3584]{1,0:T(8,128)(2,1)S(1)}, u32[]{:S(2)}, u32[]{:S(2)}) %collective-permute-start.11) | collective-permute-done | bytes 458784 | tf_op jit(solution)/shard_map/ppermute | solution.py:78
  70.6 1.7 %collective-permute-done.13 = bf16[64,3584]{1,0:T(8,128)(2,1)S(1)} collective-permute-done((bf16[64,3584]{1,0:T(8,128)(2,1)S(1)}, bf16[64,3584]{1,0:T(8,128)(2,1)S(1)}, u32[]{:S(2)}, u32[]{:S(2)}) %collective-permute-start.13) | collective-permute-done | bytes 458784 | tf_op jit(solution)/shard_map/ppermute | solution.py:78
  72.3 0.3 fusion
  72.6 14.6 %all_to_all.11.parts_ref = bf16[8,8,3584]{2,1,0:T(8,128)(2,1)S(1)} all-to-all(bf16[8,8,3584]{2,1,0:T(8,128)(2,1)S(1)} %fusion), channel_id=1, replica_groups={{0,2,8,10,32,34,40,42},{1,7,25,31,97,103,121,127},{3,5,27,29,99,101,123..., dimensions={0} | all-to-all | bytes 917504 | tf_op jit(solution)/shard_map/all_to_all | solution.py:74
  87.2 0.7 finish.1
  (30 shorter events, 1.1 us)
Async XLA Ops:
  22.0 21.1 %slice-start = ((s8[7340032]{0:T(1024)(128)(4,1)}), s8[4194304]{0:T(1024)(128)(4,1)S(1)}, s32[]{:S(2)}) async-start(s8[7340032]{0:T(1024)(128)(4,1)} %bitcast.6), calls=%async_computation.2 | async-start | bytes 8388608
  22.0 21.1 %slice-start.1 = ((s8[7340032]{0:T(1024)(128)(4,1)}), s8[3145728]{0:T(1024)(128)(4,1)S(1)}, s32[]{:S(2)}) async-start(s8[7340032]{0:T(1024)(128)(4,1)} %bitcast.6), calls=%async_computation.3 | async-start | bytes 6291456
  22.0 7.5 %collective-permute-start.2 = (bf16[64,3712]{1,0:T(8,128)(2,1)S(1)}, bf16[64,3712]{1,0:T(8,128)(2,1)S(1)}, u32[]{:S(2)}, u32[]{:S(2)}) collective-permute-start(bf16[64,3712]{1,0:T(8,128)(2,1)S(1)} %bitcast.10), channel_id=1, source_target_pairs={{0,6},{1,3},{2,4},{3,1},{4,2},{5,7},{6,0},{7,5},{8,14},{9,11},{10,... | collective-permute-start | bytes 1425416 | tf_op jit(solution)/shard_map/ppermute | solution.py:78
  22.0 7.6 %collective-permute-start.1 = (bf16[64,3712]{1,0:T(8,128)(2,1)S(1)}, bf16[64,3712]{1,0:T(8,128)(2,1)S(1)}, u32[]{:S(2)}, u32[]{:S(2)}) collective-permute-start(bf16[64,3712]{1,0:T(8,128)(2,1)S(1)} %bitcast.11), channel_id=1, source_target_pairs={{0,96},{1,33},{2,98},{3,35},{4,100},{5,37},{6,102},{7,39},{8,104},... | collective-permute-start | bytes 1425416 | tf_op jit(solution)/shard_map/ppermute | solution.py:78
  22.1 7.9 %collective-permute-start = (bf16[64,3712]{1,0:T(8,128)(2,1)S(1)}, bf16[64,3712]{1,0:T(8,128)(2,1)S(1)}, u32[]{:S(2)}, u32[]{:S(2)}) collective-permute-start(bf16[64,3712]{1,0:T(8,128)(2,1)S(1)} %bitcast.12), channel_id=1, source_target_pairs={{0,24},{1,9},{2,26},{3,11},{4,28},{5,13},{6,30},{7,15},{8,16},{9,1... | collective-permute-start | bytes 1425416 | tf_op jit(solution)/shard_map/ppermute | solution.py:78
  22.2 17.4 %collective-permute-start.6 = (bf16[64,3712]{1,0:T(8,128)(2,1)S(1)}, bf16[64,3712]{1,0:T(8,128)(2,1)S(1)}, u32[]{:S(2)}, u32[]{:S(2)}) collective-permute-start(bf16[64,3712]{1,0:T(8,128)(2,1)S(1)} %bitcast.13), channel_id=1, source_target_pairs={{0,126},{1,43},{2,124},{3,41},{4,122},{5,47},{6,120},{7,45},{8,118... | collective-permute-start | bytes 1425416 | tf_op jit(solution)/shard_map/ppermute | solution.py:78
  29.5 12.5 %collective-permute-start.4 = (bf16[64,3712]{1,0:T(8,128)(2,1)S(1)}, bf16[64,3712]{1,0:T(8,128)(2,1)S(1)}, u32[]{:S(2)}, u32[]{:S(2)}) collective-permute-start(bf16[64,3712]{1,0:T(8,128)(2,1)S(1)} %collective-permute-done.2.refs_2_), channel_id=1, source_target_pairs={{0,96},{1,33},{2,98},{3,35},{4,100},{5,37},{6,102},{7,39},{8,104},... | collective-permute-start | bytes 1425416 | tf_op jit(solution)/shard_map/ppermute | solution.py:78
  29.6 12.5 %collective-permute-start.3 = (bf16[64,3712]{1,0:T(8,128)(2,1)S(1)}, bf16[64,3712]{1,0:T(8,128)(2,1)S(1)}, u32[]{:S(2)}, u32[]{:S(2)}) collective-permute-start(bf16[64,3712]{1,0:T(8,128)(2,1)S(1)} %collective-permute-done.1.refs_1_), channel_id=1, source_target_pairs={{0,24},{1,9},{2,26},{3,11},{4,28},{5,13},{6,30},{7,15},{8,16},{9,1... | collective-permute-start | bytes 1425416 | tf_op jit(solution)/shard_map/ppermute | solution.py:78
  29.9 12.1 %collective-permute-start.5 = (bf16[64,3712]{1,0:T(8,128)(2,1)S(1)}, bf16[64,3712]{1,0:T(8,128)(2,1)S(1)}, u32[]{:S(2)}, u32[]{:S(2)}) collective-permute-start(bf16[64,3712]{1,0:T(8,128)(2,1)S(1)} %collective-permute-done.refs_0_), channel_id=1, source_target_pairs={{0,6},{1,3},{2,4},{3,1},{4,2},{5,7},{6,0},{7,5},{8,14},{9,11},{10,... | collective-permute-start | bytes 1425416 | tf_op jit(solution)/shard_map/ppermute | solution.py:78
  42.0 5.6 %slice-start.2 = ((s8[7340032]{0:T(1024)(128)(4,1)}), s8[4194304]{0:T(1024)(128)(4,1)S(1)}, s32[]{:S(2)}) async-start(s8[7340032]{0:T(1024)(128)(4,1)} %bitcast.8), calls=%async_computation.4 | async-start | bytes 8388608
  43.0 2.6 %collective-permute-start.7 = (bf16[64,7296]{1,0:T(8,128)(2,1)S(1)}, bf16[64,7296]{1,0:T(8,128)(2,1)S(1)}, u32[]{:S(2)}, u32[]{:S(2)}) collective-permute-start(bf16[64,7296]{1,0:T(8,128)(2,1)S(1)} %get-tuple-element.40), channel_id=1, source_target_pairs={{0,1},{1,0},{2,3},{3,2},{4,5},{5,4},{6,7},{7,6},{8,9},{9,8},{10,11... | collective-permute-start | bytes 2801672 | tf_op jit(solution)/shard_map/ppermute | solution.py:86
  43.1 4.5 %slice-start.3 = ((s8[7340032]{0:T(1024)(128)(4,1)}), s8[3145728]{0:T(1024)(128)(4,1)S(1)}, s32[]{:S(2)}) async-start(s8[7340032]{0:T(1024)(128)(4,1)} %bitcast.8), calls=%async_computation.5 | async-start | bytes 6291456
  48.8 2.6 %collective-permute-start.9 = (bf16[64,7168]{1,0:T(8,128)(2,1)S(1)}, bf16[64,7168]{1,0:T(8,128)(2,1)S(1)}, u32[]{:S(2)}, u32[]{:S(2)}) collective-permute-start(bf16[64,7168]{1,0:T(8,128)(2,1)S(1)} %get-tuple-element.44), channel_id=1, source_target_pairs={{0,1},{1,0},{2,3},{3,2},{4,5},{5,4},{6,7},{7,6},{8,9},{9,8},{10,11... | collective-permute-start | bytes 2752520 | tf_op jit(solution)/shard_map/ppermute | solution.py:86
  50.1 6.2 %collective-permute-start.8 = (bf16[64,7168]{1,0:T(8,128)(2,1)S(1)}, bf16[64,7168]{1,0:T(8,128)(2,1)S(1)}, u32[]{:S(2)}, u32[]{:S(2)}) collective-permute-start(bf16[64,7168]{1,0:T(8,128)(2,1)S(1)} %get-tuple-element.43), channel_id=1, source_target_pairs={{0,1},{1,0},{2,3},{3,2},{4,5},{5,4},{6,7},{7,6},{8,9},{9,8},{10,11... | collective-permute-start | bytes 2752520 | tf_op jit(solution)/shard_map/ppermute | solution.py:86
  52.4 7.7 %collective-permute-start.10 = (bf16[64,3584]{1,0:T(8,128)(2,1)S(1)}, bf16[64,3584]{1,0:T(8,128)(2,1)S(1)}, u32[]{:S(2)}, u32[]{:S(2)}) collective-permute-start(bf16[64,3584]{1,0:T(8,128)(2,1)S(1)} %get-tuple-element.48), channel_id=1, source_target_pairs={{0,96},{1,33},{2,98},{3,35},{4,100},{5,37},{6,102},{7,39},{8,104},... | collective-permute-start | bytes 1376264 | tf_op jit(solution)/shard_map/ppermute | solution.py:78
  52.8 7.6 %collective-permute-start.12 = (bf16[64,3584]{1,0:T(8,128)(2,1)S(1)}, bf16[64,3584]{1,0:T(8,128)(2,1)S(1)}, u32[]{:S(2)}, u32[]{:S(2)}) collective-permute-start(bf16[64,3584]{1,0:T(8,128)(2,1)S(1)} %get-tuple-element.50), channel_id=1, source_target_pairs={{0,6},{1,3},{2,4},{3,1},{4,2},{5,7},{6,0},{7,5},{8,14},{9,11},{10,... | collective-permute-start | bytes 1376264 | tf_op jit(solution)/shard_map/ppermute | solution.py:78
  53.1 8.7 %collective-permute-start.14 = (bf16[64,3584]{1,0:T(8,128)(2,1)S(1)}, bf16[64,3584]{1,0:T(8,128)(2,1)S(1)}, u32[]{:S(2)}, u32[]{:S(2)}) collective-permute-start(bf16[64,3584]{1,0:T(8,128)(2,1)S(1)} %get-tuple-element.52), channel_id=1, source_target_pairs={{0,24},{1,9},{2,26},{3,11},{4,28},{5,13},{6,30},{7,15},{8,16},{9,1... | collective-permute-start | bytes 1376264 | tf_op jit(solution)/shard_map/ppermute | solution.py:78
  53.1 14.3 %collective-permute-start.16 = (bf16[64,3584]{1,0:T(8,128)(2,1)S(1)}, bf16[64,3584]{1,0:T(8,128)(2,1)S(1)}, u32[]{:S(2)}, u32[]{:S(2)}) collective-permute-start(bf16[64,3584]{1,0:T(8,128)(2,1)S(1)} %get-tuple-element.45.refs_6_), channel_id=1, source_target_pairs={{0,126},{1,43},{2,124},{3,41},{4,122},{5,47},{6,120},{7,45},{8,118... | collective-permute-start | bytes 1376264 | tf_op jit(solution)/shard_map/ppermute | solution.py:78
  60.2 10.4 %collective-permute-start.11 = (bf16[64,3584]{1,0:T(8,128)(2,1)S(1)}, bf16[64,3584]{1,0:T(8,128)(2,1)S(1)}, u32[]{:S(2)}, u32[]{:S(2)}) collective-permute-start(bf16[64,3584]{1,0:T(8,128)(2,1)S(1)} %add_convert_fusion.3), channel_id=1, source_target_pairs={{0,24},{1,9},{2,26},{3,11},{4,28},{5,13},{6,30},{7,15},{8,16},{9,1... | collective-permute-start | bytes 1376264 | tf_op jit(solution)/shard_map/ppermute | solution.py:78
  60.5 11.8 %collective-permute-start.13 = (bf16[64,3584]{1,0:T(8,128)(2,1)S(1)}, bf16[64,3584]{1,0:T(8,128)(2,1)S(1)}, u32[]{:S(2)}, u32[]{:S(2)}) collective-permute-start(bf16[64,3584]{1,0:T(8,128)(2,1)S(1)} %add_convert_fusion.2), channel_id=1, source_target_pairs={{0,96},{1,33},{2,98},{3,35},{4,100},{5,37},{6,102},{7,39},{8,104},... | collective-permute-start | bytes 1376264 | tf_op jit(solution)/shard_map/ppermute | solution.py:78
  61.9 10.4 %collective-permute-start.15 = (bf16[64,3584]{1,0:T(8,128)(2,1)S(1)}, bf16[64,3584]{1,0:T(8,128)(2,1)S(1)}, u32[]{:S(2)}, u32[]{:S(2)}) collective-permute-start(bf16[64,3584]{1,0:T(8,128)(2,1)S(1)} %add_convert_fusion.1), channel_id=1, source_target_pairs={{0,6},{1,3},{2,4},{3,1},{4,2},{5,7},{6,0},{7,5},{8,14},{9,11},{10,... | collective-permute-start | bytes 1376264 | tf_op jit(solution)/shard_map/ppermute | solution.py:78

commit v12 on v11

--- a/solution.py
+++ b/solution.py
@@ -35,6 +35,13 @@
     return ((z * 4 + x) * 4 + y) * 2 + c
 
 
+def partner(z, x, y, c, axes, near):
+    at = [z, x, y]
+    for axis in axes:
+        at[axis] ^= 1 if near == ((axis == 1) == (c == 1)) else 3
+    return flat(*at, c)
+
+
 def near_groups():
     seen, groups = set(), []
     for z in range(4):
@@ -43,9 +50,8 @@
                 for c in range(2):
                     if flat(z, x, y, c) in seen:
                         continue
-                    m = 3 if c else 1
                     members = [
-                        flat(z ^ (m * i), x ^ (m * j), y ^ (m * k), c)
+                        partner(z, x, y, c, [axis for axis, cross in enumerate((i, j, k)) if cross], True)
                         for i in (0, 1) for j in (0, 1) for k in (0, 1)
                     ]
                     seen.update(members)
@@ -59,10 +65,7 @@
         for x in range(4):
             for y in range(4):
                 for c in range(2):
-                    at = [x, z, y]
-                    for axis in axes:
-                        at[axis] ^= 1 if c else 3
-                    pairs.append((flat(z, x, y, c), flat(at[1], at[0], at[2], c)))
+                    pairs.append((flat(z, x, y, c), partner(z, x, y, c, [(1, 0, 2)[axis] for axis in axes], False)))
     return pairs
 
 

time: 88.2 us -> 88.5 us (level)
  starting transfers between devices: 11.3 us -> 18.1 us
  waiting for transfers between devices: 20.8 us -> 15.6 us
  blocking collectives: 40.9 us -> 39.6 us
    ppermute x14, waiting for transfers between devices: 19.7 us -> 14.8 us  [swap_far(): return lax.ppermute(values, AXES, FAR[axis])]
    ppermute x14, starting transfers between devices: 10.6 us -> 15.4 us  [swap_far(): return lax.ppermute(values, AXES, FAR[axis])]
    all_to_all x2, blocking collectives: 35.6 us -> 32.4 us  [swap_near(): lax.all_to_all(values, AXES, 0, 0, axis_index_groups=NEAR, tiled=True)]
    all_gather x2, blocking collectives: 5.22 us -> 7.2 us  [both_cores(): lax.all_gather(values, 'dev', axis_index_groups=[[i, i + 1] for i in rang...]
    ppermute x3, starting transfers between devices: 0.75 us -> 2.71 us  [to_sibling(): return lax.ppermute(values, 'dev', [(i, i ^ 1) for i in range(32)])]
  transfers between devices with their start and end apart: 17 -> 17, of which waited for: 11 -> 9; matrix products, arithmetic and copies ran while one was open for 0% -> 0% of each run, Pallas kernels for 10% -> 10%
where the time goes in v12:
time: 88.5 us; the launch traced here: 88.2 us
  blocking collectives  39.6 us (45%)
  starting transfers between devices  18.1 us (20%)
  waiting for transfers between devices  15.6 us (18%)
  Pallas kernels  14.1 us (16%)
    all_to_all x2, blocking collectives, swap_near(): lax.all_to_all(values, AXES, 0, 0, axis_index_groups=NEAR, tiled=True)  32.4 us
    ppermute x14, starting transfers between devices, swap_far(): return lax.ppermute(values, AXES, FAR[axis])  15.4 us
    ppermute x14, waiting for transfers between devices, swap_far(): return lax.ppermute(values, AXES, FAR[axis])  14.8 us
    all_gather x2, blocking collectives, both_cores(): lax.all_gather(values, 'dev', axis_index_groups=[[i, i + 1] for i in rang...  7.2 us
    pallas_call x2, Pallas kernels, hidden_units(): pl.pallas_call(functools.partial(hidden_kernel, starts), out_shape=jax.Sh...  4.12 us
    pallas_call x2, Pallas kernels, select(): pl.pallas_call(functools.partial(select_kernel, starts, len(loads)), out_...  4.01 us
    ppermute x3, starting transfers between devices, to_sibling(): return lax.ppermute(values, 'dev', [(i, i ^ 1) for i in range(32)])  2.71 us
    pallas_call x2, Pallas kernels, down_rows(): pl.pallas_call(down_kernel, out_shape=[jax.ShapeDtypeStruct((SEL, D), BF1...  2.26 us
  transfers between devices with their start and end apart: 17, of which 9 were waited for; matrix products, arithmetic and copies ran while one was open for 0% of the time, Pallas kernels for 10%

profile of v12, /device:TPU:1, one launch (start us, length us, event | category | flops | bytes accessed | tf_op | source)
XLA Modules:
  0.0 88.2 jit_solution(17319003130640103451)
XLA Ops:
  0.0 0.9 %pack.1 = bf16[8,8,3712]{2,1,0:T(8,128)(2,1)S(1)} custom-call(s32[1]{0:T(128)} %bitcast.expert_ref, bf16[4,7168]{1,0:T(4,128)(2,1)} %tokens_hbm.1, s32[4,8]{1,0:T(4,128)} %ids_hbm.1, f32[4,8]{1,0:T(4,128)} %weights_hbm.1), custom_call_target="tpu_custom_call" | custom-call | tf_op jit(solution)/shard_map/pack/pallas_call | solution.py:119
  1.0 18.4 %all_to_all.10 = bf16[8,8,3712]{2,1,0:T(8,128)(2,1)S(1)} all-to-all(bf16[8,8,3712]{2,1,0:T(8,128)(2,1)S(1)} %pack.1), channel_id=1, replica_groups={{0,2,24,26,32,34,56,58},{1,7,9,15,97,103,105,111},{3,5,11,13,99,101,107..., dimensions={0} | all-to-all | bytes 950272 | tf_op jit(solution)/shard_map/all_to_all | solution.py:77
  19.5 1.3 %collective-permute-start = (bf16[64,3712]{1,0:T(8,128)(2,1)S(1)}, bf16[64,3712]{1,0:T(8,128)(2,1)S(1)}, u32[]{:S(2)}, u32[]{:S(2)}) collective-permute-start(bf16[64,3712]{1,0:T(8,128)(2,1)S(1)} %bitcast.12), channel_id=1, source_target_pairs={{0,8},{1,25},{2,10},{3,27},{4,12},{5,29},{6,14},{7,31},{8,0},{9,17... | collective-permute-start | bytes 1425416 | tf_op jit(solution)/shard_map/ppermute | solution.py:81
  20.8 3.6 %collective-permute-start.6 = (bf16[64,3712]{1,0:T(8,128)(2,1)S(1)}, bf16[64,3712]{1,0:T(8,128)(2,1)S(1)}, u32[]{:S(2)}, u32[]{:S(2)}) collective-permute-start(bf16[64,3712]{1,0:T(8,128)(2,1)S(1)} %bitcast.13), channel_id=1, source_target_pairs={{0,110},{1,59},{2,108},{3,57},{4,106},{5,63},{6,104},{7,61},{8,102... | collective-permute-start | bytes 1425416 | tf_op jit(solution)/shard_map/ppermute | solution.py:81
  24.4 2.8 %collective-permute-done.2.refs_2_ = bf16[64,3712]{1,0:T(8,128)(2,1)S(1)} collective-permute-done((bf16[64,3712]{1,0:T(8,128)(2,1)S(1)}, bf16[64,3712]{1,0:T(8,128)(2,1)S(1)}, u32[]{:S(2)}, u32[]{:S(2)}) %collective-permute-start.2) | collective-permute-done | bytes 475168 | tf_op jit(solution)/shard_map/ppermute | solution.py:81
  27.3 1.3 %collective-permute-start.3 = (bf16[64,3712]{1,0:T(8,128)(2,1)S(1)}, bf16[64,3712]{1,0:T(8,128)(2,1)S(1)}, u32[]{:S(2)}, u32[]{:S(2)}) collective-permute-start(bf16[64,3712]{1,0:T(8,128)(2,1)S(1)} %collective-permute-done.1.refs_1_), channel_id=1, source_target_pairs={{0,8},{1,25},{2,10},{3,27},{4,12},{5,29},{6,14},{7,31},{8,0},{9,17... | collective-permute-start | bytes 1425416 | tf_op jit(solution)/shard_map/ppermute | solution.py:81
  28.6 1.4 %collective-permute-start.5 = (bf16[64,3712]{1,0:T(8,128)(2,1)S(1)}, bf16[64,3712]{1,0:T(8,128)(2,1)S(1)}, u32[]{:S(2)}, u32[]{:S(2)}) collective-permute-start(bf16[64,3712]{1,0:T(8,128)(2,1)S(1)} %collective-permute-done.refs_0_), channel_id=1, source_target_pairs={{0,6},{1,3},{2,4},{3,1},{4,2},{5,7},{6,0},{7,5},{8,14},{9,11},{10,... | collective-permute-start | bytes 1425416 | tf_op jit(solution)/shard_map/ppermute | solution.py:81
  29.9 3.1 %select.2 = (bf16[64,7296]{1,0:T(8,128)(2,1)S(1)}, bf16[64,3584]{1,0:T(8,128)(2,1)S(1)}, bf16[64,3712]{1,0:T(8,128)(2,1)S(1)}, bf16[1,7168,512]{2,1,0:T(8,128)(2,1)S(1)}) custom-call(s32[1]{0:T(128)} %bitcast.expert_ref, bf16[64,3712]{1,0:T(8,128)(2,1)S(1)} %collective-permute-done.refs_0_, bf16[64,3712]{1,0:T(8,128)(2,1)S(1)} %collective-permute-done.1.refs_1_, ...), custom_call_target="tpu_custom_call" | custom-call | flops 1000 | bytes 1000 | tf_op jit(solution)/shard_map/select/pallas_call | solution.py:195
  33.0 4.7 %all-gather = bf16[128,3584]{1,0:T(8,128)(2,1)S(1)} all-gather(bf16[64,3584]{1,0:T(8,128)(2,1)S(1)} %get-tuple-element.30), channel_id=2, replica_groups={{0,1},{2,3},{4,5},{6,7},{8,9},{10,11},{12,13},{14,15},{16,17},{18,19},{..., dimensions={0}, use_global_device_ids=true | all-gather | bytes 1376256 | tf_op jit(solution)/shard_map/all_gather | solution.py:85
  37.8 2.5 %all-gather.1 = bf16[128,3712]{1,0:T(8,128)(2,1)S(1)} all-gather(bf16[64,3712]{1,0:T(8,128)(2,1)S(1)} %get-tuple-element.31), channel_id=3, replica_groups={{0,1},{2,3},{4,5},{6,7},{8,9},{10,11},{12,13},{14,15},{16,17},{18,19},{..., dimensions={0}, use_global_device_ids=true | all-gather | bytes 1425408 | tf_op jit(solution)/shard_map/all_gather | solution.py:85
  40.3 0.9 %select.3 = (bf16[64,7296]{1,0:T(8,128)(2,1)S(1)}, bf16[64,7296]{1,0:T(8,128)(2,1)S(1)}) custom-call(s32[1]{0:T(128)} %bitcast.expert_ref, bf16[64,3712]{1,0:T(8,128)(2,1)S(1)} %collective-permute-done.3.refs_0_, bf16[64,3712]{1,0:T(8,128)(2,1)S(1)} %collective-permute-done.5.refs_1_, bf16[64,3712]{1,0:T(8,128)(2,1)S(1)} %collective-permute-done.4.refs_2_, ...), custom_call_target="tpu_custom_call" | custom-call | flops 1000 | bytes 1000 | tf_op jit(solution)/shard_map/select/pallas_call | solution.py:195
  41.2 2.0 %collective-permute-start.7 = (bf16[64,7296]{1,0:T(8,128)(2,1)S(1)}, bf16[64,7296]{1,0:T(8,128)(2,1)S(1)}, u32[]{:S(2)}, u32[]{:S(2)}) collective-permute-start(bf16[64,7296]{1,0:T(8,128)(2,1)S(1)} %get-tuple-element.40), channel_id=1, source_target_pairs={{0,1},{1,0},{2,3},{3,2},{4,5},{5,4},{6,7},{7,6},{8,9},{9,8},{10,11... | collective-permute-start | bytes 2801672 | tf_op jit(solution)/shard_map/ppermute | solution.py:89
  43.2 2.1 %hidden.2.refs_3_.hidden_ref = bf16[128,512]{1,0:T(8,128)(2,1)S(1)} custom-call(s32[1]{0:T(128)} %bitcast.expert_ref, bf16[64,7296]{1,0:T(8,128)(2,1)S(1)} %get-tuple-element.29.mine_ref, bf16[2,64,3584]{2,1,0:T(8,128)(2,1)S(1)} %bitcast.20, bf16[2,64,3712]{2,1,0:T(8,128)(2,1)S(1)} %bitcast.19, bf16[1,7168,512]{2,1,0:T(8,128)(2,1)S(1)} %bitcast.7, ...), custom_call_target="tpu_custom_call" | custom-call | flops 1000 | bytes 1000 | tf_op jit(solution)/shard_map/hidden/pallas_call | solution.py:235
  45.3 2.1 %hidden.3.hidden_ref = bf16[128,512]{1,0:T(8,128)(2,1)S(1)} custom-call(s32[1]{0:T(128)} %bitcast.expert_ref, bf16[64,7296]{1,0:T(8,128)(2,1)S(1)} %get-tuple-element.39.refs_4_.mine_ref, bf16[64,7296]{1,0:T(8,128)(2,1)S(1)} %collective-permute-done.7.refs_0_, bf16[1,7168,512]{2,1,0:T(8,128)(2,1)S(1)} %bitcast.7, ...), custom_call_target="tpu_custom_call" | custom-call | flops 1000 | bytes 1000 | tf_op jit(solution)/shard_map/hidden/pallas_call | solution.py:235
  47.4 1.1 %down.2 = (bf16[64,7168]{1,0:T(8,128)(2,1)S(1)}, bf16[64,7168]{1,0:T(8,128)(2,1)S(1)}) custom-call(bf16[128,512]{1,0:T(8,128)(2,1)S(1)} %hidden.3.hidden_ref, bf16[1,512,7168]{2,1,0:T(8,128)(2,1)S(1)} %bitcast.9, bf16[64,3712]{1,0:T(8,128)(2,1)S(1)} %bitcast.17), custom_call_target="tpu_custom_call" | custom-call | flops 1000 | bytes 1000 | tf_op jit(solution)/shard_map/down/pallas_call | solution.py:257
  48.6 0.5 collective-permute-start.9
  49.0 1.1 %down.3 = (bf16[64,7168]{1,0:T(8,128)(2,1)S(1)}, bf16[64,7168]{1,0:T(8,128)(2,1)S(1)}) custom-call(bf16[128,512]{1,0:T(8,128)(2,1)S(1)} %hidden.2.refs_3_.hidden_ref, bf16[1,512,7168]{2,1,0:T(8,128)(2,1)S(1)} %bitcast.9, bf16[64,7168]{1,0:T(8,128)(2,1)S(1)} %get-tuple-element.41.after_ref.refs_4_), custom_call_target="tpu_custom_call" | custom-call | flops 1000 | bytes 1000 | tf_op jit(solution)/shard_map/down/pallas_call | solution.py:257
  50.4 0.7 collective-permute-done.9.refs_5_
  51.1 1.1 %spread.2 = (bf16[64,3584]{1,0:T(8,128)(2,1)S(1)}, bf16[64,3584]{1,0:T(8,128)(2,1)S(1)}, bf16[64,3584]{1,0:T(8,128)(2,1)S(1)}, bf16[64,3584]{1,0:T(8,128)(2,1)S(1)}) custom-call(s32[1]{0:T(128)} %bitcast.expert_ref, bf16[64,3712]{1,0:T(8,128)(2,1)S(1)} %collective-permute-done.3.refs_0_, bf16[64,3712]{1,0:T(8,128)(2,1)S(1)} %collective-permute-done.5.refs_1_, ...), custom_call_target="tpu_custom_call" | custom-call | flops 1000 | bytes 1000 | tf_op jit(solution)/shard_map/spread/pallas_call | solution.py:300
  52.2 0.7 collective-permute-start.10
  53.0 4.3 %collective-permute-start.16 = (bf16[64,3584]{1,0:T(8,128)(2,1)S(1)}, bf16[64,3584]{1,0:T(8,128)(2,1)S(1)}, u32[]{:S(2)}, u32[]{:S(2)}) collective-permute-start(bf16[64,3584]{1,0:T(8,128)(2,1)S(1)} %get-tuple-element.45.refs_6_), channel_id=1, source_target_pairs={{0,110},{1,59},{2,108},{3,57},{4,106},{5,63},{6,104},{7,61},{8,102... | collective-permute-start | bytes 1376264 | tf_op jit(solution)/shard_map/ppermute | solution.py:81
  57.3 1.1 %spread.3 = (bf16[64,3584]{1,0:T(8,128)(2,1)S(1)}, bf16[64,3584]{1,0:T(8,128)(2,1)S(1)}, bf16[64,3584]{1,0:T(8,128)(2,1)S(1)}, bf16[64,3584]{1,0:T(8,128)(2,1)S(1)}) custom-call(s32[1]{0:T(128)} %bitcast.expert_ref, bf16[64,3712]{1,0:T(8,128)(2,1)S(1)} %collective-permute-done.refs_0_, bf16[64,3712]{1,0:T(8,128)(2,1)S(1)} %collective-permute-done.1.refs_1_, ...), custom_call_target="tpu_custom_call" | custom-call | flops 1000 | bytes 1000 | tf_op jit(solution)/shard_map/spread/pallas_call | solution.py:300
  58.4 1.5 %collective-permute-done.10 = bf16[64,3584]{1,0:T(8,128)(2,1)S(1)} collective-permute-done((bf16[64,3584]{1,0:T(8,128)(2,1)S(1)}, bf16[64,3584]{1,0:T(8,128)(2,1)S(1)}, u32[]{:S(2)}, u32[]{:S(2)}) %collective-permute-start.10) | collective-permute-done | bytes 458784 | tf_op jit(solution)/shard_map/ppermute | solution.py:81
  60.0 0.4 collective-permute-start.11
  60.6 1.0 %collective-permute-start.13 = (bf16[64,3584]{1,0:T(8,128)(2,1)S(1)}, bf16[64,3584]{1,0:T(8,128)(2,1)S(1)}, u32[]{:S(2)}, u32[]{:S(2)}) collective-permute-start(bf16[64,3584]{1,0:T(8,128)(2,1)S(1)} %add_convert_fusion.2), channel_id=1, source_target_pairs={{0,96},{1,33},{2,98},{3,35},{4,100},{5,37},{6,102},{7,39},{8,104},... | collective-permute-start | bytes 1376264 | tf_op jit(solution)/shard_map/ppermute | solution.py:81
  61.8 1.2 %collective-permute-start.15 = (bf16[64,3584]{1,0:T(8,128)(2,1)S(1)}, bf16[64,3584]{1,0:T(8,128)(2,1)S(1)}, u32[]{:S(2)}, u32[]{:S(2)}) collective-permute-start(bf16[64,3584]{1,0:T(8,128)(2,1)S(1)} %add_convert_fusion.1), channel_id=1, source_target_pairs={{0,6},{1,3},{2,4},{3,1},{4,2},{5,7},{6,0},{7,5},{8,14},{9,11},{10,... | collective-permute-start | bytes 1376264 | tf_op jit(solution)/shard_map/ppermute | solution.py:81
  63.1 5.4 %collective-permute-done.16 = bf16[64,3584]{1,0:T(8,128)(2,1)S(1)} collective-permute-done((bf16[64,3584]{1,0:T(8,128)(2,1)S(1)}, bf16[64,3584]{1,0:T(8,128)(2,1)S(1)}, u32[]{:S(2)}, u32[]{:S(2)}) %collective-permute-start.16) | collective-permute-done | bytes 458784 | tf_op jit(solution)/shard_map/ppermute | solution.py:81
  68.5 3.0 %collective-permute-done.11 = bf16[64,3584]{1,0:T(8,128)(2,1)S(1)} collective-permute-done((bf16[64,3584]{1,0:T(8,128)(2,1)S(1)}, bf16[64,3584]{1,0:T(8,128)(2,1)S(1)}, u32[]{:S(2)}, u32[]{:S(2)}) %collective-permute-start.11) | collective-permute-done | bytes 458784 | tf_op jit(solution)/shard_map/ppermute | solution.py:81
  71.5 1.7 %collective-permute-done.13 = bf16[64,3584]{1,0:T(8,128)(2,1)S(1)} collective-permute-done((bf16[64,3584]{1,0:T(8,128)(2,1)S(1)}, bf16[64,3584]{1,0:T(8,128)(2,1)S(1)}, u32[]{:S(2)}, u32[]{:S(2)}) %collective-permute-start.13) | collective-permute-done | bytes 458784 | tf_op jit(solution)/shard_map/ppermute | solution.py:81
  73.2 0.3 fusion
  73.5 14.0 %all_to_all.11.parts_ref = bf16[8,8,3584]{2,1,0:T(8,128)(2,1)S(1)} all-to-all(bf16[8,8,3584]{2,1,0:T(8,128)(2,1)S(1)} %fusion), channel_id=1, replica_groups={{0,2,24,26,32,34,56,58},{1,7,9,15,97,103,105,111},{3,5,11,13,99,101,107..., dimensions={0} | all-to-all | bytes 917504 | tf_op jit(solution)/shard_map/all_to_all | solution.py:77
  87.5 0.7 finish.1
  (30 shorter events, 1.2 us)
Async XLA Ops:
  19.4 23.8 %slice-start = ((s8[7340032]{0:T(1024)(128)(4,1)}), s8[4194304]{0:T(1024)(128)(4,1)S(1)}, s32[]{:S(2)}) async-start(s8[7340032]{0:T(1024)(128)(4,1)} %bitcast.6), calls=%async_computation.2 | async-start | bytes 8388608
  19.4 23.8 %slice-start.1 = ((s8[7340032]{0:T(1024)(128)(4,1)}), s8[3145728]{0:T(1024)(128)(4,1)S(1)}, s32[]{:S(2)}) async-start(s8[7340032]{0:T(1024)(128)(4,1)} %bitcast.6), calls=%async_computation.3 | async-start | bytes 6291456
  19.4 7.8 %collective-permute-start.2 = (bf16[64,3712]{1,0:T(8,128)(2,1)S(1)}, bf16[64,3712]{1,0:T(8,128)(2,1)S(1)}, u32[]{:S(2)}, u32[]{:S(2)}) collective-permute-start(bf16[64,3712]{1,0:T(8,128)(2,1)S(1)} %bitcast.10), channel_id=1, source_target_pairs={{0,6},{1,3},{2,4},{3,1},{4,2},{5,7},{6,0},{7,5},{8,14},{9,11},{10,... | collective-permute-start | bytes 1425416 | tf_op jit(solution)/shard_map/ppermute | solution.py:81
  19.4 7.9 %collective-permute-start.1 = (bf16[64,3712]{1,0:T(8,128)(2,1)S(1)}, bf16[64,3712]{1,0:T(8,128)(2,1)S(1)}, u32[]{:S(2)}, u32[]{:S(2)}) collective-permute-start(bf16[64,3712]{1,0:T(8,128)(2,1)S(1)} %bitcast.11), channel_id=1, source_target_pairs={{0,96},{1,33},{2,98},{3,35},{4,100},{5,37},{6,102},{7,39},{8,104},... | collective-permute-start | bytes 1425416 | tf_op jit(solution)/shard_map/ppermute | solution.py:81
  19.5 9.1 %collective-permute-start = (bf16[64,3712]{1,0:T(8,128)(2,1)S(1)}, bf16[64,3712]{1,0:T(8,128)(2,1)S(1)}, u32[]{:S(2)}, u32[]{:S(2)}) collective-permute-start(bf16[64,3712]{1,0:T(8,128)(2,1)S(1)} %bitcast.12), channel_id=1, source_target_pairs={{0,8},{1,25},{2,10},{3,27},{4,12},{5,29},{6,14},{7,31},{8,0},{9,17... | collective-permute-start | bytes 1425416 | tf_op jit(solution)/shard_map/ppermute | solution.py:81
  20.8 19.4 %collective-permute-start.6 = (bf16[64,3712]{1,0:T(8,128)(2,1)S(1)}, bf16[64,3712]{1,0:T(8,128)(2,1)S(1)}, u32[]{:S(2)}, u32[]{:S(2)}) collective-permute-start(bf16[64,3712]{1,0:T(8,128)(2,1)S(1)} %bitcast.13), channel_id=1, source_target_pairs={{0,110},{1,59},{2,108},{3,57},{4,106},{5,63},{6,104},{7,61},{8,102... | collective-permute-start | bytes 1425416 | tf_op jit(solution)/shard_map/ppermute | solution.py:81
  27.2 13.1 %collective-permute-start.4 = (bf16[64,3712]{1,0:T(8,128)(2,1)S(1)}, bf16[64,3712]{1,0:T(8,128)(2,1)S(1)}, u32[]{:S(2)}, u32[]{:S(2)}) collective-permute-start(bf16[64,3712]{1,0:T(8,128)(2,1)S(1)} %collective-permute-done.2.refs_2_), channel_id=1, source_target_pairs={{0,96},{1,33},{2,98},{3,35},{4,100},{5,37},{6,102},{7,39},{8,104},... | collective-permute-start | bytes 1425416 | tf_op jit(solution)/shard_map/ppermute | solution.py:81
  27.3 13.0 %collective-permute-start.3 = (bf16[64,3712]{1,0:T(8,128)(2,1)S(1)}, bf16[64,3712]{1,0:T(8,128)(2,1)S(1)}, u32[]{:S(2)}, u32[]{:S(2)}) collective-permute-start(bf16[64,3712]{1,0:T(8,128)(2,1)S(1)} %collective-permute-done.1.refs_1_), channel_id=1, source_target_pairs={{0,8},{1,25},{2,10},{3,27},{4,12},{5,29},{6,14},{7,31},{8,0},{9,17... | collective-permute-start | bytes 1425416 | tf_op jit(solution)/shard_map/ppermute | solution.py:81
  28.6 11.7 %collective-permute-start.5 = (bf16[64,3712]{1,0:T(8,128)(2,1)S(1)}, bf16[64,3712]{1,0:T(8,128)(2,1)S(1)}, u32[]{:S(2)}, u32[]{:S(2)}) collective-permute-start(bf16[64,3712]{1,0:T(8,128)(2,1)S(1)} %collective-permute-done.refs_0_), channel_id=1, source_target_pairs={{0,6},{1,3},{2,4},{3,1},{4,2},{5,7},{6,0},{7,5},{8,14},{9,11},{10,... | collective-permute-start | bytes 1425416 | tf_op jit(solution)/shard_map/ppermute | solution.py:81
  40.3 7.2 %slice-start.2 = ((s8[7340032]{0:T(1024)(128)(4,1)}), s8[4194304]{0:T(1024)(128)(4,1)S(1)}, s32[]{:S(2)}) async-start(s8[7340032]{0:T(1024)(128)(4,1)} %bitcast.8), calls=%async_computation.4 | async-start | bytes 8388608
  41.2 4.2 %collective-permute-start.7 = (bf16[64,7296]{1,0:T(8,128)(2,1)S(1)}, bf16[64,7296]{1,0:T(8,128)(2,1)S(1)}, u32[]{:S(2)}, u32[]{:S(2)}) collective-permute-start(bf16[64,7296]{1,0:T(8,128)(2,1)S(1)} %get-tuple-element.40), channel_id=1, source_target_pairs={{0,1},{1,0},{2,3},{3,2},{4,5},{5,4},{6,7},{7,6},{8,9},{9,8},{10,11... | collective-permute-start | bytes 2801672 | tf_op jit(solution)/shard_map/ppermute | solution.py:89
  43.2 4.2 %slice-start.3 = ((s8[7340032]{0:T(1024)(128)(4,1)}), s8[3145728]{0:T(1024)(128)(4,1)S(1)}, s32[]{:S(2)}) async-start(s8[7340032]{0:T(1024)(128)(4,1)} %bitcast.8), calls=%async_computation.5 | async-start | bytes 6291456
  48.6 2.6 %collective-permute-start.9 = (bf16[64,7168]{1,0:T(8,128)(2,1)S(1)}, bf16[64,7168]{1,0:T(8,128)(2,1)S(1)}, u32[]{:S(2)}, u32[]{:S(2)}) collective-permute-start(bf16[64,7168]{1,0:T(8,128)(2,1)S(1)} %get-tuple-element.44), channel_id=1, source_target_pairs={{0,1},{1,0},{2,3},{3,2},{4,5},{5,4},{6,7},{7,6},{8,9},{9,8},{10,11... | collective-permute-start | bytes 2752520 | tf_op jit(solution)/shard_map/ppermute | solution.py:89
  50.2 7.2 %collective-permute-start.8 = (bf16[64,7168]{1,0:T(8,128)(2,1)S(1)}, bf16[64,7168]{1,0:T(8,128)(2,1)S(1)}, u32[]{:S(2)}, u32[]{:S(2)}) collective-permute-start(bf16[64,7168]{1,0:T(8,128)(2,1)S(1)} %get-tuple-element.43), channel_id=1, source_target_pairs={{0,1},{1,0},{2,3},{3,2},{4,5},{5,4},{6,7},{7,6},{8,9},{9,8},{10,11... | collective-permute-start | bytes 2752520 | tf_op jit(solution)/shard_map/ppermute | solution.py:89
  52.2 7.7 %collective-permute-start.10 = (bf16[64,3584]{1,0:T(8,128)(2,1)S(1)}, bf16[64,3584]{1,0:T(8,128)(2,1)S(1)}, u32[]{:S(2)}, u32[]{:S(2)}) collective-permute-start(bf16[64,3584]{1,0:T(8,128)(2,1)S(1)} %get-tuple-element.48), channel_id=1, source_target_pairs={{0,96},{1,33},{2,98},{3,35},{4,100},{5,37},{6,102},{7,39},{8,104},... | collective-permute-start | bytes 1376264 | tf_op jit(solution)/shard_map/ppermute | solution.py:81
  52.9 7.6 %collective-permute-start.12 = (bf16[64,3584]{1,0:T(8,128)(2,1)S(1)}, bf16[64,3584]{1,0:T(8,128)(2,1)S(1)}, u32[]{:S(2)}, u32[]{:S(2)}) collective-permute-start(bf16[64,3584]{1,0:T(8,128)(2,1)S(1)} %get-tuple-element.50), channel_id=1, source_target_pairs={{0,6},{1,3},{2,4},{3,1},{4,2},{5,7},{6,0},{7,5},{8,14},{9,11},{10,... | collective-permute-start | bytes 1376264 | tf_op jit(solution)/shard_map/ppermute | solution.py:81
  52.9 8.8 %collective-permute-start.14 = (bf16[64,3584]{1,0:T(8,128)(2,1)S(1)}, bf16[64,3584]{1,0:T(8,128)(2,1)S(1)}, u32[]{:S(2)}, u32[]{:S(2)}) collective-permute-start(bf16[64,3584]{1,0:T(8,128)(2,1)S(1)} %get-tuple-element.52), channel_id=1, source_target_pairs={{0,8},{1,25},{2,10},{3,27},{4,12},{5,29},{6,14},{7,31},{8,0},{9,17... | collective-permute-start | bytes 1376264 | tf_op jit(solution)/shard_map/ppermute | solution.py:81
  53.0 15.5 %collective-permute-start.16 = (bf16[64,3584]{1,0:T(8,128)(2,1)S(1)}, bf16[64,3584]{1,0:T(8,128)(2,1)S(1)}, u32[]{:S(2)}, u32[]{:S(2)}) collective-permute-start(bf16[64,3584]{1,0:T(8,128)(2,1)S(1)} %get-tuple-element.45.refs_6_), channel_id=1, source_target_pairs={{0,110},{1,59},{2,108},{3,57},{4,106},{5,63},{6,104},{7,61},{8,102... | collective-permute-start | bytes 1376264 | tf_op jit(solution)/shard_map/ppermute | solution.py:81
  60.0 11.5 %collective-permute-start.11 = (bf16[64,3584]{1,0:T(8,128)(2,1)S(1)}, bf16[64,3584]{1,0:T(8,128)(2,1)S(1)}, u32[]{:S(2)}, u32[]{:S(2)}) collective-permute-start(bf16[64,3584]{1,0:T(8,128)(2,1)S(1)} %add_convert_fusion.3), channel_id=1, source_target_pairs={{0,8},{1,25},{2,10},{3,27},{4,12},{5,29},{6,14},{7,31},{8,0},{9,17... | collective-permute-start | bytes 1376264 | tf_op jit(solution)/shard_map/ppermute | solution.py:81
  60.6 12.6 %collective-permute-start.13 = (bf16[64,3584]{1,0:T(8,128)(2,1)S(1)}, bf16[64,3584]{1,0:T(8,128)(2,1)S(1)}, u32[]{:S(2)}, u32[]{:S(2)}) collective-permute-start(bf16[64,3584]{1,0:T(8,128)(2,1)S(1)} %add_convert_fusion.2), channel_id=1, source_target_pairs={{0,96},{1,33},{2,98},{3,35},{4,100},{5,37},{6,102},{7,39},{8,104},... | collective-permute-start | bytes 1376264 | tf_op jit(solution)/shard_map/ppermute | solution.py:81
  61.8 11.4 %collective-permute-start.15 = (bf16[64,3584]{1,0:T(8,128)(2,1)S(1)}, bf16[64,3584]{1,0:T(8,128)(2,1)S(1)}, u32[]{:S(2)}, u32[]{:S(2)}) collective-permute-start(bf16[64,3584]{1,0:T(8,128)(2,1)S(1)} %add_convert_fusion.1), channel_id=1, source_target_pairs={{0,6},{1,3},{2,4},{3,1},{4,2},{5,7},{6,0},{7,5},{8,14},{9,11},{10,... | collective-permute-start | bytes 1376264 | tf_op jit(solution)/shard_map/ppermute | solution.py:81

commit v13 on v11

--- a/solution.py
+++ b/solution.py
@@ -262,48 +262,58 @@
     )(hidden, down, after)
 
 
-def spread_kernel(expert_ref, *refs):
-    refs = list(refs)
-    exts = [refs.pop(0) for _ in range(4)]
-    mine_ref, theirs_ref = refs[:2]
-    outs = [refs[3 + i] for i in range(4)]
-    place_scr = refs[7]
+def places_kernel(expert_ref, a_ref, b_ref, c_ref, d_ref, after_ref, out_ref):
+    del after_ref
     own = expert_ref[0]
     turn = lax.broadcasted_iota(jnp.int32, (EXT, EXT), 1)
     experts = jnp.where(turn == 0, own, own ^ 1)
     wanted = jnp.where(expert_lanes(experts, (EXT, EXT), 0) & (turn < 2), 1.0, 0.0).astype(BF16)
-    ext = jnp.concatenate([ref[:, HALF:] for ref in exts], axis=0)
+    ext = jnp.concatenate([ref[:, HALF:] for ref in (a_ref, b_ref, c_ref, d_ref)], axis=0)
     chosen = jnp.dot(ext, wanted, preferred_element_type=F32) > 0
-    first = lax.broadcasted_iota(jnp.int32, (PART, PART), 0)
-    second = lax.broadcasted_iota(jnp.int32, (PART, PART), 1)
-    earlier = jnp.where((first // 4 == second // 4) & (second < first), 1.0, 0.0).astype(BF16)
+    row = lax.broadcasted_iota(jnp.int32, (PART, PART), 0)
+    other = lax.broadcasted_iota(jnp.int32, (PART, PART), 1)
+    earlier = jnp.where((row // 4 == other // 4) & (other < row), 1.0, 0.0).astype(BF16)
     rank = jnp.dot(earlier, jnp.where(chosen, 1.0, 0.0).astype(BF16), preferred_element_type=F32)
     token = lax.broadcasted_iota(jnp.int32, (PART, EXT), 0)
     place = jnp.where(chosen, token // 8 * 2 + rank.astype(jnp.int32), -1)
-    column = lax.broadcasted_iota(jnp.int32, (PART, 2 * SEL), 1)
-    hit = jnp.where(column < SEL, place[:, 0:1], place[:, 1:2]) == column % SEL
-    is_left = lax.broadcasted_iota(jnp.int32, (PART, 2 * SEL), 0) % 8 < 4
-    place_scr[:, : 2 * SEL] = jnp.where(hit & is_left, 1.0, 0.0).astype(BF16)
-    place_scr[:, 2 * SEL :] = jnp.where(hit & ~is_left, 1.0, 0.0).astype(BF16)
+    column = lax.broadcasted_iota(jnp.int32, (PART, 4 * SEL), 1)
+    hit = jnp.where(column // SEL % 2 == 0, place[:, 0:1], place[:, 1:2]) == column % SEL
+    is_left = row % 8 < 4
+    out_ref[...] = jnp.where(hit & (is_left == (column < 2 * SEL)), 1.0, 0.0).astype(BF16)
+
+
+def places(expert, blocks, after):
+    return pl.pallas_call(
+        places_kernel,
+        out_shape=jax.ShapeDtypeStruct((PART, 4 * SEL), BF16),
+        in_specs=[SMEM] + [VMEM] * 4 + [ANY],
+        out_specs=VMEM,
+        compiler_params=SMALL,
+        cost_estimate=BRIEF,
+        name="places",
+    )(expert, *blocks, after)
+
+
+def spread_kernel(place_ref, mine_ref, theirs_ref, after_ref, *outs):
+    del after_ref
     for n in range(0, HALF, 512):
         left, right = slice(n, n + 512), slice(HALF + n, HALF + n + 512)
         y = jnp.concatenate([mine_ref[:, left], theirs_ref[:, left], mine_ref[:, right], theirs_ref[:, right]], axis=0)
-        value = jnp.dot(place_scr[...], y, preferred_element_type=F32).astype(BF16)
+        value = jnp.dot(place_ref[...], y, preferred_element_type=F32).astype(BF16)
         for i in range(4):
             outs[i][:, left] = value[i * BLOCK : (i + 1) * BLOCK]
 
 
-def spread(expert, blocks, mine, theirs, after):
+def spread(place, mine, theirs, after):
     return pl.pallas_call(
         spread_kernel,
         out_shape=[jax.ShapeDtypeStruct((BLOCK, HALF), BF16)] * 4,
-        in_specs=[SMEM] + [VMEM] * 6 + [ANY],
+        in_specs=[VMEM] * 3 + [ANY],
         out_specs=[VMEM] * 4,
-        scratch_shapes=[pltpu.VMEM((PART, 4 * SEL), BF16)],
         compiler_params=SMALL,
         cost_estimate=BRIEF,
         name="spread",
-    )(expert, *blocks, mine, theirs, after)
+    )(place, mine, theirs, after)
 
 
 def add(*terms):
@@ -351,10 +361,11 @@
     returned = to_sibling(theirs)
     result_near, theirs = down_rows(hidden_near, down, result)
     returned_near = to_sibling(theirs)
-    y_xy, y_zx, y_yz, y_xyz = spread(expert, far, result, returned, result_near)
+    place_far = places(expert, far, result_near)
+    y_xy, y_zx, y_yz, y_xyz = spread(place_far, result, returned, result_near)
     at_x, at_y, at_z = swap_far(y_xy, 1), swap_far(y_yz, 2), swap_far(y_zx, 0)
     at_own = swap_far(y_xyz, 3)
-    y_x, y_y, y_z, y_own = spread(expert, near, result_near, returned_near, y_xyz)
+    y_x, y_y, y_z, y_own = spread(places(expert, near, y_xyz), result_near, returned_near, y_xyz)
     total = add(
         y_own,
         swap_far(add(y_x, at_x), 0),

time: 88.2 us -> 87.8 us (level)
  no operation moved by 1% of the time
where the time goes in v13:
time: 87.8 us; the launch traced here: 87.5 us
  blocking collectives  40.9 us (47%)
  waiting for transfers between devices  20.3 us (23%)
  Pallas kernels  14.2 us (16%)
  starting transfers between devices  11.3 us (13%)
    all_to_all x2, blocking collectives, swap_near(): lax.all_to_all(values, AXES, 0, 0, axis_index_groups=NEAR, tiled=True)  35.6 us
    ppermute x14, waiting for transfers between devices, swap_far(): return lax.ppermute(values, AXES, FAR[axis])  19.6 us
    ppermute x14, starting transfers between devices, swap_far(): return lax.ppermute(values, AXES, FAR[axis])  10.6 us
    all_gather x2, blocking collectives, both_cores(): lax.all_gather(values, 'dev', axis_index_groups=[[i, i + 1] for i in rang...  5.22 us
    pallas_call x2, Pallas kernels, hidden_units(): pl.pallas_call(functools.partial(hidden_kernel, starts), out_shape=jax.Sh...  4.12 us
    pallas_call x2, Pallas kernels, select(): pl.pallas_call(functools.partial(select_kernel, starts, len(loads)), out_...  4.01 us
    pallas_call x2, Pallas kernels, down_rows(): pl.pallas_call(down_kernel, out_shape=[jax.ShapeDtypeStruct((SEL, D), BF1...  2.28 us
  transfers between devices with their start and end apart: 17, of which 11 were waited for; matrix products, arithmetic and copies ran while one was open for 0% of the time, Pallas kernels for 10%

profile of v13, /device:TPU:1, one launch (start us, length us, event | category | flops | bytes accessed | tf_op | source)
XLA Modules:
  0.0 87.5 jit_solution(6366536820152261331)
XLA Ops:
  0.0 0.9 %pack.1 = bf16[8,8,3712]{2,1,0:T(8,128)(2,1)S(1)} custom-call(s32[1]{0:T(128)} %bitcast.expert_ref, bf16[4,7168]{1,0:T(4,128)(2,1)} %tokens_hbm.1, s32[4,8]{1,0:T(4,128)} %ids_hbm.1, f32[4,8]{1,0:T(4,128)} %weights_hbm.1), custom_call_target="tpu_custom_call" | custom-call | tf_op jit(solution)/shard_map/pack/pallas_call | solution.py:116
  1.0 21.0 %all_to_all.10 = bf16[8,8,3712]{2,1,0:T(8,128)(2,1)S(1)} all-to-all(bf16[8,8,3712]{2,1,0:T(8,128)(2,1)S(1)} %pack.1), channel_id=1, replica_groups={{0,2,8,10,32,34,40,42},{1,7,25,31,97,103,121,127},{3,5,27,29,99,101,123..., dimensions={0} | all-to-all | bytes 950272 | tf_op jit(solution)/shard_map/all_to_all | solution.py:74
  22.2 3.6 %collective-permute-start.6 = (bf16[64,3712]{1,0:T(8,128)(2,1)S(1)}, bf16[64,3712]{1,0:T(8,128)(2,1)S(1)}, u32[]{:S(2)}, u32[]{:S(2)}) collective-permute-start(bf16[64,3712]{1,0:T(8,128)(2,1)S(1)} %bitcast.13), channel_id=1, source_target_pairs={{0,126},{1,43},{2,124},{3,41},{4,122},{5,47},{6,120},{7,45},{8,118... | collective-permute-start | bytes 1425416 | tf_op jit(solution)/shard_map/ppermute | solution.py:78
  25.8 3.7 %collective-permute-done.2.refs_2_.c_ref = bf16[64,3712]{1,0:T(8,128)(2,1)S(1)} collective-permute-done((bf16[64,3712]{1,0:T(8,128)(2,1)S(1)}, bf16[64,3712]{1,0:T(8,128)(2,1)S(1)}, u32[]{:S(2)}, u32[]{:S(2)}) %collective-permute-start.2) | collective-permute-done | bytes 475168 | tf_op jit(solution)/shard_map/ppermute | solution.py:78
  29.6 0.4 collective-permute-done.refs_0_.a_ref
  29.9 1.3 %collective-permute-start.5 = (bf16[64,3712]{1,0:T(8,128)(2,1)S(1)}, bf16[64,3712]{1,0:T(8,128)(2,1)S(1)}, u32[]{:S(2)}, u32[]{:S(2)}) collective-permute-start(bf16[64,3712]{1,0:T(8,128)(2,1)S(1)} %collective-permute-done.refs_0_.a_ref), channel_id=1, source_target_pairs={{0,6},{1,3},{2,4},{3,1},{4,2},{5,7},{6,0},{7,5},{8,14},{9,11},{10,... | collective-permute-start | bytes 1425416 | tf_op jit(solution)/shard_map/ppermute | solution.py:78
  31.2 3.1 %select.2 = (bf16[64,7296]{1,0:T(8,128)(2,1)S(1)}, bf16[64,3584]{1,0:T(8,128)(2,1)S(1)}, bf16[64,3712]{1,0:T(8,128)(2,1)S(1)}, bf16[1,7168,512]{2,1,0:T(8,128)(2,1)S(1)}) custom-call(s32[1]{0:T(128)} %bitcast.expert_ref, bf16[64,3712]{1,0:T(8,128)(2,1)S(1)} %collective-permute-done.refs_0_.a_ref, bf16[64,3712]{1,0:T(8,128)(2,1)S(1)} %collective-permute-done.1.refs_1_.b_ref, ...), custom_call_target="tpu_custom_call" | custom-call | flops 1000 | bytes 1000 | tf_op jit(solution)/shard_map/select/pallas_call | solution.py:192
  34.3 2.7 %all-gather = bf16[128,3584]{1,0:T(8,128)(2,1)S(1)} all-gather(bf16[64,3584]{1,0:T(8,128)(2,1)S(1)} %get-tuple-element.29), channel_id=2, replica_groups={{0,1},{2,3},{4,5},{6,7},{8,9},{10,11},{12,13},{14,15},{16,17},{18,19},{..., dimensions={0}, use_global_device_ids=true | all-gather | bytes 1376256 | tf_op jit(solution)/shard_map/all_gather | solution.py:82
  37.1 2.5 %all-gather.1 = bf16[128,3712]{1,0:T(8,128)(2,1)S(1)} all-gather(bf16[64,3712]{1,0:T(8,128)(2,1)S(1)} %get-tuple-element.30), channel_id=3, replica_groups={{0,1},{2,3},{4,5},{6,7},{8,9},{10,11},{12,13},{14,15},{16,17},{18,19},{..., dimensions={0}, use_global_device_ids=true | all-gather | bytes 1425408 | tf_op jit(solution)/shard_map/all_gather | solution.py:82
  39.6 2.5 %collective-permute-done.4.refs_2_.c_ref = bf16[64,3712]{1,0:T(8,128)(2,1)S(1)} collective-permute-done((bf16[64,3712]{1,0:T(8,128)(2,1)S(1)}, bf16[64,3712]{1,0:T(8,128)(2,1)S(1)}, u32[]{:S(2)}, u32[]{:S(2)}) %collective-permute-start.4) | collective-permute-done | bytes 475168 | tf_op jit(solution)/shard_map/ppermute | solution.py:78
  42.0 0.9 %select.3 = (bf16[64,7296]{1,0:T(8,128)(2,1)S(1)}, bf16[64,7296]{1,0:T(8,128)(2,1)S(1)}) custom-call(s32[1]{0:T(128)} %bitcast.expert_ref, bf16[64,3712]{1,0:T(8,128)(2,1)S(1)} %collective-permute-done.3.refs_0_.a_ref, bf16[64,3712]{1,0:T(8,128)(2,1)S(1)} %collective-permute-done.5.refs_1_.b_ref, bf16[64,3712]{1,0:T(8,128)(2,1)S(1)} %collective-permute-done.4.refs_2_.c_ref, ...), custom_call_target="tpu_custom_call" | custom-call | flops 1000 | bytes 1000 | tf_op jit(solution)/shard_map/select/pallas_call | solution.py:192
  43.1 2.1 %hidden.2.refs_3_.hidden_ref = bf16[128,512]{1,0:T(8,128)(2,1)S(1)} custom-call(s32[1]{0:T(128)} %bitcast.expert_ref, bf16[64,7296]{1,0:T(8,128)(2,1)S(1)} %get-tuple-element.35.mine_ref, bf16[2,64,3584]{2,1,0:T(8,128)(2,1)S(1)} %bitcast.20, bf16[2,64,3712]{2,1,0:T(8,128)(2,1)S(1)} %bitcast.19, bf16[1,7168,512]{2,1,0:T(8,128)(2,1)S(1)} %bitcast.7, ...), custom_call_target="tpu_custom_call" | custom-call | flops 1000 | bytes 1000 | tf_op jit(solution)/shard_map/hidden/pallas_call | solution.py:232
  45.2 0.4 collective-permute-done.7.refs_0_
  45.5 2.1 %hidden.3.hidden_ref = bf16[128,512]{1,0:T(8,128)(2,1)S(1)} custom-call(s32[1]{0:T(128)} %bitcast.expert_ref, bf16[64,7296]{1,0:T(8,128)(2,1)S(1)} %get-tuple-element.39.refs_4_.mine_ref, bf16[64,7296]{1,0:T(8,128)(2,1)S(1)} %collective-permute-done.7.refs_0_, bf16[1,7168,512]{2,1,0:T(8,128)(2,1)S(1)} %bitcast.7, ...), custom_call_target="tpu_custom_call" | custom-call | flops 1000 | bytes 1000 | tf_op jit(solution)/shard_map/hidden/pallas_call | solution.py:232
  47.6 1.1 %down.2 = (bf16[64,7168]{1,0:T(8,128)(2,1)S(1)}, bf16[64,7168]{1,0:T(8,128)(2,1)S(1)}) custom-call(bf16[128,512]{1,0:T(8,128)(2,1)S(1)} %hidden.3.hidden_ref, bf16[1,512,7168]{2,1,0:T(8,128)(2,1)S(1)} %bitcast.9, bf16[64,3712]{1,0:T(8,128)(2,1)S(1)} %bitcast.17), custom_call_target="tpu_custom_call" | custom-call | flops 1000 | bytes 1000 | tf_op jit(solution)/shard_map/down/pallas_call | solution.py:254
  49.0 1.1 %down.3 = (bf16[64,7168]{1,0:T(8,128)(2,1)S(1)}, bf16[64,7168]{1,0:T(8,128)(2,1)S(1)}) custom-call(bf16[128,512]{1,0:T(8,128)(2,1)S(1)} %hidden.2.refs_3_.hidden_ref, bf16[1,512,7168]{2,1,0:T(8,128)(2,1)S(1)} %bitcast.9, bf16[64,7168]{1,0:T(8,128)(2,1)S(1)} %get-tuple-element.41.after_ref.mine_ref), custom_call_target="tpu_custom_call" | custom-call | flops 1000 | bytes 1000 | tf_op jit(solution)/shard_map/down/pallas_call | solution.py:254
  50.1 0.4 collective-permute-start.9
  50.6 0.4 places.2.place_ref
  51.0 0.3 collective-permute-done.8.theirs_ref
  51.3 0.7 spread.2
  52.0 0.4 collective-permute-start.10
  52.4 0.3 collective-permute-start.12
  52.7 3.2 %collective-permute-start.16 = (bf16[64,3584]{1,0:T(8,128)(2,1)S(1)}, bf16[64,3584]{1,0:T(8,128)(2,1)S(1)}, u32[]{:S(2)}, u32[]{:S(2)}) collective-permute-start(bf16[64,3584]{1,0:T(8,128)(2,1)S(1)} %get-tuple-element.44.after_ref), channel_id=1, source_target_pairs={{0,126},{1,43},{2,124},{3,41},{4,122},{5,47},{6,120},{7,45},{8,118... | collective-permute-start | bytes 1376264 | tf_op jit(solution)/shard_map/ppermute | solution.py:78
  55.9 0.4 places.3.place_ref
  56.4 0.7 spread.3
  57.0 2.7 %collective-permute-done.10 = bf16[64,3584]{1,0:T(8,128)(2,1)S(1)} collective-permute-done((bf16[64,3584]{1,0:T(8,128)(2,1)S(1)}, bf16[64,3584]{1,0:T(8,128)(2,1)S(1)}, u32[]{:S(2)}, u32[]{:S(2)}) %collective-permute-start.10) | collective-permute-done | bytes 458784 | tf_op jit(solution)/shard_map/ppermute | solution.py:78
  60.1 1.3 %collective-permute-start.13 = (bf16[64,3584]{1,0:T(8,128)(2,1)S(1)}, bf16[64,3584]{1,0:T(8,128)(2,1)S(1)}, u32[]{:S(2)}, u32[]{:S(2)}) collective-permute-start(bf16[64,3584]{1,0:T(8,128)(2,1)S(1)} %add_convert_fusion.2), channel_id=1, source_target_pairs={{0,96},{1,33},{2,98},{3,35},{4,100},{5,37},{6,102},{7,39},{8,104},... | collective-permute-start | bytes 1376264 | tf_op jit(solution)/shard_map/ppermute | solution.py:78
  61.6 5.4 %collective-permute-done.16 = bf16[64,3584]{1,0:T(8,128)(2,1)S(1)} collective-permute-done((bf16[64,3584]{1,0:T(8,128)(2,1)S(1)}, bf16[64,3584]{1,0:T(8,128)(2,1)S(1)}, u32[]{:S(2)}, u32[]{:S(2)}) %collective-permute-start.16) | collective-permute-done | bytes 458784 | tf_op jit(solution)/shard_map/ppermute | solution.py:78
  67.0 3.2 %collective-permute-done.11 = bf16[64,3584]{1,0:T(8,128)(2,1)S(1)} collective-permute-done((bf16[64,3584]{1,0:T(8,128)(2,1)S(1)}, bf16[64,3584]{1,0:T(8,128)(2,1)S(1)}, u32[]{:S(2)}, u32[]{:S(2)}) %collective-permute-start.11) | collective-permute-done | bytes 458784 | tf_op jit(solution)/shard_map/ppermute | solution.py:78
  70.2 1.7 %collective-permute-done.13 = bf16[64,3584]{1,0:T(8,128)(2,1)S(1)} collective-permute-done((bf16[64,3584]{1,0:T(8,128)(2,1)S(1)}, bf16[64,3584]{1,0:T(8,128)(2,1)S(1)}, u32[]{:S(2)}, u32[]{:S(2)}) %collective-permute-start.13) | collective-permute-done | bytes 458784 | tf_op jit(solution)/shard_map/ppermute | solution.py:78
  72.2 14.6 %all_to_all.11.parts_ref = bf16[8,8,3584]{2,1,0:T(8,128)(2,1)S(1)} all-to-all(bf16[8,8,3584]{2,1,0:T(8,128)(2,1)S(1)} %fusion), channel_id=1, replica_groups={{0,2,8,10,32,34,40,42},{1,7,25,31,97,103,121,127},{3,5,27,29,99,101,123..., dimensions={0} | all-to-all | bytes 917504 | tf_op jit(solution)/shard_map/all_to_all | solution.py:74
  86.8 0.7 finish.1
  (32 shorter events, 1.6 us)
Async XLA Ops:
  22.0 21.1 %slice-start = ((s8[7340032]{0:T(1024)(128)(4,1)}), s8[4194304]{0:T(1024)(128)(4,1)S(1)}, s32[]{:S(2)}) async-start(s8[7340032]{0:T(1024)(128)(4,1)} %bitcast.6), calls=%async_computation.2 | async-start | bytes 8388608
  22.0 21.1 %slice-start.1 = ((s8[7340032]{0:T(1024)(128)(4,1)}), s8[3145728]{0:T(1024)(128)(4,1)S(1)}, s32[]{:S(2)}) async-start(s8[7340032]{0:T(1024)(128)(4,1)} %bitcast.6), calls=%async_computation.3 | async-start | bytes 6291456
  22.0 7.5 %collective-permute-start.2 = (bf16[64,3712]{1,0:T(8,128)(2,1)S(1)}, bf16[64,3712]{1,0:T(8,128)(2,1)S(1)}, u32[]{:S(2)}, u32[]{:S(2)}) collective-permute-start(bf16[64,3712]{1,0:T(8,128)(2,1)S(1)} %bitcast.10), channel_id=1, source_target_pairs={{0,6},{1,3},{2,4},{3,1},{4,2},{5,7},{6,0},{7,5},{8,14},{9,11},{10,... | collective-permute-start | bytes 1425416 | tf_op jit(solution)/shard_map/ppermute | solution.py:78
  22.0 7.6 %collective-permute-start.1 = (bf16[64,3712]{1,0:T(8,128)(2,1)S(1)}, bf16[64,3712]{1,0:T(8,128)(2,1)S(1)}, u32[]{:S(2)}, u32[]{:S(2)}) collective-permute-start(bf16[64,3712]{1,0:T(8,128)(2,1)S(1)} %bitcast.11), channel_id=1, source_target_pairs={{0,96},{1,33},{2,98},{3,35},{4,100},{5,37},{6,102},{7,39},{8,104},... | collective-permute-start | bytes 1425416 | tf_op jit(solution)/shard_map/ppermute | solution.py:78
  22.1 7.9 %collective-permute-start = (bf16[64,3712]{1,0:T(8,128)(2,1)S(1)}, bf16[64,3712]{1,0:T(8,128)(2,1)S(1)}, u32[]{:S(2)}, u32[]{:S(2)}) collective-permute-start(bf16[64,3712]{1,0:T(8,128)(2,1)S(1)} %bitcast.12), channel_id=1, source_target_pairs={{0,24},{1,9},{2,26},{3,11},{4,28},{5,13},{6,30},{7,15},{8,16},{9,1... | collective-permute-start | bytes 1425416 | tf_op jit(solution)/shard_map/ppermute | solution.py:78
  22.2 17.4 %collective-permute-start.6 = (bf16[64,3712]{1,0:T(8,128)(2,1)S(1)}, bf16[64,3712]{1,0:T(8,128)(2,1)S(1)}, u32[]{:S(2)}, u32[]{:S(2)}) collective-permute-start(bf16[64,3712]{1,0:T(8,128)(2,1)S(1)} %bitcast.13), channel_id=1, source_target_pairs={{0,126},{1,43},{2,124},{3,41},{4,122},{5,47},{6,120},{7,45},{8,118... | collective-permute-start | bytes 1425416 | tf_op jit(solution)/shard_map/ppermute | solution.py:78
  29.5 12.5 %collective-permute-start.4 = (bf16[64,3712]{1,0:T(8,128)(2,1)S(1)}, bf16[64,3712]{1,0:T(8,128)(2,1)S(1)}, u32[]{:S(2)}, u32[]{:S(2)}) collective-permute-start(bf16[64,3712]{1,0:T(8,128)(2,1)S(1)} %collective-permute-done.2.refs_2_.c_ref), channel_id=1, source_target_pairs={{0,96},{1,33},{2,98},{3,35},{4,100},{5,37},{6,102},{7,39},{8,104},... | collective-permute-start | bytes 1425416 | tf_op jit(solution)/shard_map/ppermute | solution.py:78
  29.6 12.5 %collective-permute-start.3 = (bf16[64,3712]{1,0:T(8,128)(2,1)S(1)}, bf16[64,3712]{1,0:T(8,128)(2,1)S(1)}, u32[]{:S(2)}, u32[]{:S(2)}) collective-permute-start(bf16[64,3712]{1,0:T(8,128)(2,1)S(1)} %collective-permute-done.1.refs_1_.b_ref), channel_id=1, source_target_pairs={{0,24},{1,9},{2,26},{3,11},{4,28},{5,13},{6,30},{7,15},{8,16},{9,1... | collective-permute-start | bytes 1425416 | tf_op jit(solution)/shard_map/ppermute | solution.py:78
  29.9 12.1 %collective-permute-start.5 = (bf16[64,3712]{1,0:T(8,128)(2,1)S(1)}, bf16[64,3712]{1,0:T(8,128)(2,1)S(1)}, u32[]{:S(2)}, u32[]{:S(2)}) collective-permute-start(bf16[64,3712]{1,0:T(8,128)(2,1)S(1)} %collective-permute-done.refs_0_.a_ref), channel_id=1, source_target_pairs={{0,6},{1,3},{2,4},{3,1},{4,2},{5,7},{6,0},{7,5},{8,14},{9,11},{10,... | collective-permute-start | bytes 1425416 | tf_op jit(solution)/shard_map/ppermute | solution.py:78
  42.0 5.6 %slice-start.2 = ((s8[7340032]{0:T(1024)(128)(4,1)}), s8[4194304]{0:T(1024)(128)(4,1)S(1)}, s32[]{:S(2)}) async-start(s8[7340032]{0:T(1024)(128)(4,1)} %bitcast.8), calls=%async_computation.4 | async-start | bytes 8388608
  43.0 2.6 %collective-permute-start.7 = (bf16[64,7296]{1,0:T(8,128)(2,1)S(1)}, bf16[64,7296]{1,0:T(8,128)(2,1)S(1)}, u32[]{:S(2)}, u32[]{:S(2)}) collective-permute-start(bf16[64,7296]{1,0:T(8,128)(2,1)S(1)} %get-tuple-element.40), channel_id=1, source_target_pairs={{0,1},{1,0},{2,3},{3,2},{4,5},{5,4},{6,7},{7,6},{8,9},{9,8},{10,11... | collective-permute-start | bytes 2801672 | tf_op jit(solution)/shard_map/ppermute | solution.py:86
  43.1 4.5 %slice-start.3 = ((s8[7340032]{0:T(1024)(128)(4,1)}), s8[3145728]{0:T(1024)(128)(4,1)S(1)}, s32[]{:S(2)}) async-start(s8[7340032]{0:T(1024)(128)(4,1)} %bitcast.8), calls=%async_computation.5 | async-start | bytes 6291456
  48.8 2.6 %collective-permute-start.8 = (bf16[64,7168]{1,0:T(8,128)(2,1)S(1)}, bf16[64,7168]{1,0:T(8,128)(2,1)S(1)}, u32[]{:S(2)}, u32[]{:S(2)}) collective-permute-start(bf16[64,7168]{1,0:T(8,128)(2,1)S(1)} %get-tuple-element.43), channel_id=1, source_target_pairs={{0,1},{1,0},{2,3},{3,2},{4,5},{5,4},{6,7},{7,6},{8,9},{9,8},{10,11... | collective-permute-start | bytes 2752520 | tf_op jit(solution)/shard_map/ppermute | solution.py:86
  50.1 6.2 %collective-permute-start.9 = (bf16[64,7168]{1,0:T(8,128)(2,1)S(1)}, bf16[64,7168]{1,0:T(8,128)(2,1)S(1)}, u32[]{:S(2)}, u32[]{:S(2)}) collective-permute-start(bf16[64,7168]{1,0:T(8,128)(2,1)S(1)} %get-tuple-element.45), channel_id=1, source_target_pairs={{0,1},{1,0},{2,3},{3,2},{4,5},{5,4},{6,7},{7,6},{8,9},{9,8},{10,11... | collective-permute-start | bytes 2752520 | tf_op jit(solution)/shard_map/ppermute | solution.py:86
  52.0 7.7 %collective-permute-start.10 = (bf16[64,3584]{1,0:T(8,128)(2,1)S(1)}, bf16[64,3584]{1,0:T(8,128)(2,1)S(1)}, u32[]{:S(2)}, u32[]{:S(2)}) collective-permute-start(bf16[64,3584]{1,0:T(8,128)(2,1)S(1)} %get-tuple-element.48), channel_id=1, source_target_pairs={{0,96},{1,33},{2,98},{3,35},{4,100},{5,37},{6,102},{7,39},{8,104},... | collective-permute-start | bytes 1376264 | tf_op jit(solution)/shard_map/ppermute | solution.py:78
  52.4 7.6 %collective-permute-start.12 = (bf16[64,3584]{1,0:T(8,128)(2,1)S(1)}, bf16[64,3584]{1,0:T(8,128)(2,1)S(1)}, u32[]{:S(2)}, u32[]{:S(2)}) collective-permute-start(bf16[64,3584]{1,0:T(8,128)(2,1)S(1)} %get-tuple-element.50), channel_id=1, source_target_pairs={{0,6},{1,3},{2,4},{3,1},{4,2},{5,7},{6,0},{7,5},{8,14},{9,11},{10,... | collective-permute-start | bytes 1376264 | tf_op jit(solution)/shard_map/ppermute | solution.py:78
  52.7 8.7 %collective-permute-start.14 = (bf16[64,3584]{1,0:T(8,128)(2,1)S(1)}, bf16[64,3584]{1,0:T(8,128)(2,1)S(1)}, u32[]{:S(2)}, u32[]{:S(2)}) collective-permute-start(bf16[64,3584]{1,0:T(8,128)(2,1)S(1)} %get-tuple-element.52), channel_id=1, source_target_pairs={{0,24},{1,9},{2,26},{3,11},{4,28},{5,13},{6,30},{7,15},{8,16},{9,1... | collective-permute-start | bytes 1376264 | tf_op jit(solution)/shard_map/ppermute | solution.py:78
  52.7 14.3 %collective-permute-start.16 = (bf16[64,3584]{1,0:T(8,128)(2,1)S(1)}, bf16[64,3584]{1,0:T(8,128)(2,1)S(1)}, u32[]{:S(2)}, u32[]{:S(2)}) collective-permute-start(bf16[64,3584]{1,0:T(8,128)(2,1)S(1)} %get-tuple-element.44.after_ref), channel_id=1, source_target_pairs={{0,126},{1,43},{2,124},{3,41},{4,122},{5,47},{6,120},{7,45},{8,118... | collective-permute-start | bytes 1376264 | tf_op jit(solution)/shard_map/ppermute | solution.py:78
  59.8 10.4 %collective-permute-start.11 = (bf16[64,3584]{1,0:T(8,128)(2,1)S(1)}, bf16[64,3584]{1,0:T(8,128)(2,1)S(1)}, u32[]{:S(2)}, u32[]{:S(2)}) collective-permute-start(bf16[64,3584]{1,0:T(8,128)(2,1)S(1)} %add_convert_fusion.3), channel_id=1, source_target_pairs={{0,24},{1,9},{2,26},{3,11},{4,28},{5,13},{6,30},{7,15},{8,16},{9,1... | collective-permute-start | bytes 1376264 | tf_op jit(solution)/shard_map/ppermute | solution.py:78
  60.1 11.8 %collective-permute-start.13 = (bf16[64,3584]{1,0:T(8,128)(2,1)S(1)}, bf16[64,3584]{1,0:T(8,128)(2,1)S(1)}, u32[]{:S(2)}, u32[]{:S(2)}) collective-permute-start(bf16[64,3584]{1,0:T(8,128)(2,1)S(1)} %add_convert_fusion.2), channel_id=1, source_target_pairs={{0,96},{1,33},{2,98},{3,35},{4,100},{5,37},{6,102},{7,39},{8,104},... | collective-permute-start | bytes 1376264 | tf_op jit(solution)/shard_map/ppermute | solution.py:78
  61.5 10.4 %collective-permute-start.15 = (bf16[64,3584]{1,0:T(8,128)(2,1)S(1)}, bf16[64,3584]{1,0:T(8,128)(2,1)S(1)}, u32[]{:S(2)}, u32[]{:S(2)}) collective-permute-start(bf16[64,3584]{1,0:T(8,128)(2,1)S(1)} %add_convert_fusion.1), channel_id=1, source_target_pairs={{0,6},{1,3},{2,4},{3,1},{4,2},{5,7},{6,0},{7,5},{8,14},{9,11},{10,... | collective-permute-start | bytes 1376264 | tf_op jit(solution)/shard_map/ppermute | solution.py:78

commit v14 on v13

--- a/solution.py
+++ b/solution.py
@@ -347,11 +347,12 @@
     own = swap_near(pack(expert, tokens, ids, weights)).reshape(BLOCK, WIDE)
     x, y, z = swap_far(own, 0), swap_far(own, 1), swap_far(own, 2)
     xyz = swap_far(own, 3)
-    xy, yz, zx = swap_far(y, 0), swap_far(z, 1), swap_far(x, 2)
+    xy, yz, zx = swap_far(x, 1), swap_far(y, 2), swap_far(z, 0)
     near = (x, y, z, own)
     mine_near, *sent, up = select(expert, near, own, TWO, (up,))
     got_near = [both_cores(piece) for piece in sent]
-    xy, yz, zx, xyz, *got_near = lax.optimization_barrier((xy, yz, zx, xyz, *got_near))
+    place_near = places(expert, near, got_near[0])
+    xy, yz, zx, xyz, place_near, *got_near = lax.optimization_barrier((xy, yz, zx, xyz, place_near, *got_near))
     far = (xy, zx, yz, xyz)
     mine_far, sent = select(expert, far, own, ONE)
     got_far = [to_sibling(sent)]
@@ -365,7 +366,7 @@
     y_xy, y_zx, y_yz, y_xyz = spread(place_far, result, returned, result_near)
     at_x, at_y, at_z = swap_far(y_xy, 1), swap_far(y_yz, 2), swap_far(y_zx, 0)
     at_own = swap_far(y_xyz, 3)
-    y_x, y_y, y_z, y_own = spread(places(expert, near, y_xyz), result_near, returned_near, y_xyz)
+    y_x, y_y, y_z, y_own = spread(place_near, result_near, returned_near, y_xyz)
     total = add(
         y_own,
         swap_far(add(y_x, at_x), 0),

time: 87.8 us -> 88.4 us (level)
  no operation moved by 1% of the time
where the time goes in v14:
time: 88.4 us; the launch traced here: 88.2 us
  blocking collectives  41.4 us (47%)
  waiting for transfers between devices  20 us (23%)
  Pallas kernels  14.2 us (16%)
  starting transfers between devices  11.7 us (13%)
    all_to_all x2, blocking collectives, swap_near(): lax.all_to_all(values, AXES, 0, 0, axis_index_groups=NEAR, tiled=True)  36.2 us
    ppermute x14, waiting for transfers between devices, swap_far(): return lax.ppermute(values, AXES, FAR[axis])  19.3 us
    ppermute x14, starting transfers between devices, swap_far(): return lax.ppermute(values, AXES, FAR[axis])  11 us
    all_gather x2, blocking collectives, both_cores(): lax.all_gather(values, 'dev', axis_index_groups=[[i, i + 1] for i in rang...  5.16 us
    pallas_call x2, Pallas kernels, hidden_units(): pl.pallas_call(functools.partial(hidden_kernel, starts), out_shape=jax.Sh...  4.14 us
    pallas_call x2, Pallas kernels, select(): pl.pallas_call(functools.partial(select_kernel, starts, len(loads)), out_...  4 us
    pallas_call x2, Pallas kernels, down_rows(): pl.pallas_call(down_kernel, out_shape=[jax.ShapeDtypeStruct((SEL, D), BF1...  2.27 us
  transfers between devices with their start and end apart: 17, of which 11 were waited for; matrix products, arithmetic and copies ran while one was open for 0% of the time, Pallas kernels for 10%

profile of v14, /device:TPU:1, one launch (start us, length us, event | category | flops | bytes accessed | tf_op | source)
XLA Modules:
  0.0 88.2 jit_solution(169139522917047283)
XLA Ops:
  0.0 0.9 %pack.1 = bf16[8,8,3712]{2,1,0:T(8,128)(2,1)S(1)} custom-call(s32[1]{0:T(128)} %bitcast.expert_ref, bf16[4,7168]{1,0:T(4,128)(2,1)} %tokens_hbm.1, s32[4,8]{1,0:T(4,128)} %ids_hbm.1, f32[4,8]{1,0:T(4,128)} %weights_hbm.1), custom_call_target="tpu_custom_call" | custom-call | tf_op jit(solution)/shard_map/pack/pallas_call | solution.py:116
  1.0 21.0 %all_to_all.10 = bf16[8,8,3712]{2,1,0:T(8,128)(2,1)S(1)} all-to-all(bf16[8,8,3712]{2,1,0:T(8,128)(2,1)S(1)} %pack.1), channel_id=1, replica_groups={{0,2,8,10,32,34,40,42},{1,7,25,31,97,103,121,127},{3,5,27,29,99,101,123..., dimensions={0} | all-to-all | bytes 950272 | tf_op jit(solution)/shard_map/all_to_all | solution.py:74
  22.2 3.6 %collective-permute-start.6 = (bf16[64,3712]{1,0:T(8,128)(2,1)S(1)}, bf16[64,3712]{1,0:T(8,128)(2,1)S(1)}, u32[]{:S(2)}, u32[]{:S(2)}) collective-permute-start(bf16[64,3712]{1,0:T(8,128)(2,1)S(1)} %bitcast.13), channel_id=1, source_target_pairs={{0,126},{1,43},{2,124},{3,41},{4,122},{5,47},{6,120},{7,45},{8,118... | collective-permute-start | bytes 1425416 | tf_op jit(solution)/shard_map/ppermute | solution.py:78
  25.8 3.7 %collective-permute-done.4.refs_2_.c_ref = bf16[64,3712]{1,0:T(8,128)(2,1)S(1)} collective-permute-done((bf16[64,3712]{1,0:T(8,128)(2,1)S(1)}, bf16[64,3712]{1,0:T(8,128)(2,1)S(1)}, u32[]{:S(2)}, u32[]{:S(2)}) %collective-permute-start.4) | collective-permute-done | bytes 475168 | tf_op jit(solution)/shard_map/ppermute | solution.py:78
  29.6 1.7 %collective-permute-start.3 = (bf16[64,3712]{1,0:T(8,128)(2,1)S(1)}, bf16[64,3712]{1,0:T(8,128)(2,1)S(1)}, u32[]{:S(2)}, u32[]{:S(2)}) collective-permute-start(bf16[64,3712]{1,0:T(8,128)(2,1)S(1)} %collective-permute-done.2.refs_1_.b_ref), channel_id=1, source_target_pairs={{0,6},{1,3},{2,4},{3,1},{4,2},{5,7},{6,0},{7,5},{8,14},{9,11},{10,... | collective-permute-start | bytes 1425416 | tf_op jit(solution)/shard_map/ppermute | solution.py:78
  31.3 3.1 %select.2 = (bf16[64,7296]{1,0:T(8,128)(2,1)S(1)}, bf16[64,3584]{1,0:T(8,128)(2,1)S(1)}, bf16[64,3712]{1,0:T(8,128)(2,1)S(1)}, bf16[1,7168,512]{2,1,0:T(8,128)(2,1)S(1)}) custom-call(s32[1]{0:T(128)} %bitcast.expert_ref, bf16[64,3712]{1,0:T(8,128)(2,1)S(1)} %collective-permute-done.refs_0_.a_ref, bf16[64,3712]{1,0:T(8,128)(2,1)S(1)} %collective-permute-done.2.refs_1_.b_ref, ...), custom_call_target="tpu_custom_call" | custom-call | flops 1000 | bytes 1000 | tf_op jit(solution)/shard_map/select/pallas_call | solution.py:192
  34.4 2.7 %all-gather = bf16[128,3584]{1,0:T(8,128)(2,1)S(1)} all-gather(bf16[64,3584]{1,0:T(8,128)(2,1)S(1)} %get-tuple-element.30), channel_id=2, replica_groups={{0,1},{2,3},{4,5},{6,7},{8,9},{10,11},{12,13},{14,15},{16,17},{18,19},{..., dimensions={0}, use_global_device_ids=true | all-gather | bytes 1376256 | tf_op jit(solution)/shard_map/all_gather | solution.py:82
  37.1 0.4 places.2.place_ref
  37.5 2.5 %all-gather.1 = bf16[128,3712]{1,0:T(8,128)(2,1)S(1)} all-gather(bf16[64,3712]{1,0:T(8,128)(2,1)S(1)} %get-tuple-element.31), channel_id=3, replica_groups={{0,1},{2,3},{4,5},{6,7},{8,9},{10,11},{12,13},{14,15},{16,17},{18,19},{..., dimensions={0}, use_global_device_ids=true | all-gather | bytes 1425408 | tf_op jit(solution)/shard_map/all_gather | solution.py:82
  40.2 0.7 collective-permute-done.3.refs_2_.c_ref
  40.8 1.3 %collective-permute-done.1.refs_0_.a_ref = bf16[64,3712]{1,0:T(8,128)(2,1)S(1)} collective-permute-done((bf16[64,3712]{1,0:T(8,128)(2,1)S(1)}, bf16[64,3712]{1,0:T(8,128)(2,1)S(1)}, u32[]{:S(2)}, u32[]{:S(2)}) %collective-permute-start.1) | collective-permute-done | bytes 475168 | tf_op jit(solution)/shard_map/ppermute | solution.py:78
  42.1 0.9 %select.3 = (bf16[64,7296]{1,0:T(8,128)(2,1)S(1)}, bf16[64,7296]{1,0:T(8,128)(2,1)S(1)}) custom-call(s32[1]{0:T(128)} %bitcast.expert_ref, bf16[64,3712]{1,0:T(8,128)(2,1)S(1)} %collective-permute-done.1.refs_0_.a_ref, bf16[64,3712]{1,0:T(8,128)(2,1)S(1)} %collective-permute-done.5.refs_1_.b_ref, bf16[64,3712]{1,0:T(8,128)(2,1)S(1)} %collective-permute-done.3.refs_2_.c_ref, ...), custom_call_target="tpu_custom_call" | custom-call | flops 1000 | bytes 1000 | tf_op jit(solution)/shard_map/select/pallas_call | solution.py:192
  43.2 2.1 %hidden.2.refs_3_.hidden_ref = bf16[128,512]{1,0:T(8,128)(2,1)S(1)} custom-call(s32[1]{0:T(128)} %bitcast.expert_ref, bf16[64,7296]{1,0:T(8,128)(2,1)S(1)} %get-tuple-element.33.mine_ref, bf16[2,64,3584]{2,1,0:T(8,128)(2,1)S(1)} %bitcast.20, bf16[2,64,3712]{2,1,0:T(8,128)(2,1)S(1)} %bitcast.21, bf16[1,7168,512]{2,1,0:T(8,128)(2,1)S(1)} %bitcast.7, ...), custom_call_target="tpu_custom_call" | custom-call | flops 1000 | bytes 1000 | tf_op jit(solution)/shard_map/hidden/pallas_call | solution.py:232
  45.3 0.4 collective-permute-done.7.refs_0_
  45.6 2.1 %hidden.3.hidden_ref = bf16[128,512]{1,0:T(8,128)(2,1)S(1)} custom-call(s32[1]{0:T(128)} %bitcast.expert_ref, bf16[64,7296]{1,0:T(8,128)(2,1)S(1)} %get-tuple-element.41.refs_4_.mine_ref, bf16[64,7296]{1,0:T(8,128)(2,1)S(1)} %collective-permute-done.7.refs_0_, bf16[1,7168,512]{2,1,0:T(8,128)(2,1)S(1)} %bitcast.7, ...), custom_call_target="tpu_custom_call" | custom-call | flops 1000 | bytes 1000 | tf_op jit(solution)/shard_map/hidden/pallas_call | solution.py:232
  47.7 1.1 %down.2 = (bf16[64,7168]{1,0:T(8,128)(2,1)S(1)}, bf16[64,7168]{1,0:T(8,128)(2,1)S(1)}) custom-call(bf16[128,512]{1,0:T(8,128)(2,1)S(1)} %hidden.3.hidden_ref, bf16[1,512,7168]{2,1,0:T(8,128)(2,1)S(1)} %bitcast.9, bf16[64,3712]{1,0:T(8,128)(2,1)S(1)} %bitcast.18), custom_call_target="tpu_custom_call" | custom-call | flops 1000 | bytes 1000 | tf_op jit(solution)/shard_map/down/pallas_call | solution.py:254
  49.1 1.1 %down.3 = (bf16[64,7168]{1,0:T(8,128)(2,1)S(1)}, bf16[64,7168]{1,0:T(8,128)(2,1)S(1)}) custom-call(bf16[128,512]{1,0:T(8,128)(2,1)S(1)} %hidden.2.refs_3_.hidden_ref, bf16[1,512,7168]{2,1,0:T(8,128)(2,1)S(1)} %bitcast.9, bf16[64,7168]{1,0:T(8,128)(2,1)S(1)} %get-tuple-element.43.after_ref.mine_ref), custom_call_target="tpu_custom_call" | custom-call | flops 1000 | bytes 1000 | tf_op jit(solution)/shard_map/down/pallas_call | solution.py:254
  50.2 0.5 collective-permute-start.8
  50.7 0.4 places.3.place_ref
  51.1 0.3 collective-permute-done.9.theirs_ref
  51.4 0.7 spread.2
  52.4 0.4 collective-permute-start.12
  52.7 3.3 %collective-permute-start.16 = (bf16[64,3584]{1,0:T(8,128)(2,1)S(1)}, bf16[64,3584]{1,0:T(8,128)(2,1)S(1)}, u32[]{:S(2)}, u32[]{:S(2)}) collective-permute-start(bf16[64,3584]{1,0:T(8,128)(2,1)S(1)} %get-tuple-element.47.after_ref), channel_id=1, source_target_pairs={{0,126},{1,43},{2,124},{3,41},{4,122},{5,47},{6,120},{7,45},{8,118... | collective-permute-start | bytes 1376264 | tf_op jit(solution)/shard_map/ppermute | solution.py:78
  56.0 0.6 spread.3
  56.6 3.1 %collective-permute-done.10 = bf16[64,3584]{1,0:T(8,128)(2,1)S(1)} collective-permute-done((bf16[64,3584]{1,0:T(8,128)(2,1)S(1)}, bf16[64,3584]{1,0:T(8,128)(2,1)S(1)}, u32[]{:S(2)}, u32[]{:S(2)}) %collective-permute-start.10) | collective-permute-done | bytes 458784 | tf_op jit(solution)/shard_map/ppermute | solution.py:78
  60.1 1.3 %collective-permute-start.13 = (bf16[64,3584]{1,0:T(8,128)(2,1)S(1)}, bf16[64,3584]{1,0:T(8,128)(2,1)S(1)}, u32[]{:S(2)}, u32[]{:S(2)}) collective-permute-start(bf16[64,3584]{1,0:T(8,128)(2,1)S(1)} %add_convert_fusion.2), channel_id=1, source_target_pairs={{0,96},{1,33},{2,98},{3,35},{4,100},{5,37},{6,102},{7,39},{8,104},... | collective-permute-start | bytes 1376264 | tf_op jit(solution)/shard_map/ppermute | solution.py:78
  61.6 5.5 %collective-permute-done.16 = bf16[64,3584]{1,0:T(8,128)(2,1)S(1)} collective-permute-done((bf16[64,3584]{1,0:T(8,128)(2,1)S(1)}, bf16[64,3584]{1,0:T(8,128)(2,1)S(1)}, u32[]{:S(2)}, u32[]{:S(2)}) %collective-permute-start.16) | collective-permute-done | bytes 458784 | tf_op jit(solution)/shard_map/ppermute | solution.py:78
  67.1 3.1 %collective-permute-done.11 = bf16[64,3584]{1,0:T(8,128)(2,1)S(1)} collective-permute-done((bf16[64,3584]{1,0:T(8,128)(2,1)S(1)}, bf16[64,3584]{1,0:T(8,128)(2,1)S(1)}, u32[]{:S(2)}, u32[]{:S(2)}) %collective-permute-start.11) | collective-permute-done | bytes 458784 | tf_op jit(solution)/shard_map/ppermute | solution.py:78
  70.2 1.8 %collective-permute-done.13 = bf16[64,3584]{1,0:T(8,128)(2,1)S(1)} collective-permute-done((bf16[64,3584]{1,0:T(8,128)(2,1)S(1)}, bf16[64,3584]{1,0:T(8,128)(2,1)S(1)}, u32[]{:S(2)}, u32[]{:S(2)}) %collective-permute-start.13) | collective-permute-done | bytes 458784 | tf_op jit(solution)/shard_map/ppermute | solution.py:78
  72.0 0.3 fusion
  72.3 15.2 %all_to_all.11.parts_ref = bf16[8,8,3584]{2,1,0:T(8,128)(2,1)S(1)} all-to-all(bf16[8,8,3584]{2,1,0:T(8,128)(2,1)S(1)} %fusion), channel_id=1, replica_groups={{0,2,8,10,32,34,40,42},{1,7,25,31,97,103,121,127},{3,5,27,29,99,101,123..., dimensions={0} | all-to-all | bytes 917504 | tf_op jit(solution)/shard_map/all_to_all | solution.py:74
  87.5 0.7 finish.1
  (32 shorter events, 1.6 us)
Async XLA Ops:
  22.0 21.2 %slice-start = ((s8[7340032]{0:T(1024)(128)(4,1)}), s8[4194304]{0:T(1024)(128)(4,1)S(1)}, s32[]{:S(2)}) async-start(s8[7340032]{0:T(1024)(128)(4,1)} %bitcast.6), calls=%async_computation.2 | async-start | bytes 8388608
  22.0 21.2 %slice-start.1 = ((s8[7340032]{0:T(1024)(128)(4,1)}), s8[3145728]{0:T(1024)(128)(4,1)S(1)}, s32[]{:S(2)}) async-start(s8[7340032]{0:T(1024)(128)(4,1)} %bitcast.6), calls=%async_computation.3 | async-start | bytes 6291456
  22.0 7.5 %collective-permute-start.4 = (bf16[64,3712]{1,0:T(8,128)(2,1)S(1)}, bf16[64,3712]{1,0:T(8,128)(2,1)S(1)}, u32[]{:S(2)}, u32[]{:S(2)}) collective-permute-start(bf16[64,3712]{1,0:T(8,128)(2,1)S(1)} %bitcast.10), channel_id=1, source_target_pairs={{0,6},{1,3},{2,4},{3,1},{4,2},{5,7},{6,0},{7,5},{8,14},{9,11},{10,... | collective-permute-start | bytes 1425416 | tf_op jit(solution)/shard_map/ppermute | solution.py:78
  22.0 7.6 %collective-permute-start.2 = (bf16[64,3712]{1,0:T(8,128)(2,1)S(1)}, bf16[64,3712]{1,0:T(8,128)(2,1)S(1)}, u32[]{:S(2)}, u32[]{:S(2)}) collective-permute-start(bf16[64,3712]{1,0:T(8,128)(2,1)S(1)} %bitcast.11), channel_id=1, source_target_pairs={{0,96},{1,33},{2,98},{3,35},{4,100},{5,37},{6,102},{7,39},{8,104},... | collective-permute-start | bytes 1425416 | tf_op jit(solution)/shard_map/ppermute | solution.py:78
  22.1 9.2 %collective-permute-start = (bf16[64,3712]{1,0:T(8,128)(2,1)S(1)}, bf16[64,3712]{1,0:T(8,128)(2,1)S(1)}, u32[]{:S(2)}, u32[]{:S(2)}) collective-permute-start(bf16[64,3712]{1,0:T(8,128)(2,1)S(1)} %bitcast.12), channel_id=1, source_target_pairs={{0,24},{1,9},{2,26},{3,11},{4,28},{5,13},{6,30},{7,15},{8,16},{9,1... | collective-permute-start | bytes 1425416 | tf_op jit(solution)/shard_map/ppermute | solution.py:78
  22.2 17.9 %collective-permute-start.6 = (bf16[64,3712]{1,0:T(8,128)(2,1)S(1)}, bf16[64,3712]{1,0:T(8,128)(2,1)S(1)}, u32[]{:S(2)}, u32[]{:S(2)}) collective-permute-start(bf16[64,3712]{1,0:T(8,128)(2,1)S(1)} %bitcast.13), channel_id=1, source_target_pairs={{0,126},{1,43},{2,124},{3,41},{4,122},{5,47},{6,120},{7,45},{8,118... | collective-permute-start | bytes 1425416 | tf_op jit(solution)/shard_map/ppermute | solution.py:78
  29.5 10.7 %collective-permute-start.5 = (bf16[64,3712]{1,0:T(8,128)(2,1)S(1)}, bf16[64,3712]{1,0:T(8,128)(2,1)S(1)}, u32[]{:S(2)}, u32[]{:S(2)}) collective-permute-start(bf16[64,3712]{1,0:T(8,128)(2,1)S(1)} %collective-permute-done.4.refs_2_.c_ref), channel_id=1, source_target_pairs={{0,24},{1,9},{2,26},{3,11},{4,28},{5,13},{6,30},{7,15},{8,16},{9,1... | collective-permute-start | bytes 1425416 | tf_op jit(solution)/shard_map/ppermute | solution.py:78
  29.6 11.3 %collective-permute-start.3 = (bf16[64,3712]{1,0:T(8,128)(2,1)S(1)}, bf16[64,3712]{1,0:T(8,128)(2,1)S(1)}, u32[]{:S(2)}, u32[]{:S(2)}) collective-permute-start(bf16[64,3712]{1,0:T(8,128)(2,1)S(1)} %collective-permute-done.2.refs_1_.b_ref), channel_id=1, source_target_pairs={{0,6},{1,3},{2,4},{3,1},{4,2},{5,7},{6,0},{7,5},{8,14},{9,11},{10,... | collective-permute-start | bytes 1425416 | tf_op jit(solution)/shard_map/ppermute | solution.py:78
  31.2 10.9 %collective-permute-start.1 = (bf16[64,3712]{1,0:T(8,128)(2,1)S(1)}, bf16[64,3712]{1,0:T(8,128)(2,1)S(1)}, u32[]{:S(2)}, u32[]{:S(2)}) collective-permute-start(bf16[64,3712]{1,0:T(8,128)(2,1)S(1)} %collective-permute-done.refs_0_.a_ref), channel_id=1, source_target_pairs={{0,96},{1,33},{2,98},{3,35},{4,100},{5,37},{6,102},{7,39},{8,104},... | collective-permute-start | bytes 1425416 | tf_op jit(solution)/shard_map/ppermute | solution.py:78
  42.1 5.6 %slice-start.2 = ((s8[7340032]{0:T(1024)(128)(4,1)}), s8[4194304]{0:T(1024)(128)(4,1)S(1)}, s32[]{:S(2)}) async-start(s8[7340032]{0:T(1024)(128)(4,1)} %bitcast.8), calls=%async_computation.4 | async-start | bytes 8388608
  43.0 2.6 %collective-permute-start.7 = (bf16[64,7296]{1,0:T(8,128)(2,1)S(1)}, bf16[64,7296]{1,0:T(8,128)(2,1)S(1)}, u32[]{:S(2)}, u32[]{:S(2)}) collective-permute-start(bf16[64,7296]{1,0:T(8,128)(2,1)S(1)} %get-tuple-element.42), channel_id=1, source_target_pairs={{0,1},{1,0},{2,3},{3,2},{4,5},{5,4},{6,7},{7,6},{8,9},{9,8},{10,11... | collective-permute-start | bytes 2801672 | tf_op jit(solution)/shard_map/ppermute | solution.py:86
  43.2 4.5 %slice-start.3 = ((s8[7340032]{0:T(1024)(128)(4,1)}), s8[3145728]{0:T(1024)(128)(4,1)S(1)}, s32[]{:S(2)}) async-start(s8[7340032]{0:T(1024)(128)(4,1)} %bitcast.8), calls=%async_computation.5 | async-start | bytes 6291456
  48.9 2.6 %collective-permute-start.9 = (bf16[64,7168]{1,0:T(8,128)(2,1)S(1)}, bf16[64,7168]{1,0:T(8,128)(2,1)S(1)}, u32[]{:S(2)}, u32[]{:S(2)}) collective-permute-start(bf16[64,7168]{1,0:T(8,128)(2,1)S(1)} %get-tuple-element.46), channel_id=1, source_target_pairs={{0,1},{1,0},{2,3},{3,2},{4,5},{5,4},{6,7},{7,6},{8,9},{9,8},{10,11... | collective-permute-start | bytes 2752520 | tf_op jit(solution)/shard_map/ppermute | solution.py:86
  50.2 5.8 %collective-permute-start.8 = (bf16[64,7168]{1,0:T(8,128)(2,1)S(1)}, bf16[64,7168]{1,0:T(8,128)(2,1)S(1)}, u32[]{:S(2)}, u32[]{:S(2)}) collective-permute-start(bf16[64,7168]{1,0:T(8,128)(2,1)S(1)} %get-tuple-element.45), channel_id=1, source_target_pairs={{0,1},{1,0},{2,3},{3,2},{4,5},{5,4},{6,7},{7,6},{8,9},{9,8},{10,11... | collective-permute-start | bytes 2752520 | tf_op jit(solution)/shard_map/ppermute | solution.py:86
  52.1 7.7 %collective-permute-start.10 = (bf16[64,3584]{1,0:T(8,128)(2,1)S(1)}, bf16[64,3584]{1,0:T(8,128)(2,1)S(1)}, u32[]{:S(2)}, u32[]{:S(2)}) collective-permute-start(bf16[64,3584]{1,0:T(8,128)(2,1)S(1)} %get-tuple-element.50), channel_id=1, source_target_pairs={{0,96},{1,33},{2,98},{3,35},{4,100},{5,37},{6,102},{7,39},{8,104},... | collective-permute-start | bytes 1376264 | tf_op jit(solution)/shard_map/ppermute | solution.py:78
  52.4 7.6 %collective-permute-start.12 = (bf16[64,3584]{1,0:T(8,128)(2,1)S(1)}, bf16[64,3584]{1,0:T(8,128)(2,1)S(1)}, u32[]{:S(2)}, u32[]{:S(2)}) collective-permute-start(bf16[64,3584]{1,0:T(8,128)(2,1)S(1)} %get-tuple-element.52), channel_id=1, source_target_pairs={{0,6},{1,3},{2,4},{3,1},{4,2},{5,7},{6,0},{7,5},{8,14},{9,11},{10,... | collective-permute-start | bytes 1376264 | tf_op jit(solution)/shard_map/ppermute | solution.py:78
  52.7 8.7 %collective-permute-start.14 = (bf16[64,3584]{1,0:T(8,128)(2,1)S(1)}, bf16[64,3584]{1,0:T(8,128)(2,1)S(1)}, u32[]{:S(2)}, u32[]{:S(2)}) collective-permute-start(bf16[64,3584]{1,0:T(8,128)(2,1)S(1)} %get-tuple-element.54), channel_id=1, source_target_pairs={{0,24},{1,9},{2,26},{3,11},{4,28},{5,13},{6,30},{7,15},{8,16},{9,1... | collective-permute-start | bytes 1376264 | tf_op jit(solution)/shard_map/ppermute | solution.py:78
  52.7 14.4 %collective-permute-start.16 = (bf16[64,3584]{1,0:T(8,128)(2,1)S(1)}, bf16[64,3584]{1,0:T(8,128)(2,1)S(1)}, u32[]{:S(2)}, u32[]{:S(2)}) collective-permute-start(bf16[64,3584]{1,0:T(8,128)(2,1)S(1)} %get-tuple-element.47.after_ref), channel_id=1, source_target_pairs={{0,126},{1,43},{2,124},{3,41},{4,122},{5,47},{6,120},{7,45},{8,118... | collective-permute-start | bytes 1376264 | tf_op jit(solution)/shard_map/ppermute | solution.py:78
  59.9 10.3 %collective-permute-start.11 = (bf16[64,3584]{1,0:T(8,128)(2,1)S(1)}, bf16[64,3584]{1,0:T(8,128)(2,1)S(1)}, u32[]{:S(2)}, u32[]{:S(2)}) collective-permute-start(bf16[64,3584]{1,0:T(8,128)(2,1)S(1)} %add_convert_fusion.3), channel_id=1, source_target_pairs={{0,24},{1,9},{2,26},{3,11},{4,28},{5,13},{6,30},{7,15},{8,16},{9,1... | collective-permute-start | bytes 1376264 | tf_op jit(solution)/shard_map/ppermute | solution.py:78
  60.1 11.9 %collective-permute-start.13 = (bf16[64,3584]{1,0:T(8,128)(2,1)S(1)}, bf16[64,3584]{1,0:T(8,128)(2,1)S(1)}, u32[]{:S(2)}, u32[]{:S(2)}) collective-permute-start(bf16[64,3584]{1,0:T(8,128)(2,1)S(1)} %add_convert_fusion.2), channel_id=1, source_target_pairs={{0,96},{1,33},{2,98},{3,35},{4,100},{5,37},{6,102},{7,39},{8,104},... | collective-permute-start | bytes 1376264 | tf_op jit(solution)/shard_map/ppermute | solution.py:78
  61.6 10.4 %collective-permute-start.15 = (bf16[64,3584]{1,0:T(8,128)(2,1)S(1)}, bf16[64,3584]{1,0:T(8,128)(2,1)S(1)}, u32[]{:S(2)}, u32[]{:S(2)}) collective-permute-start(bf16[64,3584]{1,0:T(8,128)(2,1)S(1)} %add_convert_fusion.1), channel_id=1, source_target_pairs={{0,6},{1,3},{2,4},{3,1},{4,2},{5,7},{6,0},{7,5},{8,14},{9,11},{10,... | collective-permute-start | bytes 1376264 | tf_op jit(solution)/shard_map/ppermute | solution.py:78

commit v15 on v13

--- a/solution.py
+++ b/solution.py
@@ -362,10 +362,11 @@
     result_near, theirs = down_rows(hidden_near, down, result)
     returned_near = to_sibling(theirs)
     place_far = places(expert, far, result_near)
-    y_xy, y_zx, y_yz, y_xyz = spread(place_far, result, returned, result_near)
+    place_near = places(expert, near, place_far)
+    y_xy, y_zx, y_yz, y_xyz = spread(place_far, result, returned, place_near)
     at_x, at_y, at_z = swap_far(y_xy, 1), swap_far(y_yz, 2), swap_far(y_zx, 0)
     at_own = swap_far(y_xyz, 3)
-    y_x, y_y, y_z, y_own = spread(places(expert, near, y_xyz), result_near, returned_near, y_xyz)
+    y_x, y_y, y_z, y_own = spread(place_near, result_near, returned_near, y_xyz)
     total = add(
         y_own,
         swap_far(add(y_x, at_x), 0),

time: 87.8 us -> 87.9 us (level)
  transfers between devices with their start and end apart: 17 -> 17, of which waited for: 11 -> 10; matrix products, arithmetic and copies ran while one was open for 0% -> 0% of each run, Pallas kernels for 10% -> 10%
where the time goes in v15:
time: 87.9 us; the launch traced here: 87.7 us
  blocking collectives  40.9 us (47%)
  waiting for transfers between devices  20.4 us (23%)
  Pallas kernels  14.2 us (16%)
  starting transfers between devices  11.3 us (13%)
    all_to_all x2, blocking collectives, swap_near(): lax.all_to_all(values, AXES, 0, 0, axis_index_groups=NEAR, tiled=True)  35.6 us
    ppermute x14, waiting for transfers between devices, swap_far(): return lax.ppermute(values, AXES, FAR[axis])  20.1 us
    ppermute x14, starting transfers between devices, swap_far(): return lax.ppermute(values, AXES, FAR[axis])  10.6 us
    all_gather x2, blocking collectives, both_cores(): lax.all_gather(values, 'dev', axis_index_groups=[[i, i + 1] for i in rang...  5.22 us
    pallas_call x2, Pallas kernels, hidden_units(): pl.pallas_call(functools.partial(hidden_kernel, starts), out_shape=jax.Sh...  4.12 us
    pallas_call x2, Pallas kernels, select(): pl.pallas_call(functools.partial(select_kernel, starts, len(loads)), out_...  4.01 us
    pallas_call x2, Pallas kernels, down_rows(): pl.pallas_call(down_kernel, out_shape=[jax.ShapeDtypeStruct((SEL, D), BF1...  2.28 us
  transfers between devices with their start and end apart: 17, of which 10 were waited for; matrix products, arithmetic and copies ran while one was open for 0% of the time, Pallas kernels for 10%

profile of v15, /device:TPU:1, one launch (start us, length us, event | category | flops | bytes accessed | tf_op | source)
XLA Modules:
  0.0 87.7 jit_solution(15470440346347289695)
XLA Ops:
  0.0 0.9 %pack.1 = bf16[8,8,3712]{2,1,0:T(8,128)(2,1)S(1)} custom-call(s32[1]{0:T(128)} %bitcast.expert_ref, bf16[4,7168]{1,0:T(4,128)(2,1)} %tokens_hbm.1, s32[4,8]{1,0:T(4,128)} %ids_hbm.1, f32[4,8]{1,0:T(4,128)} %weights_hbm.1), custom_call_target="tpu_custom_call" | custom-call | tf_op jit(solution)/shard_map/pack/pallas_call | solution.py:116
  1.0 21.0 %all_to_all.10 = bf16[8,8,3712]{2,1,0:T(8,128)(2,1)S(1)} all-to-all(bf16[8,8,3712]{2,1,0:T(8,128)(2,1)S(1)} %pack.1), channel_id=1, replica_groups={{0,2,8,10,32,34,40,42},{1,7,25,31,97,103,121,127},{3,5,27,29,99,101,123..., dimensions={0} | all-to-all | bytes 950272 | tf_op jit(solution)/shard_map/all_to_all | solution.py:74
  22.2 3.6 %collective-permute-start.6 = (bf16[64,3712]{1,0:T(8,128)(2,1)S(1)}, bf16[64,3712]{1,0:T(8,128)(2,1)S(1)}, u32[]{:S(2)}, u32[]{:S(2)}) collective-permute-start(bf16[64,3712]{1,0:T(8,128)(2,1)S(1)} %bitcast.13), channel_id=1, source_target_pairs={{0,126},{1,43},{2,124},{3,41},{4,122},{5,47},{6,120},{7,45},{8,118... | collective-permute-start | bytes 1425416 | tf_op jit(solution)/shard_map/ppermute | solution.py:78
  25.8 3.7 %collective-permute-done.2.refs_2_.c_ref = bf16[64,3712]{1,0:T(8,128)(2,1)S(1)} collective-permute-done((bf16[64,3712]{1,0:T(8,128)(2,1)S(1)}, bf16[64,3712]{1,0:T(8,128)(2,1)S(1)}, u32[]{:S(2)}, u32[]{:S(2)}) %collective-permute-start.2) | collective-permute-done | bytes 475168 | tf_op jit(solution)/shard_map/ppermute | solution.py:78
  29.6 0.4 collective-permute-done.refs_0_.a_ref
  29.9 1.3 %collective-permute-start.5 = (bf16[64,3712]{1,0:T(8,128)(2,1)S(1)}, bf16[64,3712]{1,0:T(8,128)(2,1)S(1)}, u32[]{:S(2)}, u32[]{:S(2)}) collective-permute-start(bf16[64,3712]{1,0:T(8,128)(2,1)S(1)} %collective-permute-done.refs_0_.a_ref), channel_id=1, source_target_pairs={{0,6},{1,3},{2,4},{3,1},{4,2},{5,7},{6,0},{7,5},{8,14},{9,11},{10,... | collective-permute-start | bytes 1425416 | tf_op jit(solution)/shard_map/ppermute | solution.py:78
  31.2 3.1 %select.2 = (bf16[64,7296]{1,0:T(8,128)(2,1)S(1)}, bf16[64,3584]{1,0:T(8,128)(2,1)S(1)}, bf16[64,3712]{1,0:T(8,128)(2,1)S(1)}, bf16[1,7168,512]{2,1,0:T(8,128)(2,1)S(1)}) custom-call(s32[1]{0:T(128)} %bitcast.expert_ref, bf16[64,3712]{1,0:T(8,128)(2,1)S(1)} %collective-permute-done.refs_0_.a_ref, bf16[64,3712]{1,0:T(8,128)(2,1)S(1)} %collective-permute-done.1.refs_1_.b_ref, ...), custom_call_target="tpu_custom_call" | custom-call | flops 1000 | bytes 1000 | tf_op jit(solution)/shard_map/select/pallas_call | solution.py:192
  34.3 2.7 %all-gather = bf16[128,3584]{1,0:T(8,128)(2,1)S(1)} all-gather(bf16[64,3584]{1,0:T(8,128)(2,1)S(1)} %get-tuple-element.29), channel_id=2, replica_groups={{0,1},{2,3},{4,5},{6,7},{8,9},{10,11},{12,13},{14,15},{16,17},{18,19},{..., dimensions={0}, use_global_device_ids=true | all-gather | bytes 1376256 | tf_op jit(solution)/shard_map/all_gather | solution.py:82
  37.1 2.5 %all-gather.1 = bf16[128,3712]{1,0:T(8,128)(2,1)S(1)} all-gather(bf16[64,3712]{1,0:T(8,128)(2,1)S(1)} %get-tuple-element.30), channel_id=3, replica_groups={{0,1},{2,3},{4,5},{6,7},{8,9},{10,11},{12,13},{14,15},{16,17},{18,19},{..., dimensions={0}, use_global_device_ids=true | all-gather | bytes 1425408 | tf_op jit(solution)/shard_map/all_gather | solution.py:82
  39.6 2.5 %collective-permute-done.4.refs_2_.c_ref = bf16[64,3712]{1,0:T(8,128)(2,1)S(1)} collective-permute-done((bf16[64,3712]{1,0:T(8,128)(2,1)S(1)}, bf16[64,3712]{1,0:T(8,128)(2,1)S(1)}, u32[]{:S(2)}, u32[]{:S(2)}) %collective-permute-start.4) | collective-permute-done | bytes 475168 | tf_op jit(solution)/shard_map/ppermute | solution.py:78
  42.0 0.9 %select.3 = (bf16[64,7296]{1,0:T(8,128)(2,1)S(1)}, bf16[64,7296]{1,0:T(8,128)(2,1)S(1)}) custom-call(s32[1]{0:T(128)} %bitcast.expert_ref, bf16[64,3712]{1,0:T(8,128)(2,1)S(1)} %collective-permute-done.3.refs_0_.a_ref, bf16[64,3712]{1,0:T(8,128)(2,1)S(1)} %collective-permute-done.5.refs_1_.b_ref, bf16[64,3712]{1,0:T(8,128)(2,1)S(1)} %collective-permute-done.4.refs_2_.c_ref, ...), custom_call_target="tpu_custom_call" | custom-call | flops 1000 | bytes 1000 | tf_op jit(solution)/shard_map/select/pallas_call | solution.py:192
  43.1 2.1 %hidden.2.refs_3_.hidden_ref = bf16[128,512]{1,0:T(8,128)(2,1)S(1)} custom-call(s32[1]{0:T(128)} %bitcast.expert_ref, bf16[64,7296]{1,0:T(8,128)(2,1)S(1)} %get-tuple-element.35.mine_ref, bf16[2,64,3584]{2,1,0:T(8,128)(2,1)S(1)} %bitcast.20, bf16[2,64,3712]{2,1,0:T(8,128)(2,1)S(1)} %bitcast.19, bf16[1,7168,512]{2,1,0:T(8,128)(2,1)S(1)} %bitcast.7, ...), custom_call_target="tpu_custom_call" | custom-call | flops 1000 | bytes 1000 | tf_op jit(solution)/shard_map/hidden/pallas_call | solution.py:232
  45.2 0.4 collective-permute-done.7.refs_0_
  45.5 2.1 %hidden.3.hidden_ref = bf16[128,512]{1,0:T(8,128)(2,1)S(1)} custom-call(s32[1]{0:T(128)} %bitcast.expert_ref, bf16[64,7296]{1,0:T(8,128)(2,1)S(1)} %get-tuple-element.39.refs_4_.mine_ref, bf16[64,7296]{1,0:T(8,128)(2,1)S(1)} %collective-permute-done.7.refs_0_, bf16[1,7168,512]{2,1,0:T(8,128)(2,1)S(1)} %bitcast.7, ...), custom_call_target="tpu_custom_call" | custom-call | flops 1000 | bytes 1000 | tf_op jit(solution)/shard_map/hidden/pallas_call | solution.py:232
  47.6 1.1 %down.2 = (bf16[64,7168]{1,0:T(8,128)(2,1)S(1)}, bf16[64,7168]{1,0:T(8,128)(2,1)S(1)}) custom-call(bf16[128,512]{1,0:T(8,128)(2,1)S(1)} %hidden.3.hidden_ref, bf16[1,512,7168]{2,1,0:T(8,128)(2,1)S(1)} %bitcast.9, bf16[64,3712]{1,0:T(8,128)(2,1)S(1)} %bitcast.17), custom_call_target="tpu_custom_call" | custom-call | flops 1000 | bytes 1000 | tf_op jit(solution)/shard_map/down/pallas_call | solution.py:254
  49.0 1.1 %down.3 = (bf16[64,7168]{1,0:T(8,128)(2,1)S(1)}, bf16[64,7168]{1,0:T(8,128)(2,1)S(1)}) custom-call(bf16[128,512]{1,0:T(8,128)(2,1)S(1)} %hidden.2.refs_3_.hidden_ref, bf16[1,512,7168]{2,1,0:T(8,128)(2,1)S(1)} %bitcast.9, bf16[64,7168]{1,0:T(8,128)(2,1)S(1)} %get-tuple-element.41.after_ref.mine_ref), custom_call_target="tpu_custom_call" | custom-call | flops 1000 | bytes 1000 | tf_op jit(solution)/shard_map/down/pallas_call | solution.py:254
  50.1 0.4 collective-permute-start.8
  50.6 0.4 places.2.after_ref.place_ref
  51.0 0.4 places.3.after_ref.place_ref
  51.5 0.7 spread.2
  52.1 0.4 collective-permute-start.10
  52.5 0.3 collective-permute-start.12
  52.9 3.2 %collective-permute-start.16 = (bf16[64,3584]{1,0:T(8,128)(2,1)S(1)}, bf16[64,3584]{1,0:T(8,128)(2,1)S(1)}, u32[]{:S(2)}, u32[]{:S(2)}) collective-permute-start(bf16[64,3584]{1,0:T(8,128)(2,1)S(1)} %get-tuple-element.45.after_ref), channel_id=1, source_target_pairs={{0,126},{1,43},{2,124},{3,41},{4,122},{5,47},{6,120},{7,45},{8,118... | collective-permute-start | bytes 1376264 | tf_op jit(solution)/shard_map/ppermute | solution.py:78
  56.1 0.6 spread.3
  56.7 3.1 %collective-permute-done.10 = bf16[64,3584]{1,0:T(8,128)(2,1)S(1)} collective-permute-done((bf16[64,3584]{1,0:T(8,128)(2,1)S(1)}, bf16[64,3584]{1,0:T(8,128)(2,1)S(1)}, u32[]{:S(2)}, u32[]{:S(2)}) %collective-permute-start.10) | collective-permute-done | bytes 458784 | tf_op jit(solution)/shard_map/ppermute | solution.py:78
  60.2 1.3 %collective-permute-start.13 = (bf16[64,3584]{1,0:T(8,128)(2,1)S(1)}, bf16[64,3584]{1,0:T(8,128)(2,1)S(1)}, u32[]{:S(2)}, u32[]{:S(2)}) collective-permute-start(bf16[64,3584]{1,0:T(8,128)(2,1)S(1)} %add_convert_fusion.2), channel_id=1, source_target_pairs={{0,96},{1,33},{2,98},{3,35},{4,100},{5,37},{6,102},{7,39},{8,104},... | collective-permute-start | bytes 1376264 | tf_op jit(solution)/shard_map/ppermute | solution.py:78
  61.8 5.4 %collective-permute-done.16 = bf16[64,3584]{1,0:T(8,128)(2,1)S(1)} collective-permute-done((bf16[64,3584]{1,0:T(8,128)(2,1)S(1)}, bf16[64,3584]{1,0:T(8,128)(2,1)S(1)}, u32[]{:S(2)}, u32[]{:S(2)}) %collective-permute-start.16) | collective-permute-done | bytes 458784 | tf_op jit(solution)/shard_map/ppermute | solution.py:78
  67.2 3.2 %collective-permute-done.11 = bf16[64,3584]{1,0:T(8,128)(2,1)S(1)} collective-permute-done((bf16[64,3584]{1,0:T(8,128)(2,1)S(1)}, bf16[64,3584]{1,0:T(8,128)(2,1)S(1)}, u32[]{:S(2)}, u32[]{:S(2)}) %collective-permute-start.11) | collective-permute-done | bytes 458784 | tf_op jit(solution)/shard_map/ppermute | solution.py:78
  70.4 1.7 %collective-permute-done.13 = bf16[64,3584]{1,0:T(8,128)(2,1)S(1)} collective-permute-done((bf16[64,3584]{1,0:T(8,128)(2,1)S(1)}, bf16[64,3584]{1,0:T(8,128)(2,1)S(1)}, u32[]{:S(2)}, u32[]{:S(2)}) %collective-permute-start.13) | collective-permute-done | bytes 458784 | tf_op jit(solution)/shard_map/ppermute | solution.py:78
  72.1 0.3 fusion
  72.3 14.6 %all_to_all.11.parts_ref = bf16[8,8,3584]{2,1,0:T(8,128)(2,1)S(1)} all-to-all(bf16[8,8,3584]{2,1,0:T(8,128)(2,1)S(1)} %fusion), channel_id=1, replica_groups={{0,2,8,10,32,34,40,42},{1,7,25,31,97,103,121,127},{3,5,27,29,99,101,123..., dimensions={0} | all-to-all | bytes 917504 | tf_op jit(solution)/shard_map/all_to_all | solution.py:74
  87.0 0.7 finish.1
  (32 shorter events, 1.3 us)
Async XLA Ops:
  22.0 21.1 %slice-start = ((s8[7340032]{0:T(1024)(128)(4,1)}), s8[4194304]{0:T(1024)(128)(4,1)S(1)}, s32[]{:S(2)}) async-start(s8[7340032]{0:T(1024)(128)(4,1)} %bitcast.6), calls=%async_computation.2 | async-start | bytes 8388608
  22.0 21.1 %slice-start.1 = ((s8[7340032]{0:T(1024)(128)(4,1)}), s8[3145728]{0:T(1024)(128)(4,1)S(1)}, s32[]{:S(2)}) async-start(s8[7340032]{0:T(1024)(128)(4,1)} %bitcast.6), calls=%async_computation.3 | async-start | bytes 6291456
  22.0 7.5 %collective-permute-start.2 = (bf16[64,3712]{1,0:T(8,128)(2,1)S(1)}, bf16[64,3712]{1,0:T(8,128)(2,1)S(1)}, u32[]{:S(2)}, u32[]{:S(2)}) collective-permute-start(bf16[64,3712]{1,0:T(8,128)(2,1)S(1)} %bitcast.10), channel_id=1, source_target_pairs={{0,6},{1,3},{2,4},{3,1},{4,2},{5,7},{6,0},{7,5},{8,14},{9,11},{10,... | collective-permute-start | bytes 1425416 | tf_op jit(solution)/shard_map/ppermute | solution.py:78
  22.0 7.6 %collective-permute-start.1 = (bf16[64,3712]{1,0:T(8,128)(2,1)S(1)}, bf16[64,3712]{1,0:T(8,128)(2,1)S(1)}, u32[]{:S(2)}, u32[]{:S(2)}) collective-permute-start(bf16[64,3712]{1,0:T(8,128)(2,1)S(1)} %bitcast.11), channel_id=1, source_target_pairs={{0,96},{1,33},{2,98},{3,35},{4,100},{5,37},{6,102},{7,39},{8,104},... | collective-permute-start | bytes 1425416 | tf_op jit(solution)/shard_map/ppermute | solution.py:78
  22.1 7.9 %collective-permute-start = (bf16[64,3712]{1,0:T(8,128)(2,1)S(1)}, bf16[64,3712]{1,0:T(8,128)(2,1)S(1)}, u32[]{:S(2)}, u32[]{:S(2)}) collective-permute-start(bf16[64,3712]{1,0:T(8,128)(2,1)S(1)} %bitcast.12), channel_id=1, source_target_pairs={{0,24},{1,9},{2,26},{3,11},{4,28},{5,13},{6,30},{7,15},{8,16},{9,1... | collective-permute-start | bytes 1425416 | tf_op jit(solution)/shard_map/ppermute | solution.py:78
  22.2 17.4 %collective-permute-start.6 = (bf16[64,3712]{1,0:T(8,128)(2,1)S(1)}, bf16[64,3712]{1,0:T(8,128)(2,1)S(1)}, u32[]{:S(2)}, u32[]{:S(2)}) collective-permute-start(bf16[64,3712]{1,0:T(8,128)(2,1)S(1)} %bitcast.13), channel_id=1, source_target_pairs={{0,126},{1,43},{2,124},{3,41},{4,122},{5,47},{6,120},{7,45},{8,118... | collective-permute-start | bytes 1425416 | tf_op jit(solution)/shard_map/ppermute | solution.py:78
  29.5 12.5 %collective-permute-start.4 = (bf16[64,3712]{1,0:T(8,128)(2,1)S(1)}, bf16[64,3712]{1,0:T(8,128)(2,1)S(1)}, u32[]{:S(2)}, u32[]{:S(2)}) collective-permute-start(bf16[64,3712]{1,0:T(8,128)(2,1)S(1)} %collective-permute-done.2.refs_2_.c_ref), channel_id=1, source_target_pairs={{0,96},{1,33},{2,98},{3,35},{4,100},{5,37},{6,102},{7,39},{8,104},... | collective-permute-start | bytes 1425416 | tf_op jit(solution)/shard_map/ppermute | solution.py:78
  29.6 12.5 %collective-permute-start.3 = (bf16[64,3712]{1,0:T(8,128)(2,1)S(1)}, bf16[64,3712]{1,0:T(8,128)(2,1)S(1)}, u32[]{:S(2)}, u32[]{:S(2)}) collective-permute-start(bf16[64,3712]{1,0:T(8,128)(2,1)S(1)} %collective-permute-done.1.refs_1_.b_ref), channel_id=1, source_target_pairs={{0,24},{1,9},{2,26},{3,11},{4,28},{5,13},{6,30},{7,15},{8,16},{9,1... | collective-permute-start | bytes 1425416 | tf_op jit(solution)/shard_map/ppermute | solution.py:78
  29.9 12.1 %collective-permute-start.5 = (bf16[64,3712]{1,0:T(8,128)(2,1)S(1)}, bf16[64,3712]{1,0:T(8,128)(2,1)S(1)}, u32[]{:S(2)}, u32[]{:S(2)}) collective-permute-start(bf16[64,3712]{1,0:T(8,128)(2,1)S(1)} %collective-permute-done.refs_0_.a_ref), channel_id=1, source_target_pairs={{0,6},{1,3},{2,4},{3,1},{4,2},{5,7},{6,0},{7,5},{8,14},{9,11},{10,... | collective-permute-start | bytes 1425416 | tf_op jit(solution)/shard_map/ppermute | solution.py:78
  42.0 5.6 %slice-start.2 = ((s8[7340032]{0:T(1024)(128)(4,1)}), s8[4194304]{0:T(1024)(128)(4,1)S(1)}, s32[]{:S(2)}) async-start(s8[7340032]{0:T(1024)(128)(4,1)} %bitcast.8), calls=%async_computation.4 | async-start | bytes 8388608
  43.0 2.6 %collective-permute-start.7 = (bf16[64,7296]{1,0:T(8,128)(2,1)S(1)}, bf16[64,7296]{1,0:T(8,128)(2,1)S(1)}, u32[]{:S(2)}, u32[]{:S(2)}) collective-permute-start(bf16[64,7296]{1,0:T(8,128)(2,1)S(1)} %get-tuple-element.40), channel_id=1, source_target_pairs={{0,1},{1,0},{2,3},{3,2},{4,5},{5,4},{6,7},{7,6},{8,9},{9,8},{10,11... | collective-permute-start | bytes 2801672 | tf_op jit(solution)/shard_map/ppermute | solution.py:86
  43.1 4.5 %slice-start.3 = ((s8[7340032]{0:T(1024)(128)(4,1)}), s8[3145728]{0:T(1024)(128)(4,1)S(1)}, s32[]{:S(2)}) async-start(s8[7340032]{0:T(1024)(128)(4,1)} %bitcast.8), calls=%async_computation.5 | async-start | bytes 6291456
  48.8 2.7 %collective-permute-start.9 = (bf16[64,7168]{1,0:T(8,128)(2,1)S(1)}, bf16[64,7168]{1,0:T(8,128)(2,1)S(1)}, u32[]{:S(2)}, u32[]{:S(2)}) collective-permute-start(bf16[64,7168]{1,0:T(8,128)(2,1)S(1)} %get-tuple-element.44), channel_id=1, source_target_pairs={{0,1},{1,0},{2,3},{3,2},{4,5},{5,4},{6,7},{7,6},{8,9},{9,8},{10,11... | collective-permute-start | bytes 2752520 | tf_op jit(solution)/shard_map/ppermute | solution.py:86
  50.1 5.9 %collective-permute-start.8 = (bf16[64,7168]{1,0:T(8,128)(2,1)S(1)}, bf16[64,7168]{1,0:T(8,128)(2,1)S(1)}, u32[]{:S(2)}, u32[]{:S(2)}) collective-permute-start(bf16[64,7168]{1,0:T(8,128)(2,1)S(1)} %get-tuple-element.43), channel_id=1, source_target_pairs={{0,1},{1,0},{2,3},{3,2},{4,5},{5,4},{6,7},{7,6},{8,9},{9,8},{10,11... | collective-permute-start | bytes 2752520 | tf_op jit(solution)/shard_map/ppermute | solution.py:86
  52.1 7.7 %collective-permute-start.10 = (bf16[64,3584]{1,0:T(8,128)(2,1)S(1)}, bf16[64,3584]{1,0:T(8,128)(2,1)S(1)}, u32[]{:S(2)}, u32[]{:S(2)}) collective-permute-start(bf16[64,3584]{1,0:T(8,128)(2,1)S(1)} %get-tuple-element.48), channel_id=1, source_target_pairs={{0,96},{1,33},{2,98},{3,35},{4,100},{5,37},{6,102},{7,39},{8,104},... | collective-permute-start | bytes 1376264 | tf_op jit(solution)/shard_map/ppermute | solution.py:78
  52.5 7.6 %collective-permute-start.12 = (bf16[64,3584]{1,0:T(8,128)(2,1)S(1)}, bf16[64,3584]{1,0:T(8,128)(2,1)S(1)}, u32[]{:S(2)}, u32[]{:S(2)}) collective-permute-start(bf16[64,3584]{1,0:T(8,128)(2,1)S(1)} %get-tuple-element.50), channel_id=1, source_target_pairs={{0,6},{1,3},{2,4},{3,1},{4,2},{5,7},{6,0},{7,5},{8,14},{9,11},{10,... | collective-permute-start | bytes 1376264 | tf_op jit(solution)/shard_map/ppermute | solution.py:78
  52.9 8.7 %collective-permute-start.14 = (bf16[64,3584]{1,0:T(8,128)(2,1)S(1)}, bf16[64,3584]{1,0:T(8,128)(2,1)S(1)}, u32[]{:S(2)}, u32[]{:S(2)}) collective-permute-start(bf16[64,3584]{1,0:T(8,128)(2,1)S(1)} %get-tuple-element.52), channel_id=1, source_target_pairs={{0,24},{1,9},{2,26},{3,11},{4,28},{5,13},{6,30},{7,15},{8,16},{9,1... | collective-permute-start | bytes 1376264 | tf_op jit(solution)/shard_map/ppermute | solution.py:78
  52.9 14.3 %collective-permute-start.16 = (bf16[64,3584]{1,0:T(8,128)(2,1)S(1)}, bf16[64,3584]{1,0:T(8,128)(2,1)S(1)}, u32[]{:S(2)}, u32[]{:S(2)}) collective-permute-start(bf16[64,3584]{1,0:T(8,128)(2,1)S(1)} %get-tuple-element.45.after_ref), channel_id=1, source_target_pairs={{0,126},{1,43},{2,124},{3,41},{4,122},{5,47},{6,120},{7,45},{8,118... | collective-permute-start | bytes 1376264 | tf_op jit(solution)/shard_map/ppermute | solution.py:78
  60.0 10.4 %collective-permute-start.11 = (bf16[64,3584]{1,0:T(8,128)(2,1)S(1)}, bf16[64,3584]{1,0:T(8,128)(2,1)S(1)}, u32[]{:S(2)}, u32[]{:S(2)}) collective-permute-start(bf16[64,3584]{1,0:T(8,128)(2,1)S(1)} %add_convert_fusion.3), channel_id=1, source_target_pairs={{0,24},{1,9},{2,26},{3,11},{4,28},{5,13},{6,30},{7,15},{8,16},{9,1... | collective-permute-start | bytes 1376264 | tf_op jit(solution)/shard_map/ppermute | solution.py:78
  60.2 11.8 %collective-permute-start.13 = (bf16[64,3584]{1,0:T(8,128)(2,1)S(1)}, bf16[64,3584]{1,0:T(8,128)(2,1)S(1)}, u32[]{:S(2)}, u32[]{:S(2)}) collective-permute-start(bf16[64,3584]{1,0:T(8,128)(2,1)S(1)} %add_convert_fusion.2), channel_id=1, source_target_pairs={{0,96},{1,33},{2,98},{3,35},{4,100},{5,37},{6,102},{7,39},{8,104},... | collective-permute-start | bytes 1376264 | tf_op jit(solution)/shard_map/ppermute | solution.py:78
  61.6 10.4 %collective-permute-start.15 = (bf16[64,3584]{1,0:T(8,128)(2,1)S(1)}, bf16[64,3584]{1,0:T(8,128)(2,1)S(1)}, u32[]{:S(2)}, u32[]{:S(2)}) collective-permute-start(bf16[64,3584]{1,0:T(8,128)(2,1)S(1)} %add_convert_fusion.1), channel_id=1, source_target_pairs={{0,6},{1,3},{2,4},{3,1},{4,2},{5,7},{6,0},{7,5},{8,14},{9,11},{10,... | collective-permute-start | bytes 1376264 | tf_op jit(solution)/shard_map/ppermute | solution.py:78
